TPU v7x, 32 devices: a whole 2x2x4 slice. The times are simulated.
32 devices in a mesh: fsdp: 8 (over z, x), ctx: 4 (over y, core).
Axes of the slice: x: 2, y: 2, z: 4, core: 2. Of those that a mesh axis runs over, the one named last changes fastest.
Arguments:
- tokens: bfloat16 [512, 4096], P('ctx'), may hold values from -6 to 6
- in_weight: bfloat16 [4096, 3, 4096], P('ctx', None, 'fsdp'), may hold values from -0.09375 to 0.09375
- conv_taps: float32 [7, 3, 4096], P(None, None, 'fsdp'), may hold values from -2 to 2
- decay_rate: float32 [16, 4096], P(None, 'fsdp'), may hold values from 3.90625e-05 to 0.05
- residue: float32 [16, 4096], P(None, 'fsdp'), may hold values from -1.5 to 1.5
- skip_gain: float32 [4096], P('fsdp'), may hold values from -3 to 3
- out_weight: bfloat16 [4096, 4096], P('ctx', 'fsdp'), may hold values from -0.09375 to 0.09375
- grad_mixed: bfloat16 [512, 4096], P('ctx'), may hold values from -6 to 6
Outputs:
- mixed: bfloat16 [512, 4096], P('ctx', 'fsdp')
- grad_tokens: bfloat16 [512, 4096], P('ctx', 'fsdp')
- grad_in_weight: float32 [4096, 3, 4096], P('ctx', None, 'fsdp')
- grad_out_weight: float32 [4096, 4096], P('ctx', 'fsdp')
All inputs are finite; a program needn't handle non-finite values.
Results may differ from a plain program's by a relative error of at most 0.014.
Values may be sent and summed in bfloat16 or wider, within the bound.
No kernel may reach another device: no remote copies, remote signals or barrier semaphores. Data moves between devices by JAX's collectives and lax.ppermute only.
A program may use at most 128 MiB of HBM per device.

v0:
```python
import functools

import jax
import jax.numpy as jnp
from jax import lax
from jax.experimental import pallas as pl
from jax.experimental.pallas import tpu as pltpu
from jax.sharding import PartitionSpec as P

BF16 = jnp.bfloat16
F32 = jnp.float32
LANES = 128
CHUNKS = 8
MARGIN = 8
VMEM_LIMIT = 48 * 1024 * 1024


VMEM = pl.BlockSpec(memory_space=pltpu.VMEM)


def call(body, outs, scratch=(), in_specs=None, flops=0, nbytes=0):
    return pl.pallas_call(
        body,
        out_shape=outs,
        **({} if in_specs is None else {"in_specs": in_specs}),
        scratch_shapes=list(scratch),
        compiler_params=pltpu.CompilerParams(vmem_limit_bytes=VMEM_LIMIT),
        cost_estimate=pl.CostEstimate(flops=flops, bytes_accessed=nbytes, transcendentals=0),
    )


def flipped(value, axis, mask):
    count = lax.axis_size(axis)
    return lax.ppermute(value, axis, [(source, source ^ mask) for source in range(count)])


def block_at(index, size):
    return pl.ds(pl.multiple_of(index * size, size), size)


def dot(left, right, contract):
    return lax.dot_general(left, right, ((contract[:1], contract[1:]), ((), ())), preferred_element_type=F32)


def shifted(value, steps, backward):
    rows = lax.broadcasted_iota(jnp.int32, value.shape, 0)
    if backward:
        return jnp.where(rows < CHUNKS - steps, pltpu.roll(value, CHUNKS - steps, 0), 0.0)
    return jnp.where(rows >= steps, pltpu.roll(value, steps, 0), 0.0)


def modal_scan(source, target, decay, spread, gain, backward):
    poles, width = decay.shape
    steps = source.shape[0] // CHUNKS
    wide = lambda table, n: jnp.broadcast_to(table[n : n + 1, :], (CHUNKS, width))
    decays = [wide(decay, n) for n in range(poles)]

    def rows(i):
        return pl.ds(steps - 1 - i if backward else i, CHUNKS, stride=steps)

    def gather_up(i, states):
        entry = source[rows(i), :]
        return tuple(d * s + entry for d, s in zip(decays, states))

    zero = jnp.zeros((CHUNKS, width), F32)
    ends = lax.fori_loop(0, steps, gather_up, (zero,) * poles, unroll=4)
    states = []
    for n in range(poles):
        factor = wide(spread, n)
        state = shifted(ends[n], 1, backward)
        reach = 1
        while reach < CHUNKS:
            state = state + factor * shifted(state, reach, backward)
            factor = factor * factor
            reach *= 2
        states.append(state)
    gains = [wide(gain, n) for n in range(poles)]

    def advance(i, states):
        entry = source[rows(i), :]
        states = tuple(d * s + entry for d, s in zip(decays, states))
        terms = [g * s for g, s in zip(gains, states)]
        while len(terms) > 1:
            terms = [a + b for a, b in zip(terms[::2], terms[1::2])]
        target[rows(i), :] = terms[0]
        return states

    lax.fori_loop(0, steps, advance, tuple(states), unroll=2)


def row_blocks(length):
    size = 64 if length % 64 == 0 else length
    return [(start, size) for start in range(0, length, size)]


def forward_body(parts, kinds, taps, decay, spread, gain, skip, query, key, value, long_out, gated, feats, signal, summed):
    length, width = query.shape
    blocks = row_blocks(length)
    for j in range(3):
        feats[j, :MARGIN, :] = jnp.zeros((MARGIN, width), F32)
        for start, size in blocks:
            total = kinds(parts, j, pl.ds(start, size))
            feats[j, MARGIN + start : MARGIN + start + size, :] = total.astype(BF16).astype(F32)
    for start, size in blocks:
        mixed = []
        for j in range(3):
            total = taps[j, 0:1, :] * feats[j, MARGIN + start : MARGIN + start + size, :]
            for lag in range(1, taps.shape[1]):
                first = MARGIN + start - lag
                total = total + taps[j, lag : lag + 1, :] * feats[j, first : first + size, :]
            mixed.append(total)
        at = slice(start, start + size)
        query[at, :], key[at, :], value[at, :] = mixed
        signal[at, :] = mixed[1] * mixed[2]
    modal_scan(signal, summed, decay[...], spread[...], gain[...], False)
    for start, size in blocks:
        at = slice(start, start + size)
        result = summed[at, :] + skip[...] * signal[at, :]
        long_out[at, :] = result
        gated[at, :] = (query[at, :] * result).astype(BF16)


def backward_body(parts, kinds, taps, decay, spread, gain, skip, query, key, value, long_out, grads, mixin, grad_long, summed):
    length, width = query.shape
    blocks = row_blocks(length)
    for start, size in blocks:
        at = slice(start, start + size)
        grad_gated = kinds(parts, 0, pl.ds(start, size))
        mixin[0, at, :] = grad_gated * long_out[at, :]
        grad_long[at, :] = grad_gated * query[at, :]
    modal_scan(grad_long, summed, decay[...], spread[...], gain[...], True)
    for start, size in blocks:
        at = slice(start, start + size)
        grad_signal = summed[at, :] + skip[...] * grad_long[at, :]
        mixin[1, at, :] = grad_signal * value[at, :]
        mixin[2, at, :] = grad_signal * key[at, :]
    for j in range(3):
        mixin[j, length : length + MARGIN, :] = jnp.zeros((MARGIN, width), F32)
        for start, size in blocks:
            total = taps[j, 0:1, :] * mixin[j, start : start + size, :]
            for lag in range(1, taps.shape[1]):
                total = total + taps[j, lag : lag + 1, :] * mixin[j, start + lag : start + lag + size, :]
            grads[j, start : start + size, :] = total.astype(BF16)


def sum_of_three(parts, j, at):
    own, near, far = parts
    return own[j, at, :] + near[j, at, :].astype(F32) + far[j, at, :].astype(F32)


def plain(parts, j, at):
    return parts[0][j, at, :].astype(F32)


def filter_forward(parts, kinds, tables, length, width):
    count = len(parts)

    def body(*refs):
        forward_body(refs[:count], kinds, *refs[count:])

    wide = jax.ShapeDtypeStruct((length, width), F32)
    return call(
        body,
        (wide, wide, wide, wide, jax.ShapeDtypeStruct((length, width), BF16)),
        [
            pltpu.VMEM((3, MARGIN + length, width), F32),
            pltpu.VMEM((length, width), F32),
            pltpu.VMEM((length, width), F32),
        ],
        flops=200 * length * width,
        nbytes=40 * length * width,
    )(*parts, *tables)


def filter_backward(parts, kinds, tables, saved, length, width):
    count = len(parts)

    def body(*refs):
        backward_body(refs[:count], kinds, *refs[count:])

    return call(
        body,
        jax.ShapeDtypeStruct((3, length, width), BF16),
        [
            pltpu.VMEM((3, length + MARGIN, width), F32),
            pltpu.VMEM((length, width), F32),
            pltpu.VMEM((length, width), F32),
        ],
        flops=200 * length * width,
        nbytes=40 * length * width,
    )(*parts, *tables, *saved)


HBM = pl.BlockSpec(memory_space=pl.ANY)


def own_columns(rows):
    me = lax.axis_index("ctx")
    side = lax.axis_index("fsdp") & 1
    width = rows.shape[1] // 4
    part = lambda mask: lax.dynamic_slice_in_dim(rows, (me ^ mask) * width, width, 1)
    pairs = [(4 * f + k, 4 * f + (k ^ 2 ^ (f & 1))) for f in range(8) for k in range(4)]
    fetched = lax.ppermute(part(2 ^ side), ("fsdp", "ctx"), pairs)
    return part(0), flipped(part(1), "ctx", 1), fetched, flipped(fetched, "fsdp", 1)


def project(pieces, weight, after=()):
    groups, depth, channels = weight.shape
    part = pieces[0].shape[0]
    length = 4 * part
    width = channels // 4

    def body(a, b, c, d, weight, *refs):
        held, own, far, give, give_far, product = refs[len(after) :]
        me = lax.axis_index("ctx")
        side = lax.axis_index("fsdp") & 1
        for mask, piece in ((0, a), (1, b), (2 ^ side, c), (3 ^ side, d)):
            held[block_at(me ^ mask, part), :] = piece[...]
        for j in range(groups):
            product[...] = dot(held[...], weight[j], (1, 0))
            own[j] = product[:, block_at(me, width)]
            far[j] = product[:, block_at(me ^ 2, width)].astype(BF16)
            give[j] = product[:, block_at(me ^ 1, width)].astype(BF16)
            give_far[j] = product[:, block_at(me ^ 3, width)].astype(BF16)

    sums = jax.ShapeDtypeStruct((groups, length, width), BF16)
    return call(
        body,
        (
            jax.ShapeDtypeStruct((length, depth), BF16),
            jax.ShapeDtypeStruct((groups, length, width), F32),
            sums,
            sums,
            sums,
        ),
        [pltpu.VMEM((length, channels), F32)],
        in_specs=[VMEM] * 5 + [HBM] * len(after),
    )(*pieces, weight, *after)


def add_pair(left, right, after):
    def body(left, right, *refs):
        refs[-1][...] = (left[...].astype(F32) + right[...].astype(F32)).astype(BF16)

    return call(body, jax.ShapeDtypeStruct(left.shape, BF16), in_specs=[VMEM] * 2 + [HBM] * len(after))(
        left, right, *after
    )


def channel_sums(projected, after=()):
    own, far, give, give_far = projected
    passed = add_pair(far, flipped(give_far, "ctx", 1), after)
    return own, flipped(give, "ctx", 1), flipped(passed, "ctx", 2)


def all_channels(value):
    far = flipped(value, "ctx", 2)
    return value, far, flipped(value, "ctx", 1), flipped(far, "ctx", 1)


def output_halves(gathered, weight, after=()):
    groups, length, width = gathered[0].shape
    depth = weight.shape[1]
    piece = depth // 4
    channels = 4 * width
    side = lambda: lax.axis_index("fsdp") & 1

    def product(whole, weight, index):
        total = None
        for j in range(groups):
            term = dot(whole[j], weight[j, block_at(index, piece), :], (1, 1))
            total = term if total is None else total + term
        return total.astype(BF16)

    def first_body(own, far, near, near_far, weight, *refs):
        whole, give = refs[len(after) :]
        me = lax.axis_index("ctx")
        for j in range(groups):
            for mask, value in ((0, own), (2, far), (1, near), (3, near_far)):
                whole[j, :, block_at(me ^ mask, width)] = value[j]
        give[...] = product(whole, weight, 2 - 2 * side())

    def second_body(whole, weight, give, keep, keep_second):
        give[...] = product(whole, weight, 3 - 2 * side())
        keep[...] = product(whole, weight, 2 * side())
        keep_second[...] = product(whole, weight, 2 * side() + 1)

    part = jax.ShapeDtypeStruct((length, piece), BF16)
    whole, give = call(
        first_body,
        (jax.ShapeDtypeStruct((groups, length, channels), BF16), part),
        in_specs=[VMEM] * 5 + [HBM] * len(after),
    )(*gathered, weight, *after)
    give_second, keep, keep_second = call(second_body, (part,) * 3)(whole, weight)
    return whole, (keep, keep_second), (give, give_second)


def split_sum(keep, given, after=()):
    length, width = keep.shape
    part = length // 4

    def body(keep, given, *refs):
        place = lax.axis_index("fsdp") >> 1
        for mask, out in enumerate(refs[len(after) :]):
            at = block_at(place ^ mask, part)
            out[...] = (keep[at, :].astype(F32) + given[at, :].astype(F32)).astype(BF16)

    return call(
        body, (jax.ShapeDtypeStruct((part, width), BF16),) * 4, in_specs=[VMEM] * 2 + [HBM] * len(after)
    )(keep, given, *after)


def placed(block, mask):
    pairs = []
    for f in range(8):
        for k in range(4):
            z, x = f // 2, f % 2
            pairs.append((4 * f + k, 4 * (2 * k + x) + (z ^ mask)))
    return lax.ppermute(block, ("fsdp", "ctx"), pairs)


def join(quarters):
    part, width = quarters[0][0].shape

    def body(*refs):
        out = refs[-1]
        for half in range(2):
            total = refs[4 * half][...].astype(F32)
            for ref in refs[4 * half + 1 : 4 * half + 4]:
                total = total + ref[...].astype(F32)
            out[:, half * width : (half + 1) * width] = total.astype(BF16)

    return call(body, jax.ShapeDtypeStruct((part, 2 * width), BF16))(*quarters[0], *quarters[1])


def block_sums(keeps, givens):
    quarters = []
    for keep, given in zip(keeps, givens):
        blocks = split_sum(keep, given)
        quarters.append([placed(block, mask) for mask, block in enumerate(blocks)])
    return join(quarters)


def weight_gradient(rows, values):
    length, depth = rows.shape
    groups, _, channels = values.shape
    tile = 256

    def body(rows, values, out):
        out[0] = dot(rows[...], values[0], (0, 0))

    return pl.pallas_call(
        body,
        out_shape=jax.ShapeDtypeStruct((groups, depth, channels), F32),
        grid=(groups, depth // tile),
        in_specs=[
            pl.BlockSpec((length, tile), lambda j, i: (0, i)),
            pl.BlockSpec((1, length, channels), lambda j, i: (j, 0, 0)),
        ],
        out_specs=pl.BlockSpec((1, tile, channels), lambda j, i: (j, i, 0)),
        compiler_params=pltpu.CompilerParams(vmem_limit_bytes=VMEM_LIMIT),
        cost_estimate=pl.CostEstimate(
            flops=2 * length * depth * channels * groups,
            bytes_accessed=4 * groups * depth * channels,
            transcendentals=0,
        ),
    )(rows, values)


def four_by_eight(tokens, weights, tables, out_weight, grad_mixed):
    length, width = 4 * tokens.shape[0], weights.shape[2] // 4
    token_pieces = own_columns(tokens)
    grad_pieces = own_columns(grad_mixed)
    whole_tokens, *projected = project(token_pieces, weights, grad_pieces[2:3])
    feats = channel_sums(projected, grad_pieces[3:])
    whole_cotangents, *projected = project(grad_pieces, out_weight[None])
    grad_gated = channel_sums(projected)
    *saved, gated = filter_forward(feats, sum_of_three, tables, length, width)
    whole_gated, keeps, gives = output_halves(all_channels(gated[None]), out_weight[None])
    givens = [flipped(give, "fsdp", 1) for give in gives]
    mixed = block_sums(keeps, givens)
    grads = filter_backward(grad_gated, sum_of_three, tables, saved, length, width)
    whole_grads, keeps, gives = output_halves(all_channels(grads), weights, givens[:1])
    grad_tokens = block_sums(keeps, [flipped(give, "fsdp", 1) for give in gives])
    grad_in = weight_gradient(whole_tokens, whole_grads)
    grad_out = weight_gradient(whole_cotangents, whole_gated)[0]
    return mixed, grad_tokens, grad_in, grad_out


def to_placement(value):
    count = lax.axis_size("ctx")
    ratio = lax.axis_size("fsdp") // count
    pairs = []
    for f in range(ratio * count):
        for k in range(count):
            target = (k * ratio + f % ratio, f // ratio)
            pairs.append((f * count + k, target[0] * count + target[1]))
    return lax.ppermute(value, ("fsdp", "ctx"), pairs)


def any_mesh(tokens, weights, tables, out_weight, grad_mixed):
    count = lax.axis_size("ctx")
    columns = lambda rows: lax.all_to_all(rows, "ctx", split_axis=1, concat_axis=0, tiled=True)
    whole_tokens, whole_cotangents = columns(tokens), columns(grad_mixed)
    length, width = whole_tokens.shape[0], weights.shape[2] // count

    def channel_sums(rows, weight):
        partial = jnp.einsum("td,jdc->jtc", rows, weight, preferred_element_type=F32)
        return lax.psum_scatter(partial.astype(BF16), "ctx", scatter_dimension=2, tiled=True)

    def block_sums(values, weight):
        partial = jnp.einsum("jtc,jdc->td", values, weight, preferred_element_type=F32)
        ratio = lax.axis_size("fsdp") // count
        pieces = partial.astype(BF16).reshape(count, length // count, ratio, -1).transpose(0, 2, 1, 3)
        pieces = pieces.reshape(count * ratio, length // count, -1)
        return to_placement(lax.psum_scatter(pieces, "fsdp", scatter_dimension=0, tiled=True)[0])

    feats = channel_sums(whole_tokens, weights)
    grad_gated = channel_sums(whole_cotangents, out_weight[None])
    *saved, gated = filter_forward((feats,), plain, tables, length, width)
    grads = filter_backward((grad_gated,), plain, tables, saved, length, width)
    whole_gated = lax.all_gather(gated, "ctx", axis=1, tiled=True)
    whole_grads = lax.all_gather(grads, "ctx", axis=2, tiled=True)
    mixed = block_sums(whole_gated[None], out_weight[None])
    grad_tokens = block_sums(whole_grads, weights)
    grad_in = jnp.einsum("td,jtc->jdc", whole_tokens, whole_grads, preferred_element_type=F32)
    grad_out = jnp.einsum("td,tc->dc", whole_cotangents, whole_gated, preferred_element_type=F32)
    return mixed, grad_tokens, grad_in, grad_out


def per_device(tokens, in_weight, conv_taps, decay_rate, residue, skip_gain, out_weight, grad_mixed):
    count, blocks = lax.axis_size("ctx"), lax.axis_size("fsdp")
    weights = in_weight.transpose(1, 0, 2)
    length = count * tokens.shape[0]
    width = weights.shape[2] // count
    mine = lambda table: lax.dynamic_slice_in_dim(table, lax.axis_index("ctx") * width, width, table.ndim - 1)
    rate = mine(decay_rate)
    gain = mine(residue) * jnp.sqrt(-jnp.expm1(-2.0 * rate))
    tables = (mine(conv_taps.transpose(1, 0, 2)), jnp.exp(-rate), jnp.exp(-rate * (length // CHUNKS)), gain, mine(skip_gain[None]))
    tuned = count == 4 and blocks == 8 and width % LANES == 0
    plan = four_by_eight if tuned else any_mesh
    mixed, grad_tokens, grad_in, grad_out = plan(tokens, weights, tables, out_weight, grad_mixed)
    return mixed, grad_tokens, grad_in.transpose(1, 0, 2), grad_out


def solution(mesh):
    return jax.shard_map(
        per_device,
        mesh=mesh,
        in_specs=(
            P("ctx", None),
            P("ctx", None, "fsdp"),
            P(None, None, "fsdp"),
            P(None, "fsdp"),
            P(None, "fsdp"),
            P("fsdp"),
            P("ctx", "fsdp"),
            P("ctx", None),
        ),
        out_specs=(P("ctx", "fsdp"), P("ctx", "fsdp"), P("ctx", None, "fsdp"), P("ctx", "fsdp")),
        check_vma=False,
    )
```

profile of v0, /device:TPU:1, one launch (start us, length us, event | category | flops | bytes accessed | tf_op | source)
XLA Modules:
  0.0 137.2 jit_solution(8233663991518065697)
XLA Ops:
  1.8 2.1 %collective-permute-start.1 = (bf16[128,1024]{1,0:T(8,128)(2,1)S(1)}, bf16[128,1024]{1,0:T(8,128)(2,1)S(1)}, u32[]{:S(2)}, u32[]{:S(2)}) collective-permute-start(bf16[128,1024]{1,0:T(8,128)(2,1)S(1)} %get-tuple-element.89), channel_id=1, source_target_pairs={{0,2},{1,3},{2,0},{3,1},{4,7},{5,6},{6,5},{7,4},{8,10},{9,11},{10,... | collective-permute-start | bytes 786440 | tf_op jit(solution)/shard_map/ppermute | solution.py:203
  6.2 3.8 %collective-permute-done.1.c = bf16[128,1024]{1,0:T(8,128)(2,1)S(1)} collective-permute-done((bf16[128,1024]{1,0:T(8,128)(2,1)S(1)}, bf16[128,1024]{1,0:T(8,128)(2,1)S(1)}, u32[]{:S(2)}, u32[]{:S(2)}) %collective-permute-start.1) | collective-permute-done | bytes 262176 | tf_op jit(solution)/shard_map/ppermute | solution.py:203
  10.0 2.9 %collective-permute-start.2 = (bf16[128,1024]{1,0:T(8,128)(2,1)S(1)}, bf16[128,1024]{1,0:T(8,128)(2,1)S(1)}, u32[]{:S(2)}, u32[]{:S(2)}) collective-permute-start(bf16[128,1024]{1,0:T(8,128)(2,1)S(1)} %collective-permute-done.1.c), channel_id=1, source_target_pairs={{0,4},{4,0},{8,12},{12,8},{16,20},{20,16},{24,28},{28,24},{1,5},{5... | collective-permute-start | bytes 786440 | tf_op jit(solution)/shard_map/ppermute | solution.py:34
  12.9 2.7 %collective-permute-done.3.refs_0_.c = bf16[128,1024]{1,0:T(8,128)(2,1)S(1)} collective-permute-done((bf16[128,1024]{1,0:T(8,128)(2,1)S(1)}, bf16[128,1024]{1,0:T(8,128)(2,1)S(1)}, u32[]{:S(2)}, u32[]{:S(2)}) %collective-permute-start.3) | collective-permute-done | bytes 262176 | tf_op jit(solution)/shard_map/ppermute | solution.py:203
  15.6 3.0 %collective-permute-done.2.d = bf16[128,1024]{1,0:T(8,128)(2,1)S(1)} collective-permute-done((bf16[128,1024]{1,0:T(8,128)(2,1)S(1)}, bf16[128,1024]{1,0:T(8,128)(2,1)S(1)}, u32[]{:S(2)}, u32[]{:S(2)}) %collective-permute-start.2) | collective-permute-done | bytes 262176 | tf_op jit(solution)/shard_map/ppermute | solution.py:34
  18.7 5.0 %shard_map.111 = (bf16[512,1024]{1,0:T(8,128)(2,1)S(1)}, f32[3,512,128]{2,1,0:T(8,128)S(1)}, bf16[3,512,128]{2,1,0:T(8,128)(2,1)S(1)}, bf16[3,512,128]{2,1,0:T(8,128)(2,1)}, bf16[3,512,128]{2,1,0:T(8,128)(2,1)S(1)}) custom-call(bf16[128,1024]{1,0:T(8,128)(2,1)S(1)} %get-tuple-element.90.a, bf16[128,1024]{1,0:T(8,128)(2,1)S(1)} %collective-permute-done.b, ...), custom_call_target="tpu_custom_call" | custom-call | tf_op jit(solution)/shard_map/pallas_call | solution.py:227
  24.6 1.5 %collective-permute-start.5 = (bf16[3,512,128]{2,1,0:T(8,128)(2,1)S(1)}, bf16[3,512,128]{2,1,0:T(8,128)(2,1)S(1)}, u32[]{:S(2)}, u32[]{:S(2)}) collective-permute-start(bf16[3,512,128]{2,1,0:T(8,128)(2,1)S(1)} %get-tuple-element.48), channel_id=1, source_target_pairs={{0,1},{1,0},{2,3},{3,2},{4,5},{5,4},{6,7},{7,6},{8,9},{9,8},{10,11... | collective-permute-start | bytes 1179656 | tf_op jit(solution)/shard_map/ppermute | solution.py:34
  28.0 6.0 %collective-permute-done.6.refs_0_.d = bf16[128,1024]{1,0:T(8,128)(2,1)S(1)} collective-permute-done((bf16[128,1024]{1,0:T(8,128)(2,1)S(1)}, bf16[128,1024]{1,0:T(8,128)(2,1)S(1)}, u32[]{:S(2)}, u32[]{:S(2)}) %collective-permute-start.6) | collective-permute-done | bytes 262176 | tf_op jit(solution)/shard_map/ppermute | solution.py:34
  36.0 1.6 %shard_map.119 = (bf16[512,1024]{1,0:T(8,128)(2,1)S(1)}, f32[1,512,128]{2,1,0:T(8,128)S(1)}, bf16[1,512,128]{2,1,0:T(8,128)(2,1)S(1)}, bf16[1,512,128]{2,1,0:T(8,128)(2,1)S(1)}, bf16[1,512,128]{2,1,0:T(8,128)(2,1)}) custom-call(bf16[128,1024]{1,0:T(8,128)(2,1)S(1)} %get-tuple-element.88.a, bf16[128,1024]{1,0:T(8,128)(2,1)S(1)} %collective-permute-done.21.b, ...), custom_call_target="tpu_custom_call" | custom-call | tf_op jit(solution)/shard_map/pallas_call | solution.py:227
  46.1 3.3 %shard_map.113 = (f32[512,128]{1,0:T(8,128)S(1)}, f32[512,128]{1,0:T(8,128)S(1)}, f32[512,128]{1,0:T(8,128)S(1)}, f32[512,128]{1,0:T(8,128)S(1)}, bf16[512,128]{1,0:T(8,128)(2,1)S(1)}) custom-call(f32[3,512,128]{2,1,0:T(8,128)S(1)} %copy-done.4, bf16[3,512,128]{2,1,0:T(8,128)(2,1)} %collective-permute-done.4.refs_1_, ...), custom_call_target="tpu_custom_call" | custom-call | flops 13107200 | bytes 2621440 | tf_op jit(solution)/shard_map/pallas_call | solution.py:162
  49.4 2.1 %shard_map.121.own = bf16[3,512,128]{2,1,0:T(8,128)(2,1)S(1)} custom-call(f32[1,512,128]{2,1,0:T(8,128)S(1)} %get-tuple-element.63.refs_0_, bf16[1,512,128]{2,1,0:T(8,128)(2,1)S(1)} %collective-permute-done.22.refs_1_, bf16[1,512,128]{2,1,0:T(8,128)(2,1)S(1)} %collective-permute-done.24.refs_2_, f32[3,7,128]{2,1,0:T(8,128)S(1)} %dynamic-slice_bitcast_fusion.refs_3_, ...), custom_call_target="tpu_custom_call" | custom-call | flops 13107200 | bytes 2621440 | tf_op jit(solution)/shard_map/pallas_call | solution.py:181
  53.1 2.8 %collective-permute-start.9 = (bf16[1,512,128]{2,1,0:T(8,128)(2,1)S(1)}, bf16[1,512,128]{2,1,0:T(8,128)(2,1)S(1)}, u32[]{:S(2)}, u32[]{:S(2)}) collective-permute-start(bf16[1,512,128]{2,1,0:T(8,128)(2,1)S(1)} %bitcast.16), channel_id=1, source_target_pairs={{0,1},{1,0},{2,3},{3,2},{4,5},{5,4},{6,7},{7,6},{8,9},{9,8},{10,11... | collective-permute-start | bytes 393224 | tf_op jit(solution)/shard_map/ppermute | solution.py:34
  55.9 6.9 %collective-permute-done.8.far = bf16[1,512,128]{2,1,0:T(8,128)(2,1)S(1)} collective-permute-done((bf16[1,512,128]{2,1,0:T(8,128)(2,1)S(1)}, bf16[1,512,128]{2,1,0:T(8,128)(2,1)S(1)}, u32[]{:S(2)}, u32[]{:S(2)}) %collective-permute-start.8) | collective-permute-done | bytes 131104 | tf_op jit(solution)/shard_map/ppermute | solution.py:34
  62.8 3.1 %collective-permute-start.10 = (bf16[1,512,128]{2,1,0:T(8,128)(2,1)S(1)}, bf16[1,512,128]{2,1,0:T(8,128)(2,1)S(1)}, u32[]{:S(2)}, u32[]{:S(2)}) collective-permute-start(bf16[1,512,128]{2,1,0:T(8,128)(2,1)S(1)} %collective-permute-done.8.far), channel_id=1, source_target_pairs={{0,1},{1,0},{2,3},{3,2},{4,5},{5,4},{6,7},{7,6},{8,9},{9,8},{10,11... | collective-permute-start | bytes 393224 | tf_op jit(solution)/shard_map/ppermute | solution.py:34
  67.3 1.5 %collective-permute-start.11 = (bf16[512,256]{1,0:T(8,128)(2,1)S(1)}, bf16[512,256]{1,0:T(8,128)(2,1)S(1)}, u32[]{:S(2)}, u32[]{:S(2)}) collective-permute-start(bf16[512,256]{1,0:T(8,128)(2,1)S(1)} %get-tuple-element.52), channel_id=1, source_target_pairs={{0,4},{4,0},{8,12},{12,8},{16,20},{20,16},{24,28},{28,24},{1,5},{5... | collective-permute-start | bytes 786440 | tf_op jit(solution)/shard_map/ppermute | solution.py:34
  69.6 5.3 %collective-permute-done.11.given.refs_0_ = bf16[512,256]{1,0:T(8,128)(2,1)S(1)} collective-permute-done((bf16[512,256]{1,0:T(8,128)(2,1)S(1)}, bf16[512,256]{1,0:T(8,128)(2,1)S(1)}, u32[]{:S(2)}, u32[]{:S(2)}) %collective-permute-start.11) | collective-permute-done | bytes 262176 | tf_op jit(solution)/shard_map/ppermute | solution.py:34
  74.9 2.7 %shard_map.122 = (bf16[3,512,512]{2,1,0:T(8,128)(2,1)S(1)}, bf16[512,256]{1,0:T(8,128)(2,1)S(1)}) custom-call(bf16[3,512,128]{2,1,0:T(8,128)(2,1)S(1)} %shard_map.121.own, bf16[3,512,128]{2,1,0:T(8,128)(2,1)S(1)} %collective-permute-done.25.far, bf16[3,512,128]{2,1,0:T(8,128)(2,1)S(1)} %collective-permute-done.26.near, ...), custom_call_target="tpu_custom_call" | custom-call | tf_op jit(solution)/shard_map/pallas_call | solution.py:289
  77.7 1.5 %collective-permute-start.28 = (bf16[512,256]{1,0:T(8,128)(2,1)S(1)}, bf16[512,256]{1,0:T(8,128)(2,1)S(1)}, u32[]{:S(2)}, u32[]{:S(2)}) collective-permute-start(bf16[512,256]{1,0:T(8,128)(2,1)S(1)} %get-tuple-element.73), channel_id=1, source_target_pairs={{0,4},{4,0},{8,12},{12,8},{16,20},{20,16},{24,28},{28,24},{1,5},{5... | collective-permute-start | bytes 786440 | tf_op jit(solution)/shard_map/ppermute | solution.py:34
  80.8 5.6 %collective-permute-start.12 = (bf16[128,256]{1,0:T(8,128)(2,1)S(1)}, bf16[128,256]{1,0:T(8,128)(2,1)S(1)}, u32[]{:S(2)}, u32[]{:S(2)}) collective-permute-start(bf16[128,256]{1,0:T(8,128)(2,1)S(1)} %get-tuple-element.53), channel_id=1, source_target_pairs={{0,0},{1,8},{2,16},{3,24},{4,4},{5,12},{6,20},{7,28},{8,1},{9,9},{... | collective-permute-start | bytes 196616 | tf_op jit(solution)/shard_map/ppermute | solution.py:319
  86.5 3.7 %collective-permute-start.14 = (bf16[128,256]{1,0:T(8,128)(2,1)S(1)}, bf16[128,256]{1,0:T(8,128)(2,1)S(1)}, u32[]{:S(2)}, u32[]{:S(2)}) collective-permute-start(bf16[128,256]{1,0:T(8,128)(2,1)S(1)} %get-tuple-element.55), channel_id=1, source_target_pairs={{0,2},{1,10},{2,18},{3,26},{4,6},{5,14},{6,22},{7,30},{8,3},{9,11}... | collective-permute-start | bytes 196616 | tf_op jit(solution)/shard_map/ppermute | solution.py:319
  90.3 8.3 %collective-permute-start.17 = (bf16[128,256]{1,0:T(8,128)(2,1)S(1)}, bf16[128,256]{1,0:T(8,128)(2,1)S(1)}, u32[]{:S(2)}, u32[]{:S(2)}) collective-permute-start(bf16[128,256]{1,0:T(8,128)(2,1)S(1)} %get-tuple-element.59), channel_id=1, source_target_pairs={{0,0},{1,8},{2,16},{3,24},{4,4},{5,12},{6,20},{7,28},{8,1},{9,9},{... | collective-permute-start | bytes 196616 | tf_op jit(solution)/shard_map/ppermute | solution.py:319
  100.0 3.3 %collective-permute-start.19 = (bf16[128,256]{1,0:T(8,128)(2,1)S(1)}, bf16[128,256]{1,0:T(8,128)(2,1)S(1)}, u32[]{:S(2)}, u32[]{:S(2)}) collective-permute-start(bf16[128,256]{1,0:T(8,128)(2,1)S(1)} %get-tuple-element.61), channel_id=1, source_target_pairs={{0,2},{1,10},{2,18},{3,26},{4,6},{5,14},{6,22},{7,30},{8,3},{9,11}... | collective-permute-start | bytes 196616 | tf_op jit(solution)/shard_map/ppermute | solution.py:319
  103.3 1.9 %collective-permute-start.20 = (bf16[128,256]{1,0:T(8,128)(2,1)S(1)}, bf16[128,256]{1,0:T(8,128)(2,1)S(1)}, u32[]{:S(2)}, u32[]{:S(2)}) collective-permute-start(bf16[128,256]{1,0:T(8,128)(2,1)S(1)} %get-tuple-element.62), channel_id=1, source_target_pairs={{0,3},{1,11},{2,19},{3,27},{4,7},{5,15},{6,23},{7,31},{8,2},{9,10}... | collective-permute-start | bytes 196616 | tf_op jit(solution)/shard_map/ppermute | solution.py:319
  105.3 1.9 %collective-permute-start.29 = (bf16[128,256]{1,0:T(8,128)(2,1)S(1)}, bf16[128,256]{1,0:T(8,128)(2,1)S(1)}, u32[]{:S(2)}, u32[]{:S(2)}) collective-permute-start(bf16[128,256]{1,0:T(8,128)(2,1)S(1)} %get-tuple-element.74), channel_id=1, source_target_pairs={{0,0},{1,8},{2,16},{3,24},{4,4},{5,12},{6,20},{7,28},{8,1},{9,9},{... | collective-permute-start | bytes 196616 | tf_op jit(solution)/shard_map/ppermute | solution.py:319
  107.3 2.0 %collective-permute-done.19.refs_6_ = bf16[128,256]{1,0:T(8,128)(2,1)S(1)} collective-permute-done((bf16[128,256]{1,0:T(8,128)(2,1)S(1)}, bf16[128,256]{1,0:T(8,128)(2,1)S(1)}, u32[]{:S(2)}, u32[]{:S(2)}) %collective-permute-start.19) | collective-permute-done | bytes 65568 | tf_op jit(solution)/shard_map/ppermute | solution.py:319
  109.3 4.9 %collective-permute-start.31 = (bf16[128,256]{1,0:T(8,128)(2,1)S(1)}, bf16[128,256]{1,0:T(8,128)(2,1)S(1)}, u32[]{:S(2)}, u32[]{:S(2)}) collective-permute-start(bf16[128,256]{1,0:T(8,128)(2,1)S(1)} %get-tuple-element.76), channel_id=1, source_target_pairs={{0,2},{1,10},{2,18},{3,26},{4,6},{5,14},{6,22},{7,30},{8,3},{9,11}... | collective-permute-start | bytes 196616 | tf_op jit(solution)/shard_map/ppermute | solution.py:319
  114.2 2.7 %shard_map.128 = f32[1,1024,512]{2,1,0:T(8,128)} custom-call(bf16[512,1024]{1,0:T(8,128)(2,1)S(1)} %get-tuple-element.85.rows, bf16[1,512,512]{2,1,0:T(8,128)(2,1)S(1)} %get-tuple-element.50.whole.values), custom_call_target="tpu_custom_call" | custom-call | flops 536870912 | bytes 2097152 | tf_op jit(solution)/shard_map/pallas_call | solution.py:352
  117.6 1.6 %collective-permute-start.32 = (bf16[128,256]{1,0:T(8,128)(2,1)S(1)}, bf16[128,256]{1,0:T(8,128)(2,1)S(1)}, u32[]{:S(2)}, u32[]{:S(2)}) collective-permute-start(bf16[128,256]{1,0:T(8,128)(2,1)S(1)} %get-tuple-element.77), channel_id=1, source_target_pairs={{0,3},{1,11},{2,19},{3,27},{4,7},{5,15},{6,23},{7,31},{8,2},{9,10}... | collective-permute-start | bytes 196616 | tf_op jit(solution)/shard_map/ppermute | solution.py:319
  119.3 1.9 %collective-permute-start.34 = (bf16[128,256]{1,0:T(8,128)(2,1)S(1)}, bf16[128,256]{1,0:T(8,128)(2,1)S(1)}, u32[]{:S(2)}, u32[]{:S(2)}) collective-permute-start(bf16[128,256]{1,0:T(8,128)(2,1)S(1)} %get-tuple-element.80), channel_id=1, source_target_pairs={{0,0},{1,8},{2,16},{3,24},{4,4},{5,12},{6,20},{7,28},{8,1},{9,9},{... | collective-permute-start | bytes 196616 | tf_op jit(solution)/shard_map/ppermute | solution.py:319
  121.3 5.1 %collective-permute-start.36 = (bf16[128,256]{1,0:T(8,128)(2,1)S(1)}, bf16[128,256]{1,0:T(8,128)(2,1)S(1)}, u32[]{:S(2)}, u32[]{:S(2)}) collective-permute-start(bf16[128,256]{1,0:T(8,128)(2,1)S(1)} %get-tuple-element.82), channel_id=1, source_target_pairs={{0,2},{1,10},{2,18},{3,26},{4,6},{5,14},{6,22},{7,30},{8,3},{9,11}... | collective-permute-start | bytes 196616 | tf_op jit(solution)/shard_map/ppermute | solution.py:319
  126.4 7.3 %shard_map.127 = f32[3,1024,512]{2,1,0:T(8,128)} custom-call(bf16[512,1024]{1,0:T(8,128)(2,1)S(1)} %get-tuple-element.84.rows, bf16[3,512,512]{2,1,0:T(8,128)(2,1)S(1)} %get-tuple-element.71.whole.values), custom_call_target="tpu_custom_call" | custom-call | flops 1610612736 | bytes 6291456 | tf_op jit(solution)/shard_map/pallas_call | solution.py:352
  133.7 2.8 %collective-permute-done.37.refs_7_ = bf16[128,256]{1,0:T(8,128)(2,1)S(1)} collective-permute-done((bf16[128,256]{1,0:T(8,128)(2,1)S(1)}, bf16[128,256]{1,0:T(8,128)(2,1)S(1)}, u32[]{:S(2)}, u32[]{:S(2)}) %collective-permute-start.37) | collective-permute-done | bytes 65568 | tf_op jit(solution)/shard_map/ppermute | solution.py:319
  (83 shorter events, 25.2 us)
Async XLA Ops:
  1.8 8.2 %collective-permute-start.1 = (bf16[128,1024]{1,0:T(8,128)(2,1)S(1)}, bf16[128,1024]{1,0:T(8,128)(2,1)S(1)}, u32[]{:S(2)}, u32[]{:S(2)}) collective-permute-start(bf16[128,1024]{1,0:T(8,128)(2,1)S(1)} %get-tuple-element.89), channel_id=1, source_target_pairs={{0,2},{1,3},{2,0},{3,1},{4,7},{5,6},{6,5},{7,4},{8,10},{9,11},{10,... | collective-permute-start | bytes 786440 | tf_op jit(solution)/shard_map/ppermute | solution.py:203
  4.0 8.9 %collective-permute-start = (bf16[128,1024]{1,0:T(8,128)(2,1)S(1)}, bf16[128,1024]{1,0:T(8,128)(2,1)S(1)}, u32[]{:S(2)}, u32[]{:S(2)}) collective-permute-start(bf16[128,1024]{1,0:T(8,128)(2,1)S(1)} %get-tuple-element.91), channel_id=1, source_target_pairs={{0,1},{1,0},{2,3},{3,2},{4,5},{5,4},{6,7},{7,6},{8,9},{9,8},{10,11... | collective-permute-start | bytes 786440 | tf_op jit(solution)/shard_map/ppermute | solution.py:34
  6.1 9.5 %collective-permute-start.3 = (bf16[128,1024]{1,0:T(8,128)(2,1)S(1)}, bf16[128,1024]{1,0:T(8,128)(2,1)S(1)}, u32[]{:S(2)}, u32[]{:S(2)}) collective-permute-start(bf16[128,1024]{1,0:T(8,128)(2,1)S(1)} %get-tuple-element.87), channel_id=1, source_target_pairs={{0,2},{1,3},{2,0},{3,1},{4,7},{5,6},{6,5},{7,4},{8,10},{9,11},{10,... | collective-permute-start | bytes 786440 | tf_op jit(solution)/shard_map/ppermute | solution.py:203
  10.0 8.7 %collective-permute-start.2 = (bf16[128,1024]{1,0:T(8,128)(2,1)S(1)}, bf16[128,1024]{1,0:T(8,128)(2,1)S(1)}, u32[]{:S(2)}, u32[]{:S(2)}) collective-permute-start(bf16[128,1024]{1,0:T(8,128)(2,1)S(1)} %collective-permute-done.1.c), channel_id=1, source_target_pairs={{0,4},{4,0},{8,12},{12,8},{16,20},{20,16},{24,28},{28,24},{1,5},{5... | collective-permute-start | bytes 786440 | tf_op jit(solution)/shard_map/ppermute | solution.py:34
  24.6 9.4 %collective-permute-start.5 = (bf16[3,512,128]{2,1,0:T(8,128)(2,1)S(1)}, bf16[3,512,128]{2,1,0:T(8,128)(2,1)S(1)}, u32[]{:S(2)}, u32[]{:S(2)}) collective-permute-start(bf16[3,512,128]{2,1,0:T(8,128)(2,1)S(1)} %get-tuple-element.48), channel_id=1, source_target_pairs={{0,1},{1,0},{2,3},{3,2},{4,5},{5,4},{6,7},{7,6},{8,9},{9,8},{10,11... | collective-permute-start | bytes 1179656 | tf_op jit(solution)/shard_map/ppermute | solution.py:34
  26.0 7.9 %collective-permute-start.6 = (bf16[128,1024]{1,0:T(8,128)(2,1)S(1)}, bf16[128,1024]{1,0:T(8,128)(2,1)S(1)}, u32[]{:S(2)}, u32[]{:S(2)}) collective-permute-start(bf16[128,1024]{1,0:T(8,128)(2,1)S(1)} %collective-permute-done.3.refs_0_.c), channel_id=1, source_target_pairs={{0,4},{4,0},{8,12},{12,8},{16,20},{20,16},{24,28},{28,24},{1,5},{5... | collective-permute-start | bytes 786440 | tf_op jit(solution)/shard_map/ppermute | solution.py:34
  27.5 8.5 %collective-permute-start.21 = (bf16[128,1024]{1,0:T(8,128)(2,1)S(1)}, bf16[128,1024]{1,0:T(8,128)(2,1)S(1)}, u32[]{:S(2)}, u32[]{:S(2)}) collective-permute-start(bf16[128,1024]{1,0:T(8,128)(2,1)S(1)} %get-tuple-element.86), channel_id=1, source_target_pairs={{0,1},{1,0},{2,3},{3,2},{4,5},{5,4},{6,7},{7,6},{8,9},{9,8},{10,11... | collective-permute-start | bytes 786440 | tf_op jit(solution)/shard_map/ppermute | solution.py:34
  27.8 17.2 %collective-permute-start.4 = (bf16[3,512,128]{2,1,0:T(8,128)(2,1)}, bf16[3,512,128]{2,1,0:T(8,128)(2,1)}, u32[]{:S(2)}, u32[]{:S(2)}) collective-permute-start(bf16[3,512,128]{2,1,0:T(8,128)(2,1)} %get-tuple-element.46), channel_id=1, source_target_pairs={{0,1},{1,0},{2,3},{3,2},{4,5},{5,4},{6,7},{7,6},{8,9},{9,8},{10,11... | collective-permute-start | bytes 1179656 | tf_op jit(solution)/shard_map/ppermute | solution.py:34
  34.8 10.2 %collective-permute-start.7 = (bf16[3,512,128]{2,1,0:T(8,128)(2,1)}, bf16[3,512,128]{2,1,0:T(8,128)(2,1)}, u32[]{:S(2)}, u32[]{:S(2)}) collective-permute-start(bf16[3,512,128]{2,1,0:T(8,128)(2,1)} %shard_map.112), channel_id=1, source_target_pairs={{0,2},{1,3},{2,0},{3,1},{4,6},{5,7},{6,4},{7,5},{8,10},{9,11},{10,... | collective-permute-start | bytes 1179656 | tf_op jit(solution)/shard_map/ppermute | solution.py:34
  40.0 9.4 %collective-permute-start.22 = (bf16[1,512,128]{2,1,0:T(8,128)(2,1)}, bf16[1,512,128]{2,1,0:T(8,128)(2,1)S(1)}, u32[]{:S(2)}, u32[]{:S(2)}) collective-permute-start(bf16[1,512,128]{2,1,0:T(8,128)(2,1)} %copy-done.7), channel_id=1, source_target_pairs={{0,1},{1,0},{2,3},{3,2},{4,5},{5,4},{6,7},{7,6},{8,9},{9,8},{10,11... | collective-permute-start | bytes 393224 | tf_op jit(solution)/shard_map/ppermute | solution.py:34
  51.5 14.4 %collective-permute-start.25 = (bf16[3,512,128]{2,1,0:T(8,128)(2,1)S(1)}, bf16[3,512,128]{2,1,0:T(8,128)(2,1)S(1)}, u32[]{:S(2)}, u32[]{:S(2)}) collective-permute-start(bf16[3,512,128]{2,1,0:T(8,128)(2,1)S(1)} %shard_map.121.own), channel_id=1, source_target_pairs={{0,2},{1,3},{2,0},{3,1},{4,6},{5,7},{6,4},{7,5},{8,10},{9,11},{10,... | collective-permute-start | bytes 1179656 | tf_op jit(solution)/shard_map/ppermute | solution.py:34
  52.8 10.0 %collective-permute-start.8 = (bf16[1,512,128]{2,1,0:T(8,128)(2,1)S(1)}, bf16[1,512,128]{2,1,0:T(8,128)(2,1)S(1)}, u32[]{:S(2)}, u32[]{:S(2)}) collective-permute-start(bf16[1,512,128]{2,1,0:T(8,128)(2,1)S(1)} %bitcast.15), channel_id=1, source_target_pairs={{0,2},{1,3},{2,0},{3,1},{4,6},{5,7},{6,4},{7,5},{8,10},{9,11},{10,... | collective-permute-start | bytes 393224 | tf_op jit(solution)/shard_map/ppermute | solution.py:34
  53.1 13.4 %collective-permute-start.9 = (bf16[1,512,128]{2,1,0:T(8,128)(2,1)S(1)}, bf16[1,512,128]{2,1,0:T(8,128)(2,1)S(1)}, u32[]{:S(2)}, u32[]{:S(2)}) collective-permute-start(bf16[1,512,128]{2,1,0:T(8,128)(2,1)S(1)} %bitcast.16), channel_id=1, source_target_pairs={{0,1},{1,0},{2,3},{3,2},{4,5},{5,4},{6,7},{7,6},{8,9},{9,8},{10,11... | collective-permute-start | bytes 393224 | tf_op jit(solution)/shard_map/ppermute | solution.py:34
  66.0 9.0 %collective-permute-start.27 = (bf16[3,512,128]{2,1,0:T(8,128)(2,1)S(1)}, bf16[3,512,128]{2,1,0:T(8,128)(2,1)S(1)}, u32[]{:S(2)}, u32[]{:S(2)}) collective-permute-start(bf16[3,512,128]{2,1,0:T(8,128)(2,1)S(1)} %collective-permute-done.25.far), channel_id=1, source_target_pairs={{0,1},{1,0},{2,3},{3,2},{4,5},{5,4},{6,7},{7,6},{8,9},{9,8},{10,11... | collective-permute-start | bytes 1179656 | tf_op jit(solution)/shard_map/ppermute | solution.py:34
  69.5 17.0 %collective-permute-start.16 = (bf16[512,256]{1,0:T(8,128)(2,1)S(1)}, bf16[512,256]{1,0:T(8,128)(2,1)S(1)}, u32[]{:S(2)}, u32[]{:S(2)}) collective-permute-start(bf16[512,256]{1,0:T(8,128)(2,1)S(1)} %get-tuple-element.58), channel_id=1, source_target_pairs={{0,4},{4,0},{8,12},{12,8},{16,20},{20,16},{24,28},{28,24},{1,5},{5... | collective-permute-start | bytes 786440 | tf_op jit(solution)/shard_map/ppermute | solution.py:34
  77.7 25.6 %collective-permute-start.28 = (bf16[512,256]{1,0:T(8,128)(2,1)S(1)}, bf16[512,256]{1,0:T(8,128)(2,1)S(1)}, u32[]{:S(2)}, u32[]{:S(2)}) collective-permute-start(bf16[512,256]{1,0:T(8,128)(2,1)S(1)} %get-tuple-element.73), channel_id=1, source_target_pairs={{0,4},{4,0},{8,12},{12,8},{16,20},{20,16},{24,28},{28,24},{1,5},{5... | collective-permute-start | bytes 786440 | tf_op jit(solution)/shard_map/ppermute | solution.py:34
  80.6 38.6 %collective-permute-start.33 = (bf16[512,256]{1,0:T(8,128)(2,1)S(1)}, bf16[512,256]{1,0:T(8,128)(2,1)S(1)}, u32[]{:S(2)}, u32[]{:S(2)}) collective-permute-start(bf16[512,256]{1,0:T(8,128)(2,1)S(1)} %get-tuple-element.79), channel_id=1, source_target_pairs={{0,4},{4,0},{8,12},{12,8},{16,20},{20,16},{24,28},{28,24},{1,5},{5... | collective-permute-start | bytes 786440 | tf_op jit(solution)/shard_map/ppermute | solution.py:34
  80.8 9.4 %collective-permute-start.12 = (bf16[128,256]{1,0:T(8,128)(2,1)S(1)}, bf16[128,256]{1,0:T(8,128)(2,1)S(1)}, u32[]{:S(2)}, u32[]{:S(2)}) collective-permute-start(bf16[128,256]{1,0:T(8,128)(2,1)S(1)} %get-tuple-element.53), channel_id=1, source_target_pairs={{0,0},{1,8},{2,16},{3,24},{4,4},{5,12},{6,20},{7,28},{8,1},{9,9},{... | collective-permute-start | bytes 196616 | tf_op jit(solution)/shard_map/ppermute | solution.py:319
  86.5 12.1 %collective-permute-start.14 = (bf16[128,256]{1,0:T(8,128)(2,1)S(1)}, bf16[128,256]{1,0:T(8,128)(2,1)S(1)}, u32[]{:S(2)}, u32[]{:S(2)}) collective-permute-start(bf16[128,256]{1,0:T(8,128)(2,1)S(1)} %get-tuple-element.55), channel_id=1, source_target_pairs={{0,2},{1,10},{2,18},{3,26},{4,6},{5,14},{6,22},{7,30},{8,3},{9,11}... | collective-permute-start | bytes 196616 | tf_op jit(solution)/shard_map/ppermute | solution.py:319
  90.2 9.8 %collective-permute-start.15 = (bf16[128,256]{1,0:T(8,128)(2,1)S(1)}, bf16[128,256]{1,0:T(8,128)(2,1)S(1)}, u32[]{:S(2)}, u32[]{:S(2)}) collective-permute-start(bf16[128,256]{1,0:T(8,128)(2,1)S(1)} %get-tuple-element.56), channel_id=1, source_target_pairs={{0,3},{1,11},{2,19},{3,27},{4,7},{5,15},{6,23},{7,31},{8,2},{9,10}... | collective-permute-start | bytes 196616 | tf_op jit(solution)/shard_map/ppermute | solution.py:319
  90.3 15.0 %collective-permute-start.17 = (bf16[128,256]{1,0:T(8,128)(2,1)S(1)}, bf16[128,256]{1,0:T(8,128)(2,1)S(1)}, u32[]{:S(2)}, u32[]{:S(2)}) collective-permute-start(bf16[128,256]{1,0:T(8,128)(2,1)S(1)} %get-tuple-element.59), channel_id=1, source_target_pairs={{0,0},{1,8},{2,16},{3,24},{4,4},{5,12},{6,20},{7,28},{8,1},{9,9},{... | collective-permute-start | bytes 196616 | tf_op jit(solution)/shard_map/ppermute | solution.py:319
  98.6 8.6 %collective-permute-start.18 = (bf16[128,256]{1,0:T(8,128)(2,1)S(1)}, bf16[128,256]{1,0:T(8,128)(2,1)S(1)}, u32[]{:S(2)}, u32[]{:S(2)}) collective-permute-start(bf16[128,256]{1,0:T(8,128)(2,1)S(1)} %get-tuple-element.60), channel_id=1, source_target_pairs={{0,1},{1,9},{2,17},{3,25},{4,5},{5,13},{6,21},{7,29},{8,0},{9,8},{... | collective-permute-start | bytes 196616 | tf_op jit(solution)/shard_map/ppermute | solution.py:319
  100.0 9.4 %collective-permute-start.19 = (bf16[128,256]{1,0:T(8,128)(2,1)S(1)}, bf16[128,256]{1,0:T(8,128)(2,1)S(1)}, u32[]{:S(2)}, u32[]{:S(2)}) collective-permute-start(bf16[128,256]{1,0:T(8,128)(2,1)S(1)} %get-tuple-element.61), channel_id=1, source_target_pairs={{0,2},{1,10},{2,18},{3,26},{4,6},{5,14},{6,22},{7,30},{8,3},{9,11}... | collective-permute-start | bytes 196616 | tf_op jit(solution)/shard_map/ppermute | solution.py:319
  103.3 13.6 %collective-permute-start.20 = (bf16[128,256]{1,0:T(8,128)(2,1)S(1)}, bf16[128,256]{1,0:T(8,128)(2,1)S(1)}, u32[]{:S(2)}, u32[]{:S(2)}) collective-permute-start(bf16[128,256]{1,0:T(8,128)(2,1)S(1)} %get-tuple-element.62), channel_id=1, source_target_pairs={{0,3},{1,11},{2,19},{3,27},{4,7},{5,15},{6,23},{7,31},{8,2},{9,10}... | collective-permute-start | bytes 196616 | tf_op jit(solution)/shard_map/ppermute | solution.py:319
  105.3 15.9 %collective-permute-start.29 = (bf16[128,256]{1,0:T(8,128)(2,1)S(1)}, bf16[128,256]{1,0:T(8,128)(2,1)S(1)}, u32[]{:S(2)}, u32[]{:S(2)}) collective-permute-start(bf16[128,256]{1,0:T(8,128)(2,1)S(1)} %get-tuple-element.74), channel_id=1, source_target_pairs={{0,0},{1,8},{2,16},{3,24},{4,4},{5,12},{6,20},{7,28},{8,1},{9,9},{... | collective-permute-start | bytes 196616 | tf_op jit(solution)/shard_map/ppermute | solution.py:319
  107.2 14.0 %collective-permute-start.30 = (bf16[128,256]{1,0:T(8,128)(2,1)S(1)}, bf16[128,256]{1,0:T(8,128)(2,1)S(1)}, u32[]{:S(2)}, u32[]{:S(2)}) collective-permute-start(bf16[128,256]{1,0:T(8,128)(2,1)S(1)} %get-tuple-element.75), channel_id=1, source_target_pairs={{0,1},{1,9},{2,17},{3,25},{4,5},{5,13},{6,21},{7,29},{8,0},{9,8},{... | collective-permute-start | bytes 196616 | tf_op jit(solution)/shard_map/ppermute | solution.py:319
  109.3 17.0 %collective-permute-start.31 = (bf16[128,256]{1,0:T(8,128)(2,1)S(1)}, bf16[128,256]{1,0:T(8,128)(2,1)S(1)}, u32[]{:S(2)}, u32[]{:S(2)}) collective-permute-start(bf16[128,256]{1,0:T(8,128)(2,1)S(1)} %get-tuple-element.76), channel_id=1, source_target_pairs={{0,2},{1,10},{2,18},{3,26},{4,6},{5,14},{6,22},{7,30},{8,3},{9,11}... | collective-permute-start | bytes 196616 | tf_op jit(solution)/shard_map/ppermute | solution.py:319
  117.6 16.1 %collective-permute-start.32 = (bf16[128,256]{1,0:T(8,128)(2,1)S(1)}, bf16[128,256]{1,0:T(8,128)(2,1)S(1)}, u32[]{:S(2)}, u32[]{:S(2)}) collective-permute-start(bf16[128,256]{1,0:T(8,128)(2,1)S(1)} %get-tuple-element.77), channel_id=1, source_target_pairs={{0,3},{1,11},{2,19},{3,27},{4,7},{5,15},{6,23},{7,31},{8,2},{9,10}... | collective-permute-start | bytes 196616 | tf_op jit(solution)/shard_map/ppermute | solution.py:319
  119.3 14.4 %collective-permute-start.34 = (bf16[128,256]{1,0:T(8,128)(2,1)S(1)}, bf16[128,256]{1,0:T(8,128)(2,1)S(1)}, u32[]{:S(2)}, u32[]{:S(2)}) collective-permute-start(bf16[128,256]{1,0:T(8,128)(2,1)S(1)} %get-tuple-element.80), channel_id=1, source_target_pairs={{0,0},{1,8},{2,16},{3,24},{4,4},{5,12},{6,20},{7,28},{8,1},{9,9},{... | collective-permute-start | bytes 196616 | tf_op jit(solution)/shard_map/ppermute | solution.py:319
  121.2 12.5 %collective-permute-start.35 = (bf16[128,256]{1,0:T(8,128)(2,1)S(1)}, bf16[128,256]{1,0:T(8,128)(2,1)S(1)}, u32[]{:S(2)}, u32[]{:S(2)}) collective-permute-start(bf16[128,256]{1,0:T(8,128)(2,1)S(1)} %get-tuple-element.81), channel_id=1, source_target_pairs={{0,1},{1,9},{2,17},{3,25},{4,5},{5,13},{6,21},{7,29},{8,0},{9,8},{... | collective-permute-start | bytes 196616 | tf_op jit(solution)/shard_map/ppermute | solution.py:319
  121.3 12.4 %collective-permute-start.36 = (bf16[128,256]{1,0:T(8,128)(2,1)S(1)}, bf16[128,256]{1,0:T(8,128)(2,1)S(1)}, u32[]{:S(2)}, u32[]{:S(2)}) collective-permute-start(bf16[128,256]{1,0:T(8,128)(2,1)S(1)} %get-tuple-element.82), channel_id=1, source_target_pairs={{0,2},{1,10},{2,18},{3,26},{4,6},{5,14},{6,22},{7,30},{8,3},{9,11}... | collective-permute-start | bytes 196616 | tf_op jit(solution)/shard_map/ppermute | solution.py:319
  126.4 10.1 %collective-permute-start.37 = (bf16[128,256]{1,0:T(8,128)(2,1)S(1)}, bf16[128,256]{1,0:T(8,128)(2,1)S(1)}, u32[]{:S(2)}, u32[]{:S(2)}) collective-permute-start(bf16[128,256]{1,0:T(8,128)(2,1)S(1)} %get-tuple-element.83), channel_id=1, source_target_pairs={{0,3},{1,11},{2,19},{3,27},{4,7},{5,15},{6,23},{7,31},{8,2},{9,10}... | collective-permute-start | bytes 196616 | tf_op jit(solution)/shard_map/ppermute | solution.py:319
  (14 other events, 111.6 us)
where the time goes:
time: 138 us; the launch traced here: 137 us
  starting transfers between devices  61.9 us (45%)
  waiting for transfers between devices  35.7 us (26%)
  Pallas kernels  30.6 us (22%)
  local copies, waits for them, and re-layouts  7.32 us (5%)
    ppermute x16, starting transfers between devices, placed(): return lax.ppermute(block, ('fsdp', 'ctx'), pairs)  38.5 us
    ppermute x20, waiting for transfers between devices, flipped(): lax.ppermute(value, axis, [(source, source ^ mask) for source in range(co...  23 us
    ppermute x20, starting transfers between devices, flipped(): lax.ppermute(value, axis, [(source, source ^ mask) for source in range(co...  21.2 us
    pallas_call x2, Pallas kernels, weight_gradient(): pl.pallas_call(body, out_shape=jax.ShapeDtypeStruct((groups, depth, chann...  9.97 us
    pallas_call x2, Pallas kernels, project(): call(body, (jax.ShapeDtypeStruct((length, depth), BF16), jax.ShapeDtypeSt...  6.61 us
    ppermute x2, waiting for transfers between devices, own_columns(): fetched = lax.ppermute(part(2 ^ side), ('fsdp', 'ctx'), pairs)  6.54 us
    ppermute x16, waiting for transfers between devices, placed(): return lax.ppermute(block, ('fsdp', 'ctx'), pairs)  6.17 us
    unnamed x16, local copies, waits for them, and re-layouts  4.23 us
  transfers between devices with their start and end apart: 38, of which 11 were waited for; matrix products, arithmetic and copies ran while one was open for 2% of the time, Pallas kernels for 17%

commit v1 on v0

--- a/solution.py
+++ b/solution.py
@@ -12,10 +12,11 @@
 LANES = 128
 CHUNKS = 8
 MARGIN = 8
-VMEM_LIMIT = 48 * 1024 * 1024
+VMEM_LIMIT = 16 * 1024 * 1024
 
 
 VMEM = pl.BlockSpec(memory_space=pltpu.VMEM)
+HBM = pl.BlockSpec(memory_space=pl.ANY)
 
 
 def call(body, outs, scratch=(), in_specs=None, flops=0, nbytes=0):
@@ -36,6 +37,17 @@
 
 def block_at(index, size):
     return pl.ds(pl.multiple_of(index * size, size), size)
+
+
+def to_placement(value):
+    count = lax.axis_size("ctx")
+    ratio = lax.axis_size("fsdp") // count
+    pairs = []
+    for f in range(ratio * count):
+        for k in range(count):
+            target = (k * ratio + f % ratio, f // ratio)
+            pairs.append((f * count + k, target[0] * count + target[1]))
+    return lax.ppermute(value, ("fsdp", "ctx"), pairs)
 
 
 def dot(left, right, contract):
@@ -167,16 +179,15 @@
             pltpu.VMEM((length, width), F32),
             pltpu.VMEM((length, width), F32),
         ],
-        flops=200 * length * width,
-        nbytes=40 * length * width,
     )(*parts, *tables)
 
 
-def filter_backward(parts, kinds, tables, saved, length, width):
+def filter_backward(parts, kinds, tables, saved, length, width, after=()):
     count = len(parts)
+    inputs = count + len(tables) + len(saved)
 
     def body(*refs):
-        backward_body(refs[:count], kinds, *refs[count:])
+        backward_body(refs[:count], kinds, *refs[count:inputs], *refs[inputs + len(after) :])
 
     return call(
         body,
@@ -186,21 +197,31 @@
             pltpu.VMEM((length, width), F32),
             pltpu.VMEM((length, width), F32),
         ],
-        flops=200 * length * width,
-        nbytes=40 * length * width,
-    )(*parts, *tables, *saved)
-
-
-HBM = pl.BlockSpec(memory_space=pl.ANY)
-
-
-def own_columns(rows):
+        in_specs=[VMEM] * inputs + [HBM] * len(after),
+    )(*parts, *tables, *saved, *after)
+
+
+def later(value, after):
+    def body(value, after, out):
+        pass
+
+    return pl.pallas_call(
+        body,
+        out_shape=jax.ShapeDtypeStruct(value.shape, value.dtype),
+        in_specs=[HBM, HBM],
+        out_specs=HBM,
+        input_output_aliases={0: 0},
+    )(value, after)
+
+
+def own_columns(rows, after=None):
     me = lax.axis_index("ctx")
     side = lax.axis_index("fsdp") & 1
     width = rows.shape[1] // 4
     part = lambda mask: lax.dynamic_slice_in_dim(rows, (me ^ mask) * width, width, 1)
     pairs = [(4 * f + k, 4 * f + (k ^ 2 ^ (f & 1))) for f in range(8) for k in range(4)]
-    fetched = lax.ppermute(part(2 ^ side), ("fsdp", "ctx"), pairs)
+    fetch = part(2 ^ side) if after is None else later(part(2 ^ side), after)
+    fetched = lax.ppermute(fetch, ("fsdp", "ctx"), pairs)
     return part(0), flipped(part(1), "ctx", 1), fetched, flipped(fetched, "fsdp", 1)
 
 
@@ -258,87 +279,93 @@
     return value, far, flipped(value, "ctx", 1), flipped(far, "ctx", 1)
 
 
-def output_halves(gathered, weight, after=()):
+def output_pieces(gathered, weight, after=()):
     groups, length, width = gathered[0].shape
-    depth = weight.shape[1]
-    piece = depth // 4
+    piece = weight.shape[1] // 4
+    part = length // 4
     channels = 4 * width
-    side = lambda: lax.axis_index("fsdp") & 1
-
-    def product(whole, weight, index):
+
+    def product(whole, weight, at, index):
         total = None
         for j in range(groups):
-            term = dot(whole[j], weight[j, block_at(index, piece), :], (1, 1))
+            term = dot(whole[j, at, :], weight[j, block_at(index, piece), :], (1, 1))
             total = term if total is None else total + term
         return total.astype(BF16)
 
+    def pieces(whole, weight, side, low, first, second):
+        first[...] = product(whole, weight, slice(None), 2 * side)
+        for high in range(2):
+            rows = slice(high * part, (high + 1) * part)
+            for s in range(2):
+                columns = slice(s * piece, (s + 1) * piece)
+                second[rows, columns] = product(whole, weight, block_at(2 * high + low, part), 2 * s + 1)
+
     def first_body(own, far, near, near_far, weight, *refs):
-        whole, give = refs[len(after) :]
+        whole, first, second = refs[len(after) :]
         me = lax.axis_index("ctx")
+        place = lax.axis_index("fsdp")
         for j in range(groups):
             for mask, value in ((0, own), (2, far), (1, near), (3, near_far)):
                 whole[j, :, block_at(me ^ mask, width)] = value[j]
-        give[...] = product(whole, weight, 2 - 2 * side())
-
-    def second_body(whole, weight, give, keep, keep_second):
-        give[...] = product(whole, weight, 3 - 2 * side())
-        keep[...] = product(whole, weight, 2 * side())
-        keep_second[...] = product(whole, weight, 2 * side() + 1)
-
-    part = jax.ShapeDtypeStruct((length, piece), BF16)
-    whole, give = call(
+        pieces(whole, weight, 1 - (place & 1), 1 - ((place >> 1) & 1), first, second)
+
+    def second_body(whole, weight, first, second):
+        place = lax.axis_index("fsdp")
+        pieces(whole, weight, place & 1, (place >> 1) & 1, first, second)
+
+    parts = (jax.ShapeDtypeStruct((length, piece), BF16), jax.ShapeDtypeStruct((2 * part, 2 * piece), BF16))
+    whole, *gives = call(
         first_body,
-        (jax.ShapeDtypeStruct((groups, length, channels), BF16), part),
+        (jax.ShapeDtypeStruct((groups, length, channels), BF16), *parts),
         in_specs=[VMEM] * 5 + [HBM] * len(after),
     )(*gathered, weight, *after)
-    give_second, keep, keep_second = call(second_body, (part,) * 3)(whole, weight)
-    return whole, (keep, keep_second), (give, give_second)
-
-
-def split_sum(keep, given, after=()):
-    length, width = keep.shape
+    keeps = call(second_body, parts)(whole, weight)
+    return whole, keeps, gives
+
+
+def exchange(gives):
+    return flipped(gives[0], "fsdp", 1), flipped(gives[1], "fsdp", 2)
+
+
+def block_sums(keeps, givens):
+    length, piece = keeps[0].shape
     part = length // 4
-
-    def body(keep, given, *refs):
-        place = lax.axis_index("fsdp") >> 1
-        for mask, out in enumerate(refs[len(after) :]):
-            at = block_at(place ^ mask, part)
-            out[...] = (keep[at, :].astype(F32) + given[at, :].astype(F32)).astype(BF16)
-
-    return call(
-        body, (jax.ShapeDtypeStruct((part, width), BF16),) * 4, in_specs=[VMEM] * 2 + [HBM] * len(after)
-    )(keep, given, *after)
-
-
-def placed(block, mask):
-    pairs = []
-    for f in range(8):
-        for k in range(4):
-            z, x = f // 2, f % 2
-            pairs.append((4 * f + k, 4 * (2 * k + x) + (z ^ mask)))
-    return lax.ppermute(block, ("fsdp", "ctx"), pairs)
-
-
-def join(quarters):
-    part, width = quarters[0][0].shape
-
-    def body(*refs):
-        out = refs[-1]
-        for half in range(2):
-            total = refs[4 * half][...].astype(F32)
-            for ref in refs[4 * half + 1 : 4 * half + 4]:
-                total = total + ref[...].astype(F32)
-            out[:, half * width : (half + 1) * width] = total.astype(BF16)
-
-    return call(body, jax.ShapeDtypeStruct((part, 2 * width), BF16))(*quarters[0], *quarters[1])
-
-
-def block_sums(keeps, givens):
-    quarters = []
-    for keep, given in zip(keeps, givens):
-        blocks = split_sum(keep, given)
-        quarters.append([placed(block, mask) for mask, block in enumerate(blocks)])
-    return join(quarters)
+    both = lambda keep, given, rows, columns: keep[rows, columns].astype(F32) + given[rows, columns].astype(F32)
+
+    def second_body(keep_x, given_x, keep_z, given_z, give_z, give_x, next_z, next_x):
+        place = lax.axis_index("fsdp")
+        side, low = place & 1, (place >> 1) & 1
+        for high in range(2):
+            rows = slice(high * part, (high + 1) * part)
+            take = lambda bit: both(keep_x, given_x, block_at(2 * high + bit, part), slice(None))
+            give_z[rows, :] = take(1 - low).astype(BF16)
+            next_z[rows, :] = take(low)
+        take = lambda bit: both(keep_z, given_z, slice(None), block_at(bit, piece))
+        give_x[...] = take(1 - side).astype(BF16)
+        next_x[...] = take(side)
+
+    square = lambda kind: jax.ShapeDtypeStruct((2 * part, piece), kind)
+    give_z, give_x, next_z, next_x = call(second_body, (square(BF16), square(BF16), square(F32), square(F32)))(
+        keeps[0], givens[0], keeps[1], givens[1]
+    )
+
+    def third_body(keep_z, given_z, keep_x, given_x, give, keep):
+        high = lax.axis_index("fsdp") >> 2
+        for bit, out in ((1 - high, give), (high, keep)):
+            at = block_at(bit, part)
+            for half, (mine, other) in enumerate(((keep_z, given_z), (keep_x, given_x))):
+                columns = slice(half * piece, (half + 1) * piece)
+                out[:, columns] = both(mine, other, at, slice(None)).astype(out.dtype)
+
+    block = lambda kind: jax.ShapeDtypeStruct((part, 2 * piece), kind)
+    give, keep = call(third_body, (block(BF16), block(F32)))(
+        next_z, flipped(give_z, "fsdp", 2), next_x, flipped(give_x, "fsdp", 1)
+    )
+
+    def last_body(keep, given, out):
+        out[...] = (keep[...] + given[...].astype(F32)).astype(BF16)
+
+    return to_placement(call(last_body, block(BF16))(keep, flipped(give, "fsdp", 4)))
 
 
 def weight_gradient(rows, values):
@@ -370,32 +397,22 @@
 def four_by_eight(tokens, weights, tables, out_weight, grad_mixed):
     length, width = 4 * tokens.shape[0], weights.shape[2] // 4
     token_pieces = own_columns(tokens)
-    grad_pieces = own_columns(grad_mixed)
+    grad_pieces = own_columns(grad_mixed, token_pieces[2])
     whole_tokens, *projected = project(token_pieces, weights, grad_pieces[2:3])
-    feats = channel_sums(projected, grad_pieces[3:])
+    feats = channel_sums(projected)
     whole_cotangents, *projected = project(grad_pieces, out_weight[None])
     grad_gated = channel_sums(projected)
     *saved, gated = filter_forward(feats, sum_of_three, tables, length, width)
-    whole_gated, keeps, gives = output_halves(all_channels(gated[None]), out_weight[None])
-    givens = [flipped(give, "fsdp", 1) for give in gives]
+    all_gated = all_channels(gated[None])
+    whole_gated, keeps, gives = output_pieces(all_gated, out_weight[None])
+    givens = exchange(gives)
     mixed = block_sums(keeps, givens)
-    grads = filter_backward(grad_gated, sum_of_three, tables, saved, length, width)
-    whole_grads, keeps, gives = output_halves(all_channels(grads), weights, givens[:1])
-    grad_tokens = block_sums(keeps, [flipped(give, "fsdp", 1) for give in gives])
+    grads = filter_backward(grad_gated, sum_of_three, tables, saved, length, width, all_gated[1:2])
+    whole_grads, keeps, gives = output_pieces(all_channels(grads), weights, givens)
+    grad_tokens = block_sums(keeps, exchange(gives))
     grad_in = weight_gradient(whole_tokens, whole_grads)
     grad_out = weight_gradient(whole_cotangents, whole_gated)[0]
     return mixed, grad_tokens, grad_in, grad_out
-
-
-def to_placement(value):
-    count = lax.axis_size("ctx")
-    ratio = lax.axis_size("fsdp") // count
-    pairs = []
-    for f in range(ratio * count):
-        for k in range(count):
-            target = (k * ratio + f % ratio, f // ratio)
-            pairs.append((f * count + k, target[0] * count + target[1]))
-    return lax.ppermute(value, ("fsdp", "ctx"), pairs)
 
 
 def any_mesh(tokens, weights, tables, out_weight, grad_mixed):

time: 138 us -> 123 us (0.89)
  starting transfers between devices: 61.9 us -> 36.6 us
  waiting for transfers between devices: 35.7 us -> 46 us
  local copies, waits for them, and re-layouts: 7.32 us -> 11.3 us
  Pallas kernels: 30.6 us -> 27.4 us
    ppermute x18 -> x4, starting transfers between devices: 40.7 us -> 11 us  [the longest x2 7.68 us: to_placement(): return lax.ppermute(value, ('fsdp', 'ctx'), pairs)]
    ppermute x20 -> x26, waiting for transfers between devices: 23 us -> 42 us  [flipped(): lax.ppermute(value, axis, [(source, source ^ mask) for source in range(co...]
    ppermute x18 -> x4, waiting for transfers between devices: 12.7 us -> 4.02 us  [the longest x2 4.01 us: own_columns(): fetched = lax.ppermute(fetch, ('fsdp', 'ctx'), pairs)]
    ppermute x20 -> x26, starting transfers between devices: 21.2 us -> 25.6 us  [flipped(): lax.ppermute(value, axis, [(source, source ^ mask) for source in range(co...]
    unnamed x16 -> x20, local copies, waits for them, and re-layouts: 4.23 us -> 6.49 us
    pallas_call x10 -> x11, Pallas kernels: 6.84 us -> 4.83 us  [the longest x2 2.4 us: output_pieces(): call(first_body, (jax.ShapeDtypeStruct((groups, length, channels), BF16),...]
    dynamic_slice x2, local copies, waits for them, and re-layouts: 2.33 us -> 4.03 us  [own_columns(): lax.dynamic_slice_in_dim(rows, (me ^ mask) * width, width, 1)]
  transfers between devices with their start and end apart: 38 -> 30, of which waited for: 11 -> 11; matrix products, arithmetic and copies ran while one was open for 2% -> 3% of each run, Pallas kernels for 17% -> 16%
where the time goes in v1:
time: 123 us
  waiting for transfers between devices  46 us (37%)
  starting transfers between devices  36.6 us (30%)
  Pallas kernels  27.4 us (22%)
  local copies, waits for them, and re-layouts  11.3 us (9%)
    ppermute x26, waiting for transfers between devices, flipped(): lax.ppermute(value, axis, [(source, source ^ mask) for source in range(co...  42 us
    ppermute x26, starting transfers between devices, flipped(): lax.ppermute(value, axis, [(source, source ^ mask) for source in range(co...  25.6 us
    pallas_call x2, Pallas kernels, weight_gradient(): pl.pallas_call(body, out_shape=jax.ShapeDtypeStruct((groups, depth, chann...  9.99 us
    ppermute x2, starting transfers between devices, to_placement(): return lax.ppermute(value, ('fsdp', 'ctx'), pairs)  7.68 us
    unnamed x20, local copies, waits for them, and re-layouts  6.49 us
    pallas_call x2, Pallas kernels, project(): call(body, (jax.ShapeDtypeStruct((length, depth), BF16), jax.ShapeDtypeSt...  6.31 us
    dynamic_slice x2, local copies, waits for them, and re-layouts, own_columns(): lax.dynamic_slice_in_dim(rows, (me ^ mask) * width, width, 1)  4.03 us
    ppermute x2, waiting for transfers between devices, own_columns(): fetched = lax.ppermute(fetch, ('fsdp', 'ctx'), pairs)  4.01 us
  transfers between devices with their start and end apart: 30, of which 11 were waited for; matrix products, arithmetic and copies ran while one was open for 3% of the time, Pallas kernels for 16%

profile of v1, /device:TPU:1, one launch (start us, length us, event | category | flops | bytes accessed | tf_op | source)
XLA Modules:
  0.0 122.9 jit_solution(4380582197098139272)
XLA Ops:
  0.7 2.0 %constant_dynamic-slice_fusion.3 = (bf16[128,1024]{1,0:T(8,128)(2,1)S(1)}, bf16[128,1024]{1,0:T(8,128)(2,1)S(1)}, bf16[128,1024]{1,0:T(8,128)(2,1)}) fusion(bf16[128,4096]{1,0:T(8,128)(2,1)} %param.8, s32[]{:T(128)S(6)} %select_n.20, s32[]{:T(128)S(6)} %select_n.8, s32[]{:T(128)S(6)} %select_n.9), kind=kLoop, calls=%fused_computation.7 | loop fusion | bytes 1572876 | tf_op jit(solution)/shard_map/dynamic_slice | solution.py:221
  2.7 2.1 %collective-permute-start.1 = (bf16[128,1024]{1,0:T(8,128)(2,1)S(1)}, bf16[128,1024]{1,0:T(8,128)(2,1)}, u32[]{:S(2)}, u32[]{:S(2)}) collective-permute-start(bf16[128,1024]{1,0:T(8,128)(2,1)S(1)} %get-tuple-element.81), channel_id=1, source_target_pairs={{0,2},{1,3},{2,0},{3,1},{4,7},{5,6},{6,5},{7,4},{8,10},{9,11},{10,... | collective-permute-start | bytes 786440 | tf_op jit(solution)/shard_map/ppermute | solution.py:224
  5.7 2.0 %constant_dynamic-slice_fusion = (bf16[128,1024]{1,0:T(8,128)(2,1)}, bf16[128,1024]{1,0:T(8,128)(2,1)}, bf16[128,1024]{1,0:T(8,128)(2,1)}) fusion(bf16[128,4096]{1,0:T(8,128)(2,1)} %param.15, s32[]{:T(128)S(6)} %select_n.9, s32[]{:T(128)S(6)} %select_n.20, s32[]{:T(128)S(6)} %select_n.8), kind=kLoop, calls=%fused_computation.4 | loop fusion | bytes 1572876 | tf_op jit(solution)/shard_map/dynamic_slice | solution.py:221
  7.7 3.2 %collective-permute-done.1.after.c = bf16[128,1024]{1,0:T(8,128)(2,1)} collective-permute-done((bf16[128,1024]{1,0:T(8,128)(2,1)S(1)}, bf16[128,1024]{1,0:T(8,128)(2,1)}, u32[]{:S(2)}, u32[]{:S(2)}) %collective-permute-start.1) | collective-permute-done | bytes 262176 | tf_op jit(solution)/shard_map/ppermute | solution.py:224
  10.9 2.8 %collective-permute-start.2 = (bf16[128,1024]{1,0:T(8,128)(2,1)}, bf16[128,1024]{1,0:T(8,128)(2,1)}, u32[]{:S(2)}, u32[]{:S(2)}) collective-permute-start(bf16[128,1024]{1,0:T(8,128)(2,1)} %collective-permute-done.1.after.c), channel_id=1, source_target_pairs={{0,4},{4,0},{8,12},{12,8},{16,20},{20,16},{24,28},{28,24},{1,5},{5... | collective-permute-start | bytes 786440 | tf_op jit(solution)/shard_map/ppermute | solution.py:35
  15.0 5.4 %collective-permute-done.2.d = bf16[128,1024]{1,0:T(8,128)(2,1)} collective-permute-done((bf16[128,1024]{1,0:T(8,128)(2,1)}, bf16[128,1024]{1,0:T(8,128)(2,1)}, u32[]{:S(2)}, u32[]{:S(2)}) %collective-permute-start.2) | collective-permute-done | bytes 262176 | tf_op jit(solution)/shard_map/ppermute | solution.py:35
  21.2 4.2 %shard_map.112 = (bf16[512,1024]{1,0:T(8,128)(2,1)S(1)}, f32[3,512,128]{2,1,0:T(8,128)S(1)}, bf16[3,512,128]{2,1,0:T(8,128)(2,1)S(1)}, bf16[3,512,128]{2,1,0:T(8,128)(2,1)}, bf16[3,512,128]{2,1,0:T(8,128)(2,1)S(1)}) custom-call(bf16[128,1024]{1,0:T(8,128)(2,1)S(1)} %get-tuple-element.82.a, bf16[128,1024]{1,0:T(8,128)(2,1)} %collective-permute-done.b, ...), custom_call_target="tpu_custom_call" | custom-call | tf_op jit(solution)/shard_map/pallas_call | solution.py:248
  27.3 1.5 %collective-permute-start.5 = (bf16[3,512,128]{2,1,0:T(8,128)(2,1)S(1)}, bf16[3,512,128]{2,1,0:T(8,128)(2,1)S(1)}, u32[]{:S(2)}, u32[]{:S(2)}) collective-permute-start(bf16[3,512,128]{2,1,0:T(8,128)(2,1)S(1)} %get-tuple-element.44), channel_id=1, source_target_pairs={{0,1},{1,0},{2,3},{3,2},{4,5},{5,4},{6,7},{7,6},{8,9},{9,8},{10,11... | collective-permute-start | bytes 1179656 | tf_op jit(solution)/shard_map/ppermute | solution.py:35
  31.4 1.3 %collective-permute-start.6 = (bf16[3,512,128]{2,1,0:T(8,128)(2,1)}, bf16[3,512,128]{2,1,0:T(8,128)(2,1)}, u32[]{:S(2)}, u32[]{:S(2)}) collective-permute-start(bf16[3,512,128]{2,1,0:T(8,128)(2,1)} %shard_map.113), channel_id=1, source_target_pairs={{0,2},{1,3},{2,0},{3,1},{4,6},{5,7},{6,4},{7,5},{8,10},{9,11},{10,... | collective-permute-start | bytes 1179656 | tf_op jit(solution)/shard_map/ppermute | solution.py:35
  32.7 3.8 %collective-permute-done.17.d = bf16[128,1024]{1,0:T(8,128)(2,1)} collective-permute-done((bf16[128,1024]{1,0:T(8,128)(2,1)}, bf16[128,1024]{1,0:T(8,128)(2,1)}, u32[]{:S(2)}, u32[]{:S(2)}) %collective-permute-start.17) | collective-permute-done | bytes 262176 | tf_op jit(solution)/shard_map/ppermute | solution.py:35
  38.6 2.1 %shard_map.120 = (bf16[512,1024]{1,0:T(8,128)(2,1)S(1)}, f32[1,512,128]{2,1,0:T(8,128)S(1)}, bf16[1,512,128]{2,1,0:T(8,128)(2,1)S(1)}, bf16[1,512,128]{2,1,0:T(8,128)(2,1)S(1)}, bf16[1,512,128]{2,1,0:T(8,128)(2,1)S(1)}) custom-call(bf16[128,1024]{1,0:T(8,128)(2,1)S(1)} %copy-done.6, bf16[128,1024]{1,0:T(8,128)(2,1)S(1)} %collective-permute-done.16.b, ...), custom_call_target="tpu_custom_call" | custom-call | tf_op jit(solution)/shard_map/pallas_call | solution.py:248
  40.7 1.4 %collective-permute-start.19 = (bf16[1,512,128]{2,1,0:T(8,128)(2,1)S(1)}, bf16[1,512,128]{2,1,0:T(8,128)(2,1)S(1)}, u32[]{:S(2)}, u32[]{:S(2)}) collective-permute-start(bf16[1,512,128]{2,1,0:T(8,128)(2,1)S(1)} %get-tuple-element.60), channel_id=1, source_target_pairs={{0,1},{1,0},{2,3},{3,2},{4,5},{5,4},{6,7},{7,6},{8,9},{9,8},{10,11... | collective-permute-start | bytes 393224 | tf_op jit(solution)/shard_map/ppermute | solution.py:35
  43.7 1.4 %collective-permute-start.20 = (bf16[1,512,128]{2,1,0:T(8,128)(2,1)S(1)}, bf16[1,512,128]{2,1,0:T(8,128)(2,1)S(1)}, u32[]{:S(2)}, u32[]{:S(2)}) collective-permute-start(bf16[1,512,128]{2,1,0:T(8,128)(2,1)S(1)} %shard_map.121), channel_id=1, source_target_pairs={{0,2},{1,3},{2,0},{3,1},{4,6},{5,7},{6,4},{7,5},{8,10},{9,11},{10,... | collective-permute-start | bytes 393224 | tf_op jit(solution)/shard_map/ppermute | solution.py:35
  46.3 3.3 %shard_map.114 = (f32[512,128]{1,0:T(8,128)S(1)}, f32[512,128]{1,0:T(8,128)S(1)}, f32[512,128]{1,0:T(8,128)S(1)}, f32[512,128]{1,0:T(8,128)S(1)}, bf16[512,128]{1,0:T(8,128)(2,1)S(1)}) custom-call(f32[3,512,128]{2,1,0:T(8,128)S(1)} %copy-done.8, bf16[3,512,128]{2,1,0:T(8,128)(2,1)} %collective-permute-done.4.refs_1_, ...), custom_call_target="tpu_custom_call" | custom-call | tf_op jit(solution)/shard_map/pallas_call | solution.py:174
  49.7 4.1 %collective-permute-done.7.far.refs_12_ = bf16[1,512,128]{2,1,0:T(8,128)(2,1)S(1)} collective-permute-done((bf16[1,512,128]{2,1,0:T(8,128)(2,1)S(1)}, bf16[1,512,128]{2,1,0:T(8,128)(2,1)S(1)}, u32[]{:S(2)}, u32[]{:S(2)}) %collective-permute-start.7) | collective-permute-done | bytes 131104 | tf_op jit(solution)/shard_map/ppermute | solution.py:35
  53.8 2.1 %shard_map.122.own = bf16[3,512,128]{2,1,0:T(8,128)(2,1)S(1)} custom-call(f32[1,512,128]{2,1,0:T(8,128)S(1)} %get-tuple-element.57.refs_0_, bf16[1,512,128]{2,1,0:T(8,128)(2,1)S(1)} %collective-permute-done.18.refs_1_, bf16[1,512,128]{2,1,0:T(8,128)(2,1)S(1)} %collective-permute-done.20.refs_2_, f32[3,7,128]{2,1,0:T(8,128)S(1)} %dynamic-slice_bitcast_fusion.refs_3_, ...), custom_call_target="tpu_custom_call" | custom-call | tf_op jit(solution)/shard_map/pallas_call | solution.py:192
  56.2 1.9 %collective-permute-start.8 = (bf16[1,512,128]{2,1,0:T(8,128)(2,1)S(1)}, bf16[1,512,128]{2,1,0:T(8,128)(2,1)S(1)}, u32[]{:S(2)}, u32[]{:S(2)}) collective-permute-start(bf16[1,512,128]{2,1,0:T(8,128)(2,1)S(1)} %bitcast.16), channel_id=1, source_target_pairs={{0,1},{1,0},{2,3},{3,2},{4,5},{5,4},{6,7},{7,6},{8,9},{9,8},{10,11... | collective-permute-start | bytes 393224 | tf_op jit(solution)/shard_map/ppermute | solution.py:35
  58.6 6.4 %collective-permute-done.21.far = bf16[3,512,128]{2,1,0:T(8,128)(2,1)S(1)} collective-permute-done((bf16[3,512,128]{2,1,0:T(8,128)(2,1)S(1)}, bf16[3,512,128]{2,1,0:T(8,128)(2,1)S(1)}, u32[]{:S(2)}, u32[]{:S(2)}) %collective-permute-start.21) | collective-permute-done | bytes 393248 | tf_op jit(solution)/shard_map/ppermute | solution.py:35
  65.0 2.6 %collective-permute-start.23 = (bf16[3,512,128]{2,1,0:T(8,128)(2,1)S(1)}, bf16[3,512,128]{2,1,0:T(8,128)(2,1)S(1)}, u32[]{:S(2)}, u32[]{:S(2)}) collective-permute-start(bf16[3,512,128]{2,1,0:T(8,128)(2,1)S(1)} %collective-permute-done.21.far), channel_id=1, source_target_pairs={{0,1},{1,0},{2,3},{3,2},{4,5},{5,4},{6,7},{7,6},{8,9},{9,8},{10,11... | collective-permute-start | bytes 1179656 | tf_op jit(solution)/shard_map/ppermute | solution.py:35
  68.4 1.3 %collective-permute-start.11 = (bf16[256,512]{1,0:T(8,128)(2,1)S(1)}, bf16[256,512]{1,0:T(8,128)(2,1)S(1)}, u32[]{:S(2)}, u32[]{:S(2)}) collective-permute-start(bf16[256,512]{1,0:T(8,128)(2,1)S(1)} %get-tuple-element.50), channel_id=1, source_target_pairs={{0,8},{4,12},{8,0},{12,4},{16,24},{20,28},{24,16},{28,20},{1,9},{5... | collective-permute-start | bytes 786440 | tf_op jit(solution)/shard_map/ppermute | solution.py:35
  69.7 6.5 %collective-permute-done.10.given_x.refs_0_ = bf16[512,256]{1,0:T(8,128)(2,1)S(1)} collective-permute-done((bf16[512,256]{1,0:T(8,128)(2,1)S(1)}, bf16[512,256]{1,0:T(8,128)(2,1)S(1)}, u32[]{:S(2)}, u32[]{:S(2)}) %collective-permute-start.10) | collective-permute-done | bytes 262176 | tf_op jit(solution)/shard_map/ppermute | solution.py:35
  76.2 1.7 %shard_map.123 = (bf16[3,512,512]{2,1,0:T(8,128)(2,1)S(1)}, bf16[512,256]{1,0:T(8,128)(2,1)S(1)}, bf16[256,512]{1,0:T(8,128)(2,1)S(1)}) custom-call(bf16[3,512,128]{2,1,0:T(8,128)(2,1)S(1)} %shard_map.122.own, bf16[3,512,128]{2,1,0:T(8,128)(2,1)S(1)} %collective-permute-done.21.far, bf16[3,512,128]{2,1,0:T(8,128)(2,1)S(1)} %collective-permute-done.22.near, ...), custom_call_target="tpu_custom_call" | custom-call | tf_op jit(solution)/shard_map/pallas_call | solution.py:317
  79.2 1.3 %collective-permute-start.25 = (bf16[256,512]{1,0:T(8,128)(2,1)S(1)}, bf16[256,512]{1,0:T(8,128)(2,1)S(1)}, u32[]{:S(2)}, u32[]{:S(2)}) collective-permute-start(bf16[256,512]{1,0:T(8,128)(2,1)S(1)} %get-tuple-element.69), channel_id=1, source_target_pairs={{0,8},{4,12},{8,0},{12,4},{16,24},{20,28},{24,16},{28,20},{1,9},{5... | collective-permute-start | bytes 786440 | tf_op jit(solution)/shard_map/ppermute | solution.py:35
  81.8 6.6 %collective-permute-done.12.given_z = bf16[256,256]{1,0:T(8,128)(2,1)S(1)} collective-permute-done((bf16[256,256]{1,0:T(8,128)(2,1)S(1)}, bf16[256,256]{1,0:T(8,128)(2,1)S(1)}, u32[]{:S(2)}, u32[]{:S(2)}) %collective-permute-start.12) | collective-permute-done | bytes 131104 | tf_op jit(solution)/shard_map/ppermute | solution.py:35
  88.5 2.4 %collective-permute-start.14 = (bf16[128,512]{1,0:T(8,128)(2,1)S(1)}, bf16[128,512]{1,0:T(8,128)(2,1)S(1)}, u32[]{:S(2)}, u32[]{:S(2)}) collective-permute-start(bf16[128,512]{1,0:T(8,128)(2,1)S(1)} %get-tuple-element.56), channel_id=1, source_target_pairs={{0,16},{4,20},{8,24},{12,28},{16,0},{20,4},{24,8},{28,12},{1,17},{... | collective-permute-start | bytes 393224 | tf_op jit(solution)/shard_map/ppermute | solution.py:35
  90.9 1.4 %shard_map.124 = (bf16[512,256]{1,0:T(8,128)(2,1)S(1)}, bf16[256,512]{1,0:T(8,128)(2,1)S(1)}) custom-call(bf16[3,512,512]{2,1,0:T(8,128)(2,1)S(1)} %get-tuple-element.65.whole.values, bf16[3,1024,512]{2,1,0:T(8,128)(2,1)S(1)} %bitcast.11), custom_call_target="tpu_custom_call" | custom-call | tf_op jit(solution)/shard_map/pallas_call | solution.py:322
  92.5 1.4 %collective-permute-start.26 = (bf16[256,256]{1,0:T(8,128)(2,1)S(1)}, bf16[256,256]{1,0:T(8,128)(2,1)S(1)}, u32[]{:S(2)}, u32[]{:S(2)}) collective-permute-start(bf16[256,256]{1,0:T(8,128)(2,1)S(1)} %get-tuple-element.71), channel_id=1, source_target_pairs={{0,8},{4,12},{8,0},{12,4},{16,24},{20,28},{24,16},{28,20},{1,9},{5... | collective-permute-start | bytes 393224 | tf_op jit(solution)/shard_map/ppermute | solution.py:35
  94.7 5.8 %collective-permute-start.15 = (bf16[128,512]{1,0:T(8,128)(2,1)S(1)}, bf16[128,512]{1,0:T(8,128)(2,1)S(1)}, u32[]{:S(2)}, u32[]{:S(2)}) collective-permute-start(bf16[128,512]{1,0:T(8,128)(2,1)S(1)} %shard_map.119), channel_id=1, source_target_pairs={{0,0},{1,8},{2,16},{3,24},{4,4},{5,12},{6,20},{7,28},{8,1},{9,9},{... | collective-permute-start | bytes 393224 | tf_op jit(solution)/shard_map/ppermute | solution.py:50
  101.6 2.7 %shard_map.129 = f32[1,1024,512]{2,1,0:T(8,128)} custom-call(bf16[512,1024]{1,0:T(8,128)(2,1)S(1)} %get-tuple-element.77.rows, bf16[1,512,512]{2,1,0:T(8,128)(2,1)S(1)} %get-tuple-element.46.whole.values), custom_call_target="tpu_custom_call" | custom-call | flops 536870912 | bytes 2097152 | tf_op jit(solution)/shard_map/pallas_call | solution.py:379
  104.3 8.0 %collective-permute-done.28.given = bf16[128,512]{1,0:T(8,128)(2,1)S(1)} collective-permute-done((bf16[128,512]{1,0:T(8,128)(2,1)S(1)}, bf16[128,512]{1,0:T(8,128)(2,1)S(1)}, u32[]{:S(2)}, u32[]{:S(2)}) %collective-permute-start.28) | collective-permute-done | bytes 131104 | tf_op jit(solution)/shard_map/ppermute | solution.py:35
  112.4 1.9 %collective-permute-start.29 = (bf16[128,512]{1,0:T(8,128)(2,1)S(1)}, bf16[128,512]{1,0:T(8,128)(2,1)S(1)}, u32[]{:S(2)}, u32[]{:S(2)}) collective-permute-start(bf16[128,512]{1,0:T(8,128)(2,1)S(1)} %shard_map.127), channel_id=1, source_target_pairs={{0,0},{1,8},{2,16},{3,24},{4,4},{5,12},{6,20},{7,28},{8,1},{9,9},{... | collective-permute-start | bytes 393224 | tf_op jit(solution)/shard_map/ppermute | solution.py:50
  114.3 7.3 %shard_map.128 = f32[3,1024,512]{2,1,0:T(8,128)} custom-call(bf16[512,1024]{1,0:T(8,128)(2,1)S(1)} %copy-done.5, bf16[3,512,512]{2,1,0:T(8,128)(2,1)S(1)} %get-tuple-element.65.whole.values), custom_call_target="tpu_custom_call" | custom-call | flops 1610612736 | bytes 6291456 | tf_op jit(solution)/shard_map/pallas_call | solution.py:379
  (72 shorter events, 20.3 us)
Async XLA Ops:
  0.6 32.1 %copy-start = (f32[7,3,512]{2,0,1:T(8,128)S(1)}, f32[7,3,512]{2,0,1:T(8,128)}, u32[]{:S(2)}) copy-start(f32[7,3,512]{2,0,1:T(8,128)} %param.10) | copy-start | bytes 129028
  2.7 8.2 %collective-permute-start.1 = (bf16[128,1024]{1,0:T(8,128)(2,1)S(1)}, bf16[128,1024]{1,0:T(8,128)(2,1)}, u32[]{:S(2)}, u32[]{:S(2)}) collective-permute-start(bf16[128,1024]{1,0:T(8,128)(2,1)S(1)} %get-tuple-element.81), channel_id=1, source_target_pairs={{0,2},{1,3},{2,0},{3,1},{4,7},{5,6},{6,5},{7,4},{8,10},{9,11},{10,... | collective-permute-start | bytes 786440 | tf_op jit(solution)/shard_map/ppermute | solution.py:224
  4.8 10.2 %collective-permute-start = (bf16[128,1024]{1,0:T(8,128)(2,1)}, bf16[128,1024]{1,0:T(8,128)(2,1)}, u32[]{:S(2)}, u32[]{:S(2)}) collective-permute-start(bf16[128,1024]{1,0:T(8,128)(2,1)} %get-tuple-element.83), channel_id=1, source_target_pairs={{0,1},{1,0},{2,3},{3,2},{4,5},{5,4},{6,7},{7,6},{8,9},{9,8},{10,11... | collective-permute-start | bytes 786440 | tf_op jit(solution)/shard_map/ppermute | solution.py:35
  10.9 9.4 %collective-permute-start.2 = (bf16[128,1024]{1,0:T(8,128)(2,1)}, bf16[128,1024]{1,0:T(8,128)(2,1)}, u32[]{:S(2)}, u32[]{:S(2)}) collective-permute-start(bf16[128,1024]{1,0:T(8,128)(2,1)} %collective-permute-done.1.after.c), channel_id=1, source_target_pairs={{0,4},{4,0},{8,12},{12,8},{16,20},{20,16},{24,28},{28,24},{1,5},{5... | collective-permute-start | bytes 786440 | tf_op jit(solution)/shard_map/ppermute | solution.py:35
  13.7 7.5 %collective-permute-start.3 = (bf16[128,1024]{1,0:T(8,128)(2,1)}, bf16[128,1024]{1,0:T(8,128)(2,1)}, u32[]{:S(2)}, u32[]{:S(2)}) collective-permute-start(bf16[128,1024]{1,0:T(8,128)(2,1)} %shard_map.111), channel_id=1, source_target_pairs={{0,2},{1,3},{2,0},{3,1},{4,7},{5,6},{6,5},{7,4},{8,10},{9,11},{10,... | collective-permute-start | bytes 786440 | tf_op jit(solution)/shard_map/ppermute | solution.py:224
  27.3 3.2 %collective-permute-start.5 = (bf16[3,512,128]{2,1,0:T(8,128)(2,1)S(1)}, bf16[3,512,128]{2,1,0:T(8,128)(2,1)S(1)}, u32[]{:S(2)}, u32[]{:S(2)}) collective-permute-start(bf16[3,512,128]{2,1,0:T(8,128)(2,1)S(1)} %get-tuple-element.44), channel_id=1, source_target_pairs={{0,1},{1,0},{2,3},{3,2},{4,5},{5,4},{6,7},{7,6},{8,9},{9,8},{10,11... | collective-permute-start | bytes 1179656 | tf_op jit(solution)/shard_map/ppermute | solution.py:35
  28.8 3.9 %collective-permute-start.16 = (bf16[128,1024]{1,0:T(8,128)(2,1)}, bf16[128,1024]{1,0:T(8,128)(2,1)S(1)}, u32[]{:S(2)}, u32[]{:S(2)}) collective-permute-start(bf16[128,1024]{1,0:T(8,128)(2,1)} %get-tuple-element.78), channel_id=1, source_target_pairs={{0,1},{1,0},{2,3},{3,2},{4,5},{5,4},{6,7},{7,6},{8,9},{9,8},{10,11... | collective-permute-start | bytes 786440 | tf_op jit(solution)/shard_map/ppermute | solution.py:35
  28.8 7.7 %collective-permute-start.17 = (bf16[128,1024]{1,0:T(8,128)(2,1)}, bf16[128,1024]{1,0:T(8,128)(2,1)}, u32[]{:S(2)}, u32[]{:S(2)}) collective-permute-start(bf16[128,1024]{1,0:T(8,128)(2,1)} %collective-permute-done.3.refs_0_.c), channel_id=1, source_target_pairs={{0,4},{4,0},{8,12},{12,8},{16,20},{20,16},{24,28},{28,24},{1,5},{5... | collective-permute-start | bytes 786440 | tf_op jit(solution)/shard_map/ppermute | solution.py:35
  28.9 16.2 %collective-permute-start.4 = (bf16[3,512,128]{2,1,0:T(8,128)(2,1)}, bf16[3,512,128]{2,1,0:T(8,128)(2,1)}, u32[]{:S(2)}, u32[]{:S(2)}) collective-permute-start(bf16[3,512,128]{2,1,0:T(8,128)(2,1)} %get-tuple-element.42), channel_id=1, source_target_pairs={{0,1},{1,0},{2,3},{3,2},{4,5},{5,4},{6,7},{7,6},{8,9},{9,8},{10,11... | collective-permute-start | bytes 1179656 | tf_op jit(solution)/shard_map/ppermute | solution.py:35
  31.4 13.7 %collective-permute-start.6 = (bf16[3,512,128]{2,1,0:T(8,128)(2,1)}, bf16[3,512,128]{2,1,0:T(8,128)(2,1)}, u32[]{:S(2)}, u32[]{:S(2)}) collective-permute-start(bf16[3,512,128]{2,1,0:T(8,128)(2,1)} %shard_map.113), channel_id=1, source_target_pairs={{0,2},{1,3},{2,0},{3,1},{4,6},{5,7},{6,4},{7,5},{8,10},{9,11},{10,... | collective-permute-start | bytes 1179656 | tf_op jit(solution)/shard_map/ppermute | solution.py:35
  38.6 28.9 %copy-start.3 = (bf16[1024,512]{1,0:T(8,128)(2,1)S(1)}, bf16[1024,512]{1,0:T(8,128)(2,1)}, u32[]{:S(2)}) copy-start(bf16[1024,512]{1,0:T(8,128)(2,1)} %param.14) | copy-start | bytes 3145732
  40.7 3.0 %collective-permute-start.19 = (bf16[1,512,128]{2,1,0:T(8,128)(2,1)S(1)}, bf16[1,512,128]{2,1,0:T(8,128)(2,1)S(1)}, u32[]{:S(2)}, u32[]{:S(2)}) collective-permute-start(bf16[1,512,128]{2,1,0:T(8,128)(2,1)S(1)} %get-tuple-element.60), channel_id=1, source_target_pairs={{0,1},{1,0},{2,3},{3,2},{4,5},{5,4},{6,7},{7,6},{8,9},{9,8},{10,11... | collective-permute-start | bytes 393224 | tf_op jit(solution)/shard_map/ppermute | solution.py:35
  43.6 6.1 %collective-permute-start.18 = (bf16[1,512,128]{2,1,0:T(8,128)(2,1)S(1)}, bf16[1,512,128]{2,1,0:T(8,128)(2,1)S(1)}, u32[]{:S(2)}, u32[]{:S(2)}) collective-permute-start(bf16[1,512,128]{2,1,0:T(8,128)(2,1)S(1)} %get-tuple-element.58), channel_id=1, source_target_pairs={{0,1},{1,0},{2,3},{3,2},{4,5},{5,4},{6,7},{7,6},{8,9},{9,8},{10,11... | collective-permute-start | bytes 393224 | tf_op jit(solution)/shard_map/ppermute | solution.py:35
  43.7 6.0 %collective-permute-start.20 = (bf16[1,512,128]{2,1,0:T(8,128)(2,1)S(1)}, bf16[1,512,128]{2,1,0:T(8,128)(2,1)S(1)}, u32[]{:S(2)}, u32[]{:S(2)}) collective-permute-start(bf16[1,512,128]{2,1,0:T(8,128)(2,1)S(1)} %shard_map.121), channel_id=1, source_target_pairs={{0,2},{1,3},{2,0},{3,1},{4,6},{5,7},{6,4},{7,5},{8,10},{9,11},{10,... | collective-permute-start | bytes 393224 | tf_op jit(solution)/shard_map/ppermute | solution.py:35
  49.5 4.3 %collective-permute-start.7 = (bf16[1,512,128]{2,1,0:T(8,128)(2,1)S(1)}, bf16[1,512,128]{2,1,0:T(8,128)(2,1)S(1)}, u32[]{:S(2)}, u32[]{:S(2)}) collective-permute-start(bf16[1,512,128]{2,1,0:T(8,128)(2,1)S(1)} %bitcast.15), channel_id=1, source_target_pairs={{0,2},{1,3},{2,0},{3,1},{4,6},{5,7},{6,4},{7,5},{8,10},{9,11},{10,... | collective-permute-start | bytes 393224 | tf_op jit(solution)/shard_map/ppermute | solution.py:35
  56.0 9.0 %collective-permute-start.21 = (bf16[3,512,128]{2,1,0:T(8,128)(2,1)S(1)}, bf16[3,512,128]{2,1,0:T(8,128)(2,1)S(1)}, u32[]{:S(2)}, u32[]{:S(2)}) collective-permute-start(bf16[3,512,128]{2,1,0:T(8,128)(2,1)S(1)} %shard_map.122.own), channel_id=1, source_target_pairs={{0,2},{1,3},{2,0},{3,1},{4,6},{5,7},{6,4},{7,5},{8,10},{9,11},{10,... | collective-permute-start | bytes 1179656 | tf_op jit(solution)/shard_map/ppermute | solution.py:35
  56.2 11.4 %collective-permute-start.8 = (bf16[1,512,128]{2,1,0:T(8,128)(2,1)S(1)}, bf16[1,512,128]{2,1,0:T(8,128)(2,1)S(1)}, u32[]{:S(2)}, u32[]{:S(2)}) collective-permute-start(bf16[1,512,128]{2,1,0:T(8,128)(2,1)S(1)} %bitcast.16), channel_id=1, source_target_pairs={{0,1},{1,0},{2,3},{3,2},{4,5},{5,4},{6,7},{7,6},{8,9},{9,8},{10,11... | collective-permute-start | bytes 393224 | tf_op jit(solution)/shard_map/ppermute | solution.py:35
  58.1 9.5 %collective-permute-start.9 = (bf16[1,512,128]{2,1,0:T(8,128)(2,1)S(1)}, bf16[1,512,128]{2,1,0:T(8,128)(2,1)S(1)}, u32[]{:S(2)}, u32[]{:S(2)}) collective-permute-start(bf16[1,512,128]{2,1,0:T(8,128)(2,1)S(1)} %collective-permute-done.7.far.refs_12_), channel_id=1, source_target_pairs={{0,1},{1,0},{2,3},{3,2},{4,5},{5,4},{6,7},{7,6},{8,9},{9,8},{10,11... | collective-permute-start | bytes 393224 | tf_op jit(solution)/shard_map/ppermute | solution.py:35
  58.1 18.1 %collective-permute-start.22 = (bf16[3,512,128]{2,1,0:T(8,128)(2,1)S(1)}, bf16[3,512,128]{2,1,0:T(8,128)(2,1)S(1)}, u32[]{:S(2)}, u32[]{:S(2)}) collective-permute-start(bf16[3,512,128]{2,1,0:T(8,128)(2,1)S(1)} %shard_map.122.own), channel_id=1, source_target_pairs={{0,1},{1,0},{2,3},{3,2},{4,5},{5,4},{6,7},{7,6},{8,9},{9,8},{10,11... | collective-permute-start | bytes 1179656 | tf_op jit(solution)/shard_map/ppermute | solution.py:35
  65.0 11.3 %collective-permute-start.23 = (bf16[3,512,128]{2,1,0:T(8,128)(2,1)S(1)}, bf16[3,512,128]{2,1,0:T(8,128)(2,1)S(1)}, u32[]{:S(2)}, u32[]{:S(2)}) collective-permute-start(bf16[3,512,128]{2,1,0:T(8,128)(2,1)S(1)} %collective-permute-done.21.far), channel_id=1, source_target_pairs={{0,1},{1,0},{2,3},{3,2},{4,5},{5,4},{6,7},{7,6},{8,9},{9,8},{10,11... | collective-permute-start | bytes 1179656 | tf_op jit(solution)/shard_map/ppermute | solution.py:35
  68.2 8.0 %collective-permute-start.10 = (bf16[512,256]{1,0:T(8,128)(2,1)S(1)}, bf16[512,256]{1,0:T(8,128)(2,1)S(1)}, u32[]{:S(2)}, u32[]{:S(2)}) collective-permute-start(bf16[512,256]{1,0:T(8,128)(2,1)S(1)} %get-tuple-element.48), channel_id=1, source_target_pairs={{0,4},{4,0},{8,12},{12,8},{16,20},{20,16},{24,28},{28,24},{1,5},{5... | collective-permute-start | bytes 786440 | tf_op jit(solution)/shard_map/ppermute | solution.py:35
  68.4 7.8 %collective-permute-start.11 = (bf16[256,512]{1,0:T(8,128)(2,1)S(1)}, bf16[256,512]{1,0:T(8,128)(2,1)S(1)}, u32[]{:S(2)}, u32[]{:S(2)}) collective-permute-start(bf16[256,512]{1,0:T(8,128)(2,1)S(1)} %get-tuple-element.50), channel_id=1, source_target_pairs={{0,8},{4,12},{8,0},{12,4},{16,24},{20,28},{24,16},{28,20},{1,9},{5... | collective-permute-start | bytes 786440 | tf_op jit(solution)/shard_map/ppermute | solution.py:35
  78.0 14.3 %collective-permute-start.24 = (bf16[512,256]{1,0:T(8,128)(2,1)S(1)}, bf16[512,256]{1,0:T(8,128)(2,1)S(1)}, u32[]{:S(2)}, u32[]{:S(2)}) collective-permute-start(bf16[512,256]{1,0:T(8,128)(2,1)S(1)} %get-tuple-element.67), channel_id=1, source_target_pairs={{0,4},{4,0},{8,12},{12,8},{16,20},{20,16},{24,28},{28,24},{1,5},{5... | collective-permute-start | bytes 786440 | tf_op jit(solution)/shard_map/ppermute | solution.py:35
  79.2 13.1 %collective-permute-start.25 = (bf16[256,512]{1,0:T(8,128)(2,1)S(1)}, bf16[256,512]{1,0:T(8,128)(2,1)S(1)}, u32[]{:S(2)}, u32[]{:S(2)}) collective-permute-start(bf16[256,512]{1,0:T(8,128)(2,1)S(1)} %get-tuple-element.69), channel_id=1, source_target_pairs={{0,8},{4,12},{8,0},{12,4},{16,24},{20,28},{24,16},{28,20},{1,9},{5... | collective-permute-start | bytes 786440 | tf_op jit(solution)/shard_map/ppermute | solution.py:35
  81.2 7.2 %collective-permute-start.12 = (bf16[256,256]{1,0:T(8,128)(2,1)S(1)}, bf16[256,256]{1,0:T(8,128)(2,1)S(1)}, u32[]{:S(2)}, u32[]{:S(2)}) collective-permute-start(bf16[256,256]{1,0:T(8,128)(2,1)S(1)} %get-tuple-element.52), channel_id=1, source_target_pairs={{0,8},{4,12},{8,0},{12,4},{16,24},{20,28},{24,16},{28,20},{1,9},{5... | collective-permute-start | bytes 393224 | tf_op jit(solution)/shard_map/ppermute | solution.py:35
  81.5 7.0 %collective-permute-start.13 = (bf16[256,256]{1,0:T(8,128)(2,1)S(1)}, bf16[256,256]{1,0:T(8,128)(2,1)S(1)}, u32[]{:S(2)}, u32[]{:S(2)}) collective-permute-start(bf16[256,256]{1,0:T(8,128)(2,1)S(1)} %get-tuple-element.54), channel_id=1, source_target_pairs={{0,4},{4,0},{8,12},{12,8},{16,20},{20,16},{24,28},{28,24},{1,5},{5... | collective-permute-start | bytes 393224 | tf_op jit(solution)/shard_map/ppermute | solution.py:35
  88.5 6.2 %collective-permute-start.14 = (bf16[128,512]{1,0:T(8,128)(2,1)S(1)}, bf16[128,512]{1,0:T(8,128)(2,1)S(1)}, u32[]{:S(2)}, u32[]{:S(2)}) collective-permute-start(bf16[128,512]{1,0:T(8,128)(2,1)S(1)} %get-tuple-element.56), channel_id=1, source_target_pairs={{0,16},{4,20},{8,24},{12,28},{16,0},{20,4},{24,8},{28,12},{1,17},{... | collective-permute-start | bytes 393224 | tf_op jit(solution)/shard_map/ppermute | solution.py:35
  92.5 8.0 %collective-permute-start.26 = (bf16[256,256]{1,0:T(8,128)(2,1)S(1)}, bf16[256,256]{1,0:T(8,128)(2,1)S(1)}, u32[]{:S(2)}, u32[]{:S(2)}) collective-permute-start(bf16[256,256]{1,0:T(8,128)(2,1)S(1)} %get-tuple-element.71), channel_id=1, source_target_pairs={{0,8},{4,12},{8,0},{12,4},{16,24},{20,28},{24,16},{28,20},{1,9},{5... | collective-permute-start | bytes 393224 | tf_op jit(solution)/shard_map/ppermute | solution.py:35
  93.8 6.6 %collective-permute-start.27 = (bf16[256,256]{1,0:T(8,128)(2,1)S(1)}, bf16[256,256]{1,0:T(8,128)(2,1)S(1)}, u32[]{:S(2)}, u32[]{:S(2)}) collective-permute-start(bf16[256,256]{1,0:T(8,128)(2,1)S(1)} %get-tuple-element.73), channel_id=1, source_target_pairs={{0,4},{4,0},{8,12},{12,8},{16,20},{20,16},{24,28},{28,24},{1,5},{5... | collective-permute-start | bytes 393224 | tf_op jit(solution)/shard_map/ppermute | solution.py:35
  94.7 9.6 %collective-permute-start.15 = (bf16[128,512]{1,0:T(8,128)(2,1)S(1)}, bf16[128,512]{1,0:T(8,128)(2,1)S(1)}, u32[]{:S(2)}, u32[]{:S(2)}) collective-permute-start(bf16[128,512]{1,0:T(8,128)(2,1)S(1)} %shard_map.119), channel_id=1, source_target_pairs={{0,0},{1,8},{2,16},{3,24},{4,4},{5,12},{6,20},{7,28},{8,1},{9,9},{... | collective-permute-start | bytes 393224 | tf_op jit(solution)/shard_map/ppermute | solution.py:50
  100.6 11.8 %collective-permute-start.28 = (bf16[128,512]{1,0:T(8,128)(2,1)S(1)}, bf16[128,512]{1,0:T(8,128)(2,1)S(1)}, u32[]{:S(2)}, u32[]{:S(2)}) collective-permute-start(bf16[128,512]{1,0:T(8,128)(2,1)S(1)} %get-tuple-element.75), channel_id=1, source_target_pairs={{0,16},{4,20},{8,24},{12,28},{16,0},{20,4},{24,8},{28,12},{1,17},{... | collective-permute-start | bytes 393224 | tf_op jit(solution)/shard_map/ppermute | solution.py:35
  112.4 9.2 %collective-permute-start.29 = (bf16[128,512]{1,0:T(8,128)(2,1)S(1)}, bf16[128,512]{1,0:T(8,128)(2,1)S(1)}, u32[]{:S(2)}, u32[]{:S(2)}) collective-permute-start(bf16[128,512]{1,0:T(8,128)(2,1)S(1)} %shard_map.127), channel_id=1, source_target_pairs={{0,0},{1,8},{2,16},{3,24},{4,4},{5,12},{6,20},{7,28},{8,1},{9,9},{... | collective-permute-start | bytes 393224 | tf_op jit(solution)/shard_map/ppermute | solution.py:50
  (7 other events, 47.6 us)

commit v2 on v1

--- a/solution.py
+++ b/solution.py
@@ -13,20 +13,25 @@
 CHUNKS = 8
 MARGIN = 8
 VMEM_LIMIT = 16 * 1024 * 1024
+FLOPS_PER_US = 1_150_000_000
 
 
 VMEM = pl.BlockSpec(memory_space=pltpu.VMEM)
 HBM = pl.BlockSpec(memory_space=pl.ANY)
 
 
-def call(body, outs, scratch=(), in_specs=None, flops=0, nbytes=0):
+def cost(us):
+    return pl.CostEstimate(flops=int(us * FLOPS_PER_US), bytes_accessed=0, transcendentals=0)
+
+
+def call(body, outs, scratch=(), in_specs=None, us=0.5):
     return pl.pallas_call(
         body,
         out_shape=outs,
         **({} if in_specs is None else {"in_specs": in_specs}),
         scratch_shapes=list(scratch),
         compiler_params=pltpu.CompilerParams(vmem_limit_bytes=VMEM_LIMIT),
-        cost_estimate=pl.CostEstimate(flops=flops, bytes_accessed=nbytes, transcendentals=0),
+        cost_estimate=cost(us),
     )
 
 
@@ -111,8 +116,8 @@
     for j in range(3):
         feats[j, :MARGIN, :] = jnp.zeros((MARGIN, width), F32)
         for start, size in blocks:
-            total = kinds(parts, j, pl.ds(start, size))
-            feats[j, MARGIN + start : MARGIN + start + size, :] = total.astype(BF16).astype(F32)
+            row, total = kinds(parts, j, start, size)
+            feats[j, pl.ds(MARGIN + row, size), :] = total.astype(BF16).astype(F32)
     for start, size in blocks:
         mixed = []
         for j in range(3):
@@ -136,8 +141,8 @@
     length, width = query.shape
     blocks = row_blocks(length)
     for start, size in blocks:
-        at = slice(start, start + size)
-        grad_gated = kinds(parts, 0, pl.ds(start, size))
+        row, grad_gated = kinds(parts, 0, start, size)
+        at = pl.ds(row, size)
         mixin[0, at, :] = grad_gated * long_out[at, :]
         grad_long[at, :] = grad_gated * query[at, :]
     modal_scan(grad_long, summed, decay[...], spread[...], gain[...], True)
@@ -155,13 +160,17 @@
             grads[j, start : start + size, :] = total.astype(BF16)
 
 
-def sum_of_three(parts, j, at):
-    own, near, far = parts
-    return own[j, at, :] + near[j, at, :].astype(F32) + far[j, at, :].astype(F32)
-
-
-def plain(parts, j, at):
-    return parts[0][j, at, :].astype(F32)
+def sum_of_three(parts, j, start, size):
+    half = parts[0].shape[1]
+    other, local = divmod(start, half)
+    own, near, far = parts[3 * other : 3 * other + 3]
+    at = slice(local, local + size)
+    total = own[j, at, :] + near[j, at, :].astype(F32) + far[j, at, :].astype(F32)
+    return pl.multiple_of(((lax.axis_index("ctx") >> 1) ^ other) * half + local, MARGIN), total
+
+
+def plain(parts, j, start, size):
+    return start, parts[0][j, start : start + size, :].astype(F32)
 
 
 def filter_forward(parts, kinds, tables, length, width):
@@ -179,6 +188,7 @@
             pltpu.VMEM((length, width), F32),
             pltpu.VMEM((length, width), F32),
         ],
+        us=3.2,
     )(*parts, *tables)
 
 
@@ -198,6 +208,7 @@
             pltpu.VMEM((length, width), F32),
         ],
         in_specs=[VMEM] * inputs + [HBM] * len(after),
+        us=2.1,
     )(*parts, *tables, *saved, *after)
 
 
@@ -214,29 +225,39 @@
     )(value, after)
 
 
-def own_columns(rows, after=None):
-    me = lax.axis_index("ctx")
-    side = lax.axis_index("fsdp") & 1
-    width = rows.shape[1] // 4
-    part = lambda mask: lax.dynamic_slice_in_dim(rows, (me ^ mask) * width, width, 1)
+def column_blocks(rows):
+    length, width = rows.shape[0], rows.shape[1] // 4
+
+    def body(rows, own, near, far, arrived):
+        me = lax.axis_index("ctx")
+        side = lax.axis_index("fsdp") & 1
+        copies = []
+        for n, (mask, out) in enumerate(((2 ^ side, far), (1, near), (0, own))):
+            copies.append(pltpu.make_async_copy(rows.at[:, block_at(me ^ mask, width)], out, arrived.at[n]))
+            copies[-1].start()
+        for copy in copies:
+            copy.wait()
+
+    block = jax.ShapeDtypeStruct((length, width), rows.dtype)
+    return call(body, (block,) * 3, [pltpu.SemaphoreType.DMA((3,))], in_specs=[HBM], us=0.7)(rows)
+
+
+def fetched(block):
     pairs = [(4 * f + k, 4 * f + (k ^ 2 ^ (f & 1))) for f in range(8) for k in range(4)]
-    fetch = part(2 ^ side) if after is None else later(part(2 ^ side), after)
-    fetched = lax.ppermute(fetch, ("fsdp", "ctx"), pairs)
-    return part(0), flipped(part(1), "ctx", 1), fetched, flipped(fetched, "fsdp", 1)
-
-
-def project(pieces, weight, after=()):
+    return lax.ppermute(block, ("fsdp", "ctx"), pairs)
+
+
+def project(pieces, other, weight):
     groups, depth, channels = weight.shape
     part = pieces[0].shape[0]
-    length = 4 * part
+    length = 2 * part
     width = channels // 4
 
-    def body(a, b, c, d, weight, *refs):
-        held, own, far, give, give_far, product = refs[len(after) :]
+    def body(first, second, weight, own, far, give, give_far, held, product):
         me = lax.axis_index("ctx")
-        side = lax.axis_index("fsdp") & 1
-        for mask, piece in ((0, a), (1, b), (2 ^ side, c), (3 ^ side, d)):
-            held[block_at(me ^ mask, part), :] = piece[...]
+        core = (me ^ lax.axis_index("fsdp")) & 1 if other else me & 1
+        held[block_at(core, part), :] = first[...]
+        held[block_at(1 - core, part), :] = second[...]
         for j in range(groups):
             product[...] = dot(held[...], weight[j], (1, 0))
             own[j] = product[:, block_at(me, width)]
@@ -247,34 +268,31 @@
     sums = jax.ShapeDtypeStruct((groups, length, width), BF16)
     return call(
         body,
-        (
-            jax.ShapeDtypeStruct((length, depth), BF16),
-            jax.ShapeDtypeStruct((groups, length, width), F32),
-            sums,
-            sums,
-            sums,
-        ),
-        [pltpu.VMEM((length, channels), F32)],
-        in_specs=[VMEM] * 5 + [HBM] * len(after),
-    )(*pieces, weight, *after)
-
-
-def add_pair(left, right, after):
-    def body(left, right, *refs):
-        refs[-1][...] = (left[...].astype(F32) + right[...].astype(F32)).astype(BF16)
-
-    return call(body, jax.ShapeDtypeStruct(left.shape, BF16), in_specs=[VMEM] * 2 + [HBM] * len(after))(
-        left, right, *after
-    )
-
-
-def channel_sums(projected, after=()):
-    own, far, give, give_far = projected
-    passed = add_pair(far, flipped(give_far, "ctx", 1), after)
+        (jax.ShapeDtypeStruct((groups, length, width), F32), sums, sums, sums),
+        [pltpu.VMEM((length, depth), BF16), pltpu.VMEM((length, channels), F32)],
+        us=0.7 * groups,
+    )(*pieces, weight)
+
+
+def add_far(left, right):
+    def body(left, right, out):
+        out[...] = (left[...].astype(F32) + right[...].astype(F32)).astype(BF16)
+
+    return call(body, jax.ShapeDtypeStruct(left.shape, BF16))(left, right)
+
+
+def channel_sums(pieces, other, weight):
+    own, far, give, give_far = project(pieces, other, weight)
+    passed = add_far(far, flipped(give_far, "ctx", 1))
     return own, flipped(give, "ctx", 1), flipped(passed, "ctx", 2)
 
 
-def all_channels(value):
+def by_token(here, there):
+    return here[0], here[1], there[2], there[0], there[1], here[2]
+
+
+def all_channels(value, after=None):
+    value = value if after is None else later(value, after)
     far = flipped(value, "ctx", 2)
     return value, far, flipped(value, "ctx", 1), flipped(far, "ctx", 1)
 
@@ -318,8 +336,9 @@
         first_body,
         (jax.ShapeDtypeStruct((groups, length, channels), BF16), *parts),
         in_specs=[VMEM] * 5 + [HBM] * len(after),
+        us=0.6 * groups,
     )(*gathered, weight, *after)
-    keeps = call(second_body, parts)(whole, weight)
+    keeps = call(second_body, parts, us=0.4 * groups)(whole, weight)
     return whole, keeps, gives
 
 
@@ -368,50 +387,63 @@
     return to_placement(call(last_body, block(BF16))(keep, flipped(give, "fsdp", 4)))
 
 
+def turned(pieces):
+    part, depth = pieces[0].shape
+
+    def body(a, b, c, d, out):
+        me = lax.axis_index("ctx")
+        side = lax.axis_index("fsdp") & 1
+        for mask, piece in ((0, a), (1, b), (2 ^ side, c), (3 ^ side, d)):
+            out[:, block_at(me ^ mask, part)] = piece[...].T
+
+    return call(body, jax.ShapeDtypeStruct((depth, 4 * part), pieces[0].dtype), us=1.0)(*pieces)
+
+
 def weight_gradient(rows, values):
-    length, depth = rows.shape
+    depth, length = rows.shape
     groups, _, channels = values.shape
-    tile = 256
+    tile = depth // 2
 
     def body(rows, values, out):
-        out[0] = dot(rows[...], values[0], (0, 0))
+        out[0] = dot(rows[...], values[0], (1, 0))
 
     return pl.pallas_call(
         body,
         out_shape=jax.ShapeDtypeStruct((groups, depth, channels), F32),
         grid=(groups, depth // tile),
         in_specs=[
-            pl.BlockSpec((length, tile), lambda j, i: (0, i)),
+            pl.BlockSpec((tile, length), lambda j, i: (i, 0)),
             pl.BlockSpec((1, length, channels), lambda j, i: (j, 0, 0)),
         ],
         out_specs=pl.BlockSpec((1, tile, channels), lambda j, i: (j, i, 0)),
         compiler_params=pltpu.CompilerParams(vmem_limit_bytes=VMEM_LIMIT),
-        cost_estimate=pl.CostEstimate(
-            flops=2 * length * depth * channels * groups,
-            bytes_accessed=4 * groups * depth * channels,
-            transcendentals=0,
-        ),
+        cost_estimate=cost(1.5 * groups),
     )(rows, values)
 
 
 def four_by_eight(tokens, weights, tables, out_weight, grad_mixed):
     length, width = 4 * tokens.shape[0], weights.shape[2] // 4
-    token_pieces = own_columns(tokens)
-    grad_pieces = own_columns(grad_mixed, token_pieces[2])
-    whole_tokens, *projected = project(token_pieces, weights, grad_pieces[2:3])
-    feats = channel_sums(projected)
-    whole_cotangents, *projected = project(grad_pieces, out_weight[None])
-    grad_gated = channel_sums(projected)
-    *saved, gated = filter_forward(feats, sum_of_three, tables, length, width)
+    own, near, far = column_blocks(tokens)
+    here = (own, flipped(near, "ctx", 1))
+    far = fetched(far)
+    there = (far, flipped(far, "fsdp", 1))
+    feats_here = channel_sums(here, 0, weights)
+    grad_own, grad_near, grad_far = column_blocks(grad_mixed)
+    grad_here = (grad_own, flipped(grad_near, "ctx", 1))
+    grad_far = fetched(later(grad_far, feats_here[2]))
+    grad_there = (grad_far, flipped(grad_far, "fsdp", 1))
+    feats_there = channel_sums(there, 1, weights)
+    grads_here = channel_sums(grad_here, 0, out_weight[None])
+    grads_there = channel_sums(grad_there, 1, out_weight[None])
+    *saved, gated = filter_forward(by_token(feats_here, feats_there), sum_of_three, tables, length, width)
     all_gated = all_channels(gated[None])
     whole_gated, keeps, gives = output_pieces(all_gated, out_weight[None])
-    givens = exchange(gives)
-    mixed = block_sums(keeps, givens)
-    grads = filter_backward(grad_gated, sum_of_three, tables, saved, length, width, all_gated[1:2])
-    whole_grads, keeps, gives = output_pieces(all_channels(grads), weights, givens)
+    mixed = block_sums(keeps, exchange(gives))
+    grads = filter_backward(by_token(grads_here, grads_there), sum_of_three, tables, saved, length, width)
+    whole_grads, keeps, gives = output_pieces(all_channels(grads, all_gated[1]), weights)
     grad_tokens = block_sums(keeps, exchange(gives))
-    grad_in = weight_gradient(whole_tokens, whole_grads)
-    grad_out = weight_gradient(whole_cotangents, whole_gated)[0]
+    grad_in = weight_gradient(turned(here + there), whole_grads)
+    grad_out = weight_gradient(turned(grad_here + grad_there), whole_gated)[0]
     return mixed, grad_tokens, grad_in, grad_out
 
 
@@ -454,7 +486,7 @@
     rate = mine(decay_rate)
     gain = mine(residue) * jnp.sqrt(-jnp.expm1(-2.0 * rate))
     tables = (mine(conv_taps.transpose(1, 0, 2)), jnp.exp(-rate), jnp.exp(-rate * (length // CHUNKS)), gain, mine(skip_gain[None]))
-    tuned = count == 4 and blocks == 8 and width % LANES == 0
+    tuned = count == 4 and blocks == 8 and width % LANES == 0 and tokens.shape[0] % LANES == 0
     plan = four_by_eight if tuned else any_mesh
     mixed, grad_tokens, grad_in, grad_out = plan(tokens, weights, tables, out_weight, grad_mixed)
     return mixed, grad_tokens, grad_in.transpose(1, 0, 2), grad_out

time: 123 us -> 118 us (0.959)
  waiting for transfers between devices: 46 us -> 35.3 us
  starting transfers between devices: 36.6 us -> 42.4 us
  Pallas kernels: 27.4 us -> 25.6 us
    ppermute x26 -> x32, waiting for transfers between devices: 42 us -> 28.2 us  [flipped(): lax.ppermute(value, axis, [(source, source ^ mask) for source in range(co...]
    unnamed x20 -> x58, local copies, waits for them, and re-layouts: 6.49 us -> 11.7 us
    dynamic_slice x2 -> x0, local copies, waits for them, and re-layouts: 4.03 us -> none  [own_columns(): lax.dynamic_slice_in_dim(rows, (me ^ mask) * width, width, 1)]
    pallas_call x2, Pallas kernels: 9.99 us -> 6.55 us  [weight_gradient(): pl.pallas_call(body, out_shape=jax.ShapeDtypeStruct((groups, depth, chann...]
    ppermute x2, waiting for transfers between devices: 0.01 us -> 2.94 us  [to_placement(): return lax.ppermute(value, ('fsdp', 'ctx'), pairs)]
    pallas_call x6 -> x14, Pallas kernels: 9.25 us -> 11.9 us  [the longest x4 6.89 us: project(): call(body, (jax.ShapeDtypeStruct((groups, length, width), F32), sums, sum...]
    ppermute x2, starting transfers between devices: 7.68 us -> 10.3 us  [to_placement(): return lax.ppermute(value, ('fsdp', 'ctx'), pairs)]
    ppermute x26 -> x32, starting transfers between devices: 25.6 us -> 28.1 us  [flipped(): lax.ppermute(value, axis, [(source, source ^ mask) for source in range(co...]
  transfers between devices with their start and end apart: 30 -> 36, of which waited for: 11 -> 15; matrix products, arithmetic and copies ran while one was open for 3% -> 1% of each run, Pallas kernels for 16% -> 22%
where the time goes in v2:
time: 118 us; the launch traced here: 117 us
  starting transfers between devices  42.4 us (36%)
  waiting for transfers between devices  35.3 us (30%)
  Pallas kernels  25.6 us (22%)
  local copies, waits for them, and re-layouts  12.4 us (11%)
    ppermute x32, waiting for transfers between devices, flipped(): lax.ppermute(value, axis, [(source, source ^ mask) for source in range(co...  28.2 us
    ppermute x32, starting transfers between devices, flipped(): lax.ppermute(value, axis, [(source, source ^ mask) for source in range(co...  28.1 us
    unnamed x58, local copies, waits for them, and re-layouts  11.7 us
    ppermute x2, starting transfers between devices, to_placement(): return lax.ppermute(value, ('fsdp', 'ctx'), pairs)  10.3 us
    pallas_call x4, Pallas kernels, project(): call(body, (jax.ShapeDtypeStruct((groups, length, width), F32), sums, sum...  6.89 us
    pallas_call x2, Pallas kernels, weight_gradient(): pl.pallas_call(body, out_shape=jax.ShapeDtypeStruct((groups, depth, chann...  6.55 us
    ppermute x2, waiting for transfers between devices, fetched(): return lax.ppermute(block, ('fsdp', 'ctx'), pairs)  4.17 us
    ppermute x2, starting transfers between devices, fetched(): return lax.ppermute(block, ('fsdp', 'ctx'), pairs)  3.94 us
  transfers between devices with their start and end apart: 36, of which 15 were waited for; matrix products, arithmetic and copies ran while one was open for 1% of the time, Pallas kernels for 22%

profile of v2, /device:TPU:1, one launch (start us, length us, event | category | flops | bytes accessed | tf_op | source)
XLA Modules:
  0.0 117.4 jit_solution(3592028855614883854)
XLA Ops:
  2.1 2.7 %collective-permute-start.2 = (bf16[128,1024]{1,0:T(8,128)(2,1)S(1)}, bf16[128,1024]{1,0:T(8,128)(2,1)}, u32[]{:S(2)}, u32[]{:S(2)}) collective-permute-start(bf16[128,1024]{1,0:T(8,128)(2,1)S(1)} %get-tuple-element.57), channel_id=1, source_target_pairs={{0,2},{1,3},{2,0},{3,1},{4,7},{5,6},{6,5},{7,4},{8,10},{9,11},{10,... | collective-permute-start | bytes 786440 | tf_op jit(solution)/shard_map/ppermute | solution.py:247
  4.8 2.0 %copy-done.8 = bf16[1024,3,512]{2,0,1:T(8,128)(2,1)S(1)} copy-done((bf16[1024,3,512]{2,0,1:T(8,128)(2,1)S(1)}, bf16[1024,3,512]{2,0,1:T(8,128)(2,1)}, u32[]{:S(2)}) %copy-start.8) | copy-done | bytes 3145752
  9.2 2.3 %collective-permute-done.2.first.c = bf16[128,1024]{1,0:T(8,128)(2,1)} collective-permute-done((bf16[128,1024]{1,0:T(8,128)(2,1)S(1)}, bf16[128,1024]{1,0:T(8,128)(2,1)}, u32[]{:S(2)}, u32[]{:S(2)}) %collective-permute-start.2) | collective-permute-done | bytes 262176 | tf_op jit(solution)/shard_map/ppermute | solution.py:247
  11.5 1.4 %collective-permute-start.3 = (bf16[128,1024]{1,0:T(8,128)(2,1)}, bf16[128,1024]{1,0:T(8,128)(2,1)}, u32[]{:S(2)}, u32[]{:S(2)}) collective-permute-start(bf16[128,1024]{1,0:T(8,128)(2,1)} %collective-permute-done.2.first.c), channel_id=1, source_target_pairs={{0,4},{4,0},{8,12},{12,8},{16,20},{20,16},{24,28},{28,24},{1,5},{5... | collective-permute-start | bytes 786440 | tf_op jit(solution)/shard_map/ppermute | solution.py:40
  16.5 2.8 %collective-permute-done.8.refs_5_.after = bf16[3,256,128]{2,1,0:T(8,128)(2,1)S(1)} collective-permute-done((bf16[3,256,128]{2,1,0:T(8,128)(2,1)S(1)}, bf16[3,256,128]{2,1,0:T(8,128)(2,1)S(1)}, u32[]{:S(2)}, u32[]{:S(2)}) %collective-permute-start.8) | collective-permute-done | bytes 196640 | tf_op jit(solution)/shard_map/ppermute | solution.py:40
  22.6 2.4 %shard_map.113 = (f32[3,256,128]{2,1,0:T(8,128)S(1)}, bf16[3,256,128]{2,1,0:T(8,128)(2,1)S(1)}, bf16[3,256,128]{2,1,0:T(8,128)(2,1)S(1)}, bf16[3,256,128]{2,1,0:T(8,128)(2,1)S(1)}) custom-call(bf16[128,1024]{1,0:T(8,128)(2,1)} %collective-permute-done.2.first.c, bf16[128,1024]{1,0:T(8,128)(2,1)} %collective-permute-done.3.second.d, ...), custom_call_target="tpu_custom_call" | custom-call | flops 2415000064 | tf_op jit(solution)/shard_map/pallas_call | solution.py:269
  25.1 1.9 %collective-permute-done.20.first.c = bf16[128,1024]{1,0:T(8,128)(2,1)} collective-permute-done((bf16[128,1024]{1,0:T(8,128)(2,1)}, bf16[128,1024]{1,0:T(8,128)(2,1)}, u32[]{:S(2)}, u32[]{:S(2)}) %collective-permute-start.20) | collective-permute-done | bytes 262176 | tf_op jit(solution)/shard_map/ppermute | solution.py:247
  27.0 2.5 %collective-permute-start.21 = (bf16[128,1024]{1,0:T(8,128)(2,1)}, bf16[128,1024]{1,0:T(8,128)(2,1)S(1)}, u32[]{:S(2)}, u32[]{:S(2)}) collective-permute-start(bf16[128,1024]{1,0:T(8,128)(2,1)} %collective-permute-done.20.first.c), channel_id=1, source_target_pairs={{0,4},{4,0},{8,12},{12,8},{16,20},{20,16},{24,28},{28,24},{1,5},{5... | collective-permute-start | bytes 786440 | tf_op jit(solution)/shard_map/ppermute | solution.py:40
  31.0 1.5 %shard_map.123 = (f32[1,256,128]{2,1,0:T(8,128)S(1)}, bf16[1,256,128]{2,1,0:T(8,128)(2,1)S(1)}, bf16[1,256,128]{2,1,0:T(8,128)(2,1)S(1)}, bf16[1,256,128]{2,1,0:T(8,128)(2,1)S(1)}) custom-call(bf16[128,1024]{1,0:T(8,128)(2,1)S(1)} %copy-done.22, bf16[128,1024]{1,0:T(8,128)(2,1)} %collective-permute-done.18.second.b, bf16[1,1024,512]{2,1,0:T(8,128)(2,1)S(1)} %bitcast.13), custom_call_target="tpu_custom_call" | custom-call | flops 805000000 | tf_op jit(solution)/shard_map/pallas_call | solution.py:269
  33.7 1.4 %collective-permute-done.21.second.d = bf16[128,1024]{1,0:T(8,128)(2,1)S(1)} collective-permute-done((bf16[128,1024]{1,0:T(8,128)(2,1)}, bf16[128,1024]{1,0:T(8,128)(2,1)S(1)}, u32[]{:S(2)}, u32[]{:S(2)}) %collective-permute-start.21) | collective-permute-done | bytes 262176 | tf_op jit(solution)/shard_map/ppermute | solution.py:40
  35.1 1.6 %shard_map.125 = (f32[1,256,128]{2,1,0:T(8,128)S(1)}, bf16[1,256,128]{2,1,0:T(8,128)(2,1)S(1)}, bf16[1,256,128]{2,1,0:T(8,128)(2,1)S(1)}, bf16[1,256,128]{2,1,0:T(8,128)(2,1)S(1)}) custom-call(bf16[128,1024]{1,0:T(8,128)(2,1)} %collective-permute-done.20.first.c, bf16[128,1024]{1,0:T(8,128)(2,1)S(1)} %collective-permute-done.21.second.d, ...), custom_call_target="tpu_custom_call" | custom-call | flops 805000000 | tf_op jit(solution)/shard_map/pallas_call | solution.py:269
  36.7 1.9 %collective-permute-start.22 = (bf16[1,256,128]{2,1,0:T(8,128)(2,1)S(1)}, bf16[1,256,128]{2,1,0:T(8,128)(2,1)S(1)}, u32[]{:S(2)}, u32[]{:S(2)}) collective-permute-start(bf16[1,256,128]{2,1,0:T(8,128)(2,1)S(1)} %get-tuple-element.82), channel_id=1, source_target_pairs={{0,1},{1,0},{2,3},{3,2},{4,5},{5,4},{6,7},{7,6},{8,9},{9,8},{10,11... | collective-permute-start | bytes 196616 | tf_op jit(solution)/shard_map/ppermute | solution.py:40
  41.9 2.2 %shard_map.116 = (f32[512,128]{1,0:T(8,128)S(1)}, f32[512,128]{1,0:T(8,128)S(1)}, f32[512,128]{1,0:T(8,128)S(1)}, f32[512,128]{1,0:T(8,128)S(1)}, bf16[512,128]{1,0:T(8,128)(2,1)S(1)}) custom-call(f32[3,256,128]{2,1,0:T(8,128)S(1)} %copy-done.27, bf16[3,256,128]{2,1,0:T(8,128)(2,1)S(1)} %collective-permute-done.1.refs_1_, ...), custom_call_target="tpu_custom_call" | custom-call | flops 3680000000 | tf_op jit(solution)/shard_map/pallas_call | solution.py:183
  44.7 2.1 %shard_map.128.value = bf16[3,512,128]{2,1,0:T(8,128)(2,1)S(1)} custom-call(f32[1,256,128]{2,1,0:T(8,128)S(1)} %get-tuple-element.78.refs_0_, bf16[1,256,128]{2,1,0:T(8,128)(2,1)S(1)} %collective-permute-done.19.refs_1_, bf16[1,256,128]{2,1,0:T(8,128)(2,1)S(1)} %collective-permute-done.23.refs_2_, f32[1,256,128]{2,1,0:T(8,128)S(1)} %get-tuple-element.83.refs_3_, ...), custom_call_target="tpu_custom_call" | custom-call | flops 2415000064 | tf_op jit(solution)/shard_map/pallas_call | solution.py:202
  49.7 1.5 %collective-permute-start.10 = (bf16[1,512,128]{2,1,0:T(8,128)(2,1)S(1)}, bf16[1,512,128]{2,1,0:T(8,128)(2,1)S(1)}, u32[]{:S(2)}, u32[]{:S(2)}) collective-permute-start(bf16[1,512,128]{2,1,0:T(8,128)(2,1)S(1)} %bitcast.18), channel_id=1, source_target_pairs={{0,1},{1,0},{2,3},{3,2},{4,5},{5,4},{6,7},{7,6},{8,9},{9,8},{10,11... | collective-permute-start | bytes 393224 | tf_op jit(solution)/shard_map/ppermute | solution.py:40
  51.6 7.5 %collective-permute-done.27.far = bf16[3,512,128]{2,1,0:T(8,128)(2,1)S(1)} collective-permute-done((bf16[3,512,128]{2,1,0:T(8,128)(2,1)}, bf16[3,512,128]{2,1,0:T(8,128)(2,1)S(1)}, u32[]{:S(2)}, u32[]{:S(2)}) %collective-permute-start.27) | collective-permute-done | bytes 393248 | tf_op jit(solution)/shard_map/ppermute | solution.py:40
  59.1 2.1 %collective-permute-start.29 = (bf16[3,512,128]{2,1,0:T(8,128)(2,1)S(1)}, bf16[3,512,128]{2,1,0:T(8,128)(2,1)S(1)}, u32[]{:S(2)}, u32[]{:S(2)}) collective-permute-start(bf16[3,512,128]{2,1,0:T(8,128)(2,1)S(1)} %collective-permute-done.27.far), channel_id=1, source_target_pairs={{0,1},{1,0},{2,3},{3,2},{4,5},{5,4},{6,7},{7,6},{8,9},{9,8},{10,11... | collective-permute-start | bytes 1179656 | tf_op jit(solution)/shard_map/ppermute | solution.py:40
  64.0 1.5 %collective-permute-start.12 = (bf16[512,256]{1,0:T(8,128)(2,1)S(1)}, bf16[512,256]{1,0:T(8,128)(2,1)S(1)}, u32[]{:S(2)}, u32[]{:S(2)}) collective-permute-start(bf16[512,256]{1,0:T(8,128)(2,1)S(1)} %get-tuple-element.67), channel_id=1, source_target_pairs={{0,4},{4,0},{8,12},{12,8},{16,20},{20,16},{24,28},{28,24},{1,5},{5... | collective-permute-start | bytes 786440 | tf_op jit(solution)/shard_map/ppermute | solution.py:40
  65.6 1.4 %collective-permute-start.13 = (bf16[256,512]{1,0:T(8,128)(2,1)S(1)}, bf16[256,512]{1,0:T(8,128)(2,1)S(1)}, u32[]{:S(2)}, u32[]{:S(2)}) collective-permute-start(bf16[256,512]{1,0:T(8,128)(2,1)S(1)} %get-tuple-element.69), channel_id=1, source_target_pairs={{0,8},{4,12},{8,0},{12,4},{16,24},{20,28},{24,16},{28,20},{1,9},{5... | collective-permute-start | bytes 786440 | tf_op jit(solution)/shard_map/ppermute | solution.py:40
  67.5 4.5 %collective-permute-done.12.given_x = bf16[512,256]{1,0:T(8,128)(2,1)S(1)} collective-permute-done((bf16[512,256]{1,0:T(8,128)(2,1)S(1)}, bf16[512,256]{1,0:T(8,128)(2,1)S(1)}, u32[]{:S(2)}, u32[]{:S(2)}) %collective-permute-start.12) | collective-permute-done | bytes 262176 | tf_op jit(solution)/shard_map/ppermute | solution.py:40
  73.3 1.5 %collective-permute-start.14 = (bf16[256,256]{1,0:T(8,128)(2,1)S(1)}, bf16[256,256]{1,0:T(8,128)(2,1)S(1)}, u32[]{:S(2)}, u32[]{:S(2)}) collective-permute-start(bf16[256,256]{1,0:T(8,128)(2,1)S(1)} %get-tuple-element.71), channel_id=1, source_target_pairs={{0,8},{4,12},{8,0},{12,4},{16,24},{20,28},{24,16},{28,20},{1,9},{5... | collective-permute-start | bytes 393224 | tf_op jit(solution)/shard_map/ppermute | solution.py:40
  75.1 1.8 %shard_map.130 = (bf16[3,512,512]{2,1,0:T(8,128)(2,1)S(1)}, bf16[512,256]{1,0:T(8,128)(2,1)S(1)}, bf16[256,512]{1,0:T(8,128)(2,1)S(1)}) custom-call(bf16[3,512,128]{2,1,0:T(8,128)(2,1)S(1)} %copy-done.2, bf16[3,512,128]{2,1,0:T(8,128)(2,1)S(1)} %collective-permute-done.27.far, bf16[3,512,128]{2,1,0:T(8,128)(2,1)S(1)} %collective-permute-done.28.near, ...), custom_call_target="tpu_custom_call" | custom-call | flops 2070000000 | tf_op jit(solution)/shard_map/pallas_call | solution.py:335
  79.6 2.5 %collective-permute-start.16 = (bf16[128,512]{1,0:T(8,128)(2,1)S(1)}, bf16[128,512]{1,0:T(8,128)(2,1)S(1)}, u32[]{:S(2)}, u32[]{:S(2)}) collective-permute-start(bf16[128,512]{1,0:T(8,128)(2,1)S(1)} %get-tuple-element.75), channel_id=1, source_target_pairs={{0,16},{4,20},{8,24},{12,28},{16,0},{20,4},{24,8},{28,12},{1,17},{... | collective-permute-start | bytes 393224 | tf_op jit(solution)/shard_map/ppermute | solution.py:40
  82.1 1.5 %shard_map.131 = (bf16[512,256]{1,0:T(8,128)(2,1)S(1)}, bf16[256,512]{1,0:T(8,128)(2,1)S(1)}) custom-call(bf16[3,512,512]{2,1,0:T(8,128)(2,1)S(1)} %get-tuple-element.91.whole.values, bf16[3,1024,512]{2,1,0:T(8,128)(2,1)S(1)} %bitcast.12), custom_call_target="tpu_custom_call" | custom-call | flops 1380000000 | tf_op jit(solution)/shard_map/pallas_call | solution.py:341
  83.6 1.6 %collective-permute-done.30.given_x = bf16[512,256]{1,0:T(8,128)(2,1)S(1)} collective-permute-done((bf16[512,256]{1,0:T(8,128)(2,1)S(1)}, bf16[512,256]{1,0:T(8,128)(2,1)S(1)}, u32[]{:S(2)}, u32[]{:S(2)}) %collective-permute-start.30) | collective-permute-done | bytes 262176 | tf_op jit(solution)/shard_map/ppermute | solution.py:40
  87.6 8.4 %collective-permute-start.17 = (bf16[128,512]{1,0:T(8,128)(2,1)S(1)}, bf16[128,512]{1,0:T(8,128)(2,1)S(1)}, u32[]{:S(2)}, u32[]{:S(2)}) collective-permute-start(bf16[128,512]{1,0:T(8,128)(2,1)S(1)} %shard_map.121), channel_id=1, source_target_pairs={{0,0},{1,8},{2,16},{3,24},{4,4},{5,12},{6,20},{7,28},{8,1},{9,9},{... | collective-permute-start | bytes 393224 | tf_op jit(solution)/shard_map/ppermute | solution.py:55
  97.4 1.9 %shard_map.138 = f32[1,1024,512]{2,1,0:T(8,128)} custom-call(bf16[1024,512]{1,0:T(8,128)(2,1)S(1)} %shard_map.137.rows, bf16[1,512,512]{2,1,0:T(8,128)(2,1)S(1)} %get-tuple-element.65.whole.values), custom_call_target="tpu_custom_call" | custom-call | flops 1724999936 | tf_op jit(solution)/shard_map/pallas_call | solution.py:410
  99.2 1.5 %collective-permute-done.17 = bf16[128,512]{1,0:T(8,128)(2,1)S(1)} collective-permute-done((bf16[128,512]{1,0:T(8,128)(2,1)S(1)}, bf16[128,512]{1,0:T(8,128)(2,1)S(1)}, u32[]{:S(2)}, u32[]{:S(2)}) %collective-permute-start.17) | collective-permute-done | bytes 131104 | tf_op jit(solution)/shard_map/ppermute | solution.py:55
  100.7 7.3 %collective-permute-done.34.given = bf16[128,512]{1,0:T(8,128)(2,1)S(1)} collective-permute-done((bf16[128,512]{1,0:T(8,128)(2,1)S(1)}, bf16[128,512]{1,0:T(8,128)(2,1)S(1)}, u32[]{:S(2)}, u32[]{:S(2)}) %collective-permute-start.34) | collective-permute-done | bytes 131104 | tf_op jit(solution)/shard_map/ppermute | solution.py:40
  108.0 1.9 %collective-permute-start.35 = (bf16[128,512]{1,0:T(8,128)(2,1)S(1)}, bf16[128,512]{1,0:T(8,128)(2,1)S(1)}, u32[]{:S(2)}, u32[]{:S(2)}) collective-permute-start(bf16[128,512]{1,0:T(8,128)(2,1)S(1)} %shard_map.134), channel_id=1, source_target_pairs={{0,0},{1,8},{2,16},{3,24},{4,4},{5,12},{6,20},{7,28},{8,1},{9,9},{... | collective-permute-start | bytes 393224 | tf_op jit(solution)/shard_map/ppermute | solution.py:55
  110.0 4.7 %shard_map.136 = f32[3,1024,512]{2,1,0:T(8,128)} custom-call(bf16[1024,512]{1,0:T(8,128)(2,1)S(1)} %shard_map.135.rows, bf16[3,512,512]{2,1,0:T(8,128)(2,1)S(1)} %get-tuple-element.91.whole.values), custom_call_target="tpu_custom_call" | custom-call | flops 5175000064 | tf_op jit(solution)/shard_map/pallas_call | solution.py:410
  114.7 1.4 %collective-permute-done.35 = bf16[128,512]{1,0:T(8,128)(2,1)S(1)} collective-permute-done((bf16[128,512]{1,0:T(8,128)(2,1)S(1)}, bf16[128,512]{1,0:T(8,128)(2,1)S(1)}, u32[]{:S(2)}, u32[]{:S(2)}) %collective-permute-start.35) | collective-permute-done | bytes 131104 | tf_op jit(solution)/shard_map/ppermute | solution.py:55
  (129 shorter events, 33.3 us)
Async XLA Ops:
  2.1 9.4 %collective-permute-start.2 = (bf16[128,1024]{1,0:T(8,128)(2,1)S(1)}, bf16[128,1024]{1,0:T(8,128)(2,1)}, u32[]{:S(2)}, u32[]{:S(2)}) collective-permute-start(bf16[128,1024]{1,0:T(8,128)(2,1)S(1)} %get-tuple-element.57), channel_id=1, source_target_pairs={{0,2},{1,3},{2,0},{3,1},{4,7},{5,6},{6,5},{7,4},{8,10},{9,11},{10,... | collective-permute-start | bytes 786440 | tf_op jit(solution)/shard_map/ppermute | solution.py:247
  11.5 11.0 %collective-permute-start.3 = (bf16[128,1024]{1,0:T(8,128)(2,1)}, bf16[128,1024]{1,0:T(8,128)(2,1)}, u32[]{:S(2)}, u32[]{:S(2)}) collective-permute-start(bf16[128,1024]{1,0:T(8,128)(2,1)} %collective-permute-done.2.first.c), channel_id=1, source_target_pairs={{0,4},{4,0},{8,12},{12,8},{16,20},{20,16},{24,28},{28,24},{1,5},{5... | collective-permute-start | bytes 786440 | tf_op jit(solution)/shard_map/ppermute | solution.py:40
  13.0 6.3 %collective-permute-start.8 = (bf16[3,256,128]{2,1,0:T(8,128)(2,1)S(1)}, bf16[3,256,128]{2,1,0:T(8,128)(2,1)S(1)}, u32[]{:S(2)}, u32[]{:S(2)}) collective-permute-start(bf16[3,256,128]{2,1,0:T(8,128)(2,1)S(1)} %shard_map.115), channel_id=1, source_target_pairs={{0,2},{1,3},{2,0},{3,1},{4,6},{5,7},{6,4},{7,5},{8,10},{9,11},{10,... | collective-permute-start | bytes 589832 | tf_op jit(solution)/shard_map/ppermute | solution.py:40
  19.9 7.0 %collective-permute-start.20 = (bf16[128,1024]{1,0:T(8,128)(2,1)}, bf16[128,1024]{1,0:T(8,128)(2,1)}, u32[]{:S(2)}, u32[]{:S(2)}) collective-permute-start(bf16[128,1024]{1,0:T(8,128)(2,1)} %shard_map.124), channel_id=1, source_target_pairs={{0,2},{1,3},{2,0},{3,1},{4,7},{5,6},{6,5},{7,4},{8,10},{9,11},{10,... | collective-permute-start | bytes 786440 | tf_op jit(solution)/shard_map/ppermute | solution.py:247
  21.2 9.8 %collective-permute-start.18 = (bf16[128,1024]{1,0:T(8,128)(2,1)}, bf16[128,1024]{1,0:T(8,128)(2,1)}, u32[]{:S(2)}, u32[]{:S(2)}) collective-permute-start(bf16[128,1024]{1,0:T(8,128)(2,1)} %copy-done.18), channel_id=1, source_target_pairs={{0,1},{1,0},{2,3},{3,2},{4,5},{5,4},{6,7},{7,6},{8,9},{9,8},{10,11... | collective-permute-start | bytes 786440 | tf_op jit(solution)/shard_map/ppermute | solution.py:40
  25.0 8.1 %collective-permute-start.4 = (bf16[3,256,128]{2,1,0:T(8,128)(2,1)S(1)}, bf16[3,256,128]{2,1,0:T(8,128)(2,1)S(1)}, u32[]{:S(2)}, u32[]{:S(2)}) collective-permute-start(bf16[3,256,128]{2,1,0:T(8,128)(2,1)S(1)} %get-tuple-element.59), channel_id=1, source_target_pairs={{0,1},{1,0},{2,3},{3,2},{4,5},{5,4},{6,7},{7,6},{8,9},{9,8},{10,11... | collective-permute-start | bytes 589832 | tf_op jit(solution)/shard_map/ppermute | solution.py:40
  27.0 8.1 %collective-permute-start.21 = (bf16[128,1024]{1,0:T(8,128)(2,1)}, bf16[128,1024]{1,0:T(8,128)(2,1)S(1)}, u32[]{:S(2)}, u32[]{:S(2)}) collective-permute-start(bf16[128,1024]{1,0:T(8,128)(2,1)} %collective-permute-done.20.first.c), channel_id=1, source_target_pairs={{0,4},{4,0},{8,12},{12,8},{16,20},{20,16},{24,28},{28,24},{1,5},{5... | collective-permute-start | bytes 786440 | tf_op jit(solution)/shard_map/ppermute | solution.py:40
  30.2 9.5 %collective-permute-start.1 = (bf16[3,256,128]{2,1,0:T(8,128)(2,1)S(1)}, bf16[3,256,128]{2,1,0:T(8,128)(2,1)S(1)}, u32[]{:S(2)}, u32[]{:S(2)}) collective-permute-start(bf16[3,256,128]{2,1,0:T(8,128)(2,1)S(1)} %copy-done.20), channel_id=1, source_target_pairs={{0,1},{1,0},{2,3},{3,2},{4,5},{5,4},{6,7},{7,6},{8,9},{9,8},{10,11... | collective-permute-start | bytes 589832 | tf_op jit(solution)/shard_map/ppermute | solution.py:40
  32.5 6.9 %collective-permute-start.25 = (bf16[1,256,128]{2,1,0:T(8,128)(2,1)S(1)}, bf16[1,256,128]{2,1,0:T(8,128)(2,1)S(1)}, u32[]{:S(2)}, u32[]{:S(2)}) collective-permute-start(bf16[1,256,128]{2,1,0:T(8,128)(2,1)S(1)} %get-tuple-element.86), channel_id=1, source_target_pairs={{0,1},{1,0},{2,3},{3,2},{4,5},{5,4},{6,7},{7,6},{8,9},{9,8},{10,11... | collective-permute-start | bytes 196616 | tf_op jit(solution)/shard_map/ppermute | solution.py:40
  32.6 8.0 %collective-permute-start.6 = (bf16[3,256,128]{2,1,0:T(8,128)(2,1)S(1)}, bf16[3,256,128]{2,1,0:T(8,128)(2,1)S(1)}, u32[]{:S(2)}, u32[]{:S(2)}) collective-permute-start(bf16[3,256,128]{2,1,0:T(8,128)(2,1)S(1)} %get-tuple-element.61), channel_id=1, source_target_pairs={{0,1},{1,0},{2,3},{3,2},{4,5},{5,4},{6,7},{7,6},{8,9},{9,8},{10,11... | collective-permute-start | bytes 589832 | tf_op jit(solution)/shard_map/ppermute | solution.py:40
  33.2 8.7 %collective-permute-start.5 = (bf16[3,256,128]{2,1,0:T(8,128)(2,1)S(1)}, bf16[3,256,128]{2,1,0:T(8,128)(2,1)S(1)}, u32[]{:S(2)}, u32[]{:S(2)}) collective-permute-start(bf16[3,256,128]{2,1,0:T(8,128)(2,1)S(1)} %shard_map.114), channel_id=1, source_target_pairs={{0,2},{1,3},{2,0},{3,1},{4,6},{5,7},{6,4},{7,5},{8,10},{9,11},{10,... | collective-permute-start | bytes 589832 | tf_op jit(solution)/shard_map/ppermute | solution.py:40
  39.4 4.9 %collective-permute-start.19 = (bf16[1,256,128]{2,1,0:T(8,128)(2,1)S(1)}, bf16[1,256,128]{2,1,0:T(8,128)(2,1)S(1)}, u32[]{:S(2)}, u32[]{:S(2)}) collective-permute-start(bf16[1,256,128]{2,1,0:T(8,128)(2,1)S(1)} %get-tuple-element.79), channel_id=1, source_target_pairs={{0,1},{1,0},{2,3},{3,2},{4,5},{5,4},{6,7},{7,6},{8,9},{9,8},{10,11... | collective-permute-start | bytes 196616 | tf_op jit(solution)/shard_map/ppermute | solution.py:40
  39.5 4.7 %collective-permute-start.26 = (bf16[1,256,128]{2,1,0:T(8,128)(2,1)S(1)}, bf16[1,256,128]{2,1,0:T(8,128)(2,1)S(1)}, u32[]{:S(2)}, u32[]{:S(2)}) collective-permute-start(bf16[1,256,128]{2,1,0:T(8,128)(2,1)S(1)} %shard_map.127), channel_id=1, source_target_pairs={{0,2},{1,3},{2,0},{3,1},{4,6},{5,7},{6,4},{7,5},{8,10},{9,11},{10,... | collective-permute-start | bytes 196616 | tf_op jit(solution)/shard_map/ppermute | solution.py:40
  39.7 4.5 %collective-permute-start.24 = (bf16[1,256,128]{2,1,0:T(8,128)(2,1)S(1)}, bf16[1,256,128]{2,1,0:T(8,128)(2,1)S(1)}, u32[]{:S(2)}, u32[]{:S(2)}) collective-permute-start(bf16[1,256,128]{2,1,0:T(8,128)(2,1)S(1)} %get-tuple-element.84), channel_id=1, source_target_pairs={{0,1},{1,0},{2,3},{3,2},{4,5},{5,4},{6,7},{7,6},{8,9},{9,8},{10,11... | collective-permute-start | bytes 196616 | tf_op jit(solution)/shard_map/ppermute | solution.py:40
  44.0 4.8 %collective-permute-start.9 = (bf16[1,512,128]{2,1,0:T(8,128)(2,1)S(1)}, bf16[1,512,128]{2,1,0:T(8,128)(2,1)S(1)}, u32[]{:S(2)}, u32[]{:S(2)}) collective-permute-start(bf16[1,512,128]{2,1,0:T(8,128)(2,1)S(1)} %bitcast.17), channel_id=1, source_target_pairs={{0,2},{1,3},{2,0},{3,1},{4,6},{5,7},{6,4},{7,5},{8,10},{9,11},{10,... | collective-permute-start | bytes 393224 | tf_op jit(solution)/shard_map/ppermute | solution.py:40
  49.5 9.6 %collective-permute-start.27 = (bf16[3,512,128]{2,1,0:T(8,128)(2,1)}, bf16[3,512,128]{2,1,0:T(8,128)(2,1)S(1)}, u32[]{:S(2)}, u32[]{:S(2)}) collective-permute-start(bf16[3,512,128]{2,1,0:T(8,128)(2,1)} %shard_map.129.own), channel_id=1, source_target_pairs={{0,2},{1,3},{2,0},{3,1},{4,6},{5,7},{6,4},{7,5},{8,10},{9,11},{10,... | collective-permute-start | bytes 1179656 | tf_op jit(solution)/shard_map/ppermute | solution.py:40
  49.7 11.6 %collective-permute-start.10 = (bf16[1,512,128]{2,1,0:T(8,128)(2,1)S(1)}, bf16[1,512,128]{2,1,0:T(8,128)(2,1)S(1)}, u32[]{:S(2)}, u32[]{:S(2)}) collective-permute-start(bf16[1,512,128]{2,1,0:T(8,128)(2,1)S(1)} %bitcast.18), channel_id=1, source_target_pairs={{0,1},{1,0},{2,3},{3,2},{4,5},{5,4},{6,7},{7,6},{8,9},{9,8},{10,11... | collective-permute-start | bytes 393224 | tf_op jit(solution)/shard_map/ppermute | solution.py:40
  51.1 10.1 %collective-permute-start.11 = (bf16[1,512,128]{2,1,0:T(8,128)(2,1)}, bf16[1,512,128]{2,1,0:T(8,128)(2,1)S(1)}, u32[]{:S(2)}, u32[]{:S(2)}) collective-permute-start(bf16[1,512,128]{2,1,0:T(8,128)(2,1)} %copy-done.6), channel_id=1, source_target_pairs={{0,1},{1,0},{2,3},{3,2},{4,5},{5,4},{6,7},{7,6},{8,9},{9,8},{10,11... | collective-permute-start | bytes 393224 | tf_op jit(solution)/shard_map/ppermute | solution.py:40
  51.1 24.0 %collective-permute-start.28 = (bf16[3,512,128]{2,1,0:T(8,128)(2,1)}, bf16[3,512,128]{2,1,0:T(8,128)(2,1)S(1)}, u32[]{:S(2)}, u32[]{:S(2)}) collective-permute-start(bf16[3,512,128]{2,1,0:T(8,128)(2,1)} %shard_map.129.own), channel_id=1, source_target_pairs={{0,1},{1,0},{2,3},{3,2},{4,5},{5,4},{6,7},{7,6},{8,9},{9,8},{10,11... | collective-permute-start | bytes 1179656 | tf_op jit(solution)/shard_map/ppermute | solution.py:40
  59.1 16.0 %collective-permute-start.29 = (bf16[3,512,128]{2,1,0:T(8,128)(2,1)S(1)}, bf16[3,512,128]{2,1,0:T(8,128)(2,1)S(1)}, u32[]{:S(2)}, u32[]{:S(2)}) collective-permute-start(bf16[3,512,128]{2,1,0:T(8,128)(2,1)S(1)} %collective-permute-done.27.far), channel_id=1, source_target_pairs={{0,1},{1,0},{2,3},{3,2},{4,5},{5,4},{6,7},{7,6},{8,9},{9,8},{10,11... | collective-permute-start | bytes 1179656 | tf_op jit(solution)/shard_map/ppermute | solution.py:40
  64.0 8.0 %collective-permute-start.12 = (bf16[512,256]{1,0:T(8,128)(2,1)S(1)}, bf16[512,256]{1,0:T(8,128)(2,1)S(1)}, u32[]{:S(2)}, u32[]{:S(2)}) collective-permute-start(bf16[512,256]{1,0:T(8,128)(2,1)S(1)} %get-tuple-element.67), channel_id=1, source_target_pairs={{0,4},{4,0},{8,12},{12,8},{16,20},{20,16},{24,28},{28,24},{1,5},{5... | collective-permute-start | bytes 786440 | tf_op jit(solution)/shard_map/ppermute | solution.py:40
  65.6 7.6 %collective-permute-start.13 = (bf16[256,512]{1,0:T(8,128)(2,1)S(1)}, bf16[256,512]{1,0:T(8,128)(2,1)S(1)}, u32[]{:S(2)}, u32[]{:S(2)}) collective-permute-start(bf16[256,512]{1,0:T(8,128)(2,1)S(1)} %get-tuple-element.69), channel_id=1, source_target_pairs={{0,8},{4,12},{8,0},{12,4},{16,24},{20,28},{24,16},{28,20},{1,9},{5... | collective-permute-start | bytes 786440 | tf_op jit(solution)/shard_map/ppermute | solution.py:40
  73.3 6.3 %collective-permute-start.14 = (bf16[256,256]{1,0:T(8,128)(2,1)S(1)}, bf16[256,256]{1,0:T(8,128)(2,1)S(1)}, u32[]{:S(2)}, u32[]{:S(2)}) collective-permute-start(bf16[256,256]{1,0:T(8,128)(2,1)S(1)} %get-tuple-element.71), channel_id=1, source_target_pairs={{0,8},{4,12},{8,0},{12,4},{16,24},{20,28},{24,16},{28,20},{1,9},{5... | collective-permute-start | bytes 393224 | tf_op jit(solution)/shard_map/ppermute | solution.py:40
  74.8 4.8 %collective-permute-start.15 = (bf16[256,256]{1,0:T(8,128)(2,1)S(1)}, bf16[256,256]{1,0:T(8,128)(2,1)S(1)}, u32[]{:S(2)}, u32[]{:S(2)}) collective-permute-start(bf16[256,256]{1,0:T(8,128)(2,1)S(1)} %get-tuple-element.73), channel_id=1, source_target_pairs={{0,4},{4,0},{8,12},{12,8},{16,20},{20,16},{24,28},{28,24},{1,5},{5... | collective-permute-start | bytes 393224 | tf_op jit(solution)/shard_map/ppermute | solution.py:40
  76.9 8.3 %collective-permute-start.30 = (bf16[512,256]{1,0:T(8,128)(2,1)S(1)}, bf16[512,256]{1,0:T(8,128)(2,1)S(1)}, u32[]{:S(2)}, u32[]{:S(2)}) collective-permute-start(bf16[512,256]{1,0:T(8,128)(2,1)S(1)} %get-tuple-element.93), channel_id=1, source_target_pairs={{0,4},{4,0},{8,12},{12,8},{16,20},{20,16},{24,28},{28,24},{1,5},{5... | collective-permute-start | bytes 786440 | tf_op jit(solution)/shard_map/ppermute | solution.py:40
  78.1 7.3 %collective-permute-start.31 = (bf16[256,512]{1,0:T(8,128)(2,1)S(1)}, bf16[256,512]{1,0:T(8,128)(2,1)S(1)}, u32[]{:S(2)}, u32[]{:S(2)}) collective-permute-start(bf16[256,512]{1,0:T(8,128)(2,1)S(1)} %get-tuple-element.95), channel_id=1, source_target_pairs={{0,8},{4,12},{8,0},{12,4},{16,24},{20,28},{24,16},{28,20},{1,9},{5... | collective-permute-start | bytes 786440 | tf_op jit(solution)/shard_map/ppermute | solution.py:40
  79.6 7.9 %collective-permute-start.16 = (bf16[128,512]{1,0:T(8,128)(2,1)S(1)}, bf16[128,512]{1,0:T(8,128)(2,1)S(1)}, u32[]{:S(2)}, u32[]{:S(2)}) collective-permute-start(bf16[128,512]{1,0:T(8,128)(2,1)S(1)} %get-tuple-element.75), channel_id=1, source_target_pairs={{0,16},{4,20},{8,24},{12,28},{16,0},{20,4},{24,8},{28,12},{1,17},{... | collective-permute-start | bytes 393224 | tf_op jit(solution)/shard_map/ppermute | solution.py:40
  85.5 10.6 %collective-permute-start.32 = (bf16[256,256]{1,0:T(8,128)(2,1)S(1)}, bf16[256,256]{1,0:T(8,128)(2,1)S(1)}, u32[]{:S(2)}, u32[]{:S(2)}) collective-permute-start(bf16[256,256]{1,0:T(8,128)(2,1)S(1)} %get-tuple-element.97), channel_id=1, source_target_pairs={{0,8},{4,12},{8,0},{12,4},{16,24},{20,28},{24,16},{28,20},{1,9},{5... | collective-permute-start | bytes 393224 | tf_op jit(solution)/shard_map/ppermute | solution.py:40
  85.5 10.5 %collective-permute-start.33 = (bf16[256,256]{1,0:T(8,128)(2,1)S(1)}, bf16[256,256]{1,0:T(8,128)(2,1)S(1)}, u32[]{:S(2)}, u32[]{:S(2)}) collective-permute-start(bf16[256,256]{1,0:T(8,128)(2,1)S(1)} %get-tuple-element.99), channel_id=1, source_target_pairs={{0,4},{4,0},{8,12},{12,8},{16,20},{20,16},{24,28},{28,24},{1,5},{5... | collective-permute-start | bytes 393224 | tf_op jit(solution)/shard_map/ppermute | solution.py:40
  87.6 13.1 %collective-permute-start.17 = (bf16[128,512]{1,0:T(8,128)(2,1)S(1)}, bf16[128,512]{1,0:T(8,128)(2,1)S(1)}, u32[]{:S(2)}, u32[]{:S(2)}) collective-permute-start(bf16[128,512]{1,0:T(8,128)(2,1)S(1)} %shard_map.121), channel_id=1, source_target_pairs={{0,0},{1,8},{2,16},{3,24},{4,4},{5,12},{6,20},{7,28},{8,1},{9,9},{... | collective-permute-start | bytes 393224 | tf_op jit(solution)/shard_map/ppermute | solution.py:55
  96.1 11.9 %collective-permute-start.34 = (bf16[128,512]{1,0:T(8,128)(2,1)S(1)}, bf16[128,512]{1,0:T(8,128)(2,1)S(1)}, u32[]{:S(2)}, u32[]{:S(2)}) collective-permute-start(bf16[128,512]{1,0:T(8,128)(2,1)S(1)} %get-tuple-element.101), channel_id=1, source_target_pairs={{0,16},{4,20},{8,24},{12,28},{16,0},{20,4},{24,8},{28,12},{1,17},{... | collective-permute-start | bytes 393224 | tf_op jit(solution)/shard_map/ppermute | solution.py:40
  108.0 8.1 %collective-permute-start.35 = (bf16[128,512]{1,0:T(8,128)(2,1)S(1)}, bf16[128,512]{1,0:T(8,128)(2,1)S(1)}, u32[]{:S(2)}, u32[]{:S(2)}) collective-permute-start(bf16[128,512]{1,0:T(8,128)(2,1)S(1)} %shard_map.134), channel_id=1, source_target_pairs={{0,0},{1,8},{2,16},{3,24},{4,4},{5,12},{6,20},{7,28},{8,1},{9,9},{... | collective-permute-start | bytes 393224 | tf_op jit(solution)/shard_map/ppermute | solution.py:55
  (32 other events, 181.2 us)

commit v3 on v2

--- a/solution.py
+++ b/solution.py
@@ -13,6 +13,7 @@
 CHUNKS = 8
 MARGIN = 8
 VMEM_LIMIT = 16 * 1024 * 1024
+SMALL_LIMIT = 4 * 1024 * 1024
 FLOPS_PER_US = 1_150_000_000
 
 
@@ -212,17 +213,19 @@
     )(*parts, *tables, *saved, *after)
 
 
-def later(value, after):
-    def body(value, after, out):
+def later(value, *after):
+    def body(*refs):
         pass
 
     return pl.pallas_call(
         body,
         out_shape=jax.ShapeDtypeStruct(value.shape, value.dtype),
-        in_specs=[HBM, HBM],
+        in_specs=[HBM] * (1 + len(after)),
         out_specs=HBM,
         input_output_aliases={0: 0},
-    )(value, after)
+        compiler_params=pltpu.CompilerParams(vmem_limit_bytes=SMALL_LIMIT),
+        cost_estimate=cost(0.05),
+    )(value, *after)
 
 
 def column_blocks(rows):
@@ -291,9 +294,7 @@
     return here[0], here[1], there[2], there[0], there[1], here[2]
 
 
-def all_channels(value, after=None):
-    value = value if after is None else later(value, after)
-    far = flipped(value, "ctx", 2)
+def all_channels(value, far):
     return value, far, flipped(value, "ctx", 1), flipped(far, "ctx", 1)
 
 
@@ -404,18 +405,19 @@
     groups, _, channels = values.shape
     tile = depth // 2
 
-    def body(rows, values, out):
+    def body(rows, values, out, mark):
         out[0] = dot(rows[...], values[0], (1, 0))
+        mark[...] = jnp.zeros_like(mark)
 
     return pl.pallas_call(
         body,
-        out_shape=jax.ShapeDtypeStruct((groups, depth, channels), F32),
+        out_shape=(jax.ShapeDtypeStruct((groups, depth, channels), F32), jax.ShapeDtypeStruct((8, LANES), F32)),
         grid=(groups, depth // tile),
         in_specs=[
             pl.BlockSpec((tile, length), lambda j, i: (i, 0)),
             pl.BlockSpec((1, length, channels), lambda j, i: (j, 0, 0)),
         ],
-        out_specs=pl.BlockSpec((1, tile, channels), lambda j, i: (j, i, 0)),
+        out_specs=(pl.BlockSpec((1, tile, channels), lambda j, i: (j, i, 0)), pl.BlockSpec((8, LANES), lambda j, i: (0, 0))),
         compiler_params=pltpu.CompilerParams(vmem_limit_bytes=VMEM_LIMIT),
         cost_estimate=cost(1.5 * groups),
     )(rows, values)
@@ -436,15 +438,21 @@
     grads_here = channel_sums(grad_here, 0, out_weight[None])
     grads_there = channel_sums(grad_there, 1, out_weight[None])
     *saved, gated = filter_forward(by_token(feats_here, feats_there), sum_of_three, tables, length, width)
-    all_gated = all_channels(gated[None])
+    gated = gated[None]
+    gated_far = flipped(gated, "ctx", 2)
+    all_gated = all_channels(gated, gated_far)
     whole_gated, keeps, gives = output_pieces(all_gated, out_weight[None])
-    mixed = block_sums(keeps, exchange(gives))
+    givens = exchange(gives)
+    mixed = block_sums(keeps, givens)
     grads = filter_backward(by_token(grads_here, grads_there), sum_of_three, tables, saved, length, width)
-    whole_grads, keeps, gives = output_pieces(all_channels(grads, all_gated[1]), weights)
+    grads = later(grads, gated_far)
+    grad_out, mark = weight_gradient(turned(grad_here + grad_there), whole_gated)
+    token_rows = turned(here + there)
+    grads_far = later(flipped(grads, "ctx", 2), *givens, keeps[0], token_rows, mark)
+    whole_grads, keeps, gives = output_pieces(all_channels(grads, grads_far), weights)
     grad_tokens = block_sums(keeps, exchange(gives))
-    grad_in = weight_gradient(turned(here + there), whole_grads)
-    grad_out = weight_gradient(turned(grad_here + grad_there), whole_gated)[0]
-    return mixed, grad_tokens, grad_in, grad_out
+    grad_in, _ = weight_gradient(token_rows, whole_grads)
+    return mixed, grad_tokens, grad_in, grad_out[0]
 
 
 def any_mesh(tokens, weights, tables, out_weight, grad_mixed):

time: 118 us -> 103 us (0.87)
  waiting for transfers between devices: 35.3 us -> 28.5 us
  local copies, waits for them, and re-layouts: 12.4 us -> 7.1 us
  Pallas kernels: 25.6 us -> 20.4 us
  starting transfers between devices: 42.4 us -> 45 us
    ppermute x32, waiting for transfers between devices: 28.2 us -> 22.5 us  [flipped(): lax.ppermute(value, axis, [(source, source ^ mask) for source in range(co...]
    ppermute x32, starting transfers between devices: 28.1 us -> 33.7 us  [flipped(): lax.ppermute(value, axis, [(source, source ^ mask) for source in range(co...]
    unnamed x58 -> x16, local copies, waits for them, and re-layouts: 11.7 us -> 6.34 us
    pallas_call x4, Pallas kernels: 6.89 us -> 3.76 us  [project(): call(body, (jax.ShapeDtypeStruct((groups, length, width), F32), sums, sum...]
    ppermute x2, starting transfers between devices: 10.3 us -> 7.4 us  [to_placement(): return lax.ppermute(value, ('fsdp', 'ctx'), pairs)]
    pallas_call x2, Pallas kernels: 2.7 us -> 0.65 us  [turned(): call(body, jax.ShapeDtypeStruct((depth, 4 * part), pieces[0].dtype), us=1.0)]
  transfers between devices with their start and end apart: 36 -> 36, of which waited for: 15 -> 12; matrix products, arithmetic and copies ran while one was open for 1% -> 1% of each run, Pallas kernels for 22% -> 20%
where the time goes in v3:
time: 103 us
  starting transfers between devices  45 us (44%)
  waiting for transfers between devices  28.5 us (28%)
  Pallas kernels  20.4 us (20%)
  local copies, waits for them, and re-layouts  7.1 us (7%)
    ppermute x32, starting transfers between devices, flipped(): lax.ppermute(value, axis, [(source, source ^ mask) for source in range(co...  33.7 us
    ppermute x32, waiting for transfers between devices, flipped(): lax.ppermute(value, axis, [(source, source ^ mask) for source in range(co...  22.5 us
    ppermute x2, starting transfers between devices, to_placement(): return lax.ppermute(value, ('fsdp', 'ctx'), pairs)  7.4 us
    pallas_call x2, Pallas kernels, weight_gradient(): pl.pallas_call(body, out_shape=(jax.ShapeDtypeStruct((groups, depth, chan...  6.58 us
    unnamed x16, local copies, waits for them, and re-layouts  6.34 us
    ppermute x2, starting transfers between devices, fetched(): return lax.ppermute(block, ('fsdp', 'ctx'), pairs)  3.94 us
    pallas_call x4, Pallas kernels, project(): call(body, (jax.ShapeDtypeStruct((groups, length, width), F32), sums, sum...  3.76 us
    ppermute x2, waiting for transfers between devices, to_placement(): return lax.ppermute(value, ('fsdp', 'ctx'), pairs)  3.04 us
  transfers between devices with their start and end apart: 36, of which 12 were waited for; matrix products, arithmetic and copies ran while one was open for 1% of the time, Pallas kernels for 20%

profile of v3, /device:TPU:1, one launch (start us, length us, event | category | flops | bytes accessed | tf_op | source)
XLA Modules:
  0.0 102.7 jit_solution(8786987917115636528)
XLA Ops:
  2.1 2.7 %collective-permute-start.2 = (bf16[128,1024]{1,0:T(8,128)(2,1)S(1)}, bf16[128,1024]{1,0:T(8,128)(2,1)S(1)}, u32[]{:S(2)}, u32[]{:S(2)}) collective-permute-start(bf16[128,1024]{1,0:T(8,128)(2,1)S(1)} %get-tuple-element.60), channel_id=1, source_target_pairs={{0,2},{1,3},{2,0},{3,1},{4,7},{5,6},{6,5},{7,4},{8,10},{9,11},{10,... | collective-permute-start | bytes 786440 | tf_op jit(solution)/shard_map/ppermute | solution.py:250
  4.8 1.9 %copy-done.1 = bf16[1024,3,512]{2,0,1:T(8,128)(2,1)S(1)} copy-done((bf16[1024,3,512]{2,0,1:T(8,128)(2,1)S(1)}, bf16[1024,3,512]{2,0,1:T(8,128)(2,1)}, u32[]{:S(2)}) %copy-start.1) | copy-done | bytes 3145752
  8.4 3.0 %collective-permute-done.2.first.c = bf16[128,1024]{1,0:T(8,128)(2,1)S(1)} collective-permute-done((bf16[128,1024]{1,0:T(8,128)(2,1)S(1)}, bf16[128,1024]{1,0:T(8,128)(2,1)S(1)}, u32[]{:S(2)}, u32[]{:S(2)}) %collective-permute-start.2) | collective-permute-done | bytes 262176 | tf_op jit(solution)/shard_map/ppermute | solution.py:250
  11.4 1.4 %collective-permute-start.3 = (bf16[128,1024]{1,0:T(8,128)(2,1)S(1)}, bf16[128,1024]{1,0:T(8,128)(2,1)S(1)}, u32[]{:S(2)}, u32[]{:S(2)}) collective-permute-start(bf16[128,1024]{1,0:T(8,128)(2,1)S(1)} %collective-permute-done.2.first.c), channel_id=1, source_target_pairs={{0,4},{4,0},{8,12},{12,8},{16,20},{20,16},{24,28},{28,24},{1,5},{5... | collective-permute-start | bytes 786440 | tf_op jit(solution)/shard_map/ppermute | solution.py:41
  15.0 4.1 %collective-permute-done.8.refs_5_.refs_1_ = bf16[3,256,128]{2,1,0:T(8,128)(2,1)S(1)} collective-permute-done((bf16[3,256,128]{2,1,0:T(8,128)(2,1)S(1)}, bf16[3,256,128]{2,1,0:T(8,128)(2,1)S(1)}, u32[]{:S(2)}, u32[]{:S(2)}) %collective-permute-start.8) | collective-permute-done | bytes 196640 | tf_op jit(solution)/shard_map/ppermute | solution.py:41
  20.3 1.9 %copy-done.2 = bf16[1024,3,512]{2,0,1:T(8,128)(2,1)S(1)} copy-done((bf16[1024,3,512]{2,0,1:T(8,128)(2,1)S(1)}, bf16[1024,3,512]{2,0,1:T(8,128)(2,1)}, u32[]{:S(2)}) %copy-start.2) | copy-done | bytes 3145752
  23.5 1.5 %collective-permute-start.4 = (bf16[3,256,128]{2,1,0:T(8,128)(2,1)S(1)}, bf16[3,256,128]{2,1,0:T(8,128)(2,1)S(1)}, u32[]{:S(2)}, u32[]{:S(2)}) collective-permute-start(bf16[3,256,128]{2,1,0:T(8,128)(2,1)S(1)} %get-tuple-element.62), channel_id=1, source_target_pairs={{0,1},{1,0},{2,3},{3,2},{4,5},{5,4},{6,7},{7,6},{8,9},{9,8},{10,11... | collective-permute-start | bytes 589832 | tf_op jit(solution)/shard_map/ppermute | solution.py:41
  25.7 2.7 %collective-permute-start.21 = (bf16[128,1024]{1,0:T(8,128)(2,1)S(1)}, bf16[128,1024]{1,0:T(8,128)(2,1)S(1)}, u32[]{:S(2)}, u32[]{:S(2)}) collective-permute-start(bf16[128,1024]{1,0:T(8,128)(2,1)S(1)} %collective-permute-done.20.first.c), channel_id=1, source_target_pairs={{0,4},{4,0},{8,12},{12,8},{16,20},{20,16},{24,28},{28,24},{1,5},{5... | collective-permute-start | bytes 786440 | tf_op jit(solution)/shard_map/ppermute | solution.py:41
  31.8 2.1 %collective-permute-done.21.second.d = bf16[128,1024]{1,0:T(8,128)(2,1)S(1)} collective-permute-done((bf16[128,1024]{1,0:T(8,128)(2,1)S(1)}, bf16[128,1024]{1,0:T(8,128)(2,1)S(1)}, u32[]{:S(2)}, u32[]{:S(2)}) %collective-permute-start.21) | collective-permute-done | bytes 262176 | tf_op jit(solution)/shard_map/ppermute | solution.py:41
  33.9 1.7 %collective-permute-start.25 = (bf16[1,256,128]{2,1,0:T(8,128)(2,1)S(1)}, bf16[1,256,128]{2,1,0:T(8,128)(2,1)S(1)}, u32[]{:S(2)}, u32[]{:S(2)}) collective-permute-start(bf16[1,256,128]{2,1,0:T(8,128)(2,1)S(1)} %get-tuple-element.89), channel_id=1, source_target_pairs={{0,1},{1,0},{2,3},{3,2},{4,5},{5,4},{6,7},{7,6},{8,9},{9,8},{10,11... | collective-permute-start | bytes 196616 | tf_op jit(solution)/shard_map/ppermute | solution.py:41
  36.3 2.1 %shard_map.116 = (f32[512,128]{1,0:T(8,128)S(1)}, f32[512,128]{1,0:T(8,128)S(1)}, f32[512,128]{1,0:T(8,128)S(1)}, f32[512,128]{1,0:T(8,128)S(1)}, bf16[512,128]{1,0:T(8,128)(2,1)S(1)}) custom-call(f32[3,256,128]{2,1,0:T(8,128)S(1)} %get-tuple-element.58.refs_0_, bf16[3,256,128]{2,1,0:T(8,128)(2,1)S(1)} %collective-permute-done.1.refs_1_, ...), custom_call_target="tpu_custom_call" | custom-call | flops 3680000000 | tf_op jit(solution)/shard_map/pallas_call | solution.py:184
  38.6 1.5 %collective-permute-start.26 = (bf16[1,256,128]{2,1,0:T(8,128)(2,1)S(1)}, bf16[1,256,128]{2,1,0:T(8,128)(2,1)S(1)}, u32[]{:S(2)}, u32[]{:S(2)}) collective-permute-start(bf16[1,256,128]{2,1,0:T(8,128)(2,1)S(1)} %shard_map.127), channel_id=1, source_target_pairs={{0,2},{1,3},{2,0},{3,1},{4,6},{5,7},{6,4},{7,5},{8,10},{9,11},{10,... | collective-permute-start | bytes 196616 | tf_op jit(solution)/shard_map/ppermute | solution.py:41
  41.7 1.4 %collective-permute-done.9.far.refs_1_ = bf16[1,512,128]{2,1,0:T(8,128)(2,1)S(1)} collective-permute-done((bf16[1,512,128]{2,1,0:T(8,128)(2,1)S(1)}, bf16[1,512,128]{2,1,0:T(8,128)(2,1)S(1)}, u32[]{:S(2)}, u32[]{:S(2)}) %collective-permute-start.9) | collective-permute-done | bytes 131104 | tf_op jit(solution)/shard_map/ppermute | solution.py:41
  43.1 2.2 %collective-permute-start.11 = (bf16[1,512,128]{2,1,0:T(8,128)(2,1)S(1)}, bf16[1,512,128]{2,1,0:T(8,128)(2,1)S(1)}, u32[]{:S(2)}, u32[]{:S(2)}) collective-permute-start(bf16[1,512,128]{2,1,0:T(8,128)(2,1)S(1)} %collective-permute-done.9.far.refs_1_), channel_id=1, source_target_pairs={{0,1},{1,0},{2,3},{3,2},{4,5},{5,4},{6,7},{7,6},{8,9},{9,8},{10,11... | collective-permute-start | bytes 393224 | tf_op jit(solution)/shard_map/ppermute | solution.py:41
  45.9 2.1 %shard_map.128.refs_0_ = bf16[3,512,128]{2,1,0:T(8,128)(2,1)S(1)} custom-call(f32[1,256,128]{2,1,0:T(8,128)S(1)} %get-tuple-element.81.refs_0_, bf16[1,256,128]{2,1,0:T(8,128)(2,1)S(1)} %collective-permute-done.19.refs_1_, bf16[1,256,128]{2,1,0:T(8,128)(2,1)S(1)} %collective-permute-done.23.refs_2_, f32[1,256,128]{2,1,0:T(8,128)S(1)} %get-tuple-element.86.refs_3_, ...), custom_call_target="tpu_custom_call" | custom-call | flops 2415000064 | tf_op jit(solution)/shard_map/pallas_call | solution.py:203
  49.2 1.6 %collective-permute-start.12 = (bf16[512,256]{1,0:T(8,128)(2,1)S(1)}, bf16[512,256]{1,0:T(8,128)(2,1)S(1)}, u32[]{:S(2)}, u32[]{:S(2)}) collective-permute-start(bf16[512,256]{1,0:T(8,128)(2,1)S(1)} %get-tuple-element.70), channel_id=1, source_target_pairs={{0,4},{4,0},{8,12},{12,8},{16,20},{20,16},{24,28},{28,24},{1,5},{5... | collective-permute-start | bytes 786440 | tf_op jit(solution)/shard_map/ppermute | solution.py:41
  50.7 1.5 %collective-permute-start.13 = (bf16[256,512]{1,0:T(8,128)(2,1)S(1)}, bf16[256,512]{1,0:T(8,128)(2,1)S(1)}, u32[]{:S(2)}, u32[]{:S(2)}) collective-permute-start(bf16[256,512]{1,0:T(8,128)(2,1)S(1)} %get-tuple-element.72), channel_id=1, source_target_pairs={{0,8},{4,12},{8,0},{12,4},{16,24},{20,28},{24,16},{28,20},{1,9},{5... | collective-permute-start | bytes 786440 | tf_op jit(solution)/shard_map/ppermute | solution.py:41
  53.1 1.9 %shard_map.132 = (f32[1,1024,512]{2,1,0:T(8,128)}, f32[8,128]{1,0:T(8,128)S(1)}) custom-call(bf16[1024,512]{1,0:T(8,128)(2,1)S(1)} %shard_map.131.rows, bf16[1,512,512]{2,1,0:T(8,128)(2,1)S(1)} %get-tuple-element.68.whole.values), custom_call_target="tpu_custom_call" | custom-call | flops 1724999936 | tf_op jit(solution)/shard_map/pallas_call | solution.py:412
  55.0 2.0 %collective-permute-start.28 = (bf16[3,512,128]{2,1,0:T(8,128)(2,1)S(1)}, bf16[3,512,128]{2,1,0:T(8,128)(2,1)S(1)}, u32[]{:S(2)}, u32[]{:S(2)}) collective-permute-start(bf16[3,512,128]{2,1,0:T(8,128)(2,1)S(1)} %shard_map.129.own), channel_id=1, source_target_pairs={{0,1},{1,0},{2,3},{3,2},{4,5},{5,4},{6,7},{7,6},{8,9},{9,8},{10,11... | collective-permute-start | bytes 1179656 | tf_op jit(solution)/shard_map/ppermute | solution.py:41
  57.4 2.2 %collective-permute-start.29 = (bf16[3,512,128]{2,1,0:T(8,128)(2,1)S(1)}, bf16[3,512,128]{2,1,0:T(8,128)(2,1)S(1)}, u32[]{:S(2)}, u32[]{:S(2)}) collective-permute-start(bf16[3,512,128]{2,1,0:T(8,128)(2,1)S(1)} %shard_map.133.far), channel_id=1, source_target_pairs={{0,1},{1,0},{2,3},{3,2},{4,5},{5,4},{6,7},{7,6},{8,9},{9,8},{10,11... | collective-permute-start | bytes 1179656 | tf_op jit(solution)/shard_map/ppermute | solution.py:41
  59.8 1.4 %collective-permute-start.14 = (bf16[256,256]{1,0:T(8,128)(2,1)S(1)}, bf16[256,256]{1,0:T(8,128)(2,1)S(1)}, u32[]{:S(2)}, u32[]{:S(2)}) collective-permute-start(bf16[256,256]{1,0:T(8,128)(2,1)S(1)} %get-tuple-element.74), channel_id=1, source_target_pairs={{0,8},{4,12},{8,0},{12,4},{16,24},{20,28},{24,16},{28,20},{1,9},{5... | collective-permute-start | bytes 393224 | tf_op jit(solution)/shard_map/ppermute | solution.py:41
  61.2 1.5 %collective-permute-start.15 = (bf16[256,256]{1,0:T(8,128)(2,1)S(1)}, bf16[256,256]{1,0:T(8,128)(2,1)S(1)}, u32[]{:S(2)}, u32[]{:S(2)}) collective-permute-start(bf16[256,256]{1,0:T(8,128)(2,1)S(1)} %get-tuple-element.76), channel_id=1, source_target_pairs={{0,4},{4,0},{8,12},{12,8},{16,20},{20,16},{24,28},{28,24},{1,5},{5... | collective-permute-start | bytes 393224 | tf_op jit(solution)/shard_map/ppermute | solution.py:41
  62.7 1.7 %shard_map.134 = (bf16[3,512,512]{2,1,0:T(8,128)(2,1)S(1)}, bf16[512,256]{1,0:T(8,128)(2,1)S(1)}, bf16[256,512]{1,0:T(8,128)(2,1)S(1)}) custom-call(bf16[3,512,128]{2,1,0:T(8,128)(2,1)S(1)} %shard_map.129.own, bf16[3,512,128]{2,1,0:T(8,128)(2,1)S(1)} %shard_map.133.far, bf16[3,512,128]{2,1,0:T(8,128)(2,1)S(1)} %collective-permute-done.28.near, ...), custom_call_target="tpu_custom_call" | custom-call | flops 2070000000 | tf_op jit(solution)/shard_map/pallas_call | solution.py:336
  66.1 2.4 %collective-permute-start.16 = (bf16[128,512]{1,0:T(8,128)(2,1)S(1)}, bf16[128,512]{1,0:T(8,128)(2,1)S(1)}, u32[]{:S(2)}, u32[]{:S(2)}) collective-permute-start(bf16[128,512]{1,0:T(8,128)(2,1)S(1)} %get-tuple-element.78), channel_id=1, source_target_pairs={{0,16},{4,20},{8,24},{12,28},{16,0},{20,4},{24,8},{28,12},{1,17},{... | collective-permute-start | bytes 393224 | tf_op jit(solution)/shard_map/ppermute | solution.py:41
  68.5 1.5 %shard_map.135 = (bf16[512,256]{1,0:T(8,128)(2,1)S(1)}, bf16[256,512]{1,0:T(8,128)(2,1)S(1)}) custom-call(bf16[3,512,512]{2,1,0:T(8,128)(2,1)S(1)} %get-tuple-element.95.whole.values, bf16[3,1024,512]{2,1,0:T(8,128)(2,1)S(1)} %bitcast.12), custom_call_target="tpu_custom_call" | custom-call | flops 1380000000 | tf_op jit(solution)/shard_map/pallas_call | solution.py:342
  69.9 1.9 %collective-permute-done.30.given_x = bf16[512,256]{1,0:T(8,128)(2,1)S(1)} collective-permute-done((bf16[512,256]{1,0:T(8,128)(2,1)S(1)}, bf16[512,256]{1,0:T(8,128)(2,1)S(1)}, u32[]{:S(2)}, u32[]{:S(2)}) %collective-permute-start.30) | collective-permute-done | bytes 262176 | tf_op jit(solution)/shard_map/ppermute | solution.py:41
  71.8 2.7 %collective-permute-done.31.given_z = bf16[256,512]{1,0:T(8,128)(2,1)S(1)} collective-permute-done((bf16[256,512]{1,0:T(8,128)(2,1)S(1)}, bf16[256,512]{1,0:T(8,128)(2,1)S(1)}, u32[]{:S(2)}, u32[]{:S(2)}) %collective-permute-start.31) | collective-permute-done | bytes 262176 | tf_op jit(solution)/shard_map/ppermute | solution.py:41
  76.1 5.5 %collective-permute-start.17 = (bf16[128,512]{1,0:T(8,128)(2,1)S(1)}, bf16[128,512]{1,0:T(8,128)(2,1)S(1)}, u32[]{:S(2)}, u32[]{:S(2)}) collective-permute-start(bf16[128,512]{1,0:T(8,128)(2,1)S(1)} %shard_map.121), channel_id=1, source_target_pairs={{0,0},{1,8},{2,16},{3,24},{4,4},{5,12},{6,20},{7,28},{8,1},{9,9},{... | collective-permute-start | bytes 393224 | tf_op jit(solution)/shard_map/ppermute | solution.py:56
  82.8 2.3 %collective-permute-done.17 = bf16[128,512]{1,0:T(8,128)(2,1)S(1)} collective-permute-done((bf16[128,512]{1,0:T(8,128)(2,1)S(1)}, bf16[128,512]{1,0:T(8,128)(2,1)S(1)}, u32[]{:S(2)}, u32[]{:S(2)}) %collective-permute-start.17) | collective-permute-done | bytes 131104 | tf_op jit(solution)/shard_map/ppermute | solution.py:56
  85.1 8.9 %collective-permute-done.34.given = bf16[128,512]{1,0:T(8,128)(2,1)S(1)} collective-permute-done((bf16[128,512]{1,0:T(8,128)(2,1)S(1)}, bf16[128,512]{1,0:T(8,128)(2,1)S(1)}, u32[]{:S(2)}, u32[]{:S(2)}) %collective-permute-start.34) | collective-permute-done | bytes 131104 | tf_op jit(solution)/shard_map/ppermute | solution.py:41
  94.0 1.9 %collective-permute-start.35 = (bf16[128,512]{1,0:T(8,128)(2,1)S(1)}, bf16[128,512]{1,0:T(8,128)(2,1)S(1)}, u32[]{:S(2)}, u32[]{:S(2)}) collective-permute-start(bf16[128,512]{1,0:T(8,128)(2,1)S(1)} %shard_map.138), channel_id=1, source_target_pairs={{0,0},{1,8},{2,16},{3,24},{4,4},{5,12},{6,20},{7,28},{8,1},{9,9},{... | collective-permute-start | bytes 393224 | tf_op jit(solution)/shard_map/ppermute | solution.py:56
  96.0 4.7 %shard_map.139 = (f32[3,1024,512]{2,1,0:T(8,128)}, f32[8,128]{1,0:T(8,128)}) custom-call(bf16[1024,512]{1,0:T(8,128)(2,1)S(1)} %shard_map.130.refs_4_.rows, bf16[3,512,512]{2,1,0:T(8,128)(2,1)S(1)} %get-tuple-element.95.whole.values), custom_call_target="tpu_custom_call" | custom-call | flops 5175000064 | tf_op jit(solution)/shard_map/pallas_call | solution.py:412
  (88 shorter events, 23.8 us)
Async XLA Ops:
  2.1 9.3 %collective-permute-start.2 = (bf16[128,1024]{1,0:T(8,128)(2,1)S(1)}, bf16[128,1024]{1,0:T(8,128)(2,1)S(1)}, u32[]{:S(2)}, u32[]{:S(2)}) collective-permute-start(bf16[128,1024]{1,0:T(8,128)(2,1)S(1)} %get-tuple-element.60), channel_id=1, source_target_pairs={{0,2},{1,3},{2,0},{3,1},{4,7},{5,6},{6,5},{7,4},{8,10},{9,11},{10,... | collective-permute-start | bytes 786440 | tf_op jit(solution)/shard_map/ppermute | solution.py:250
  11.4 8.9 %collective-permute-start.3 = (bf16[128,1024]{1,0:T(8,128)(2,1)S(1)}, bf16[128,1024]{1,0:T(8,128)(2,1)S(1)}, u32[]{:S(2)}, u32[]{:S(2)}) collective-permute-start(bf16[128,1024]{1,0:T(8,128)(2,1)S(1)} %collective-permute-done.2.first.c), channel_id=1, source_target_pairs={{0,4},{4,0},{8,12},{12,8},{16,20},{20,16},{24,28},{28,24},{1,5},{5... | collective-permute-start | bytes 786440 | tf_op jit(solution)/shard_map/ppermute | solution.py:41
  12.8 6.2 %collective-permute-start.8 = (bf16[3,256,128]{2,1,0:T(8,128)(2,1)S(1)}, bf16[3,256,128]{2,1,0:T(8,128)(2,1)S(1)}, u32[]{:S(2)}, u32[]{:S(2)}) collective-permute-start(bf16[3,256,128]{2,1,0:T(8,128)(2,1)S(1)} %shard_map.115), channel_id=1, source_target_pairs={{0,2},{1,3},{2,0},{3,1},{4,6},{5,7},{6,4},{7,5},{8,10},{9,11},{10,... | collective-permute-start | bytes 589832 | tf_op jit(solution)/shard_map/ppermute | solution.py:41
  14.2 16.2 %collective-permute-start.18 = (bf16[128,1024]{1,0:T(8,128)(2,1)S(1)}, bf16[128,1024]{1,0:T(8,128)(2,1)S(1)}, u32[]{:S(2)}, u32[]{:S(2)}) collective-permute-start(bf16[128,1024]{1,0:T(8,128)(2,1)S(1)} %get-tuple-element.80), channel_id=1, source_target_pairs={{0,1},{1,0},{2,3},{3,2},{4,5},{5,4},{6,7},{7,6},{8,9},{9,8},{10,11... | collective-permute-start | bytes 786440 | tf_op jit(solution)/shard_map/ppermute | solution.py:41
  19.0 6.7 %collective-permute-start.20 = (bf16[128,1024]{1,0:T(8,128)(2,1)S(1)}, bf16[128,1024]{1,0:T(8,128)(2,1)S(1)}, u32[]{:S(2)}, u32[]{:S(2)}) collective-permute-start(bf16[128,1024]{1,0:T(8,128)(2,1)S(1)} %shard_map.124), channel_id=1, source_target_pairs={{0,2},{1,3},{2,0},{3,1},{4,7},{5,6},{6,5},{7,4},{8,10},{9,11},{10,... | collective-permute-start | bytes 786440 | tf_op jit(solution)/shard_map/ppermute | solution.py:250
  23.5 5.6 %collective-permute-start.4 = (bf16[3,256,128]{2,1,0:T(8,128)(2,1)S(1)}, bf16[3,256,128]{2,1,0:T(8,128)(2,1)S(1)}, u32[]{:S(2)}, u32[]{:S(2)}) collective-permute-start(bf16[3,256,128]{2,1,0:T(8,128)(2,1)S(1)} %get-tuple-element.62), channel_id=1, source_target_pairs={{0,1},{1,0},{2,3},{3,2},{4,5},{5,4},{6,7},{7,6},{8,9},{9,8},{10,11... | collective-permute-start | bytes 589832 | tf_op jit(solution)/shard_map/ppermute | solution.py:41
  25.7 8.2 %collective-permute-start.21 = (bf16[128,1024]{1,0:T(8,128)(2,1)S(1)}, bf16[128,1024]{1,0:T(8,128)(2,1)S(1)}, u32[]{:S(2)}, u32[]{:S(2)}) collective-permute-start(bf16[128,1024]{1,0:T(8,128)(2,1)S(1)} %collective-permute-done.20.first.c), channel_id=1, source_target_pairs={{0,4},{4,0},{8,12},{12,8},{16,20},{20,16},{24,28},{28,24},{1,5},{5... | collective-permute-start | bytes 786440 | tf_op jit(solution)/shard_map/ppermute | solution.py:41
  28.4 7.8 %collective-permute-start.1 = (bf16[3,256,128]{2,1,0:T(8,128)(2,1)S(1)}, bf16[3,256,128]{2,1,0:T(8,128)(2,1)S(1)}, u32[]{:S(2)}, u32[]{:S(2)}) collective-permute-start(bf16[3,256,128]{2,1,0:T(8,128)(2,1)S(1)} %get-tuple-element.59), channel_id=1, source_target_pairs={{0,1},{1,0},{2,3},{3,2},{4,5},{5,4},{6,7},{7,6},{8,9},{9,8},{10,11... | collective-permute-start | bytes 589832 | tf_op jit(solution)/shard_map/ppermute | solution.py:41
  29.1 7.2 %collective-permute-start.6 = (bf16[3,256,128]{2,1,0:T(8,128)(2,1)S(1)}, bf16[3,256,128]{2,1,0:T(8,128)(2,1)S(1)}, u32[]{:S(2)}, u32[]{:S(2)}) collective-permute-start(bf16[3,256,128]{2,1,0:T(8,128)(2,1)S(1)} %get-tuple-element.64), channel_id=1, source_target_pairs={{0,1},{1,0},{2,3},{3,2},{4,5},{5,4},{6,7},{7,6},{8,9},{9,8},{10,11... | collective-permute-start | bytes 589832 | tf_op jit(solution)/shard_map/ppermute | solution.py:41
  29.2 7.1 %collective-permute-start.5 = (bf16[3,256,128]{2,1,0:T(8,128)(2,1)S(1)}, bf16[3,256,128]{2,1,0:T(8,128)(2,1)S(1)}, u32[]{:S(2)}, u32[]{:S(2)}) collective-permute-start(bf16[3,256,128]{2,1,0:T(8,128)(2,1)S(1)} %shard_map.114), channel_id=1, source_target_pairs={{0,2},{1,3},{2,0},{3,1},{4,6},{5,7},{6,4},{7,5},{8,10},{9,11},{10,... | collective-permute-start | bytes 589832 | tf_op jit(solution)/shard_map/ppermute | solution.py:41
  31.0 10.4 %collective-permute-start.19 = (bf16[1,256,128]{2,1,0:T(8,128)(2,1)S(1)}, bf16[1,256,128]{2,1,0:T(8,128)(2,1)S(1)}, u32[]{:S(2)}, u32[]{:S(2)}) collective-permute-start(bf16[1,256,128]{2,1,0:T(8,128)(2,1)S(1)} %get-tuple-element.82), channel_id=1, source_target_pairs={{0,1},{1,0},{2,3},{3,2},{4,5},{5,4},{6,7},{7,6},{8,9},{9,8},{10,11... | collective-permute-start | bytes 196616 | tf_op jit(solution)/shard_map/ppermute | solution.py:41
  36.2 4.9 %collective-permute-start.22 = (bf16[1,256,128]{2,1,0:T(8,128)(2,1)S(1)}, bf16[1,256,128]{2,1,0:T(8,128)(2,1)S(1)}, u32[]{:S(2)}, u32[]{:S(2)}) collective-permute-start(bf16[1,256,128]{2,1,0:T(8,128)(2,1)S(1)} %get-tuple-element.85), channel_id=1, source_target_pairs={{0,1},{1,0},{2,3},{3,2},{4,5},{5,4},{6,7},{7,6},{8,9},{9,8},{10,11... | collective-permute-start | bytes 196616 | tf_op jit(solution)/shard_map/ppermute | solution.py:41
  38.6 6.8 %collective-permute-start.26 = (bf16[1,256,128]{2,1,0:T(8,128)(2,1)S(1)}, bf16[1,256,128]{2,1,0:T(8,128)(2,1)S(1)}, u32[]{:S(2)}, u32[]{:S(2)}) collective-permute-start(bf16[1,256,128]{2,1,0:T(8,128)(2,1)S(1)} %shard_map.127), channel_id=1, source_target_pairs={{0,2},{1,3},{2,0},{3,1},{4,6},{5,7},{6,4},{7,5},{8,10},{9,11},{10,... | collective-permute-start | bytes 196616 | tf_op jit(solution)/shard_map/ppermute | solution.py:41
  40.1 5.3 %collective-permute-start.24 = (bf16[1,256,128]{2,1,0:T(8,128)(2,1)S(1)}, bf16[1,256,128]{2,1,0:T(8,128)(2,1)S(1)}, u32[]{:S(2)}, u32[]{:S(2)}) collective-permute-start(bf16[1,256,128]{2,1,0:T(8,128)(2,1)S(1)} %get-tuple-element.87), channel_id=1, source_target_pairs={{0,1},{1,0},{2,3},{3,2},{4,5},{5,4},{6,7},{7,6},{8,9},{9,8},{10,11... | collective-permute-start | bytes 196616 | tf_op jit(solution)/shard_map/ppermute | solution.py:41
  41.2 4.8 %collective-permute-start.23 = (bf16[1,256,128]{2,1,0:T(8,128)(2,1)S(1)}, bf16[1,256,128]{2,1,0:T(8,128)(2,1)S(1)}, u32[]{:S(2)}, u32[]{:S(2)}) collective-permute-start(bf16[1,256,128]{2,1,0:T(8,128)(2,1)S(1)} %shard_map.126), channel_id=1, source_target_pairs={{0,2},{1,3},{2,0},{3,1},{4,6},{5,7},{6,4},{7,5},{8,10},{9,11},{10,... | collective-permute-start | bytes 196616 | tf_op jit(solution)/shard_map/ppermute | solution.py:41
  41.4 7.1 %collective-permute-start.10 = (bf16[1,512,128]{2,1,0:T(8,128)(2,1)S(1)}, bf16[1,512,128]{2,1,0:T(8,128)(2,1)S(1)}, u32[]{:S(2)}, u32[]{:S(2)}) collective-permute-start(bf16[1,512,128]{2,1,0:T(8,128)(2,1)S(1)} %bitcast.18), channel_id=1, source_target_pairs={{0,1},{1,0},{2,3},{3,2},{4,5},{5,4},{6,7},{7,6},{8,9},{9,8},{10,11... | collective-permute-start | bytes 393224 | tf_op jit(solution)/shard_map/ppermute | solution.py:41
  43.1 5.4 %collective-permute-start.11 = (bf16[1,512,128]{2,1,0:T(8,128)(2,1)S(1)}, bf16[1,512,128]{2,1,0:T(8,128)(2,1)S(1)}, u32[]{:S(2)}, u32[]{:S(2)}) collective-permute-start(bf16[1,512,128]{2,1,0:T(8,128)(2,1)S(1)} %collective-permute-done.9.far.refs_1_), channel_id=1, source_target_pairs={{0,1},{1,0},{2,3},{3,2},{4,5},{5,4},{6,7},{7,6},{8,9},{9,8},{10,11... | collective-permute-start | bytes 393224 | tf_op jit(solution)/shard_map/ppermute | solution.py:41
  48.1 9.4 %collective-permute-start.27 = (bf16[3,512,128]{2,1,0:T(8,128)(2,1)S(1)}, bf16[3,512,128]{2,1,0:T(8,128)(2,1)S(1)}, u32[]{:S(2)}, u32[]{:S(2)}) collective-permute-start(bf16[3,512,128]{2,1,0:T(8,128)(2,1)S(1)} %shard_map.129.own), channel_id=1, source_target_pairs={{0,2},{1,3},{2,0},{3,1},{4,6},{5,7},{6,4},{7,5},{8,10},{9,11},{10,... | collective-permute-start | bytes 1179656 | tf_op jit(solution)/shard_map/ppermute | solution.py:41
  49.2 7.9 %collective-permute-start.12 = (bf16[512,256]{1,0:T(8,128)(2,1)S(1)}, bf16[512,256]{1,0:T(8,128)(2,1)S(1)}, u32[]{:S(2)}, u32[]{:S(2)}) collective-permute-start(bf16[512,256]{1,0:T(8,128)(2,1)S(1)} %get-tuple-element.70), channel_id=1, source_target_pairs={{0,4},{4,0},{8,12},{12,8},{16,20},{20,16},{24,28},{28,24},{1,5},{5... | collective-permute-start | bytes 786440 | tf_op jit(solution)/shard_map/ppermute | solution.py:41
  50.7 6.3 %collective-permute-start.13 = (bf16[256,512]{1,0:T(8,128)(2,1)S(1)}, bf16[256,512]{1,0:T(8,128)(2,1)S(1)}, u32[]{:S(2)}, u32[]{:S(2)}) collective-permute-start(bf16[256,512]{1,0:T(8,128)(2,1)S(1)} %get-tuple-element.72), channel_id=1, source_target_pairs={{0,8},{4,12},{8,0},{12,4},{16,24},{20,28},{24,16},{28,20},{1,9},{5... | collective-permute-start | bytes 786440 | tf_op jit(solution)/shard_map/ppermute | solution.py:41
  55.0 7.7 %collective-permute-start.28 = (bf16[3,512,128]{2,1,0:T(8,128)(2,1)S(1)}, bf16[3,512,128]{2,1,0:T(8,128)(2,1)S(1)}, u32[]{:S(2)}, u32[]{:S(2)}) collective-permute-start(bf16[3,512,128]{2,1,0:T(8,128)(2,1)S(1)} %shard_map.129.own), channel_id=1, source_target_pairs={{0,1},{1,0},{2,3},{3,2},{4,5},{5,4},{6,7},{7,6},{8,9},{9,8},{10,11... | collective-permute-start | bytes 1179656 | tf_op jit(solution)/shard_map/ppermute | solution.py:41
  57.4 5.3 %collective-permute-start.29 = (bf16[3,512,128]{2,1,0:T(8,128)(2,1)S(1)}, bf16[3,512,128]{2,1,0:T(8,128)(2,1)S(1)}, u32[]{:S(2)}, u32[]{:S(2)}) collective-permute-start(bf16[3,512,128]{2,1,0:T(8,128)(2,1)S(1)} %shard_map.133.far), channel_id=1, source_target_pairs={{0,1},{1,0},{2,3},{3,2},{4,5},{5,4},{6,7},{7,6},{8,9},{9,8},{10,11... | collective-permute-start | bytes 1179656 | tf_op jit(solution)/shard_map/ppermute | solution.py:41
  59.8 5.9 %collective-permute-start.14 = (bf16[256,256]{1,0:T(8,128)(2,1)S(1)}, bf16[256,256]{1,0:T(8,128)(2,1)S(1)}, u32[]{:S(2)}, u32[]{:S(2)}) collective-permute-start(bf16[256,256]{1,0:T(8,128)(2,1)S(1)} %get-tuple-element.74), channel_id=1, source_target_pairs={{0,8},{4,12},{8,0},{12,4},{16,24},{20,28},{24,16},{28,20},{1,9},{5... | collective-permute-start | bytes 393224 | tf_op jit(solution)/shard_map/ppermute | solution.py:41
  61.2 4.8 %collective-permute-start.15 = (bf16[256,256]{1,0:T(8,128)(2,1)S(1)}, bf16[256,256]{1,0:T(8,128)(2,1)S(1)}, u32[]{:S(2)}, u32[]{:S(2)}) collective-permute-start(bf16[256,256]{1,0:T(8,128)(2,1)S(1)} %get-tuple-element.76), channel_id=1, source_target_pairs={{0,4},{4,0},{8,12},{12,8},{16,20},{20,16},{24,28},{28,24},{1,5},{5... | collective-permute-start | bytes 393224 | tf_op jit(solution)/shard_map/ppermute | solution.py:41
  64.5 7.4 %collective-permute-start.30 = (bf16[512,256]{1,0:T(8,128)(2,1)S(1)}, bf16[512,256]{1,0:T(8,128)(2,1)S(1)}, u32[]{:S(2)}, u32[]{:S(2)}) collective-permute-start(bf16[512,256]{1,0:T(8,128)(2,1)S(1)} %get-tuple-element.97), channel_id=1, source_target_pairs={{0,4},{4,0},{8,12},{12,8},{16,20},{20,16},{24,28},{28,24},{1,5},{5... | collective-permute-start | bytes 786440 | tf_op jit(solution)/shard_map/ppermute | solution.py:41
  64.5 9.9 %collective-permute-start.31 = (bf16[256,512]{1,0:T(8,128)(2,1)S(1)}, bf16[256,512]{1,0:T(8,128)(2,1)S(1)}, u32[]{:S(2)}, u32[]{:S(2)}) collective-permute-start(bf16[256,512]{1,0:T(8,128)(2,1)S(1)} %get-tuple-element.99), channel_id=1, source_target_pairs={{0,8},{4,12},{8,0},{12,4},{16,24},{20,28},{24,16},{28,20},{1,9},{5... | collective-permute-start | bytes 786440 | tf_op jit(solution)/shard_map/ppermute | solution.py:41
  66.1 10.0 %collective-permute-start.16 = (bf16[128,512]{1,0:T(8,128)(2,1)S(1)}, bf16[128,512]{1,0:T(8,128)(2,1)S(1)}, u32[]{:S(2)}, u32[]{:S(2)}) collective-permute-start(bf16[128,512]{1,0:T(8,128)(2,1)S(1)} %get-tuple-element.78), channel_id=1, source_target_pairs={{0,16},{4,20},{8,24},{12,28},{16,0},{20,4},{24,8},{28,12},{1,17},{... | collective-permute-start | bytes 393224 | tf_op jit(solution)/shard_map/ppermute | solution.py:41
  74.6 7.0 %collective-permute-start.32 = (bf16[256,256]{1,0:T(8,128)(2,1)S(1)}, bf16[256,256]{1,0:T(8,128)(2,1)S(1)}, u32[]{:S(2)}, u32[]{:S(2)}) collective-permute-start(bf16[256,256]{1,0:T(8,128)(2,1)S(1)} %get-tuple-element.101), channel_id=1, source_target_pairs={{0,8},{4,12},{8,0},{12,4},{16,24},{20,28},{24,16},{28,20},{1,9},{5... | collective-permute-start | bytes 393224 | tf_op jit(solution)/shard_map/ppermute | solution.py:41
  74.7 6.9 %collective-permute-start.33 = (bf16[256,256]{1,0:T(8,128)(2,1)S(1)}, bf16[256,256]{1,0:T(8,128)(2,1)S(1)}, u32[]{:S(2)}, u32[]{:S(2)}) collective-permute-start(bf16[256,256]{1,0:T(8,128)(2,1)S(1)} %get-tuple-element.103), channel_id=1, source_target_pairs={{0,4},{4,0},{8,12},{12,8},{16,20},{20,16},{24,28},{28,24},{1,5},{5... | collective-permute-start | bytes 393224 | tf_op jit(solution)/shard_map/ppermute | solution.py:41
  76.1 9.0 %collective-permute-start.17 = (bf16[128,512]{1,0:T(8,128)(2,1)S(1)}, bf16[128,512]{1,0:T(8,128)(2,1)S(1)}, u32[]{:S(2)}, u32[]{:S(2)}) collective-permute-start(bf16[128,512]{1,0:T(8,128)(2,1)S(1)} %shard_map.121), channel_id=1, source_target_pairs={{0,0},{1,8},{2,16},{3,24},{4,4},{5,12},{6,20},{7,28},{8,1},{9,9},{... | collective-permute-start | bytes 393224 | tf_op jit(solution)/shard_map/ppermute | solution.py:56
  81.7 12.4 %collective-permute-start.34 = (bf16[128,512]{1,0:T(8,128)(2,1)S(1)}, bf16[128,512]{1,0:T(8,128)(2,1)S(1)}, u32[]{:S(2)}, u32[]{:S(2)}) collective-permute-start(bf16[128,512]{1,0:T(8,128)(2,1)S(1)} %get-tuple-element.105), channel_id=1, source_target_pairs={{0,16},{4,20},{8,24},{12,28},{16,0},{20,4},{24,8},{28,12},{1,17},{... | collective-permute-start | bytes 393224 | tf_op jit(solution)/shard_map/ppermute | solution.py:41
  94.0 7.4 %collective-permute-start.35 = (bf16[128,512]{1,0:T(8,128)(2,1)S(1)}, bf16[128,512]{1,0:T(8,128)(2,1)S(1)}, u32[]{:S(2)}, u32[]{:S(2)}) collective-permute-start(bf16[128,512]{1,0:T(8,128)(2,1)S(1)} %shard_map.138), channel_id=1, source_target_pairs={{0,0},{1,8},{2,16},{3,24},{4,4},{5,12},{6,20},{7,28},{8,1},{9,9},{... | collective-permute-start | bytes 393224 | tf_op jit(solution)/shard_map/ppermute | solution.py:56
  (11 other events, 73.1 us)

commit v4 on v3

--- a/solution.py
+++ b/solution.py
@@ -228,6 +228,35 @@
     )(value, *after)
 
 
+def settled(value):
+    def body(value, out):
+        out[...] = value[...]
+
+    return call(body, jax.ShapeDtypeStruct(value.shape, value.dtype), us=0.3)(value)
+
+
+def loaded(values, after):
+    count = len(values)
+
+    def body(*refs):
+        sources, outs, arrived = refs[:count], refs[count + 1 : 2 * count + 1], refs[-1]
+        copies = [pltpu.make_async_copy(a, b, arrived.at[n]) for n, (a, b) in enumerate(zip(sources, outs))]
+        for copy in copies:
+            copy.start()
+        for copy in copies:
+            copy.wait()
+
+    return pl.pallas_call(
+        body,
+        out_shape=tuple(pltpu.VMEM(value.shape, value.dtype) for value in values),
+        in_specs=[HBM] * (count + 1),
+        out_specs=(VMEM,) * count,
+        scratch_shapes=[pltpu.SemaphoreType.DMA((count,))],
+        compiler_params=pltpu.CompilerParams(vmem_limit_bytes=VMEM_LIMIT),
+        cost_estimate=cost(1.3),
+    )(*[pltpu.with_memory_space_constraint(value, pltpu.HBM) for value in values], after)
+
+
 def column_blocks(rows):
     length, width = rows.shape[0], rows.shape[1] // 4
 
@@ -242,7 +271,9 @@
             copy.wait()
 
     block = jax.ShapeDtypeStruct((length, width), rows.dtype)
-    return call(body, (block,) * 3, [pltpu.SemaphoreType.DMA((3,))], in_specs=[HBM], us=0.7)(rows)
+    return call(body, (block,) * 3, [pltpu.SemaphoreType.DMA((3,))], in_specs=[HBM], us=0.7)(
+        pltpu.with_memory_space_constraint(rows, pltpu.HBM)
+    )
 
 
 def fetched(block):
@@ -287,7 +318,7 @@
 def channel_sums(pieces, other, weight):
     own, far, give, give_far = project(pieces, other, weight)
     passed = add_far(far, flipped(give_far, "ctx", 1))
-    return own, flipped(give, "ctx", 1), flipped(passed, "ctx", 2)
+    return (own, flipped(give, "ctx", 1), flipped(passed, "ctx", 2)), passed
 
 
 def by_token(here, there):
@@ -347,12 +378,13 @@
     return flipped(gives[0], "fsdp", 1), flipped(gives[1], "fsdp", 2)
 
 
-def block_sums(keeps, givens):
+def block_sums(keeps, givens, after=()):
     length, piece = keeps[0].shape
     part = length // 4
     both = lambda keep, given, rows, columns: keep[rows, columns].astype(F32) + given[rows, columns].astype(F32)
 
-    def second_body(keep_x, given_x, keep_z, given_z, give_z, give_x, next_z, next_x):
+    def second_body(keep_x, given_x, keep_z, given_z, *refs):
+        give_z, give_x, next_z, next_x = refs[len(after) :]
         place = lax.axis_index("fsdp")
         side, low = place & 1, (place >> 1) & 1
         for high in range(2):
@@ -365,9 +397,11 @@
         next_x[...] = take(side)
 
     square = lambda kind: jax.ShapeDtypeStruct((2 * part, piece), kind)
-    give_z, give_x, next_z, next_x = call(second_body, (square(BF16), square(BF16), square(F32), square(F32)))(
-        keeps[0], givens[0], keeps[1], givens[1]
-    )
+    give_z, give_x, next_z, next_x = call(
+        second_body,
+        (square(BF16), square(BF16), square(F32), square(F32)),
+        in_specs=[VMEM] * 4 + [HBM] * len(after),
+    )(keeps[0], givens[0], keeps[1], givens[1], *after)
 
     def third_body(keep_z, given_z, keep_x, given_x, give, keep):
         high = lax.axis_index("fsdp") >> 2
@@ -385,7 +419,7 @@
     def last_body(keep, given, out):
         out[...] = (keep[...] + given[...].astype(F32)).astype(BF16)
 
-    return to_placement(call(last_body, block(BF16))(keep, flipped(give, "fsdp", 4)))
+    return call(last_body, block(BF16))(keep, flipped(give, "fsdp", 4)), give
 
 
 def turned(pieces):
@@ -400,12 +434,13 @@
     return call(body, jax.ShapeDtypeStruct((depth, 4 * part), pieces[0].dtype), us=1.0)(*pieces)
 
 
-def weight_gradient(rows, values):
+def weight_gradient(rows, values, after=()):
     depth, length = rows.shape
     groups, _, channels = values.shape
     tile = depth // 2
 
-    def body(rows, values, out, mark):
+    def body(rows, values, *refs):
+        out, mark = refs[len(after) :]
         out[0] = dot(rows[...], values[0], (1, 0))
         mark[...] = jnp.zeros_like(mark)
 
@@ -416,42 +451,46 @@
         in_specs=[
             pl.BlockSpec((tile, length), lambda j, i: (i, 0)),
             pl.BlockSpec((1, length, channels), lambda j, i: (j, 0, 0)),
-        ],
+        ]
+        + [HBM] * len(after),
         out_specs=(pl.BlockSpec((1, tile, channels), lambda j, i: (j, i, 0)), pl.BlockSpec((8, LANES), lambda j, i: (0, 0))),
         compiler_params=pltpu.CompilerParams(vmem_limit_bytes=VMEM_LIMIT),
         cost_estimate=cost(1.5 * groups),
-    )(rows, values)
+    )(rows, values, *after)
 
 
 def four_by_eight(tokens, weights, tables, out_weight, grad_mixed):
     length, width = 4 * tokens.shape[0], weights.shape[2] // 4
     own, near, far = column_blocks(tokens)
+    weights, out_weight = loaded((weights, out_weight), near)
     here = (own, flipped(near, "ctx", 1))
-    far = fetched(far)
+    feats_here, passed = channel_sums(here, 0, weights)
+    far = later(fetched(far), passed)
     there = (far, flipped(far, "fsdp", 1))
-    feats_here = channel_sums(here, 0, weights)
     grad_own, grad_near, grad_far = column_blocks(grad_mixed)
     grad_here = (grad_own, flipped(grad_near, "ctx", 1))
-    grad_far = fetched(later(grad_far, feats_here[2]))
+    grad_far = fetched(later(grad_far, far))
     grad_there = (grad_far, flipped(grad_far, "fsdp", 1))
-    feats_there = channel_sums(there, 1, weights)
-    grads_here = channel_sums(grad_here, 0, out_weight[None])
-    grads_there = channel_sums(grad_there, 1, out_weight[None])
+    feats_there, _ = channel_sums(there, 1, weights)
+    grads_here, _ = channel_sums(grad_here, 0, out_weight[None])
+    grads_there, _ = channel_sums(grad_there, 1, out_weight[None])
     *saved, gated = filter_forward(by_token(feats_here, feats_there), sum_of_three, tables, length, width)
     gated = gated[None]
     gated_far = flipped(gated, "ctx", 2)
     all_gated = all_channels(gated, gated_far)
     whole_gated, keeps, gives = output_pieces(all_gated, out_weight[None])
     givens = exchange(gives)
-    mixed = block_sums(keeps, givens)
+    mixed, mixed_last = block_sums(keeps, givens)
     grads = filter_backward(by_token(grads_here, grads_there), sum_of_three, tables, saved, length, width)
     grads = later(grads, gated_far)
     grad_out, mark = weight_gradient(turned(grad_here + grad_there), whole_gated)
     token_rows = turned(here + there)
     grads_far = later(flipped(grads, "ctx", 2), *givens, keeps[0], token_rows, mark)
     whole_grads, keeps, gives = output_pieces(all_channels(grads, grads_far), weights)
-    grad_tokens = block_sums(keeps, exchange(gives))
-    grad_in, _ = weight_gradient(token_rows, whole_grads)
+    grad_in, mark = weight_gradient(token_rows, whole_grads, (mixed_last,))
+    grad_tokens, last = block_sums(keeps, exchange(gives), (mark,))
+    mixed = settled(to_placement(later(mixed, last)))
+    grad_tokens = settled(to_placement(grad_tokens))
     return mixed, grad_tokens, grad_in, grad_out[0]
 
 

time: 103 us -> 106 us (1.029)
  the two profiles are of different devices: /device:TPU:1 before, /device:TPU:4 now
where the time goes in v4:
time: 106 us; the launch traced here: 105 us
  waiting for transfers between devices  43.1 us (41%)
  starting transfers between devices  31 us (29%)
  Pallas kernels  25.9 us (24%)
  local copies, waits for them, and re-layouts  3.77 us (4%)
    ppermute x32, waiting for transfers between devices, flipped(): lax.ppermute(value, axis, [(source, source ^ mask) for source in range(co...  33.6 us
    ppermute x32, starting transfers between devices, flipped(): lax.ppermute(value, axis, [(source, source ^ mask) for source in range(co...  22.8 us
    ppermute x2, starting transfers between devices, to_placement(): return lax.ppermute(value, ('fsdp', 'ctx'), pairs)  7.64 us
    ppermute x2, waiting for transfers between devices, to_placement(): return lax.ppermute(value, ('fsdp', 'ctx'), pairs)  7.01 us
    pallas_call x2, Pallas kernels, weight_gradient(): pl.pallas_call(body, out_shape=(jax.ShapeDtypeStruct((groups, depth, chan...  6.55 us
    pallas_call x4, Pallas kernels, project(): call(body, (jax.ShapeDtypeStruct((groups, length, width), F32), sums, sum...  3.66 us
    unnamed x16, local copies, waits for them, and re-layouts  3.01 us
    ppermute x2, waiting for transfers between devices, fetched(): return lax.ppermute(block, ('fsdp', 'ctx'), pairs)  2.49 us
  transfers between devices with their start and end apart: 36, of which 17 were waited for; matrix products, arithmetic and copies ran while one was open for 1% of the time, Pallas kernels for 21%

profile of v4, /device:TPU:4, one launch (start us, length us, event | category | flops | bytes accessed | tf_op | source)
XLA Modules:
  0.0 105.5 jit_solution(3755135521766762731)
XLA Ops:
  2.0 2.2 %shard_map.112 = (bf16[3,1024,512]{2,1,0:T(8,128)(2,1)S(1)}, bf16[1024,512]{1,0:T(8,128)(2,1)S(1)}) custom-call(bf16[3,1024,512]{2,1,0:T(8,128)(2,1)} %bitcast.16, bf16[1024,512]{1,0:T(8,128)(2,1)} %refs_1_.1, bf16[128,1024]{1,0:T(8,128)(2,1)S(1)} %get-tuple-element.60.refs_2_), custom_call_target="tpu_custom_call" | custom-call | flops 1495000064 | tf_op jit(solution)/shard_map/pallas_call | solution.py:249
  4.2 1.3 %shard_map.113 = (f32[3,256,128]{2,1,0:T(8,128)S(1)}, bf16[3,256,128]{2,1,0:T(8,128)(2,1)S(1)}, bf16[3,256,128]{2,1,0:T(8,128)(2,1)S(1)}, bf16[3,256,128]{2,1,0:T(8,128)(2,1)S(1)}) custom-call(bf16[128,1024]{1,0:T(8,128)(2,1)S(1)} %get-tuple-element.59.first.a, bf16[128,1024]{1,0:T(8,128)(2,1)S(1)} %collective-permute-done.second.b, ...), custom_call_target="tpu_custom_call" | custom-call | flops 2415000064 | tf_op jit(solution)/shard_map/pallas_call | solution.py:303
  8.1 2.5 %collective-permute-done.2.refs_0_ = bf16[128,1024]{1,0:T(8,128)(2,1)S(1)} collective-permute-done((bf16[128,1024]{1,0:T(8,128)(2,1)S(1)}, bf16[128,1024]{1,0:T(8,128)(2,1)S(1)}, u32[]{:S(2)}, u32[]{:S(2)}) %collective-permute-start.2) | collective-permute-done | bytes 262176 | tf_op jit(solution)/shard_map/ppermute | solution.py:281
  13.4 5.1 %collective-permute-done.4.second.d = bf16[128,1024]{1,0:T(8,128)(2,1)S(1)} collective-permute-done((bf16[128,1024]{1,0:T(8,128)(2,1)S(1)}, bf16[128,1024]{1,0:T(8,128)(2,1)S(1)}, u32[]{:S(2)}, u32[]{:S(2)}) %collective-permute-start.4) | collective-permute-done | bytes 262176 | tf_op jit(solution)/shard_map/ppermute | solution.py:41
  18.5 1.9 %copy-done.2 = bf16[3,1024,512]{2,1,0:T(8,128)(2,1)S(1)} copy-done((bf16[3,1024,512]{2,1,0:T(8,128)(2,1)S(1)}, bf16[3,1024,512]{2,1,0:T(8,128)(2,1)}, u32[]{:S(2)}) %copy-start.2) | copy-done | bytes 3145752
  20.4 1.3 %shard_map.116 = (f32[3,256,128]{2,1,0:T(8,128)S(1)}, bf16[3,256,128]{2,1,0:T(8,128)(2,1)S(1)}, bf16[3,256,128]{2,1,0:T(8,128)(2,1)S(1)}, bf16[3,256,128]{2,1,0:T(8,128)(2,1)S(1)}) custom-call(bf16[128,1024]{1,0:T(8,128)(2,1)S(1)} %shard_map.115.first.refs_1_.c, bf16[128,1024]{1,0:T(8,128)(2,1)S(1)} %collective-permute-done.4.second.d, ...), custom_call_target="tpu_custom_call" | custom-call | flops 2415000064 | tf_op jit(solution)/shard_map/pallas_call | solution.py:303
  22.5 1.7 %collective-permute-start.20 = (bf16[128,1024]{1,0:T(8,128)(2,1)S(1)}, bf16[128,1024]{1,0:T(8,128)(2,1)S(1)}, u32[]{:S(2)}, u32[]{:S(2)}) collective-permute-start(bf16[128,1024]{1,0:T(8,128)(2,1)S(1)} %collective-permute-done.19.first.c), channel_id=1, source_target_pairs={{0,4},{4,0},{8,12},{12,8},{16,20},{20,16},{24,28},{28,24},{1,5},{5... | collective-permute-start | bytes 786440 | tf_op jit(solution)/shard_map/ppermute | solution.py:41
  25.0 1.6 %collective-permute-start.6 = (bf16[3,256,128]{2,1,0:T(8,128)(2,1)S(1)}, bf16[3,256,128]{2,1,0:T(8,128)(2,1)S(1)}, u32[]{:S(2)}, u32[]{:S(2)}) collective-permute-start(bf16[3,256,128]{2,1,0:T(8,128)(2,1)S(1)} %shard_map.117), channel_id=1, source_target_pairs={{0,2},{1,3},{2,0},{3,1},{4,6},{5,7},{6,4},{7,5},{8,10},{9,11},{10,... | collective-permute-start | bytes 589832 | tf_op jit(solution)/shard_map/ppermute | solution.py:41
  27.9 3.3 %collective-permute-done.20.second.d = bf16[128,1024]{1,0:T(8,128)(2,1)S(1)} collective-permute-done((bf16[128,1024]{1,0:T(8,128)(2,1)S(1)}, bf16[128,1024]{1,0:T(8,128)(2,1)S(1)}, u32[]{:S(2)}, u32[]{:S(2)}) %collective-permute-start.20) | collective-permute-done | bytes 262176 | tf_op jit(solution)/shard_map/ppermute | solution.py:41
  32.5 3.2 %collective-permute-done.6.refs_2_ = bf16[3,256,128]{2,1,0:T(8,128)(2,1)S(1)} collective-permute-done((bf16[3,256,128]{2,1,0:T(8,128)(2,1)S(1)}, bf16[3,256,128]{2,1,0:T(8,128)(2,1)S(1)}, u32[]{:S(2)}, u32[]{:S(2)}) %collective-permute-start.6) | collective-permute-done | bytes 196640 | tf_op jit(solution)/shard_map/ppermute | solution.py:41
  35.7 2.1 %shard_map.118 = (f32[512,128]{1,0:T(8,128)S(1)}, f32[512,128]{1,0:T(8,128)S(1)}, f32[512,128]{1,0:T(8,128)S(1)}, f32[512,128]{1,0:T(8,128)S(1)}, bf16[512,128]{1,0:T(8,128)(2,1)S(1)}) custom-call(f32[3,256,128]{2,1,0:T(8,128)S(1)} %copy-done.7, bf16[3,256,128]{2,1,0:T(8,128)(2,1)S(1)} %collective-permute-done.1.refs_1_, ...), custom_call_target="tpu_custom_call" | custom-call | flops 3680000000 | tf_op jit(solution)/shard_map/pallas_call | solution.py:184
  38.5 1.6 %collective-permute-start.25 = (bf16[1,256,128]{2,1,0:T(8,128)(2,1)S(1)}, bf16[1,256,128]{2,1,0:T(8,128)(2,1)S(1)}, u32[]{:S(2)}, u32[]{:S(2)}) collective-permute-start(bf16[1,256,128]{2,1,0:T(8,128)(2,1)S(1)} %shard_map.129), channel_id=1, source_target_pairs={{0,2},{1,3},{2,0},{3,1},{4,6},{5,7},{6,4},{7,5},{8,10},{9,11},{10,... | collective-permute-start | bytes 196616 | tf_op jit(solution)/shard_map/ppermute | solution.py:41
  40.9 2.9 %collective-permute-done.9.far.refs_1_ = bf16[1,512,128]{2,1,0:T(8,128)(2,1)S(1)} collective-permute-done((bf16[1,512,128]{2,1,0:T(8,128)(2,1)S(1)}, bf16[1,512,128]{2,1,0:T(8,128)(2,1)S(1)}, u32[]{:S(2)}, u32[]{:S(2)}) %collective-permute-start.9) | collective-permute-done | bytes 131104 | tf_op jit(solution)/shard_map/ppermute | solution.py:41
  43.8 1.2 %collective-permute-done.25.refs_5_ = bf16[1,256,128]{2,1,0:T(8,128)(2,1)S(1)} collective-permute-done((bf16[1,256,128]{2,1,0:T(8,128)(2,1)S(1)}, bf16[1,256,128]{2,1,0:T(8,128)(2,1)S(1)}, u32[]{:S(2)}, u32[]{:S(2)}) %collective-permute-start.25) | collective-permute-done | bytes 65568 | tf_op jit(solution)/shard_map/ppermute | solution.py:41
  45.7 2.1 %shard_map.130.refs_0_ = bf16[3,512,128]{2,1,0:T(8,128)(2,1)S(1)} custom-call(f32[1,256,128]{2,1,0:T(8,128)S(1)} %get-tuple-element.86.refs_0_, bf16[1,256,128]{2,1,0:T(8,128)(2,1)S(1)} %collective-permute-done.18.refs_1_, bf16[1,256,128]{2,1,0:T(8,128)(2,1)S(1)} %collective-permute-done.22.refs_2_, f32[1,256,128]{2,1,0:T(8,128)S(1)} %get-tuple-element.91.refs_3_, ...), custom_call_target="tpu_custom_call" | custom-call | flops 2415000064 | tf_op jit(solution)/shard_map/pallas_call | solution.py:203
  49.7 1.7 %collective-permute-start.13 = (bf16[256,512]{1,0:T(8,128)(2,1)S(1)}, bf16[256,512]{1,0:T(8,128)(2,1)S(1)}, u32[]{:S(2)}, u32[]{:S(2)}) collective-permute-start(bf16[256,512]{1,0:T(8,128)(2,1)S(1)} %get-tuple-element.77), channel_id=1, source_target_pairs={{0,8},{4,12},{8,0},{12,4},{16,24},{20,28},{24,16},{28,20},{1,9},{5... | collective-permute-start | bytes 786440 | tf_op jit(solution)/shard_map/ppermute | solution.py:41
  52.4 1.9 %shard_map.134 = (f32[1,1024,512]{2,1,0:T(8,128)}, f32[8,128]{1,0:T(8,128)S(1)}) custom-call(bf16[1024,512]{1,0:T(8,128)(2,1)S(1)} %shard_map.133.rows, bf16[1,512,512]{2,1,0:T(8,128)(2,1)S(1)} %get-tuple-element.73.whole.values), custom_call_target="tpu_custom_call" | custom-call | flops 1724999936 | tf_op jit(solution)/shard_map/pallas_call | solution.py:447
  54.3 3.8 %collective-permute-done.26.refs_0_ = bf16[3,512,128]{2,1,0:T(8,128)(2,1)S(1)} collective-permute-done((bf16[3,512,128]{2,1,0:T(8,128)(2,1)S(1)}, bf16[3,512,128]{2,1,0:T(8,128)(2,1)S(1)}, u32[]{:S(2)}, u32[]{:S(2)}) %collective-permute-start.26) | collective-permute-done | bytes 393248 | tf_op jit(solution)/shard_map/ppermute | solution.py:41
  58.3 1.6 %collective-permute-start.14 = (bf16[256,256]{1,0:T(8,128)(2,1)S(1)}, bf16[256,256]{1,0:T(8,128)(2,1)S(1)}, u32[]{:S(2)}, u32[]{:S(2)}) collective-permute-start(bf16[256,256]{1,0:T(8,128)(2,1)S(1)} %get-tuple-element.79), channel_id=1, source_target_pairs={{0,8},{4,12},{8,0},{12,4},{16,24},{20,28},{24,16},{28,20},{1,9},{5... | collective-permute-start | bytes 393224 | tf_op jit(solution)/shard_map/ppermute | solution.py:41
  60.3 3.9 %collective-permute-done.14.given_z = bf16[256,256]{1,0:T(8,128)(2,1)S(1)} collective-permute-done((bf16[256,256]{1,0:T(8,128)(2,1)S(1)}, bf16[256,256]{1,0:T(8,128)(2,1)S(1)}, u32[]{:S(2)}, u32[]{:S(2)}) %collective-permute-start.14) | collective-permute-done | bytes 131104 | tf_op jit(solution)/shard_map/ppermute | solution.py:41
  64.2 1.3 %collective-permute-done.15.given_x = bf16[256,256]{1,0:T(8,128)(2,1)S(1)} collective-permute-done((bf16[256,256]{1,0:T(8,128)(2,1)S(1)}, bf16[256,256]{1,0:T(8,128)(2,1)S(1)}, u32[]{:S(2)}, u32[]{:S(2)}) %collective-permute-start.15) | collective-permute-done | bytes 131104 | tf_op jit(solution)/shard_map/ppermute | solution.py:41
  65.6 1.7 %shard_map.136 = (bf16[3,512,512]{2,1,0:T(8,128)(2,1)S(1)}, bf16[512,256]{1,0:T(8,128)(2,1)S(1)}, bf16[256,512]{1,0:T(8,128)(2,1)S(1)}) custom-call(bf16[3,512,128]{2,1,0:T(8,128)(2,1)S(1)} %shard_map.131.own, bf16[3,512,128]{2,1,0:T(8,128)(2,1)S(1)} %shard_map.135.far, bf16[3,512,128]{2,1,0:T(8,128)(2,1)S(1)} %collective-permute-done.27.near, ...), custom_call_target="tpu_custom_call" | custom-call | flops 2070000000 | tf_op jit(solution)/shard_map/pallas_call | solution.py:367
  68.3 4.7 %shard_map.138 = (f32[3,1024,512]{2,1,0:T(8,128)}, f32[8,128]{1,0:T(8,128)S(1)}) custom-call(bf16[1024,512]{1,0:T(8,128)(2,1)S(1)} %shard_map.132.refs_4_.rows, bf16[3,512,512]{2,1,0:T(8,128)(2,1)S(1)} %get-tuple-element.100.whole.values, bf16[128,512]{1,0:T(8,128)(2,1)S(1)} %get-tuple-element.83.refs_0_), custom_call_target="tpu_custom_call" | custom-call | flops 5175000064 | tf_op jit(solution)/shard_map/pallas_call | solution.py:447
  72.9 1.4 %shard_map.137 = (bf16[512,256]{1,0:T(8,128)(2,1)S(1)}, bf16[256,512]{1,0:T(8,128)(2,1)S(1)}) custom-call(bf16[3,512,512]{2,1,0:T(8,128)(2,1)S(1)} %get-tuple-element.100.whole.values, bf16[3,1024,512]{2,1,0:T(8,128)(2,1)S(1)} %copy-done.3), custom_call_target="tpu_custom_call" | custom-call | flops 1380000000 | tf_op jit(solution)/shard_map/pallas_call | solution.py:373
  76.2 1.6 %collective-permute-start.32 = (bf16[256,256]{1,0:T(8,128)(2,1)S(1)}, bf16[256,256]{1,0:T(8,128)(2,1)S(1)}, u32[]{:S(2)}, u32[]{:S(2)}) collective-permute-start(bf16[256,256]{1,0:T(8,128)(2,1)S(1)} %get-tuple-element.109), channel_id=1, source_target_pairs={{0,4},{4,0},{8,12},{12,8},{16,20},{20,16},{24,28},{28,24},{1,5},{5... | collective-permute-start | bytes 393224 | tf_op jit(solution)/shard_map/ppermute | solution.py:41
  77.8 2.6 %collective-permute-start.16 = (bf16[128,512]{1,0:T(8,128)(2,1)S(1)}, bf16[128,512]{1,0:T(8,128)(2,1)S(1)}, u32[]{:S(2)}, u32[]{:S(2)}) collective-permute-start(bf16[128,512]{1,0:T(8,128)(2,1)S(1)} %get-tuple-element.83.refs_0_), channel_id=1, source_target_pairs={{0,16},{4,20},{8,24},{12,28},{16,0},{20,4},{24,8},{28,12},{1,17},{... | collective-permute-start | bytes 393224 | tf_op jit(solution)/shard_map/ppermute | solution.py:41
  81.2 2.6 %collective-permute-start.34 = (bf16[128,512]{1,0:T(8,128)(2,1)S(1)}, bf16[128,512]{1,0:T(8,128)(2,1)S(1)}, u32[]{:S(2)}, u32[]{:S(2)}) collective-permute-start(bf16[128,512]{1,0:T(8,128)(2,1)S(1)} %get-tuple-element.110.refs_1_), channel_id=1, source_target_pairs={{0,16},{4,20},{8,24},{12,28},{16,0},{20,4},{24,8},{28,12},{1,17},{... | collective-permute-start | bytes 393224 | tf_op jit(solution)/shard_map/ppermute | solution.py:41
  83.8 5.5 %collective-permute-done.16.given = bf16[128,512]{1,0:T(8,128)(2,1)S(1)} collective-permute-done((bf16[128,512]{1,0:T(8,128)(2,1)S(1)}, bf16[128,512]{1,0:T(8,128)(2,1)S(1)}, u32[]{:S(2)}, u32[]{:S(2)}) %collective-permute-start.16) | collective-permute-done | bytes 131104 | tf_op jit(solution)/shard_map/ppermute | solution.py:41
  89.4 1.9 %collective-permute-start.33 = (bf16[128,512]{1,0:T(8,128)(2,1)S(1)}, bf16[128,512]{1,0:T(8,128)(2,1)S(1)}, u32[]{:S(2)}, u32[]{:S(2)}) collective-permute-start(bf16[128,512]{1,0:T(8,128)(2,1)S(1)} %shard_map.141), channel_id=1, source_target_pairs={{0,0},{1,8},{2,16},{3,24},{4,4},{5,12},{6,20},{7,28},{8,1},{9,9},{... | collective-permute-start | bytes 393224 | tf_op jit(solution)/shard_map/ppermute | solution.py:56
  91.4 5.7 %collective-permute-start.35 = (bf16[128,512]{1,0:T(8,128)(2,1)S(1)}, bf16[128,512]{1,0:T(8,128)(2,1)S(1)}, u32[]{:S(2)}, u32[]{:S(2)}) collective-permute-start(bf16[128,512]{1,0:T(8,128)(2,1)S(1)} %shard_map.143), channel_id=1, source_target_pairs={{0,0},{1,8},{2,16},{3,24},{4,4},{5,12},{6,20},{7,28},{8,1},{9,9},{... | collective-permute-start | bytes 393224 | tf_op jit(solution)/shard_map/ppermute | solution.py:56
  97.1 4.1 %collective-permute-done.33.value = bf16[128,512]{1,0:T(8,128)(2,1)S(1)} collective-permute-done((bf16[128,512]{1,0:T(8,128)(2,1)S(1)}, bf16[128,512]{1,0:T(8,128)(2,1)S(1)}, u32[]{:S(2)}, u32[]{:S(2)}) %collective-permute-start.33) | collective-permute-done | bytes 131104 | tf_op jit(solution)/shard_map/ppermute | solution.py:56
  101.9 2.9 %collective-permute-done.35.value = bf16[128,512]{1,0:T(8,128)(2,1)S(1)} collective-permute-done((bf16[128,512]{1,0:T(8,128)(2,1)S(1)}, bf16[128,512]{1,0:T(8,128)(2,1)S(1)}, u32[]{:S(2)}, u32[]{:S(2)}) %collective-permute-start.35) | collective-permute-done | bytes 131104 | tf_op jit(solution)/shard_map/ppermute | solution.py:56
  (93 shorter events, 21.4 us)
Async XLA Ops:
  1.9 8.7 %collective-permute-start.2 = (bf16[128,1024]{1,0:T(8,128)(2,1)S(1)}, bf16[128,1024]{1,0:T(8,128)(2,1)S(1)}, u32[]{:S(2)}, u32[]{:S(2)}) collective-permute-start(bf16[128,1024]{1,0:T(8,128)(2,1)S(1)} %get-tuple-element.64), channel_id=1, source_target_pairs={{0,2},{1,3},{2,0},{3,1},{4,7},{5,6},{6,5},{7,4},{8,10},{9,11},{10,... | collective-permute-start | bytes 786440 | tf_op jit(solution)/shard_map/ppermute | solution.py:281
  10.6 7.9 %collective-permute-start.4 = (bf16[128,1024]{1,0:T(8,128)(2,1)S(1)}, bf16[128,1024]{1,0:T(8,128)(2,1)S(1)}, u32[]{:S(2)}, u32[]{:S(2)}) collective-permute-start(bf16[128,1024]{1,0:T(8,128)(2,1)S(1)} %shard_map.115.first.refs_1_.c), channel_id=1, source_target_pairs={{0,4},{4,0},{8,12},{12,8},{16,20},{20,16},{24,28},{28,24},{1,5},{5... | collective-permute-start | bytes 786440 | tf_op jit(solution)/shard_map/ppermute | solution.py:41
  12.6 12.4 %collective-permute-start.17 = (bf16[128,1024]{1,0:T(8,128)(2,1)S(1)}, bf16[128,1024]{1,0:T(8,128)(2,1)S(1)}, u32[]{:S(2)}, u32[]{:S(2)}) collective-permute-start(bf16[128,1024]{1,0:T(8,128)(2,1)S(1)} %get-tuple-element.85), channel_id=1, source_target_pairs={{0,1},{1,0},{2,3},{3,2},{4,5},{5,4},{6,7},{7,6},{8,9},{9,8},{10,11... | collective-permute-start | bytes 786440 | tf_op jit(solution)/shard_map/ppermute | solution.py:41
  12.8 9.6 %collective-permute-start.19 = (bf16[128,1024]{1,0:T(8,128)(2,1)S(1)}, bf16[128,1024]{1,0:T(8,128)(2,1)S(1)}, u32[]{:S(2)}, u32[]{:S(2)}) collective-permute-start(bf16[128,1024]{1,0:T(8,128)(2,1)S(1)} %shard_map.126), channel_id=1, source_target_pairs={{0,2},{1,3},{2,0},{3,1},{4,7},{5,6},{6,5},{7,4},{8,10},{9,11},{10,... | collective-permute-start | bytes 786440 | tf_op jit(solution)/shard_map/ppermute | solution.py:281
  22.5 8.8 %collective-permute-start.20 = (bf16[128,1024]{1,0:T(8,128)(2,1)S(1)}, bf16[128,1024]{1,0:T(8,128)(2,1)S(1)}, u32[]{:S(2)}, u32[]{:S(2)}) collective-permute-start(bf16[128,1024]{1,0:T(8,128)(2,1)S(1)} %collective-permute-done.19.first.c), channel_id=1, source_target_pairs={{0,4},{4,0},{8,12},{12,8},{16,20},{20,16},{24,28},{28,24},{1,5},{5... | collective-permute-start | bytes 786440 | tf_op jit(solution)/shard_map/ppermute | solution.py:41
  24.2 7.6 %collective-permute-start.1 = (bf16[3,256,128]{2,1,0:T(8,128)(2,1)S(1)}, bf16[3,256,128]{2,1,0:T(8,128)(2,1)S(1)}, u32[]{:S(2)}, u32[]{:S(2)}) collective-permute-start(bf16[3,256,128]{2,1,0:T(8,128)(2,1)S(1)} %get-tuple-element.63), channel_id=1, source_target_pairs={{0,1},{1,0},{2,3},{3,2},{4,5},{5,4},{6,7},{7,6},{8,9},{9,8},{10,11... | collective-permute-start | bytes 589832 | tf_op jit(solution)/shard_map/ppermute | solution.py:41
  24.4 8.0 %collective-permute-start.8 = (bf16[3,256,128]{2,1,0:T(8,128)(2,1)S(1)}, bf16[3,256,128]{2,1,0:T(8,128)(2,1)S(1)}, u32[]{:S(2)}, u32[]{:S(2)}) collective-permute-start(bf16[3,256,128]{2,1,0:T(8,128)(2,1)S(1)} %shard_map.114.refs_1_), channel_id=1, source_target_pairs={{0,2},{1,3},{2,0},{3,1},{4,6},{5,7},{6,4},{7,5},{8,10},{9,11},{10,... | collective-permute-start | bytes 589832 | tf_op jit(solution)/shard_map/ppermute | solution.py:41
  24.9 7.6 %collective-permute-start.7 = (bf16[3,256,128]{2,1,0:T(8,128)(2,1)S(1)}, bf16[3,256,128]{2,1,0:T(8,128)(2,1)S(1)}, u32[]{:S(2)}, u32[]{:S(2)}) collective-permute-start(bf16[3,256,128]{2,1,0:T(8,128)(2,1)S(1)} %get-tuple-element.70), channel_id=1, source_target_pairs={{0,1},{1,0},{2,3},{3,2},{4,5},{5,4},{6,7},{7,6},{8,9},{9,8},{10,11... | collective-permute-start | bytes 589832 | tf_op jit(solution)/shard_map/ppermute | solution.py:41
  25.0 10.7 %collective-permute-start.6 = (bf16[3,256,128]{2,1,0:T(8,128)(2,1)S(1)}, bf16[3,256,128]{2,1,0:T(8,128)(2,1)S(1)}, u32[]{:S(2)}, u32[]{:S(2)}) collective-permute-start(bf16[3,256,128]{2,1,0:T(8,128)(2,1)S(1)} %shard_map.117), channel_id=1, source_target_pairs={{0,2},{1,3},{2,0},{3,1},{4,6},{5,7},{6,4},{7,5},{8,10},{9,11},{10,... | collective-permute-start | bytes 589832 | tf_op jit(solution)/shard_map/ppermute | solution.py:41
  31.2 9.4 %collective-permute-start.18 = (bf16[1,256,128]{2,1,0:T(8,128)(2,1)S(1)}, bf16[1,256,128]{2,1,0:T(8,128)(2,1)S(1)}, u32[]{:S(2)}, u32[]{:S(2)}) collective-permute-start(bf16[1,256,128]{2,1,0:T(8,128)(2,1)S(1)} %get-tuple-element.87), channel_id=1, source_target_pairs={{0,1},{1,0},{2,3},{3,2},{4,5},{5,4},{6,7},{7,6},{8,9},{9,8},{10,11... | collective-permute-start | bytes 196616 | tf_op jit(solution)/shard_map/ppermute | solution.py:41
  31.8 6.6 %collective-permute-start.24 = (bf16[1,256,128]{2,1,0:T(8,128)(2,1)S(1)}, bf16[1,256,128]{2,1,0:T(8,128)(2,1)S(1)}, u32[]{:S(2)}, u32[]{:S(2)}) collective-permute-start(bf16[1,256,128]{2,1,0:T(8,128)(2,1)S(1)} %get-tuple-element.94), channel_id=1, source_target_pairs={{0,1},{1,0},{2,3},{3,2},{4,5},{5,4},{6,7},{7,6},{8,9},{9,8},{10,11... | collective-permute-start | bytes 196616 | tf_op jit(solution)/shard_map/ppermute | solution.py:41
  32.4 7.7 %collective-permute-start.21 = (bf16[1,256,128]{2,1,0:T(8,128)(2,1)S(1)}, bf16[1,256,128]{2,1,0:T(8,128)(2,1)S(1)}, u32[]{:S(2)}, u32[]{:S(2)}) collective-permute-start(bf16[1,256,128]{2,1,0:T(8,128)(2,1)S(1)} %get-tuple-element.90), channel_id=1, source_target_pairs={{0,1},{1,0},{2,3},{3,2},{4,5},{5,4},{6,7},{7,6},{8,9},{9,8},{10,11... | collective-permute-start | bytes 196616 | tf_op jit(solution)/shard_map/ppermute | solution.py:41
  37.9 5.9 %collective-permute-start.9 = (bf16[1,512,128]{2,1,0:T(8,128)(2,1)S(1)}, bf16[1,512,128]{2,1,0:T(8,128)(2,1)S(1)}, u32[]{:S(2)}, u32[]{:S(2)}) collective-permute-start(bf16[1,512,128]{2,1,0:T(8,128)(2,1)S(1)} %bitcast.9), channel_id=1, source_target_pairs={{0,2},{1,3},{2,0},{3,1},{4,6},{5,7},{6,4},{7,5},{8,10},{9,11},{10,... | collective-permute-start | bytes 393224 | tf_op jit(solution)/shard_map/ppermute | solution.py:41
  38.5 6.5 %collective-permute-start.25 = (bf16[1,256,128]{2,1,0:T(8,128)(2,1)S(1)}, bf16[1,256,128]{2,1,0:T(8,128)(2,1)S(1)}, u32[]{:S(2)}, u32[]{:S(2)}) collective-permute-start(bf16[1,256,128]{2,1,0:T(8,128)(2,1)S(1)} %shard_map.129), channel_id=1, source_target_pairs={{0,2},{1,3},{2,0},{3,1},{4,6},{5,7},{6,4},{7,5},{8,10},{9,11},{10,... | collective-permute-start | bytes 196616 | tf_op jit(solution)/shard_map/ppermute | solution.py:41
  40.1 5.6 %collective-permute-start.22 = (bf16[1,256,128]{2,1,0:T(8,128)(2,1)S(1)}, bf16[1,256,128]{2,1,0:T(8,128)(2,1)S(1)}, u32[]{:S(2)}, u32[]{:S(2)}) collective-permute-start(bf16[1,256,128]{2,1,0:T(8,128)(2,1)S(1)} %shard_map.128), channel_id=1, source_target_pairs={{0,2},{1,3},{2,0},{3,1},{4,6},{5,7},{6,4},{7,5},{8,10},{9,11},{10,... | collective-permute-start | bytes 196616 | tf_op jit(solution)/shard_map/ppermute | solution.py:41
  40.7 8.0 %collective-permute-start.10 = (bf16[1,512,128]{2,1,0:T(8,128)(2,1)S(1)}, bf16[1,512,128]{2,1,0:T(8,128)(2,1)S(1)}, u32[]{:S(2)}, u32[]{:S(2)}) collective-permute-start(bf16[1,512,128]{2,1,0:T(8,128)(2,1)S(1)} %bitcast.10), channel_id=1, source_target_pairs={{0,1},{1,0},{2,3},{3,2},{4,5},{5,4},{6,7},{7,6},{8,9},{9,8},{10,11... | collective-permute-start | bytes 393224 | tf_op jit(solution)/shard_map/ppermute | solution.py:41
  43.8 4.9 %collective-permute-start.11 = (bf16[1,512,128]{2,1,0:T(8,128)(2,1)S(1)}, bf16[1,512,128]{2,1,0:T(8,128)(2,1)S(1)}, u32[]{:S(2)}, u32[]{:S(2)}) collective-permute-start(bf16[1,512,128]{2,1,0:T(8,128)(2,1)S(1)} %collective-permute-done.9.far.refs_1_), channel_id=1, source_target_pairs={{0,1},{1,0},{2,3},{3,2},{4,5},{5,4},{6,7},{7,6},{8,9},{9,8},{10,11... | collective-permute-start | bytes 393224 | tf_op jit(solution)/shard_map/ppermute | solution.py:41
  47.8 10.3 %collective-permute-start.26 = (bf16[3,512,128]{2,1,0:T(8,128)(2,1)S(1)}, bf16[3,512,128]{2,1,0:T(8,128)(2,1)S(1)}, u32[]{:S(2)}, u32[]{:S(2)}) collective-permute-start(bf16[3,512,128]{2,1,0:T(8,128)(2,1)S(1)} %shard_map.131.own), channel_id=1, source_target_pairs={{0,2},{1,3},{2,0},{3,1},{4,6},{5,7},{6,4},{7,5},{8,10},{9,11},{10,... | collective-permute-start | bytes 1179656 | tf_op jit(solution)/shard_map/ppermute | solution.py:41
  49.3 8.7 %collective-permute-start.12 = (bf16[512,256]{1,0:T(8,128)(2,1)S(1)}, bf16[512,256]{1,0:T(8,128)(2,1)S(1)}, u32[]{:S(2)}, u32[]{:S(2)}) collective-permute-start(bf16[512,256]{1,0:T(8,128)(2,1)S(1)} %get-tuple-element.75), channel_id=1, source_target_pairs={{0,4},{4,0},{8,12},{12,8},{16,20},{20,16},{24,28},{28,24},{1,5},{5... | collective-permute-start | bytes 786440 | tf_op jit(solution)/shard_map/ppermute | solution.py:41
  49.7 8.3 %collective-permute-start.13 = (bf16[256,512]{1,0:T(8,128)(2,1)S(1)}, bf16[256,512]{1,0:T(8,128)(2,1)S(1)}, u32[]{:S(2)}, u32[]{:S(2)}) collective-permute-start(bf16[256,512]{1,0:T(8,128)(2,1)S(1)} %get-tuple-element.77), channel_id=1, source_target_pairs={{0,8},{4,12},{8,0},{12,4},{16,24},{20,28},{24,16},{28,20},{1,9},{5... | collective-permute-start | bytes 786440 | tf_op jit(solution)/shard_map/ppermute | solution.py:41
  51.7 13.9 %collective-permute-start.27 = (bf16[3,512,128]{2,1,0:T(8,128)(2,1)S(1)}, bf16[3,512,128]{2,1,0:T(8,128)(2,1)S(1)}, u32[]{:S(2)}, u32[]{:S(2)}) collective-permute-start(bf16[3,512,128]{2,1,0:T(8,128)(2,1)S(1)} %shard_map.131.own), channel_id=1, source_target_pairs={{0,1},{1,0},{2,3},{3,2},{4,5},{5,4},{6,7},{7,6},{8,9},{9,8},{10,11... | collective-permute-start | bytes 1179656 | tf_op jit(solution)/shard_map/ppermute | solution.py:41
  58.1 7.5 %collective-permute-start.28 = (bf16[3,512,128]{2,1,0:T(8,128)(2,1)S(1)}, bf16[3,512,128]{2,1,0:T(8,128)(2,1)S(1)}, u32[]{:S(2)}, u32[]{:S(2)}) collective-permute-start(bf16[3,512,128]{2,1,0:T(8,128)(2,1)S(1)} %shard_map.135.far), channel_id=1, source_target_pairs={{0,1},{1,0},{2,3},{3,2},{4,5},{5,4},{6,7},{7,6},{8,9},{9,8},{10,11... | collective-permute-start | bytes 1179656 | tf_op jit(solution)/shard_map/ppermute | solution.py:41
  58.3 5.9 %collective-permute-start.14 = (bf16[256,256]{1,0:T(8,128)(2,1)S(1)}, bf16[256,256]{1,0:T(8,128)(2,1)S(1)}, u32[]{:S(2)}, u32[]{:S(2)}) collective-permute-start(bf16[256,256]{1,0:T(8,128)(2,1)S(1)} %get-tuple-element.79), channel_id=1, source_target_pairs={{0,8},{4,12},{8,0},{12,4},{16,24},{20,28},{24,16},{28,20},{1,9},{5... | collective-permute-start | bytes 393224 | tf_op jit(solution)/shard_map/ppermute | solution.py:41
  59.9 5.6 %collective-permute-start.15 = (bf16[256,256]{1,0:T(8,128)(2,1)S(1)}, bf16[256,256]{1,0:T(8,128)(2,1)S(1)}, u32[]{:S(2)}, u32[]{:S(2)}) collective-permute-start(bf16[256,256]{1,0:T(8,128)(2,1)S(1)} %get-tuple-element.81), channel_id=1, source_target_pairs={{0,4},{4,0},{8,12},{12,8},{16,20},{20,16},{24,28},{28,24},{1,5},{5... | collective-permute-start | bytes 393224 | tf_op jit(solution)/shard_map/ppermute | solution.py:41
  67.4 7.6 %collective-permute-start.29 = (bf16[512,256]{1,0:T(8,128)(2,1)S(1)}, bf16[512,256]{1,0:T(8,128)(2,1)S(1)}, u32[]{:S(2)}, u32[]{:S(2)}) collective-permute-start(bf16[512,256]{1,0:T(8,128)(2,1)S(1)} %get-tuple-element.102), channel_id=1, source_target_pairs={{0,4},{4,0},{8,12},{12,8},{16,20},{20,16},{24,28},{28,24},{1,5},{5... | collective-permute-start | bytes 786440 | tf_op jit(solution)/shard_map/ppermute | solution.py:41
  67.8 7.3 %collective-permute-start.30 = (bf16[256,512]{1,0:T(8,128)(2,1)S(1)}, bf16[256,512]{1,0:T(8,128)(2,1)S(1)}, u32[]{:S(2)}, u32[]{:S(2)}) collective-permute-start(bf16[256,512]{1,0:T(8,128)(2,1)S(1)} %get-tuple-element.104), channel_id=1, source_target_pairs={{0,8},{4,12},{8,0},{12,4},{16,24},{20,28},{24,16},{28,20},{1,9},{5... | collective-permute-start | bytes 786440 | tf_op jit(solution)/shard_map/ppermute | solution.py:41
  75.2 5.2 %collective-permute-start.31 = (bf16[256,256]{1,0:T(8,128)(2,1)S(1)}, bf16[256,256]{1,0:T(8,128)(2,1)S(1)}, u32[]{:S(2)}, u32[]{:S(2)}) collective-permute-start(bf16[256,256]{1,0:T(8,128)(2,1)S(1)} %get-tuple-element.107), channel_id=1, source_target_pairs={{0,8},{4,12},{8,0},{12,4},{16,24},{20,28},{24,16},{28,20},{1,9},{5... | collective-permute-start | bytes 393224 | tf_op jit(solution)/shard_map/ppermute | solution.py:41
  76.2 5.0 %collective-permute-start.32 = (bf16[256,256]{1,0:T(8,128)(2,1)S(1)}, bf16[256,256]{1,0:T(8,128)(2,1)S(1)}, u32[]{:S(2)}, u32[]{:S(2)}) collective-permute-start(bf16[256,256]{1,0:T(8,128)(2,1)S(1)} %get-tuple-element.109), channel_id=1, source_target_pairs={{0,4},{4,0},{8,12},{12,8},{16,20},{20,16},{24,28},{28,24},{1,5},{5... | collective-permute-start | bytes 393224 | tf_op jit(solution)/shard_map/ppermute | solution.py:41
  77.8 11.5 %collective-permute-start.16 = (bf16[128,512]{1,0:T(8,128)(2,1)S(1)}, bf16[128,512]{1,0:T(8,128)(2,1)S(1)}, u32[]{:S(2)}, u32[]{:S(2)}) collective-permute-start(bf16[128,512]{1,0:T(8,128)(2,1)S(1)} %get-tuple-element.83.refs_0_), channel_id=1, source_target_pairs={{0,16},{4,20},{8,24},{12,28},{16,0},{20,4},{24,8},{28,12},{1,17},{... | collective-permute-start | bytes 393224 | tf_op jit(solution)/shard_map/ppermute | solution.py:41
  81.2 10.2 %collective-permute-start.34 = (bf16[128,512]{1,0:T(8,128)(2,1)S(1)}, bf16[128,512]{1,0:T(8,128)(2,1)S(1)}, u32[]{:S(2)}, u32[]{:S(2)}) collective-permute-start(bf16[128,512]{1,0:T(8,128)(2,1)S(1)} %get-tuple-element.110.refs_1_), channel_id=1, source_target_pairs={{0,16},{4,20},{8,24},{12,28},{16,0},{20,4},{24,8},{28,12},{1,17},{... | collective-permute-start | bytes 393224 | tf_op jit(solution)/shard_map/ppermute | solution.py:41
  89.4 11.8 %collective-permute-start.33 = (bf16[128,512]{1,0:T(8,128)(2,1)S(1)}, bf16[128,512]{1,0:T(8,128)(2,1)S(1)}, u32[]{:S(2)}, u32[]{:S(2)}) collective-permute-start(bf16[128,512]{1,0:T(8,128)(2,1)S(1)} %shard_map.141), channel_id=1, source_target_pairs={{0,0},{1,8},{2,16},{3,24},{4,4},{5,12},{6,20},{7,28},{8,1},{9,9},{... | collective-permute-start | bytes 393224 | tf_op jit(solution)/shard_map/ppermute | solution.py:56
  91.4 13.4 %collective-permute-start.35 = (bf16[128,512]{1,0:T(8,128)(2,1)S(1)}, bf16[128,512]{1,0:T(8,128)(2,1)S(1)}, u32[]{:S(2)}, u32[]{:S(2)}) collective-permute-start(bf16[128,512]{1,0:T(8,128)(2,1)S(1)} %shard_map.143), channel_id=1, source_target_pairs={{0,0},{1,8},{2,16},{3,24},{4,4},{5,12},{6,20},{7,28},{8,1},{9,9},{... | collective-permute-start | bytes 393224 | tf_op jit(solution)/shard_map/ppermute | solution.py:56
  (12 other events, 64.5 us)

commit v5 on v4

--- a/solution.py
+++ b/solution.py
@@ -12,7 +12,7 @@
 LANES = 128
 CHUNKS = 8
 MARGIN = 8
-VMEM_LIMIT = 16 * 1024 * 1024
+VMEM_LIMIT = 12 * 1024 * 1024
 SMALL_LIMIT = 4 * 1024 * 1024
 FLOPS_PER_US = 1_150_000_000
 
@@ -25,13 +25,13 @@
     return pl.CostEstimate(flops=int(us * FLOPS_PER_US), bytes_accessed=0, transcendentals=0)
 
 
-def call(body, outs, scratch=(), in_specs=None, us=0.5):
+def call(body, outs, scratch=(), in_specs=None, us=0.5, limit=VMEM_LIMIT):
     return pl.pallas_call(
         body,
         out_shape=outs,
         **({} if in_specs is None else {"in_specs": in_specs}),
         scratch_shapes=list(scratch),
-        compiler_params=pltpu.CompilerParams(vmem_limit_bytes=VMEM_LIMIT),
+        compiler_params=pltpu.CompilerParams(vmem_limit_bytes=limit),
         cost_estimate=cost(us),
     )
 
@@ -228,13 +228,6 @@
     )(value, *after)
 
 
-def settled(value):
-    def body(value, out):
-        out[...] = value[...]
-
-    return call(body, jax.ShapeDtypeStruct(value.shape, value.dtype), us=0.3)(value)
-
-
 def loaded(values, after):
     count = len(values)
 
@@ -252,7 +245,7 @@
         in_specs=[HBM] * (count + 1),
         out_specs=(VMEM,) * count,
         scratch_shapes=[pltpu.SemaphoreType.DMA((count,))],
-        compiler_params=pltpu.CompilerParams(vmem_limit_bytes=VMEM_LIMIT),
+        compiler_params=pltpu.CompilerParams(vmem_limit_bytes=SMALL_LIMIT),
         cost_estimate=cost(1.3),
     )(*[pltpu.with_memory_space_constraint(value, pltpu.HBM) for value in values], after)
 
@@ -271,7 +264,7 @@
             copy.wait()
 
     block = jax.ShapeDtypeStruct((length, width), rows.dtype)
-    return call(body, (block,) * 3, [pltpu.SemaphoreType.DMA((3,))], in_specs=[HBM], us=0.7)(
+    return call(body, (block,) * 3, [pltpu.SemaphoreType.DMA((3,))], in_specs=[HBM], us=0.7, limit=SMALL_LIMIT)(
         pltpu.with_memory_space_constraint(rows, pltpu.HBM)
     )
 
@@ -281,13 +274,14 @@
     return lax.ppermute(block, ("fsdp", "ctx"), pairs)
 
 
-def project(pieces, other, weight):
+def project(pieces, other, weight, after=()):
     groups, depth, channels = weight.shape
     part = pieces[0].shape[0]
     length = 2 * part
     width = channels // 4
 
-    def body(first, second, weight, own, far, give, give_far, held, product):
+    def body(first, second, weight, *refs):
+        own, far, give, give_far, held, product = refs[len(after) :]
         me = lax.axis_index("ctx")
         core = (me ^ lax.axis_index("fsdp")) & 1 if other else me & 1
         held[block_at(core, part), :] = first[...]
@@ -304,19 +298,20 @@
         body,
         (jax.ShapeDtypeStruct((groups, length, width), F32), sums, sums, sums),
         [pltpu.VMEM((length, depth), BF16), pltpu.VMEM((length, channels), F32)],
-        us=0.7 * groups,
-    )(*pieces, weight)
+        in_specs=[VMEM] * 3 + [HBM] * len(after),
+        us=0.45 * groups,
+    )(*pieces, weight, *after)
 
 
 def add_far(left, right):
     def body(left, right, out):
         out[...] = (left[...].astype(F32) + right[...].astype(F32)).astype(BF16)
 
-    return call(body, jax.ShapeDtypeStruct(left.shape, BF16))(left, right)
-
-
-def channel_sums(pieces, other, weight):
-    own, far, give, give_far = project(pieces, other, weight)
+    return call(body, jax.ShapeDtypeStruct(left.shape, BF16), limit=SMALL_LIMIT)(left, right)
+
+
+def channel_sums(pieces, other, weight, after=()):
+    own, far, give, give_far = project(pieces, other, weight, after)
     passed = add_far(far, flipped(give_far, "ctx", 1))
     return (own, flipped(give, "ctx", 1), flipped(passed, "ctx", 2)), passed
 
@@ -378,7 +373,16 @@
     return flipped(gives[0], "fsdp", 1), flipped(gives[1], "fsdp", 2)
 
 
-def block_sums(keeps, givens, after=()):
+def final_pairs(flip):
+    pairs = []
+    for f in range(8):
+        for k in range(4):
+            high, low, x, y, core = f >> 2, (f >> 1) & 1, f & 1, k >> 1, k & 1
+            pairs.append((4 * f + k, 4 * (4 * (y ^ high ^ flip) + 2 * core + x) + 2 * y + low))
+    return pairs
+
+
+def block_sums(keeps, givens, after=(), after_second=()):
     length, piece = keeps[0].shape
     part = length // 4
     both = lambda keep, given, rows, columns: keep[rows, columns].astype(F32) + given[rows, columns].astype(F32)
@@ -401,25 +405,36 @@
         second_body,
         (square(BF16), square(BF16), square(F32), square(F32)),
         in_specs=[VMEM] * 4 + [HBM] * len(after),
+        limit=SMALL_LIMIT,
     )(keeps[0], givens[0], keeps[1], givens[1], *after)
 
-    def third_body(keep_z, given_z, keep_x, given_x, give, keep):
-        high = lax.axis_index("fsdp") >> 2
-        for bit, out in ((1 - high, give), (high, keep)):
+    def third_body(keep_z, given_z, keep_x, given_x, *refs):
+        give, keep = refs[len(after_second) :]
+        y = lax.axis_index("ctx") >> 1
+        for bit, out in ((1 - y, give), (y, keep)):
             at = block_at(bit, part)
             for half, (mine, other) in enumerate(((keep_z, given_z), (keep_x, given_x))):
                 columns = slice(half * piece, (half + 1) * piece)
-                out[:, columns] = both(mine, other, at, slice(None)).astype(out.dtype)
-
-    block = lambda kind: jax.ShapeDtypeStruct((part, 2 * piece), kind)
-    give, keep = call(third_body, (block(BF16), block(F32)))(
-        next_z, flipped(give_z, "fsdp", 2), next_x, flipped(give_x, "fsdp", 1)
+                out[:, columns] = both(mine, other, at, slice(None)).astype(BF16)
+
+    block = jax.ShapeDtypeStruct((part, 2 * piece), BF16)
+    give, keep = call(third_body, (block, block), in_specs=[VMEM] * 4 + [HBM] * len(after_second), limit=SMALL_LIMIT)(
+        next_z, flipped(give_z, "fsdp", 2), next_x, flipped(give_x, "fsdp", 1), *after_second
     )
 
-    def last_body(keep, given, out):
-        out[...] = (keep[...] + given[...].astype(F32)).astype(BF16)
-
-    return call(last_body, block(BF16))(keep, flipped(give, "fsdp", 4)), give
+    def order_body(keep, given, first, second):
+        high = lax.axis_index("fsdp") >> 2
+        swap = high == 1
+        first[...] = jnp.where(swap, given[...].astype(F32), keep[...].astype(F32)).astype(BF16)
+        second[...] = jnp.where(swap, keep[...].astype(F32), given[...].astype(F32)).astype(BF16)
+
+    blocks = call(order_body, (block, block), limit=SMALL_LIMIT)(keep, flipped(give, "ctx", 2))
+    arrived = [lax.ppermute(value, ("fsdp", "ctx"), final_pairs(flip)) for flip, value in enumerate(blocks)]
+
+    def last_body(first, second, out):
+        out[...] = (first[...].astype(F32) + second[...].astype(F32)).astype(BF16)
+
+    return call(last_body, block, limit=SMALL_LIMIT)(*arrived), give
 
 
 def turned(pieces):
@@ -431,7 +446,7 @@
         for mask, piece in ((0, a), (1, b), (2 ^ side, c), (3 ^ side, d)):
             out[:, block_at(me ^ mask, part)] = piece[...].T
 
-    return call(body, jax.ShapeDtypeStruct((depth, 4 * part), pieces[0].dtype), us=1.0)(*pieces)
+    return call(body, jax.ShapeDtypeStruct((depth, 4 * part), pieces[0].dtype), us=0.4, limit=SMALL_LIMIT)(*pieces)
 
 
 def weight_gradient(rows, values, after=()):
@@ -469,28 +484,27 @@
     there = (far, flipped(far, "fsdp", 1))
     grad_own, grad_near, grad_far = column_blocks(grad_mixed)
     grad_here = (grad_own, flipped(grad_near, "ctx", 1))
-    grad_far = fetched(later(grad_far, far))
+    grad_far = fetched(later(grad_far, feats_here[2]))
     grad_there = (grad_far, flipped(grad_far, "fsdp", 1))
     feats_there, _ = channel_sums(there, 1, weights)
     grads_here, _ = channel_sums(grad_here, 0, out_weight[None])
-    grads_there, _ = channel_sums(grad_there, 1, out_weight[None])
     *saved, gated = filter_forward(by_token(feats_here, feats_there), sum_of_three, tables, length, width)
+    grads_there, _ = channel_sums(grad_there, 1, out_weight[None], (gated,))
     gated = gated[None]
     gated_far = flipped(gated, "ctx", 2)
     all_gated = all_channels(gated, gated_far)
     whole_gated, keeps, gives = output_pieces(all_gated, out_weight[None])
     givens = exchange(gives)
-    mixed, mixed_last = block_sums(keeps, givens)
+    mixed_halves = keeps, givens
     grads = filter_backward(by_token(grads_here, grads_there), sum_of_three, tables, saved, length, width)
     grads = later(grads, gated_far)
     grad_out, mark = weight_gradient(turned(grad_here + grad_there), whole_gated)
     token_rows = turned(here + there)
     grads_far = later(flipped(grads, "ctx", 2), *givens, keeps[0], token_rows, mark)
     whole_grads, keeps, gives = output_pieces(all_channels(grads, grads_far), weights)
-    grad_in, mark = weight_gradient(token_rows, whole_grads, (mixed_last,))
-    grad_tokens, last = block_sums(keeps, exchange(gives), (mark,))
-    mixed = settled(to_placement(later(mixed, last)))
-    grad_tokens = settled(to_placement(grad_tokens))
+    mixed, mixed_give = block_sums(*mixed_halves, (), gives[:1])
+    grad_in, mark = weight_gradient(token_rows, whole_grads, (mixed_give,))
+    grad_tokens, _ = block_sums(keeps, exchange(gives), (mark,))
     return mixed, grad_tokens, grad_in, grad_out[0]
 
 

time: 106 us -> 103 us (0.972)
  the two profiles are of different devices: /device:TPU:4 before, /device:TPU:1 now
where the time goes in v5:
time: 103 us
  starting transfers between devices  50.2 us (49%)
  Pallas kernels  26.1 us (25%)
  waiting for transfers between devices  20.8 us (20%)
  local copies, waits for them, and re-layouts  3.71 us (4%)
    ppermute x32, starting transfers between devices, flipped(): lax.ppermute(value, axis, [(source, source ^ mask) for source in range(co...  31.5 us
    ppermute x4, starting transfers between devices, block_sums(): lax.ppermute(value, ('fsdp', 'ctx'), final_pairs(flip))  14.8 us
    ppermute x32, waiting for transfers between devices, flipped(): lax.ppermute(value, axis, [(source, source ^ mask) for source in range(co...  13.7 us
    pallas_call x2, Pallas kernels, weight_gradient(): pl.pallas_call(body, out_shape=(jax.ShapeDtypeStruct((groups, depth, chan...  6.58 us
    ppermute x4, waiting for transfers between devices, block_sums(): lax.ppermute(value, ('fsdp', 'ctx'), final_pairs(flip))  4.55 us
    ppermute x2, starting transfers between devices, fetched(): return lax.ppermute(block, ('fsdp', 'ctx'), pairs)  3.99 us
    pallas_call x4, Pallas kernels, project(): call(body, (jax.ShapeDtypeStruct((groups, length, width), F32), sums, sum...  3.77 us
    unnamed x20, local copies, waits for them, and re-layouts  2.95 us
  transfers between devices with their start and end apart: 38, of which 13 were waited for; matrix products, arithmetic and copies ran while one was open for 1% of the time, Pallas kernels for 24%

profile of v5, /device:TPU:1, one launch (start us, length us, event | category | flops | bytes accessed | tf_op | source)
XLA Modules:
  0.0 102.7 jit_solution(7303565026610705700)
XLA Ops:
  1.9 2.7 %collective-permute-start.2 = (bf16[128,1024]{1,0:T(8,128)(2,1)S(1)}, bf16[128,1024]{1,0:T(8,128)(2,1)S(1)}, u32[]{:S(2)}, u32[]{:S(2)}) collective-permute-start(bf16[128,1024]{1,0:T(8,128)(2,1)S(1)} %get-tuple-element.68), channel_id=1, source_target_pairs={{0,2},{1,3},{2,0},{3,1},{4,7},{5,6},{6,5},{7,4},{8,10},{9,11},{10,... | collective-permute-start | bytes 786440 | tf_op jit(solution)/shard_map/ppermute | solution.py:274
  4.6 2.2 %shard_map.112 = (bf16[3,1024,512]{2,1,0:T(8,128)(2,1)S(1)}, bf16[1024,512]{1,0:T(8,128)(2,1)S(1)}) custom-call(bf16[3,1024,512]{2,1,0:T(8,128)(2,1)} %bitcast.16, bf16[1024,512]{1,0:T(8,128)(2,1)} %refs_1_.1, bf16[128,1024]{1,0:T(8,128)(2,1)S(1)} %get-tuple-element.64.refs_2_), custom_call_target="tpu_custom_call" | custom-call | flops 1495000064 | tf_op jit(solution)/shard_map/pallas_call | solution.py:242
  7.8 1.3 %shard_map.113 = (f32[3,256,128]{2,1,0:T(8,128)S(1)}, bf16[3,256,128]{2,1,0:T(8,128)(2,1)S(1)}, bf16[3,256,128]{2,1,0:T(8,128)(2,1)S(1)}, bf16[3,256,128]{2,1,0:T(8,128)(2,1)S(1)}) custom-call(bf16[128,1024]{1,0:T(8,128)(2,1)S(1)} %get-tuple-element.63.first.a, bf16[128,1024]{1,0:T(8,128)(2,1)S(1)} %collective-permute-done.second.b, ...), custom_call_target="tpu_custom_call" | custom-call | flops 1552499968 | tf_op jit(solution)/shard_map/pallas_call | solution.py:297
  11.2 1.4 %collective-permute-start.4 = (bf16[128,1024]{1,0:T(8,128)(2,1)S(1)}, bf16[128,1024]{1,0:T(8,128)(2,1)S(1)}, u32[]{:S(2)}, u32[]{:S(2)}) collective-permute-start(bf16[128,1024]{1,0:T(8,128)(2,1)S(1)} %shard_map.115.first.c), channel_id=1, source_target_pairs={{0,4},{4,0},{8,12},{12,8},{16,20},{20,16},{24,28},{28,24},{1,5},{5... | collective-permute-start | bytes 786440 | tf_op jit(solution)/shard_map/ppermute | solution.py:41
  13.9 4.5 %collective-permute-done.4.second.d = bf16[128,1024]{1,0:T(8,128)(2,1)S(1)} collective-permute-done((bf16[128,1024]{1,0:T(8,128)(2,1)S(1)}, bf16[128,1024]{1,0:T(8,128)(2,1)S(1)}, u32[]{:S(2)}, u32[]{:S(2)}) %collective-permute-start.4) | collective-permute-done | bytes 262176 | tf_op jit(solution)/shard_map/ppermute | solution.py:41
  18.4 1.3 %shard_map.116 = (f32[3,256,128]{2,1,0:T(8,128)S(1)}, bf16[3,256,128]{2,1,0:T(8,128)(2,1)S(1)}, bf16[3,256,128]{2,1,0:T(8,128)(2,1)S(1)}, bf16[3,256,128]{2,1,0:T(8,128)(2,1)S(1)}) custom-call(bf16[128,1024]{1,0:T(8,128)(2,1)S(1)} %shard_map.115.first.c, bf16[128,1024]{1,0:T(8,128)(2,1)S(1)} %collective-permute-done.4.second.d, ...), custom_call_target="tpu_custom_call" | custom-call | flops 1552499968 | tf_op jit(solution)/shard_map/pallas_call | solution.py:297
  20.5 1.5 %collective-permute-start.5 = (bf16[3,256,128]{2,1,0:T(8,128)(2,1)S(1)}, bf16[3,256,128]{2,1,0:T(8,128)(2,1)S(1)}, u32[]{:S(2)}, u32[]{:S(2)}) collective-permute-start(bf16[3,256,128]{2,1,0:T(8,128)(2,1)S(1)} %get-tuple-element.72), channel_id=1, source_target_pairs={{0,1},{1,0},{2,3},{3,2},{4,5},{5,4},{6,7},{7,6},{8,9},{9,8},{10,11... | collective-permute-start | bytes 589832 | tf_op jit(solution)/shard_map/ppermute | solution.py:41
  29.5 2.1 %collective-permute-done.18.first.c = bf16[128,1024]{1,0:T(8,128)(2,1)S(1)} collective-permute-done((bf16[128,1024]{1,0:T(8,128)(2,1)S(1)}, bf16[128,1024]{1,0:T(8,128)(2,1)S(1)}, u32[]{:S(2)}, u32[]{:S(2)}) %collective-permute-start.18) | collective-permute-done | bytes 262176 | tf_op jit(solution)/shard_map/ppermute | solution.py:274
  31.6 2.1 %collective-permute-start.19 = (bf16[128,1024]{1,0:T(8,128)(2,1)S(1)}, bf16[128,1024]{1,0:T(8,128)(2,1)S(1)}, u32[]{:S(2)}, u32[]{:S(2)}) collective-permute-start(bf16[128,1024]{1,0:T(8,128)(2,1)S(1)} %collective-permute-done.18.first.c), channel_id=1, source_target_pairs={{0,4},{4,0},{8,12},{12,8},{16,20},{20,16},{24,28},{28,24},{1,5},{5... | collective-permute-start | bytes 786440 | tf_op jit(solution)/shard_map/ppermute | solution.py:41
  33.7 2.1 %collective-permute-done.6.refs_2_ = bf16[3,256,128]{2,1,0:T(8,128)(2,1)S(1)} collective-permute-done((bf16[3,256,128]{2,1,0:T(8,128)(2,1)S(1)}, bf16[3,256,128]{2,1,0:T(8,128)(2,1)S(1)}, u32[]{:S(2)}, u32[]{:S(2)}) %collective-permute-start.6) | collective-permute-done | bytes 196640 | tf_op jit(solution)/shard_map/ppermute | solution.py:41
  35.9 2.1 %shard_map.118 = (f32[512,128]{1,0:T(8,128)S(1)}, f32[512,128]{1,0:T(8,128)S(1)}, f32[512,128]{1,0:T(8,128)S(1)}, f32[512,128]{1,0:T(8,128)S(1)}, bf16[512,128]{1,0:T(8,128)(2,1)S(1)}) custom-call(f32[3,256,128]{2,1,0:T(8,128)S(1)} %copy-done.7, bf16[3,256,128]{2,1,0:T(8,128)(2,1)S(1)} %collective-permute-done.1.refs_1_, ...), custom_call_target="tpu_custom_call" | custom-call | flops 3680000000 | tf_op jit(solution)/shard_map/pallas_call | solution.py:184
  38.0 1.7 %collective-permute-done.19.second.d = bf16[128,1024]{1,0:T(8,128)(2,1)S(1)} collective-permute-done((bf16[128,1024]{1,0:T(8,128)(2,1)S(1)}, bf16[128,1024]{1,0:T(8,128)(2,1)S(1)}, u32[]{:S(2)}, u32[]{:S(2)}) %collective-permute-start.19) | collective-permute-done | bytes 262176 | tf_op jit(solution)/shard_map/ppermute | solution.py:41
  40.3 1.4 %collective-permute-start.20 = (bf16[1,256,128]{2,1,0:T(8,128)(2,1)S(1)}, bf16[1,256,128]{2,1,0:T(8,128)(2,1)S(1)}, u32[]{:S(2)}, u32[]{:S(2)}) collective-permute-start(bf16[1,256,128]{2,1,0:T(8,128)(2,1)S(1)} %get-tuple-element.92), channel_id=1, source_target_pairs={{0,1},{1,0},{2,3},{3,2},{4,5},{5,4},{6,7},{7,6},{8,9},{9,8},{10,11... | collective-permute-start | bytes 196616 | tf_op jit(solution)/shard_map/ppermute | solution.py:41
  44.3 1.3 %collective-permute-start.21 = (bf16[1,256,128]{2,1,0:T(8,128)(2,1)S(1)}, bf16[1,256,128]{2,1,0:T(8,128)(2,1)S(1)}, u32[]{:S(2)}, u32[]{:S(2)}) collective-permute-start(bf16[1,256,128]{2,1,0:T(8,128)(2,1)S(1)} %shard_map.126), channel_id=1, source_target_pairs={{0,2},{1,3},{2,0},{3,1},{4,6},{5,7},{6,4},{7,5},{8,10},{9,11},{10,... | collective-permute-start | bytes 196616 | tf_op jit(solution)/shard_map/ppermute | solution.py:41
  46.3 2.1 %collective-permute-start.11 = (bf16[1,512,128]{2,1,0:T(8,128)(2,1)S(1)}, bf16[1,512,128]{2,1,0:T(8,128)(2,1)S(1)}, u32[]{:S(2)}, u32[]{:S(2)}) collective-permute-start(bf16[1,512,128]{2,1,0:T(8,128)(2,1)S(1)} %collective-permute-done.9.far.refs_1_), channel_id=1, source_target_pairs={{0,1},{1,0},{2,3},{3,2},{4,5},{5,4},{6,7},{7,6},{8,9},{9,8},{10,11... | collective-permute-start | bytes 393224 | tf_op jit(solution)/shard_map/ppermute | solution.py:41
  49.1 2.1 %shard_map.128.refs_0_ = bf16[3,512,128]{2,1,0:T(8,128)(2,1)S(1)} custom-call(f32[1,256,128]{2,1,0:T(8,128)S(1)} %get-tuple-element.88.refs_0_, bf16[1,256,128]{2,1,0:T(8,128)(2,1)S(1)} %collective-permute-done.17.refs_1_, bf16[1,256,128]{2,1,0:T(8,128)(2,1)S(1)} %collective-permute-done.21.refs_2_, f32[1,256,128]{2,1,0:T(8,128)S(1)} %get-tuple-element.93.refs_3_, ...), custom_call_target="tpu_custom_call" | custom-call | flops 2415000064 | tf_op jit(solution)/shard_map/pallas_call | solution.py:203
  53.2 1.5 %collective-permute-start.12 = (bf16[512,256]{1,0:T(8,128)(2,1)S(1)}, bf16[512,256]{1,0:T(8,128)(2,1)S(1)}, u32[]{:S(2)}, u32[]{:S(2)}) collective-permute-start(bf16[512,256]{1,0:T(8,128)(2,1)S(1)} %get-tuple-element.79), channel_id=1, source_target_pairs={{0,4},{4,0},{8,12},{12,8},{16,20},{20,16},{24,28},{28,24},{1,5},{5... | collective-permute-start | bytes 786440 | tf_op jit(solution)/shard_map/ppermute | solution.py:41
  54.8 1.3 %collective-permute-start.13 = (bf16[256,512]{1,0:T(8,128)(2,1)S(1)}, bf16[256,512]{1,0:T(8,128)(2,1)S(1)}, u32[]{:S(2)}, u32[]{:S(2)}) collective-permute-start(bf16[256,512]{1,0:T(8,128)(2,1)S(1)} %get-tuple-element.81), channel_id=1, source_target_pairs={{0,8},{4,12},{8,0},{12,4},{16,24},{20,28},{24,16},{28,20},{1,9},{5... | collective-permute-start | bytes 786440 | tf_op jit(solution)/shard_map/ppermute | solution.py:41
  56.8 2.2 %collective-permute-start.26 = (bf16[3,512,128]{2,1,0:T(8,128)(2,1)S(1)}, bf16[3,512,128]{2,1,0:T(8,128)(2,1)S(1)}, u32[]{:S(2)}, u32[]{:S(2)}) collective-permute-start(bf16[3,512,128]{2,1,0:T(8,128)(2,1)S(1)} %shard_map.129.own), channel_id=1, source_target_pairs={{0,1},{1,0},{2,3},{3,2},{4,5},{5,4},{6,7},{7,6},{8,9},{9,8},{10,11... | collective-permute-start | bytes 1179656 | tf_op jit(solution)/shard_map/ppermute | solution.py:41
  59.5 1.9 %shard_map.132 = (f32[1,1024,512]{2,1,0:T(8,128)}, f32[8,128]{1,0:T(8,128)S(1)}) custom-call(bf16[1024,512]{1,0:T(8,128)(2,1)S(1)} %shard_map.131.rows, bf16[1,512,512]{2,1,0:T(8,128)(2,1)S(1)} %get-tuple-element.77.whole.values), custom_call_target="tpu_custom_call" | custom-call | flops 1724999936 | tf_op jit(solution)/shard_map/pallas_call | solution.py:462
  61.4 2.1 %collective-permute-start.27 = (bf16[3,512,128]{2,1,0:T(8,128)(2,1)S(1)}, bf16[3,512,128]{2,1,0:T(8,128)(2,1)S(1)}, u32[]{:S(2)}, u32[]{:S(2)}) collective-permute-start(bf16[3,512,128]{2,1,0:T(8,128)(2,1)S(1)} %shard_map.133.far), channel_id=1, source_target_pairs={{0,1},{1,0},{2,3},{3,2},{4,5},{5,4},{6,7},{7,6},{8,9},{9,8},{10,11... | collective-permute-start | bytes 1179656 | tf_op jit(solution)/shard_map/ppermute | solution.py:41
  63.6 1.4 %collective-permute-start.14 = (bf16[256,256]{1,0:T(8,128)(2,1)S(1)}, bf16[256,256]{1,0:T(8,128)(2,1)S(1)}, u32[]{:S(2)}, u32[]{:S(2)}) collective-permute-start(bf16[256,256]{1,0:T(8,128)(2,1)S(1)} %get-tuple-element.83), channel_id=1, source_target_pairs={{0,8},{4,12},{8,0},{12,4},{16,24},{20,28},{24,16},{28,20},{1,9},{5... | collective-permute-start | bytes 393224 | tf_op jit(solution)/shard_map/ppermute | solution.py:41
  65.8 1.7 %shard_map.134 = (bf16[3,512,512]{2,1,0:T(8,128)(2,1)S(1)}, bf16[512,256]{1,0:T(8,128)(2,1)S(1)}, bf16[256,512]{1,0:T(8,128)(2,1)S(1)}) custom-call(bf16[3,512,128]{2,1,0:T(8,128)(2,1)S(1)} %shard_map.129.own, bf16[3,512,128]{2,1,0:T(8,128)(2,1)S(1)} %shard_map.133.far, bf16[3,512,128]{2,1,0:T(8,128)(2,1)S(1)} %collective-permute-done.26.near, ...), custom_call_target="tpu_custom_call" | custom-call | flops 2070000000 | tf_op jit(solution)/shard_map/pallas_call | solution.py:362
  69.9 4.7 %shard_map.139 = (f32[3,1024,512]{2,1,0:T(8,128)}, f32[8,128]{1,0:T(8,128)S(1)}) custom-call(bf16[1024,512]{1,0:T(8,128)(2,1)S(1)} %shard_map.130.refs_4_.rows, bf16[3,512,512]{2,1,0:T(8,128)(2,1)S(1)} %get-tuple-element.107.whole.values, bf16[128,512]{1,0:T(8,128)(2,1)S(1)} %get-tuple-element.104.refs_0_), custom_call_target="tpu_custom_call" | custom-call | flops 5175000064 | tf_op jit(solution)/shard_map/pallas_call | solution.py:462
  74.6 1.4 %shard_map.138 = (bf16[512,256]{1,0:T(8,128)(2,1)S(1)}, bf16[256,512]{1,0:T(8,128)(2,1)S(1)}) custom-call(bf16[3,512,512]{2,1,0:T(8,128)(2,1)S(1)} %get-tuple-element.107.whole.values, bf16[3,1024,512]{2,1,0:T(8,128)(2,1)S(1)} %copy-done.5), custom_call_target="tpu_custom_call" | custom-call | flops 1380000000 | tf_op jit(solution)/shard_map/pallas_call | solution.py:368
  78.6 1.4 %collective-permute-done.33.given_z = bf16[256,256]{1,0:T(8,128)(2,1)S(1)} collective-permute-done((bf16[256,256]{1,0:T(8,128)(2,1)S(1)}, bf16[256,256]{1,0:T(8,128)(2,1)S(1)}, u32[]{:S(2)}, u32[]{:S(2)}) %collective-permute-start.33) | collective-permute-done | bytes 131104 | tf_op jit(solution)/shard_map/ppermute | solution.py:41
  81.9 5.3 %collective-permute-start.29 = (bf16[128,512]{1,0:T(8,128)(2,1)S(1)}, bf16[128,512]{1,0:T(8,128)(2,1)S(1)}, u32[]{:S(2)}, u32[]{:S(2)}) collective-permute-start(bf16[128,512]{1,0:T(8,128)(2,1)S(1)} %get-tuple-element.105), channel_id=1, source_target_pairs={{0,0},{1,8},{2,18},{3,26},{4,4},{5,12},{6,22},{7,30},{8,1},{9,9},{... | collective-permute-start | bytes 393224 | tf_op jit(solution)/shard_map/ppermute | solution.py:432
  87.1 3.9 %collective-permute-start.30 = (bf16[128,512]{1,0:T(8,128)(2,1)S(1)}, bf16[128,512]{1,0:T(8,128)(2,1)S(1)}, u32[]{:S(2)}, u32[]{:S(2)}) collective-permute-start(bf16[128,512]{1,0:T(8,128)(2,1)S(1)} %get-tuple-element.106), channel_id=1, source_target_pairs={{0,16},{1,24},{2,2},{3,10},{4,20},{5,28},{6,6},{7,14},{8,17},{9,25... | collective-permute-start | bytes 393224 | tf_op jit(solution)/shard_map/ppermute | solution.py:432
  91.2 2.7 %collective-permute-start.36 = (bf16[128,512]{1,0:T(8,128)(2,1)S(1)}, bf16[128,512]{1,0:T(8,128)(2,1)S(1)}, u32[]{:S(2)}, u32[]{:S(2)}) collective-permute-start(bf16[128,512]{1,0:T(8,128)(2,1)S(1)} %get-tuple-element.118), channel_id=1, source_target_pairs={{0,0},{1,8},{2,18},{3,26},{4,4},{5,12},{6,22},{7,30},{8,1},{9,9},{... | collective-permute-start | bytes 393224 | tf_op jit(solution)/shard_map/ppermute | solution.py:432
  93.9 2.8 %collective-permute-start.37 = (bf16[128,512]{1,0:T(8,128)(2,1)S(1)}, bf16[128,512]{1,0:T(8,128)(2,1)S(1)}, u32[]{:S(2)}, u32[]{:S(2)}) collective-permute-start(bf16[128,512]{1,0:T(8,128)(2,1)S(1)} %get-tuple-element.119), channel_id=1, source_target_pairs={{0,16},{1,24},{2,2},{3,10},{4,20},{5,28},{6,6},{7,14},{8,17},{9,25... | collective-permute-start | bytes 393224 | tf_op jit(solution)/shard_map/ppermute | solution.py:432
  97.5 1.6 %collective-permute-done.36.first = bf16[128,512]{1,0:T(8,128)(2,1)S(1)} collective-permute-done((bf16[128,512]{1,0:T(8,128)(2,1)S(1)}, bf16[128,512]{1,0:T(8,128)(2,1)S(1)}, u32[]{:S(2)}, u32[]{:S(2)}) %collective-permute-start.36) | collective-permute-done | bytes 131104 | tf_op jit(solution)/shard_map/ppermute | solution.py:432
  99.0 3.0 %collective-permute-done.37.second = bf16[128,512]{1,0:T(8,128)(2,1)S(1)} collective-permute-done((bf16[128,512]{1,0:T(8,128)(2,1)S(1)}, bf16[128,512]{1,0:T(8,128)(2,1)S(1)}, u32[]{:S(2)}, u32[]{:S(2)}) %collective-permute-start.37) | collective-permute-done | bytes 131104 | tf_op jit(solution)/shard_map/ppermute | solution.py:432
  (100 shorter events, 30.7 us)
Async XLA Ops:
  1.8 6.0 %collective-permute-start = (bf16[128,1024]{1,0:T(8,128)(2,1)S(1)}, bf16[128,1024]{1,0:T(8,128)(2,1)S(1)}, u32[]{:S(2)}, u32[]{:S(2)}) collective-permute-start(bf16[128,1024]{1,0:T(8,128)(2,1)S(1)} %get-tuple-element.64.refs_2_), channel_id=1, source_target_pairs={{0,1},{1,0},{2,3},{3,2},{4,5},{5,4},{6,7},{7,6},{8,9},{9,8},{10,11... | collective-permute-start | bytes 786440 | tf_op jit(solution)/shard_map/ppermute | solution.py:41
  1.9 9.3 %collective-permute-start.2 = (bf16[128,1024]{1,0:T(8,128)(2,1)S(1)}, bf16[128,1024]{1,0:T(8,128)(2,1)S(1)}, u32[]{:S(2)}, u32[]{:S(2)}) collective-permute-start(bf16[128,1024]{1,0:T(8,128)(2,1)S(1)} %get-tuple-element.68), channel_id=1, source_target_pairs={{0,2},{1,3},{2,0},{3,1},{4,7},{5,6},{6,5},{7,4},{8,10},{9,11},{10,... | collective-permute-start | bytes 786440 | tf_op jit(solution)/shard_map/ppermute | solution.py:274
  11.2 7.2 %collective-permute-start.4 = (bf16[128,1024]{1,0:T(8,128)(2,1)S(1)}, bf16[128,1024]{1,0:T(8,128)(2,1)S(1)}, u32[]{:S(2)}, u32[]{:S(2)}) collective-permute-start(bf16[128,1024]{1,0:T(8,128)(2,1)S(1)} %shard_map.115.first.c), channel_id=1, source_target_pairs={{0,4},{4,0},{8,12},{12,8},{16,20},{20,16},{24,28},{28,24},{1,5},{5... | collective-permute-start | bytes 786440 | tf_op jit(solution)/shard_map/ppermute | solution.py:41
  12.6 11.2 %collective-permute-start.8 = (bf16[3,256,128]{2,1,0:T(8,128)(2,1)S(1)}, bf16[3,256,128]{2,1,0:T(8,128)(2,1)S(1)}, u32[]{:S(2)}, u32[]{:S(2)}) collective-permute-start(bf16[3,256,128]{2,1,0:T(8,128)(2,1)S(1)} %shard_map.114.refs_1_), channel_id=1, source_target_pairs={{0,2},{1,3},{2,0},{3,1},{4,6},{5,7},{6,4},{7,5},{8,10},{9,11},{10,... | collective-permute-start | bytes 589832 | tf_op jit(solution)/shard_map/ppermute | solution.py:41
  20.5 4.9 %collective-permute-start.5 = (bf16[3,256,128]{2,1,0:T(8,128)(2,1)S(1)}, bf16[3,256,128]{2,1,0:T(8,128)(2,1)S(1)}, u32[]{:S(2)}, u32[]{:S(2)}) collective-permute-start(bf16[3,256,128]{2,1,0:T(8,128)(2,1)S(1)} %get-tuple-element.72), channel_id=1, source_target_pairs={{0,1},{1,0},{2,3},{3,2},{4,5},{5,4},{6,7},{7,6},{8,9},{9,8},{10,11... | collective-permute-start | bytes 589832 | tf_op jit(solution)/shard_map/ppermute | solution.py:41
  23.2 10.5 %collective-permute-start.1 = (bf16[3,256,128]{2,1,0:T(8,128)(2,1)S(1)}, bf16[3,256,128]{2,1,0:T(8,128)(2,1)S(1)}, u32[]{:S(2)}, u32[]{:S(2)}) collective-permute-start(bf16[3,256,128]{2,1,0:T(8,128)(2,1)S(1)} %get-tuple-element.67), channel_id=1, source_target_pairs={{0,1},{1,0},{2,3},{3,2},{4,5},{5,4},{6,7},{7,6},{8,9},{9,8},{10,11... | collective-permute-start | bytes 589832 | tf_op jit(solution)/shard_map/ppermute | solution.py:41
  23.8 7.9 %collective-permute-start.18 = (bf16[128,1024]{1,0:T(8,128)(2,1)S(1)}, bf16[128,1024]{1,0:T(8,128)(2,1)S(1)}, u32[]{:S(2)}, u32[]{:S(2)}) collective-permute-start(bf16[128,1024]{1,0:T(8,128)(2,1)S(1)} %shard_map.124), channel_id=1, source_target_pairs={{0,2},{1,3},{2,0},{3,1},{4,7},{5,6},{6,5},{7,4},{8,10},{9,11},{10,... | collective-permute-start | bytes 786440 | tf_op jit(solution)/shard_map/ppermute | solution.py:274
  25.1 8.7 %collective-permute-start.7 = (bf16[3,256,128]{2,1,0:T(8,128)(2,1)S(1)}, bf16[3,256,128]{2,1,0:T(8,128)(2,1)S(1)}, u32[]{:S(2)}, u32[]{:S(2)}) collective-permute-start(bf16[3,256,128]{2,1,0:T(8,128)(2,1)S(1)} %get-tuple-element.74), channel_id=1, source_target_pairs={{0,1},{1,0},{2,3},{3,2},{4,5},{5,4},{6,7},{7,6},{8,9},{9,8},{10,11... | collective-permute-start | bytes 589832 | tf_op jit(solution)/shard_map/ppermute | solution.py:41
  25.5 10.4 %collective-permute-start.6 = (bf16[3,256,128]{2,1,0:T(8,128)(2,1)S(1)}, bf16[3,256,128]{2,1,0:T(8,128)(2,1)S(1)}, u32[]{:S(2)}, u32[]{:S(2)}) collective-permute-start(bf16[3,256,128]{2,1,0:T(8,128)(2,1)S(1)} %shard_map.117), channel_id=1, source_target_pairs={{0,2},{1,3},{2,0},{3,1},{4,6},{5,7},{6,4},{7,5},{8,10},{9,11},{10,... | collective-permute-start | bytes 589832 | tf_op jit(solution)/shard_map/ppermute | solution.py:41
  29.0 13.9 %collective-permute-start.23 = (bf16[1,256,128]{2,1,0:T(8,128)(2,1)S(1)}, bf16[1,256,128]{2,1,0:T(8,128)(2,1)S(1)}, u32[]{:S(2)}, u32[]{:S(2)}) collective-permute-start(bf16[1,256,128]{2,1,0:T(8,128)(2,1)S(1)} %get-tuple-element.96), channel_id=1, source_target_pairs={{0,1},{1,0},{2,3},{3,2},{4,5},{5,4},{6,7},{7,6},{8,9},{9,8},{10,11... | collective-permute-start | bytes 196616 | tf_op jit(solution)/shard_map/ppermute | solution.py:41
  31.6 8.0 %collective-permute-start.19 = (bf16[128,1024]{1,0:T(8,128)(2,1)S(1)}, bf16[128,1024]{1,0:T(8,128)(2,1)S(1)}, u32[]{:S(2)}, u32[]{:S(2)}) collective-permute-start(bf16[128,1024]{1,0:T(8,128)(2,1)S(1)} %collective-permute-done.18.first.c), channel_id=1, source_target_pairs={{0,4},{4,0},{8,12},{12,8},{16,20},{20,16},{24,28},{28,24},{1,5},{5... | collective-permute-start | bytes 786440 | tf_op jit(solution)/shard_map/ppermute | solution.py:41
  41.7 4.6 %collective-permute-start.9 = (bf16[1,512,128]{2,1,0:T(8,128)(2,1)S(1)}, bf16[1,512,128]{2,1,0:T(8,128)(2,1)S(1)}, u32[]{:S(2)}, u32[]{:S(2)}) collective-permute-start(bf16[1,512,128]{2,1,0:T(8,128)(2,1)S(1)} %bitcast.9), channel_id=1, source_target_pairs={{0,2},{1,3},{2,0},{3,1},{4,6},{5,7},{6,4},{7,5},{8,10},{9,11},{10,... | collective-permute-start | bytes 393224 | tf_op jit(solution)/shard_map/ppermute | solution.py:41
  43.0 5.5 %collective-permute-start.24 = (bf16[1,256,128]{2,1,0:T(8,128)(2,1)S(1)}, bf16[1,256,128]{2,1,0:T(8,128)(2,1)S(1)}, u32[]{:S(2)}, u32[]{:S(2)}) collective-permute-start(bf16[1,256,128]{2,1,0:T(8,128)(2,1)S(1)} %shard_map.127), channel_id=1, source_target_pairs={{0,2},{1,3},{2,0},{3,1},{4,6},{5,7},{6,4},{7,5},{8,10},{9,11},{10,... | collective-permute-start | bytes 196616 | tf_op jit(solution)/shard_map/ppermute | solution.py:41
  43.3 5.2 %collective-permute-start.22 = (bf16[1,256,128]{2,1,0:T(8,128)(2,1)S(1)}, bf16[1,256,128]{2,1,0:T(8,128)(2,1)S(1)}, u32[]{:S(2)}, u32[]{:S(2)}) collective-permute-start(bf16[1,256,128]{2,1,0:T(8,128)(2,1)S(1)} %get-tuple-element.94), channel_id=1, source_target_pairs={{0,1},{1,0},{2,3},{3,2},{4,5},{5,4},{6,7},{7,6},{8,9},{9,8},{10,11... | collective-permute-start | bytes 196616 | tf_op jit(solution)/shard_map/ppermute | solution.py:41
  44.3 4.9 %collective-permute-start.21 = (bf16[1,256,128]{2,1,0:T(8,128)(2,1)S(1)}, bf16[1,256,128]{2,1,0:T(8,128)(2,1)S(1)}, u32[]{:S(2)}, u32[]{:S(2)}) collective-permute-start(bf16[1,256,128]{2,1,0:T(8,128)(2,1)S(1)} %shard_map.126), channel_id=1, source_target_pairs={{0,2},{1,3},{2,0},{3,1},{4,6},{5,7},{6,4},{7,5},{8,10},{9,11},{10,... | collective-permute-start | bytes 196616 | tf_op jit(solution)/shard_map/ppermute | solution.py:41
  45.6 7.0 %collective-permute-start.10 = (bf16[1,512,128]{2,1,0:T(8,128)(2,1)S(1)}, bf16[1,512,128]{2,1,0:T(8,128)(2,1)S(1)}, u32[]{:S(2)}, u32[]{:S(2)}) collective-permute-start(bf16[1,512,128]{2,1,0:T(8,128)(2,1)S(1)} %bitcast.10), channel_id=1, source_target_pairs={{0,1},{1,0},{2,3},{3,2},{4,5},{5,4},{6,7},{7,6},{8,9},{9,8},{10,11... | collective-permute-start | bytes 393224 | tf_op jit(solution)/shard_map/ppermute | solution.py:41
  46.3 6.2 %collective-permute-start.11 = (bf16[1,512,128]{2,1,0:T(8,128)(2,1)S(1)}, bf16[1,512,128]{2,1,0:T(8,128)(2,1)S(1)}, u32[]{:S(2)}, u32[]{:S(2)}) collective-permute-start(bf16[1,512,128]{2,1,0:T(8,128)(2,1)S(1)} %collective-permute-done.9.far.refs_1_), channel_id=1, source_target_pairs={{0,1},{1,0},{2,3},{3,2},{4,5},{5,4},{6,7},{7,6},{8,9},{9,8},{10,11... | collective-permute-start | bytes 393224 | tf_op jit(solution)/shard_map/ppermute | solution.py:41
  51.3 10.1 %collective-permute-start.25 = (bf16[3,512,128]{2,1,0:T(8,128)(2,1)S(1)}, bf16[3,512,128]{2,1,0:T(8,128)(2,1)S(1)}, u32[]{:S(2)}, u32[]{:S(2)}) collective-permute-start(bf16[3,512,128]{2,1,0:T(8,128)(2,1)S(1)} %shard_map.129.own), channel_id=1, source_target_pairs={{0,2},{1,3},{2,0},{3,1},{4,6},{5,7},{6,4},{7,5},{8,10},{9,11},{10,... | collective-permute-start | bytes 1179656 | tf_op jit(solution)/shard_map/ppermute | solution.py:41
  53.2 8.1 %collective-permute-start.12 = (bf16[512,256]{1,0:T(8,128)(2,1)S(1)}, bf16[512,256]{1,0:T(8,128)(2,1)S(1)}, u32[]{:S(2)}, u32[]{:S(2)}) collective-permute-start(bf16[512,256]{1,0:T(8,128)(2,1)S(1)} %get-tuple-element.79), channel_id=1, source_target_pairs={{0,4},{4,0},{8,12},{12,8},{16,20},{20,16},{24,28},{28,24},{1,5},{5... | collective-permute-start | bytes 786440 | tf_op jit(solution)/shard_map/ppermute | solution.py:41
  54.8 6.6 %collective-permute-start.13 = (bf16[256,512]{1,0:T(8,128)(2,1)S(1)}, bf16[256,512]{1,0:T(8,128)(2,1)S(1)}, u32[]{:S(2)}, u32[]{:S(2)}) collective-permute-start(bf16[256,512]{1,0:T(8,128)(2,1)S(1)} %get-tuple-element.81), channel_id=1, source_target_pairs={{0,8},{4,12},{8,0},{12,4},{16,24},{20,28},{24,16},{28,20},{1,9},{5... | collective-permute-start | bytes 786440 | tf_op jit(solution)/shard_map/ppermute | solution.py:41
  56.8 9.1 %collective-permute-start.26 = (bf16[3,512,128]{2,1,0:T(8,128)(2,1)S(1)}, bf16[3,512,128]{2,1,0:T(8,128)(2,1)S(1)}, u32[]{:S(2)}, u32[]{:S(2)}) collective-permute-start(bf16[3,512,128]{2,1,0:T(8,128)(2,1)S(1)} %shard_map.129.own), channel_id=1, source_target_pairs={{0,1},{1,0},{2,3},{3,2},{4,5},{5,4},{6,7},{7,6},{8,9},{9,8},{10,11... | collective-permute-start | bytes 1179656 | tf_op jit(solution)/shard_map/ppermute | solution.py:41
  61.4 4.4 %collective-permute-start.27 = (bf16[3,512,128]{2,1,0:T(8,128)(2,1)S(1)}, bf16[3,512,128]{2,1,0:T(8,128)(2,1)S(1)}, u32[]{:S(2)}, u32[]{:S(2)}) collective-permute-start(bf16[3,512,128]{2,1,0:T(8,128)(2,1)S(1)} %shard_map.133.far), channel_id=1, source_target_pairs={{0,1},{1,0},{2,3},{3,2},{4,5},{5,4},{6,7},{7,6},{8,9},{9,8},{10,11... | collective-permute-start | bytes 1179656 | tf_op jit(solution)/shard_map/ppermute | solution.py:41
  63.6 5.2 %collective-permute-start.14 = (bf16[256,256]{1,0:T(8,128)(2,1)S(1)}, bf16[256,256]{1,0:T(8,128)(2,1)S(1)}, u32[]{:S(2)}, u32[]{:S(2)}) collective-permute-start(bf16[256,256]{1,0:T(8,128)(2,1)S(1)} %get-tuple-element.83), channel_id=1, source_target_pairs={{0,8},{4,12},{8,0},{12,4},{16,24},{20,28},{24,16},{28,20},{1,9},{5... | collective-permute-start | bytes 393224 | tf_op jit(solution)/shard_map/ppermute | solution.py:41
  65.0 4.8 %collective-permute-start.15 = (bf16[256,256]{1,0:T(8,128)(2,1)S(1)}, bf16[256,256]{1,0:T(8,128)(2,1)S(1)}, u32[]{:S(2)}, u32[]{:S(2)}) collective-permute-start(bf16[256,256]{1,0:T(8,128)(2,1)S(1)} %get-tuple-element.85), channel_id=1, source_target_pairs={{0,4},{4,0},{8,12},{12,8},{16,20},{20,16},{24,28},{28,24},{1,5},{5... | collective-permute-start | bytes 393224 | tf_op jit(solution)/shard_map/ppermute | solution.py:41
  67.6 8.4 %collective-permute-start.32 = (bf16[256,512]{1,0:T(8,128)(2,1)S(1)}, bf16[256,512]{1,0:T(8,128)(2,1)S(1)}, u32[]{:S(2)}, u32[]{:S(2)}) collective-permute-start(bf16[256,512]{1,0:T(8,128)(2,1)S(1)} %get-tuple-element.110), channel_id=1, source_target_pairs={{0,8},{4,12},{8,0},{12,4},{16,24},{20,28},{24,16},{28,20},{1,9},{5... | collective-permute-start | bytes 786440 | tf_op jit(solution)/shard_map/ppermute | solution.py:41
  68.0 8.0 %collective-permute-start.31 = (bf16[512,256]{1,0:T(8,128)(2,1)S(1)}, bf16[512,256]{1,0:T(8,128)(2,1)S(1)}, u32[]{:S(2)}, u32[]{:S(2)}) collective-permute-start(bf16[512,256]{1,0:T(8,128)(2,1)S(1)} %get-tuple-element.102.refs_0_), channel_id=1, source_target_pairs={{0,4},{4,0},{8,12},{12,8},{16,20},{20,16},{24,28},{28,24},{1,5},{5... | collective-permute-start | bytes 786440 | tf_op jit(solution)/shard_map/ppermute | solution.py:41
  77.4 4.4 %collective-permute-start.28 = (bf16[128,512]{1,0:T(8,128)(2,1)S(1)}, bf16[128,512]{1,0:T(8,128)(2,1)S(1)}, u32[]{:S(2)}, u32[]{:S(2)}) collective-permute-start(bf16[128,512]{1,0:T(8,128)(2,1)S(1)} %get-tuple-element.104.refs_0_), channel_id=1, source_target_pairs={{0,2},{1,3},{2,0},{3,1},{4,6},{5,7},{6,4},{7,5},{8,10},{9,11},{10,... | collective-permute-start | bytes 393224 | tf_op jit(solution)/shard_map/ppermute | solution.py:41
  80.7 10.4 %collective-permute-start.35 = (bf16[128,512]{1,0:T(8,128)(2,1)S(1)}, bf16[128,512]{1,0:T(8,128)(2,1)S(1)}, u32[]{:S(2)}, u32[]{:S(2)}) collective-permute-start(bf16[128,512]{1,0:T(8,128)(2,1)S(1)} %get-tuple-element.117), channel_id=1, source_target_pairs={{0,2},{1,3},{2,0},{3,1},{4,6},{5,7},{6,4},{7,5},{8,10},{9,11},{10,... | collective-permute-start | bytes 393224 | tf_op jit(solution)/shard_map/ppermute | solution.py:41
  81.9 14.9 %collective-permute-start.29 = (bf16[128,512]{1,0:T(8,128)(2,1)S(1)}, bf16[128,512]{1,0:T(8,128)(2,1)S(1)}, u32[]{:S(2)}, u32[]{:S(2)}) collective-permute-start(bf16[128,512]{1,0:T(8,128)(2,1)S(1)} %get-tuple-element.105), channel_id=1, source_target_pairs={{0,0},{1,8},{2,18},{3,26},{4,4},{5,12},{6,22},{7,30},{8,1},{9,9},{... | collective-permute-start | bytes 393224 | tf_op jit(solution)/shard_map/ppermute | solution.py:432
  87.1 9.6 %collective-permute-start.30 = (bf16[128,512]{1,0:T(8,128)(2,1)S(1)}, bf16[128,512]{1,0:T(8,128)(2,1)S(1)}, u32[]{:S(2)}, u32[]{:S(2)}) collective-permute-start(bf16[128,512]{1,0:T(8,128)(2,1)S(1)} %get-tuple-element.106), channel_id=1, source_target_pairs={{0,16},{1,24},{2,2},{3,10},{4,20},{5,28},{6,6},{7,14},{8,17},{9,25... | collective-permute-start | bytes 393224 | tf_op jit(solution)/shard_map/ppermute | solution.py:432
  91.2 7.9 %collective-permute-start.36 = (bf16[128,512]{1,0:T(8,128)(2,1)S(1)}, bf16[128,512]{1,0:T(8,128)(2,1)S(1)}, u32[]{:S(2)}, u32[]{:S(2)}) collective-permute-start(bf16[128,512]{1,0:T(8,128)(2,1)S(1)} %get-tuple-element.118), channel_id=1, source_target_pairs={{0,0},{1,8},{2,18},{3,26},{4,4},{5,12},{6,22},{7,30},{8,1},{9,9},{... | collective-permute-start | bytes 393224 | tf_op jit(solution)/shard_map/ppermute | solution.py:432
  93.9 8.1 %collective-permute-start.37 = (bf16[128,512]{1,0:T(8,128)(2,1)S(1)}, bf16[128,512]{1,0:T(8,128)(2,1)S(1)}, u32[]{:S(2)}, u32[]{:S(2)}) collective-permute-start(bf16[128,512]{1,0:T(8,128)(2,1)S(1)} %get-tuple-element.119), channel_id=1, source_target_pairs={{0,16},{1,24},{2,2},{3,10},{4,20},{5,28},{6,6},{7,14},{8,17},{9,25... | collective-permute-start | bytes 393224 | tf_op jit(solution)/shard_map/ppermute | solution.py:432
  (16 other events, 96.0 us)

commit v6 on v5

--- a/solution.py
+++ b/solution.py
@@ -174,11 +174,12 @@
     return start, parts[0][j, start : start + size, :].astype(F32)
 
 
-def filter_forward(parts, kinds, tables, length, width):
+def filter_forward(parts, kinds, tables, length, width, after=()):
     count = len(parts)
+    inputs = count + len(tables)
 
     def body(*refs):
-        forward_body(refs[:count], kinds, *refs[count:])
+        forward_body(refs[:count], kinds, *refs[count:inputs], *refs[inputs + len(after) :])
 
     wide = jax.ShapeDtypeStruct((length, width), F32)
     return call(
@@ -189,8 +190,9 @@
             pltpu.VMEM((length, width), F32),
             pltpu.VMEM((length, width), F32),
         ],
-        us=3.2,
-    )(*parts, *tables)
+        in_specs=[VMEM] * inputs + [HBM] * len(after),
+        us=2.1,
+    )(*parts, *tables, *after)
 
 
 def filter_backward(parts, kinds, tables, saved, length, width, after=()):
@@ -434,7 +436,7 @@
     def last_body(first, second, out):
         out[...] = (first[...].astype(F32) + second[...].astype(F32)).astype(BF16)
 
-    return call(last_body, block, limit=SMALL_LIMIT)(*arrived), give
+    return call(last_body, block, limit=SMALL_LIMIT)(*arrived), blocks[0]
 
 
 def turned(pieces):
@@ -452,44 +454,50 @@
 def weight_gradient(rows, values, after=()):
     depth, length = rows.shape
     groups, _, channels = values.shape
-    tile = depth // 2
+    tile = 256
+    steps = [(j, i) for j in range(groups) for i in range(depth // tile)]
 
     def body(rows, values, *refs):
-        out, mark = refs[len(after) :]
-        out[0] = dot(rows[...], values[0], (1, 0))
+        out, mark, ready, written = refs[len(after) :]
+        copies = []
+        for n, (j, i) in enumerate(steps):
+            at = slice(i * tile, (i + 1) * tile)
+            ready[j, at, :] = dot(rows[at, :], values[j], (1, 0))
+            copies.append(pltpu.make_async_copy(ready.at[j, at, :], out.at[j, at, :], written.at[n]))
+            copies[-1].start()
         mark[...] = jnp.zeros_like(mark)
-
+        for copy in copies:
+            copy.wait()
+
+    gradient = jax.ShapeDtypeStruct((groups, depth, channels), F32)
     return pl.pallas_call(
         body,
-        out_shape=(jax.ShapeDtypeStruct((groups, depth, channels), F32), jax.ShapeDtypeStruct((8, LANES), F32)),
-        grid=(groups, depth // tile),
-        in_specs=[
-            pl.BlockSpec((tile, length), lambda j, i: (i, 0)),
-            pl.BlockSpec((1, length, channels), lambda j, i: (j, 0, 0)),
-        ]
-        + [HBM] * len(after),
-        out_specs=(pl.BlockSpec((1, tile, channels), lambda j, i: (j, i, 0)), pl.BlockSpec((8, LANES), lambda j, i: (0, 0))),
+        out_shape=(gradient, jax.ShapeDtypeStruct((8, LANES), F32)),
+        in_specs=[VMEM] * 2 + [HBM] * len(after),
+        out_specs=(HBM, VMEM),
+        scratch_shapes=[pltpu.VMEM(gradient.shape, F32), pltpu.SemaphoreType.DMA((len(steps),))],
         compiler_params=pltpu.CompilerParams(vmem_limit_bytes=VMEM_LIMIT),
-        cost_estimate=cost(1.5 * groups),
+        cost_estimate=cost(1.0 * groups),
     )(rows, values, *after)
 
 
 def four_by_eight(tokens, weights, tables, out_weight, grad_mixed):
     length, width = 4 * tokens.shape[0], weights.shape[2] // 4
     own, near, far = column_blocks(tokens)
-    weights, out_weight = loaded((weights, out_weight), near)
+    (weights,) = loaded((weights,), near)
     here = (own, flipped(near, "ctx", 1))
     feats_here, passed = channel_sums(here, 0, weights)
     far = later(fetched(far), passed)
     there = (far, flipped(far, "fsdp", 1))
     grad_own, grad_near, grad_far = column_blocks(grad_mixed)
     grad_here = (grad_own, flipped(grad_near, "ctx", 1))
-    grad_far = fetched(later(grad_far, feats_here[2]))
+    grad_far = fetched(later(grad_far, far))
     grad_there = (grad_far, flipped(grad_far, "fsdp", 1))
-    feats_there, _ = channel_sums(there, 1, weights)
+    feats_there, _ = channel_sums(there, 1, weights, feats_here[2:])
     grads_here, _ = channel_sums(grad_here, 0, out_weight[None])
-    *saved, gated = filter_forward(by_token(feats_here, feats_there), sum_of_three, tables, length, width)
-    grads_there, _ = channel_sums(grad_there, 1, out_weight[None], (gated,))
+    grads_there, passed_there = channel_sums(grad_there, 1, out_weight[None])
+    feats = by_token(feats_here, feats_there)
+    *saved, gated = filter_forward(feats, sum_of_three, tables, length, width, (grads_here[2], passed_there))
     gated = gated[None]
     gated_far = flipped(gated, "ctx", 2)
     all_gated = all_channels(gated, gated_far)
@@ -502,8 +510,8 @@
     token_rows = turned(here + there)
     grads_far = later(flipped(grads, "ctx", 2), *givens, keeps[0], token_rows, mark)
     whole_grads, keeps, gives = output_pieces(all_channels(grads, grads_far), weights)
-    mixed, mixed_give = block_sums(*mixed_halves, (), gives[:1])
-    grad_in, mark = weight_gradient(token_rows, whole_grads, (mixed_give,))
+    mixed, mixed_block = block_sums(*mixed_halves, (), gives[:1])
+    grad_in, mark = weight_gradient(token_rows, whole_grads, (mixed_block,))
     grad_tokens, _ = block_sums(keeps, exchange(gives), (mark,))
     return mixed, grad_tokens, grad_in, grad_out[0]
 

time: 103 us -> 104 us (level)
  Pallas kernels: 26.1 us -> 31.4 us
  waiting for transfers between devices: 20.8 us -> 18 us
  local copies, waits for them, and re-layouts: 3.71 us -> 2.24 us
    pallas_call x4, Pallas kernels: 3.77 us -> 6.59 us  [project(): call(body, (jax.ShapeDtypeStruct((groups, length, width), F32), sums, sum...]
    ppermute x32, waiting for transfers between devices: 13.7 us -> 11.1 us  [flipped(): lax.ppermute(value, axis, [(source, source ^ mask) for source in range(co...]
    pallas_call x2, Pallas kernels: 0.65 us -> 2.62 us  [turned(): call(body, jax.ShapeDtypeStruct((depth, 4 * part), pieces[0].dtype), us=0...]
    pallas_call x4, Pallas kernels: 7.95 us -> 6.07 us  [the longest x2 4.7 us: weight_gradient(): pl.pallas_call(body, out_shape=(gradient, jax.ShapeDtypeStruct((8, LANES)...]
    ppermute x4, starting transfers between devices: 14.8 us -> 16.6 us  [block_sums(): lax.ppermute(value, ('fsdp', 'ctx'), final_pairs(flip))]
    unnamed x20 -> x24, local copies, waits for them, and re-layouts: 2.95 us -> 1.48 us
    pallas_call x1, Pallas kernels: 2.15 us -> 3.25 us  [filter_forward(): call(body, (wide, wide, wide, wide, jax.ShapeDtypeStruct((length, width),...]
    ppermute x2, starting transfers between devices: 3.99 us -> 2.93 us  [fetched(): return lax.ppermute(block, ('fsdp', 'ctx'), pairs)]
  transfers between devices with their start and end apart: 38 -> 38, of which waited for: 13 -> 16; matrix products, arithmetic and copies ran while one was open for 1% -> 2% of each run, Pallas kernels for 24% -> 25%
where the time goes in v6:
time: 104 us
  starting transfers between devices  50.3 us (48%)
  Pallas kernels  31.4 us (30%)
  waiting for transfers between devices  18 us (17%)
  local copies, waits for them, and re-layouts  2.24 us (2%)
    ppermute x32, starting transfers between devices, flipped(): lax.ppermute(value, axis, [(source, source ^ mask) for source in range(co...  30.8 us
    ppermute x4, starting transfers between devices, block_sums(): lax.ppermute(value, ('fsdp', 'ctx'), final_pairs(flip))  16.6 us
    ppermute x32, waiting for transfers between devices, flipped(): lax.ppermute(value, axis, [(source, source ^ mask) for source in range(co...  11.1 us
    pallas_call x4, Pallas kernels, project(): call(body, (jax.ShapeDtypeStruct((groups, length, width), F32), sums, sum...  6.59 us
    pallas_call x2, Pallas kernels, weight_gradient(): pl.pallas_call(body, out_shape=(gradient, jax.ShapeDtypeStruct((8, LANES)...  4.7 us
    ppermute x4, waiting for transfers between devices, block_sums(): lax.ppermute(value, ('fsdp', 'ctx'), final_pairs(flip))  4.55 us
    pallas_call x1, Pallas kernels, filter_forward(): call(body, (wide, wide, wide, wide, jax.ShapeDtypeStruct((length, width),...  3.25 us
    pallas_call x2, Pallas kernels, column_blocks(): call(body, (block,) * 3, [pltpu.SemaphoreType.DMA((3,))], in_specs=[HBM],...  3.07 us
  transfers between devices with their start and end apart: 38, of which 16 were waited for; matrix products, arithmetic and copies ran while one was open for 2% of the time, Pallas kernels for 25%

profile of v6, /device:TPU:1, one launch (start us, length us, event | category | flops | bytes accessed | tf_op | source)
XLA Modules:
  0.0 103.7 jit_solution(4827797781689972080)
XLA Ops:
  1.9 2.7 %collective-permute-start.2 = (bf16[128,1024]{1,0:T(8,128)(2,1)S(1)}, bf16[128,1024]{1,0:T(8,128)(2,1)S(1)}, u32[]{:S(2)}, u32[]{:S(2)}) collective-permute-start(bf16[128,1024]{1,0:T(8,128)(2,1)S(1)} %get-tuple-element.65), channel_id=1, source_target_pairs={{0,2},{1,3},{2,0},{3,1},{4,7},{5,6},{6,5},{7,4},{8,10},{9,11},{10,... | collective-permute-start | bytes 786440 | tf_op jit(solution)/shard_map/ppermute | solution.py:276
  4.6 1.9 %shard_map.112.weight = bf16[3,1024,512]{2,1,0:T(8,128)(2,1)S(1)} custom-call(bf16[3,1024,512]{2,1,0:T(8,128)(2,1)} %bitcast.16, bf16[128,1024]{1,0:T(8,128)(2,1)S(1)} %get-tuple-element.62.refs_1_), custom_call_target="tpu_custom_call" | custom-call | flops 1495000064 | tf_op jit(solution)/shard_map/pallas_call | solution.py:244
  6.6 1.3 %shard_map.113 = (f32[3,256,128]{2,1,0:T(8,128)S(1)}, bf16[3,256,128]{2,1,0:T(8,128)(2,1)S(1)}, bf16[3,256,128]{2,1,0:T(8,128)(2,1)S(1)}, bf16[3,256,128]{2,1,0:T(8,128)(2,1)S(1)}) custom-call(bf16[128,1024]{1,0:T(8,128)(2,1)S(1)} %get-tuple-element.61.first.a, bf16[128,1024]{1,0:T(8,128)(2,1)S(1)} %collective-permute-done.second.b, ...), custom_call_target="tpu_custom_call" | custom-call | flops 1552499968 | tf_op jit(solution)/shard_map/pallas_call | solution.py:299
  11.2 1.4 %collective-permute-start.4 = (bf16[128,1024]{1,0:T(8,128)(2,1)S(1)}, bf16[128,1024]{1,0:T(8,128)(2,1)}, u32[]{:S(2)}, u32[]{:S(2)}) collective-permute-start(bf16[128,1024]{1,0:T(8,128)(2,1)S(1)} %shard_map.115.first.refs_1_.c), channel_id=1, source_target_pairs={{0,4},{4,0},{8,12},{12,8},{16,20},{20,16},{24,28},{28,24},{1,5},{5... | collective-permute-start | bytes 786440 | tf_op jit(solution)/shard_map/ppermute | solution.py:41
  13.9 1.9 %shard_map.118 = (bf16[128,1024]{1,0:T(8,128)(2,1)S(1)}, bf16[128,1024]{1,0:T(8,128)(2,1)}, bf16[128,1024]{1,0:T(8,128)(2,1)}) custom-call(bf16[128,4096]{1,0:T(8,128)(2,1)} %rows.3), custom_call_target="tpu_custom_call" | custom-call | flops 805000000 | tf_op jit(solution)/shard_map/pallas_call | solution.py:269
  19.1 2.3 %shard_map.116 = (f32[3,256,128]{2,1,0:T(8,128)S(1)}, bf16[3,256,128]{2,1,0:T(8,128)(2,1)S(1)}, bf16[3,256,128]{2,1,0:T(8,128)(2,1)S(1)}, bf16[3,256,128]{2,1,0:T(8,128)(2,1)S(1)}) custom-call(bf16[128,1024]{1,0:T(8,128)(2,1)S(1)} %shard_map.115.first.refs_1_.c, bf16[128,1024]{1,0:T(8,128)(2,1)} %collective-permute-done.4.second.d, ...), custom_call_target="tpu_custom_call" | custom-call | flops 1552499968 | tf_op jit(solution)/shard_map/pallas_call | solution.py:299
  21.3 1.5 %collective-permute-start.6 = (bf16[3,256,128]{2,1,0:T(8,128)(2,1)S(1)}, bf16[3,256,128]{2,1,0:T(8,128)(2,1)S(1)}, u32[]{:S(2)}, u32[]{:S(2)}) collective-permute-start(bf16[3,256,128]{2,1,0:T(8,128)(2,1)S(1)} %get-tuple-element.69), channel_id=1, source_target_pairs={{0,1},{1,0},{2,3},{3,2},{4,5},{5,4},{6,7},{7,6},{8,9},{9,8},{10,11... | collective-permute-start | bytes 589832 | tf_op jit(solution)/shard_map/ppermute | solution.py:41
  22.8 1.9 %collective-permute-done.12.first.c = bf16[128,1024]{1,0:T(8,128)(2,1)} collective-permute-done((bf16[128,1024]{1,0:T(8,128)(2,1)}, bf16[128,1024]{1,0:T(8,128)(2,1)}, u32[]{:S(2)}, u32[]{:S(2)}) %collective-permute-start.12) | collective-permute-done | bytes 262176 | tf_op jit(solution)/shard_map/ppermute | solution.py:276
  25.2 1.5 %shard_map.119 = (f32[1,256,128]{2,1,0:T(8,128)S(1)}, bf16[1,256,128]{2,1,0:T(8,128)(2,1)S(1)}, bf16[1,256,128]{2,1,0:T(8,128)(2,1)S(1)}, bf16[1,256,128]{2,1,0:T(8,128)(2,1)S(1)}) custom-call(bf16[128,1024]{1,0:T(8,128)(2,1)S(1)} %copy-done.6, bf16[128,1024]{1,0:T(8,128)(2,1)} %collective-permute-done.9.second.b, bf16[1,1024,512]{2,1,0:T(8,128)(2,1)S(1)} %bitcast.9), custom_call_target="tpu_custom_call" | custom-call | flops 517500000 | tf_op jit(solution)/shard_map/pallas_call | solution.py:299
  26.7 1.4 %collective-permute-start.10 = (bf16[1,256,128]{2,1,0:T(8,128)(2,1)S(1)}, bf16[1,256,128]{2,1,0:T(8,128)(2,1)S(1)}, u32[]{:S(2)}, u32[]{:S(2)}) collective-permute-start(bf16[1,256,128]{2,1,0:T(8,128)(2,1)S(1)} %get-tuple-element.75), channel_id=1, source_target_pairs={{0,1},{1,0},{2,3},{3,2},{4,5},{5,4},{6,7},{7,6},{8,9},{9,8},{10,11... | collective-permute-start | bytes 196616 | tf_op jit(solution)/shard_map/ppermute | solution.py:41
  31.5 1.5 %shard_map.122 = (f32[1,256,128]{2,1,0:T(8,128)S(1)}, bf16[1,256,128]{2,1,0:T(8,128)(2,1)S(1)}, bf16[1,256,128]{2,1,0:T(8,128)(2,1)S(1)}, bf16[1,256,128]{2,1,0:T(8,128)(2,1)S(1)}) custom-call(bf16[128,1024]{1,0:T(8,128)(2,1)} %collective-permute-done.12.first.c, bf16[128,1024]{1,0:T(8,128)(2,1)S(1)} %collective-permute-done.13.second.d, ...), custom_call_target="tpu_custom_call" | custom-call | flops 517500000 | tf_op jit(solution)/shard_map/pallas_call | solution.py:299
  33.0 2.2 %collective-permute-start.14 = (bf16[1,256,128]{2,1,0:T(8,128)(2,1)S(1)}, bf16[1,256,128]{2,1,0:T(8,128)(2,1)S(1)}, u32[]{:S(2)}, u32[]{:S(2)}) collective-permute-start(bf16[1,256,128]{2,1,0:T(8,128)(2,1)S(1)} %get-tuple-element.78), channel_id=1, source_target_pairs={{0,1},{1,0},{2,3},{3,2},{4,5},{5,4},{6,7},{7,6},{8,9},{9,8},{10,11... | collective-permute-start | bytes 196616 | tf_op jit(solution)/shard_map/ppermute | solution.py:41
  37.1 3.3 %shard_map.124 = (f32[512,128]{1,0:T(8,128)S(1)}, f32[512,128]{1,0:T(8,128)S(1)}, f32[512,128]{1,0:T(8,128)S(1)}, f32[512,128]{1,0:T(8,128)S(1)}, bf16[512,128]{1,0:T(8,128)(2,1)S(1)}) custom-call(f32[3,256,128]{2,1,0:T(8,128)S(1)} %copy-done.11, bf16[3,256,128]{2,1,0:T(8,128)(2,1)S(1)} %collective-permute-done.1.refs_1_, ...), custom_call_target="tpu_custom_call" | custom-call | flops 2415000064 | tf_op jit(solution)/shard_map/pallas_call | solution.py:185
  44.7 2.4 %collective-permute-start.17 = (bf16[1,512,128]{2,1,0:T(8,128)(2,1)S(1)}, bf16[1,512,128]{2,1,0:T(8,128)(2,1)S(1)}, u32[]{:S(2)}, u32[]{:S(2)}) collective-permute-start(bf16[1,512,128]{2,1,0:T(8,128)(2,1)S(1)} %collective-permute-done.15.far.refs_1_), channel_id=1, source_target_pairs={{0,1},{1,0},{2,3},{3,2},{4,5},{5,4},{6,7},{7,6},{8,9},{9,8},{10,11... | collective-permute-start | bytes 393224 | tf_op jit(solution)/shard_map/ppermute | solution.py:41
  47.1 2.1 %shard_map.128.refs_0_ = bf16[3,512,128]{2,1,0:T(8,128)(2,1)S(1)} custom-call(f32[1,256,128]{2,1,0:T(8,128)S(1)} %get-tuple-element.89.refs_0_, bf16[1,256,128]{2,1,0:T(8,128)(2,1)S(1)} %collective-permute-done.22.refs_1_, bf16[1,256,128]{2,1,0:T(8,128)(2,1)S(1)} %collective-permute-done.23.refs_2_, f32[1,256,128]{2,1,0:T(8,128)S(1)} %get-tuple-element.91.refs_3_, ...), custom_call_target="tpu_custom_call" | custom-call | flops 2415000064 | tf_op jit(solution)/shard_map/pallas_call | solution.py:205
  50.8 1.4 %collective-permute-start.18 = (bf16[512,256]{1,0:T(8,128)(2,1)S(1)}, bf16[512,256]{1,0:T(8,128)(2,1)S(1)}, u32[]{:S(2)}, u32[]{:S(2)}) collective-permute-start(bf16[512,256]{1,0:T(8,128)(2,1)S(1)} %get-tuple-element.82), channel_id=1, source_target_pairs={{0,4},{4,0},{8,12},{12,8},{16,20},{20,16},{24,28},{28,24},{1,5},{5... | collective-permute-start | bytes 786440 | tf_op jit(solution)/shard_map/ppermute | solution.py:41
  52.2 1.3 %collective-permute-start.19 = (bf16[256,512]{1,0:T(8,128)(2,1)S(1)}, bf16[256,512]{1,0:T(8,128)(2,1)S(1)}, u32[]{:S(2)}, u32[]{:S(2)}) collective-permute-start(bf16[256,512]{1,0:T(8,128)(2,1)S(1)} %get-tuple-element.84), channel_id=1, source_target_pairs={{0,8},{4,12},{8,0},{12,4},{16,24},{20,28},{24,16},{28,20},{1,9},{5... | collective-permute-start | bytes 786440 | tf_op jit(solution)/shard_map/ppermute | solution.py:41
  54.8 1.4 %shard_map.131.rows = bf16[1024,512]{1,0:T(8,128)(2,1)S(1)} custom-call(bf16[128,1024]{1,0:T(8,128)(2,1)S(1)} %copy-done.6, bf16[128,1024]{1,0:T(8,128)(2,1)} %collective-permute-done.9.second.b, bf16[128,1024]{1,0:T(8,128)(2,1)} %collective-permute-done.12.first.c, bf16[128,1024]{1,0:T(8,128)(2,1)S(1)} %collective-permute-done.13.second.d), custom_call_target="tpu_custom_call" | custom-call | flops 460000000 | tf_op jit(solution)/shard_map/pallas_call | solution.py:451
  56.2 1.6 %collective-permute-start.26 = (bf16[3,512,128]{2,1,0:T(8,128)(2,1)S(1)}, bf16[3,512,128]{2,1,0:T(8,128)(2,1)S(1)}, u32[]{:S(2)}, u32[]{:S(2)}) collective-permute-start(bf16[3,512,128]{2,1,0:T(8,128)(2,1)S(1)} %shard_map.129.own), channel_id=1, source_target_pairs={{0,1},{1,0},{2,3},{3,2},{4,5},{5,4},{6,7},{7,6},{8,9},{9,8},{10,11... | collective-permute-start | bytes 1179656 | tf_op jit(solution)/shard_map/ppermute | solution.py:41
  58.4 1.6 %shard_map.132 = (f32[1,1024,512]{2,1,0:T(8,128)}, f32[8,128]{1,0:T(8,128)S(1)}) custom-call(bf16[1024,512]{1,0:T(8,128)(2,1)S(1)} %shard_map.131.rows, bf16[1,512,512]{2,1,0:T(8,128)(2,1)S(1)} %get-tuple-element.80.whole.values), custom_call_target="tpu_custom_call" | custom-call | flops 1150000000 | tf_op jit(solution)/shard_map/pallas_call | solution.py:473
  61.1 1.5 %collective-permute-start.20 = (bf16[256,256]{1,0:T(8,128)(2,1)S(1)}, bf16[256,256]{1,0:T(8,128)(2,1)S(1)}, u32[]{:S(2)}, u32[]{:S(2)}) collective-permute-start(bf16[256,256]{1,0:T(8,128)(2,1)S(1)} %get-tuple-element.86), channel_id=1, source_target_pairs={{0,8},{4,12},{8,0},{12,4},{16,24},{20,28},{24,16},{28,20},{1,9},{5... | collective-permute-start | bytes 393224 | tf_op jit(solution)/shard_map/ppermute | solution.py:41
  62.6 1.4 %collective-permute-start.21 = (bf16[256,256]{1,0:T(8,128)(2,1)S(1)}, bf16[256,256]{1,0:T(8,128)(2,1)S(1)}, u32[]{:S(2)}, u32[]{:S(2)}) collective-permute-start(bf16[256,256]{1,0:T(8,128)(2,1)S(1)} %get-tuple-element.88), channel_id=1, source_target_pairs={{0,4},{4,0},{8,12},{12,8},{16,20},{20,16},{24,28},{28,24},{1,5},{5... | collective-permute-start | bytes 393224 | tf_op jit(solution)/shard_map/ppermute | solution.py:41
  64.0 1.7 %shard_map.134 = (bf16[3,512,512]{2,1,0:T(8,128)(2,1)S(1)}, bf16[512,256]{1,0:T(8,128)(2,1)S(1)}, bf16[256,512]{1,0:T(8,128)(2,1)S(1)}) custom-call(bf16[3,512,128]{2,1,0:T(8,128)(2,1)S(1)} %shard_map.129.own, bf16[3,512,128]{2,1,0:T(8,128)(2,1)S(1)} %shard_map.133.far, bf16[3,512,128]{2,1,0:T(8,128)(2,1)S(1)} %collective-permute-done.26.near, ...), custom_call_target="tpu_custom_call" | custom-call | flops 2070000000 | tf_op jit(solution)/shard_map/pallas_call | solution.py:364
  69.8 1.5 %shard_map.138 = (bf16[512,256]{1,0:T(8,128)(2,1)S(1)}, bf16[256,512]{1,0:T(8,128)(2,1)S(1)}) custom-call(bf16[3,512,512]{2,1,0:T(8,128)(2,1)S(1)} %get-tuple-element.103.whole.values, bf16[3,1024,512]{2,1,0:T(8,128)(2,1)S(1)} %shard_map.112.weight), custom_call_target="tpu_custom_call" | custom-call | flops 1380000000 | tf_op jit(solution)/shard_map/pallas_call | solution.py:370
  71.4 3.1 %shard_map.139 = (f32[3,1024,512]{2,1,0:T(8,128)}, f32[8,128]{1,0:T(8,128)S(1)}) custom-call(bf16[1024,512]{1,0:T(8,128)(2,1)S(1)} %shard_map.130.refs_4_.rows, bf16[3,512,512]{2,1,0:T(8,128)(2,1)S(1)} %get-tuple-element.103.whole.values, bf16[128,512]{1,0:T(8,128)(2,1)S(1)} %get-tuple-element.101.refs_0_), custom_call_target="tpu_custom_call" | custom-call | flops 3449999872 | tf_op jit(solution)/shard_map/pallas_call | solution.py:473
  76.6 3.0 %collective-permute-done.33.given_z = bf16[256,256]{1,0:T(8,128)(2,1)S(1)} collective-permute-done((bf16[256,256]{1,0:T(8,128)(2,1)S(1)}, bf16[256,256]{1,0:T(8,128)(2,1)S(1)}, u32[]{:S(2)}, u32[]{:S(2)}) %collective-permute-start.33) | collective-permute-done | bytes 131104 | tf_op jit(solution)/shard_map/ppermute | solution.py:41
  81.0 7.1 %collective-permute-start.29 = (bf16[128,512]{1,0:T(8,128)(2,1)S(1)}, bf16[128,512]{1,0:T(8,128)(2,1)S(1)}, u32[]{:S(2)}, u32[]{:S(2)}) collective-permute-start(bf16[128,512]{1,0:T(8,128)(2,1)S(1)} %get-tuple-element.101.refs_0_), channel_id=1, source_target_pairs={{0,0},{1,8},{2,18},{3,26},{4,4},{5,12},{6,22},{7,30},{8,1},{9,9},{... | collective-permute-start | bytes 393224 | tf_op jit(solution)/shard_map/ppermute | solution.py:434
  88.2 3.9 %collective-permute-start.30 = (bf16[128,512]{1,0:T(8,128)(2,1)S(1)}, bf16[128,512]{1,0:T(8,128)(2,1)S(1)}, u32[]{:S(2)}, u32[]{:S(2)}) collective-permute-start(bf16[128,512]{1,0:T(8,128)(2,1)S(1)} %get-tuple-element.102), channel_id=1, source_target_pairs={{0,16},{1,24},{2,2},{3,10},{4,20},{5,28},{6,6},{7,14},{8,17},{9,25... | collective-permute-start | bytes 393224 | tf_op jit(solution)/shard_map/ppermute | solution.py:434
  92.2 2.7 %collective-permute-start.36 = (bf16[128,512]{1,0:T(8,128)(2,1)S(1)}, bf16[128,512]{1,0:T(8,128)(2,1)S(1)}, u32[]{:S(2)}, u32[]{:S(2)}) collective-permute-start(bf16[128,512]{1,0:T(8,128)(2,1)S(1)} %get-tuple-element.114), channel_id=1, source_target_pairs={{0,0},{1,8},{2,18},{3,26},{4,4},{5,12},{6,22},{7,30},{8,1},{9,9},{... | collective-permute-start | bytes 393224 | tf_op jit(solution)/shard_map/ppermute | solution.py:434
  95.0 2.8 %collective-permute-start.37 = (bf16[128,512]{1,0:T(8,128)(2,1)S(1)}, bf16[128,512]{1,0:T(8,128)(2,1)S(1)}, u32[]{:S(2)}, u32[]{:S(2)}) collective-permute-start(bf16[128,512]{1,0:T(8,128)(2,1)S(1)} %get-tuple-element.115), channel_id=1, source_target_pairs={{0,16},{1,24},{2,2},{3,10},{4,20},{5,28},{6,6},{7,14},{8,17},{9,25... | collective-permute-start | bytes 393224 | tf_op jit(solution)/shard_map/ppermute | solution.py:434
  98.5 1.3 %collective-permute-done.36.first = bf16[128,512]{1,0:T(8,128)(2,1)S(1)} collective-permute-done((bf16[128,512]{1,0:T(8,128)(2,1)S(1)}, bf16[128,512]{1,0:T(8,128)(2,1)S(1)}, u32[]{:S(2)}, u32[]{:S(2)}) %collective-permute-start.36) | collective-permute-done | bytes 131104 | tf_op jit(solution)/shard_map/ppermute | solution.py:434
  99.8 3.2 %collective-permute-done.37.second = bf16[128,512]{1,0:T(8,128)(2,1)S(1)} collective-permute-done((bf16[128,512]{1,0:T(8,128)(2,1)S(1)}, bf16[128,512]{1,0:T(8,128)(2,1)S(1)}, u32[]{:S(2)}, u32[]{:S(2)}) %collective-permute-start.37) | collective-permute-done | bytes 131104 | tf_op jit(solution)/shard_map/ppermute | solution.py:434
  (104 shorter events, 32.9 us)
Async XLA Ops:
  1.8 4.7 %collective-permute-start = (bf16[128,1024]{1,0:T(8,128)(2,1)S(1)}, bf16[128,1024]{1,0:T(8,128)(2,1)S(1)}, u32[]{:S(2)}, u32[]{:S(2)}) collective-permute-start(bf16[128,1024]{1,0:T(8,128)(2,1)S(1)} %get-tuple-element.62.refs_1_), channel_id=1, source_target_pairs={{0,1},{1,0},{2,3},{3,2},{4,5},{5,4},{6,7},{7,6},{8,9},{9,8},{10,11... | collective-permute-start | bytes 786440 | tf_op jit(solution)/shard_map/ppermute | solution.py:41
  1.9 9.3 %collective-permute-start.2 = (bf16[128,1024]{1,0:T(8,128)(2,1)S(1)}, bf16[128,1024]{1,0:T(8,128)(2,1)S(1)}, u32[]{:S(2)}, u32[]{:S(2)}) collective-permute-start(bf16[128,1024]{1,0:T(8,128)(2,1)S(1)} %get-tuple-element.65), channel_id=1, source_target_pairs={{0,2},{1,3},{2,0},{3,1},{4,7},{5,6},{6,5},{7,4},{8,10},{9,11},{10,... | collective-permute-start | bytes 786440 | tf_op jit(solution)/shard_map/ppermute | solution.py:276
  11.2 7.8 %collective-permute-start.4 = (bf16[128,1024]{1,0:T(8,128)(2,1)S(1)}, bf16[128,1024]{1,0:T(8,128)(2,1)}, u32[]{:S(2)}, u32[]{:S(2)}) collective-permute-start(bf16[128,1024]{1,0:T(8,128)(2,1)S(1)} %shard_map.115.first.refs_1_.c), channel_id=1, source_target_pairs={{0,4},{4,0},{8,12},{12,8},{16,20},{20,16},{24,28},{28,24},{1,5},{5... | collective-permute-start | bytes 786440 | tf_op jit(solution)/shard_map/ppermute | solution.py:41
  12.6 6.4 %collective-permute-start.5 = (bf16[3,256,128]{2,1,0:T(8,128)(2,1)}, bf16[3,256,128]{2,1,0:T(8,128)(2,1)}, u32[]{:S(2)}, u32[]{:S(2)}) collective-permute-start(bf16[3,256,128]{2,1,0:T(8,128)(2,1)} %shard_map.114.refs_1_), channel_id=1, source_target_pairs={{0,2},{1,3},{2,0},{3,1},{4,6},{5,7},{6,4},{7,5},{8,10},{9,11},{10,... | collective-permute-start | bytes 589832 | tf_op jit(solution)/shard_map/ppermute | solution.py:41
  16.5 8.2 %collective-permute-start.12 = (bf16[128,1024]{1,0:T(8,128)(2,1)}, bf16[128,1024]{1,0:T(8,128)(2,1)}, u32[]{:S(2)}, u32[]{:S(2)}) collective-permute-start(bf16[128,1024]{1,0:T(8,128)(2,1)} %shard_map.121), channel_id=1, source_target_pairs={{0,2},{1,3},{2,0},{3,1},{4,7},{5,6},{6,5},{7,4},{8,10},{9,11},{10,... | collective-permute-start | bytes 786440 | tf_op jit(solution)/shard_map/ppermute | solution.py:276
  16.7 8.4 %collective-permute-start.9 = (bf16[128,1024]{1,0:T(8,128)(2,1)}, bf16[128,1024]{1,0:T(8,128)(2,1)}, u32[]{:S(2)}, u32[]{:S(2)}) collective-permute-start(bf16[128,1024]{1,0:T(8,128)(2,1)} %get-tuple-element.73), channel_id=1, source_target_pairs={{0,1},{1,0},{2,3},{3,2},{4,5},{5,4},{6,7},{7,6},{8,9},{9,8},{10,11... | collective-permute-start | bytes 786440 | tf_op jit(solution)/shard_map/ppermute | solution.py:41
  21.3 9.1 %collective-permute-start.6 = (bf16[3,256,128]{2,1,0:T(8,128)(2,1)S(1)}, bf16[3,256,128]{2,1,0:T(8,128)(2,1)S(1)}, u32[]{:S(2)}, u32[]{:S(2)}) collective-permute-start(bf16[3,256,128]{2,1,0:T(8,128)(2,1)S(1)} %get-tuple-element.69), channel_id=1, source_target_pairs={{0,1},{1,0},{2,3},{3,2},{4,5},{5,4},{6,7},{7,6},{8,9},{9,8},{10,11... | collective-permute-start | bytes 589832 | tf_op jit(solution)/shard_map/ppermute | solution.py:41
  24.7 6.8 %collective-permute-start.13 = (bf16[128,1024]{1,0:T(8,128)(2,1)}, bf16[128,1024]{1,0:T(8,128)(2,1)S(1)}, u32[]{:S(2)}, u32[]{:S(2)}) collective-permute-start(bf16[128,1024]{1,0:T(8,128)(2,1)} %collective-permute-done.12.first.c), channel_id=1, source_target_pairs={{0,4},{4,0},{8,12},{12,8},{16,20},{20,16},{24,28},{28,24},{1,5},{5... | collective-permute-start | bytes 786440 | tf_op jit(solution)/shard_map/ppermute | solution.py:41
  28.1 8.0 %collective-permute-start.1 = (bf16[3,256,128]{2,1,0:T(8,128)(2,1)S(1)}, bf16[3,256,128]{2,1,0:T(8,128)(2,1)S(1)}, u32[]{:S(2)}, u32[]{:S(2)}) collective-permute-start(bf16[3,256,128]{2,1,0:T(8,128)(2,1)S(1)} %copy-done.9), channel_id=1, source_target_pairs={{0,1},{1,0},{2,3},{3,2},{4,5},{5,4},{6,7},{7,6},{8,9},{9,8},{10,11... | collective-permute-start | bytes 589832 | tf_op jit(solution)/shard_map/ppermute | solution.py:41
  29.0 7.1 %collective-permute-start.11 = (bf16[1,256,128]{2,1,0:T(8,128)(2,1)S(1)}, bf16[1,256,128]{2,1,0:T(8,128)(2,1)S(1)}, u32[]{:S(2)}, u32[]{:S(2)}) collective-permute-start(bf16[1,256,128]{2,1,0:T(8,128)(2,1)S(1)} %shard_map.120), channel_id=1, source_target_pairs={{0,2},{1,3},{2,0},{3,1},{4,6},{5,7},{6,4},{7,5},{8,10},{9,11},{10,... | collective-permute-start | bytes 196616 | tf_op jit(solution)/shard_map/ppermute | solution.py:41
  29.9 6.3 %collective-permute-start.8 = (bf16[3,256,128]{2,1,0:T(8,128)(2,1)S(1)}, bf16[3,256,128]{2,1,0:T(8,128)(2,1)S(1)}, u32[]{:S(2)}, u32[]{:S(2)}) collective-permute-start(bf16[3,256,128]{2,1,0:T(8,128)(2,1)S(1)} %get-tuple-element.71), channel_id=1, source_target_pairs={{0,1},{1,0},{2,3},{3,2},{4,5},{5,4},{6,7},{7,6},{8,9},{9,8},{10,11... | collective-permute-start | bytes 589832 | tf_op jit(solution)/shard_map/ppermute | solution.py:41
  30.5 6.6 %collective-permute-start.7 = (bf16[3,256,128]{2,1,0:T(8,128)(2,1)S(1)}, bf16[3,256,128]{2,1,0:T(8,128)(2,1)S(1)}, u32[]{:S(2)}, u32[]{:S(2)}) collective-permute-start(bf16[3,256,128]{2,1,0:T(8,128)(2,1)S(1)} %shard_map.117), channel_id=1, source_target_pairs={{0,2},{1,3},{2,0},{3,1},{4,6},{5,7},{6,4},{7,5},{8,10},{9,11},{10,... | collective-permute-start | bytes 589832 | tf_op jit(solution)/shard_map/ppermute | solution.py:41
  40.4 4.3 %collective-permute-start.15 = (bf16[1,512,128]{2,1,0:T(8,128)(2,1)S(1)}, bf16[1,512,128]{2,1,0:T(8,128)(2,1)S(1)}, u32[]{:S(2)}, u32[]{:S(2)}) collective-permute-start(bf16[1,512,128]{2,1,0:T(8,128)(2,1)S(1)} %bitcast.13), channel_id=1, source_target_pairs={{0,2},{1,3},{2,0},{3,1},{4,6},{5,7},{6,4},{7,5},{8,10},{9,11},{10,... | collective-permute-start | bytes 393224 | tf_op jit(solution)/shard_map/ppermute | solution.py:41
  41.3 5.8 %collective-permute-start.22 = (bf16[1,256,128]{2,1,0:T(8,128)(2,1)S(1)}, bf16[1,256,128]{2,1,0:T(8,128)(2,1)S(1)}, u32[]{:S(2)}, u32[]{:S(2)}) collective-permute-start(bf16[1,256,128]{2,1,0:T(8,128)(2,1)S(1)} %get-tuple-element.90), channel_id=1, source_target_pairs={{0,1},{1,0},{2,3},{3,2},{4,5},{5,4},{6,7},{7,6},{8,9},{9,8},{10,11... | collective-permute-start | bytes 196616 | tf_op jit(solution)/shard_map/ppermute | solution.py:41
  42.3 4.8 %collective-permute-start.24 = (bf16[1,256,128]{2,1,0:T(8,128)(2,1)S(1)}, bf16[1,256,128]{2,1,0:T(8,128)(2,1)S(1)}, u32[]{:S(2)}, u32[]{:S(2)}) collective-permute-start(bf16[1,256,128]{2,1,0:T(8,128)(2,1)S(1)} %get-tuple-element.92), channel_id=1, source_target_pairs={{0,1},{1,0},{2,3},{3,2},{4,5},{5,4},{6,7},{7,6},{8,9},{9,8},{10,11... | collective-permute-start | bytes 196616 | tf_op jit(solution)/shard_map/ppermute | solution.py:41
  42.3 4.8 %collective-permute-start.23 = (bf16[1,256,128]{2,1,0:T(8,128)(2,1)S(1)}, bf16[1,256,128]{2,1,0:T(8,128)(2,1)S(1)}, u32[]{:S(2)}, u32[]{:S(2)}) collective-permute-start(bf16[1,256,128]{2,1,0:T(8,128)(2,1)S(1)} %shard_map.123.refs_12_), channel_id=1, source_target_pairs={{0,2},{1,3},{2,0},{3,1},{4,6},{5,7},{6,4},{7,5},{8,10},{9,11},{10,... | collective-permute-start | bytes 196616 | tf_op jit(solution)/shard_map/ppermute | solution.py:41
  43.0 7.2 %collective-permute-start.16 = (bf16[1,512,128]{2,1,0:T(8,128)(2,1)S(1)}, bf16[1,512,128]{2,1,0:T(8,128)(2,1)S(1)}, u32[]{:S(2)}, u32[]{:S(2)}) collective-permute-start(bf16[1,512,128]{2,1,0:T(8,128)(2,1)S(1)} %bitcast.14), channel_id=1, source_target_pairs={{0,1},{1,0},{2,3},{3,2},{4,5},{5,4},{6,7},{7,6},{8,9},{9,8},{10,11... | collective-permute-start | bytes 393224 | tf_op jit(solution)/shard_map/ppermute | solution.py:41
  44.7 5.5 %collective-permute-start.17 = (bf16[1,512,128]{2,1,0:T(8,128)(2,1)S(1)}, bf16[1,512,128]{2,1,0:T(8,128)(2,1)S(1)}, u32[]{:S(2)}, u32[]{:S(2)}) collective-permute-start(bf16[1,512,128]{2,1,0:T(8,128)(2,1)S(1)} %collective-permute-done.15.far.refs_1_), channel_id=1, source_target_pairs={{0,1},{1,0},{2,3},{3,2},{4,5},{5,4},{6,7},{7,6},{8,9},{9,8},{10,11... | collective-permute-start | bytes 393224 | tf_op jit(solution)/shard_map/ppermute | solution.py:41
  49.3 10.8 %collective-permute-start.25 = (bf16[3,512,128]{2,1,0:T(8,128)(2,1)S(1)}, bf16[3,512,128]{2,1,0:T(8,128)(2,1)S(1)}, u32[]{:S(2)}, u32[]{:S(2)}) collective-permute-start(bf16[3,512,128]{2,1,0:T(8,128)(2,1)S(1)} %shard_map.129.own), channel_id=1, source_target_pairs={{0,2},{1,3},{2,0},{3,1},{4,6},{5,7},{6,4},{7,5},{8,10},{9,11},{10,... | collective-permute-start | bytes 1179656 | tf_op jit(solution)/shard_map/ppermute | solution.py:41
  50.8 9.2 %collective-permute-start.18 = (bf16[512,256]{1,0:T(8,128)(2,1)S(1)}, bf16[512,256]{1,0:T(8,128)(2,1)S(1)}, u32[]{:S(2)}, u32[]{:S(2)}) collective-permute-start(bf16[512,256]{1,0:T(8,128)(2,1)S(1)} %get-tuple-element.82), channel_id=1, source_target_pairs={{0,4},{4,0},{8,12},{12,8},{16,20},{20,16},{24,28},{28,24},{1,5},{5... | collective-permute-start | bytes 786440 | tf_op jit(solution)/shard_map/ppermute | solution.py:41
  52.2 7.8 %collective-permute-start.19 = (bf16[256,512]{1,0:T(8,128)(2,1)S(1)}, bf16[256,512]{1,0:T(8,128)(2,1)S(1)}, u32[]{:S(2)}, u32[]{:S(2)}) collective-permute-start(bf16[256,512]{1,0:T(8,128)(2,1)S(1)} %get-tuple-element.84), channel_id=1, source_target_pairs={{0,8},{4,12},{8,0},{12,4},{16,24},{20,28},{24,16},{28,20},{1,9},{5... | collective-permute-start | bytes 786440 | tf_op jit(solution)/shard_map/ppermute | solution.py:41
  56.2 7.8 %collective-permute-start.26 = (bf16[3,512,128]{2,1,0:T(8,128)(2,1)S(1)}, bf16[3,512,128]{2,1,0:T(8,128)(2,1)S(1)}, u32[]{:S(2)}, u32[]{:S(2)}) collective-permute-start(bf16[3,512,128]{2,1,0:T(8,128)(2,1)S(1)} %shard_map.129.own), channel_id=1, source_target_pairs={{0,1},{1,0},{2,3},{3,2},{4,5},{5,4},{6,7},{7,6},{8,9},{9,8},{10,11... | collective-permute-start | bytes 1179656 | tf_op jit(solution)/shard_map/ppermute | solution.py:41
  60.1 3.9 %collective-permute-start.27 = (bf16[3,512,128]{2,1,0:T(8,128)(2,1)S(1)}, bf16[3,512,128]{2,1,0:T(8,128)(2,1)S(1)}, u32[]{:S(2)}, u32[]{:S(2)}) collective-permute-start(bf16[3,512,128]{2,1,0:T(8,128)(2,1)S(1)} %shard_map.133.far), channel_id=1, source_target_pairs={{0,1},{1,0},{2,3},{3,2},{4,5},{5,4},{6,7},{7,6},{8,9},{9,8},{10,11... | collective-permute-start | bytes 1179656 | tf_op jit(solution)/shard_map/ppermute | solution.py:41
  61.1 5.2 %collective-permute-start.20 = (bf16[256,256]{1,0:T(8,128)(2,1)S(1)}, bf16[256,256]{1,0:T(8,128)(2,1)S(1)}, u32[]{:S(2)}, u32[]{:S(2)}) collective-permute-start(bf16[256,256]{1,0:T(8,128)(2,1)S(1)} %get-tuple-element.86), channel_id=1, source_target_pairs={{0,8},{4,12},{8,0},{12,4},{16,24},{20,28},{24,16},{28,20},{1,9},{5... | collective-permute-start | bytes 393224 | tf_op jit(solution)/shard_map/ppermute | solution.py:41
  62.6 4.8 %collective-permute-start.21 = (bf16[256,256]{1,0:T(8,128)(2,1)S(1)}, bf16[256,256]{1,0:T(8,128)(2,1)S(1)}, u32[]{:S(2)}, u32[]{:S(2)}) collective-permute-start(bf16[256,256]{1,0:T(8,128)(2,1)S(1)} %get-tuple-element.88), channel_id=1, source_target_pairs={{0,4},{4,0},{8,12},{12,8},{16,20},{20,16},{24,28},{28,24},{1,5},{5... | collective-permute-start | bytes 393224 | tf_op jit(solution)/shard_map/ppermute | solution.py:41
  68.3 7.3 %collective-permute-start.31 = (bf16[512,256]{1,0:T(8,128)(2,1)S(1)}, bf16[512,256]{1,0:T(8,128)(2,1)S(1)}, u32[]{:S(2)}, u32[]{:S(2)}) collective-permute-start(bf16[512,256]{1,0:T(8,128)(2,1)S(1)} %get-tuple-element.98.refs_0_), channel_id=1, source_target_pairs={{0,4},{4,0},{8,12},{12,8},{16,20},{20,16},{24,28},{28,24},{1,5},{5... | collective-permute-start | bytes 786440 | tf_op jit(solution)/shard_map/ppermute | solution.py:41
  69.5 6.1 %collective-permute-start.32 = (bf16[256,512]{1,0:T(8,128)(2,1)S(1)}, bf16[256,512]{1,0:T(8,128)(2,1)S(1)}, u32[]{:S(2)}, u32[]{:S(2)}) collective-permute-start(bf16[256,512]{1,0:T(8,128)(2,1)S(1)} %get-tuple-element.106), channel_id=1, source_target_pairs={{0,8},{4,12},{8,0},{12,4},{16,24},{20,28},{24,16},{28,20},{1,9},{5... | collective-permute-start | bytes 786440 | tf_op jit(solution)/shard_map/ppermute | solution.py:41
  80.1 12.0 %collective-permute-start.35 = (bf16[128,512]{1,0:T(8,128)(2,1)S(1)}, bf16[128,512]{1,0:T(8,128)(2,1)S(1)}, u32[]{:S(2)}, u32[]{:S(2)}) collective-permute-start(bf16[128,512]{1,0:T(8,128)(2,1)S(1)} %get-tuple-element.113), channel_id=1, source_target_pairs={{0,2},{1,3},{2,0},{3,1},{4,6},{5,7},{6,4},{7,5},{8,10},{9,11},{10,... | collective-permute-start | bytes 393224 | tf_op jit(solution)/shard_map/ppermute | solution.py:41
  81.0 16.8 %collective-permute-start.29 = (bf16[128,512]{1,0:T(8,128)(2,1)S(1)}, bf16[128,512]{1,0:T(8,128)(2,1)S(1)}, u32[]{:S(2)}, u32[]{:S(2)}) collective-permute-start(bf16[128,512]{1,0:T(8,128)(2,1)S(1)} %get-tuple-element.101.refs_0_), channel_id=1, source_target_pairs={{0,0},{1,8},{2,18},{3,26},{4,4},{5,12},{6,22},{7,30},{8,1},{9,9},{... | collective-permute-start | bytes 393224 | tf_op jit(solution)/shard_map/ppermute | solution.py:434
  88.2 9.6 %collective-permute-start.30 = (bf16[128,512]{1,0:T(8,128)(2,1)S(1)}, bf16[128,512]{1,0:T(8,128)(2,1)S(1)}, u32[]{:S(2)}, u32[]{:S(2)}) collective-permute-start(bf16[128,512]{1,0:T(8,128)(2,1)S(1)} %get-tuple-element.102), channel_id=1, source_target_pairs={{0,16},{1,24},{2,2},{3,10},{4,20},{5,28},{6,6},{7,14},{8,17},{9,25... | collective-permute-start | bytes 393224 | tf_op jit(solution)/shard_map/ppermute | solution.py:434
  92.2 7.6 %collective-permute-start.36 = (bf16[128,512]{1,0:T(8,128)(2,1)S(1)}, bf16[128,512]{1,0:T(8,128)(2,1)S(1)}, u32[]{:S(2)}, u32[]{:S(2)}) collective-permute-start(bf16[128,512]{1,0:T(8,128)(2,1)S(1)} %get-tuple-element.114), channel_id=1, source_target_pairs={{0,0},{1,8},{2,18},{3,26},{4,4},{5,12},{6,22},{7,30},{8,1},{9,9},{... | collective-permute-start | bytes 393224 | tf_op jit(solution)/shard_map/ppermute | solution.py:434
  95.0 8.1 %collective-permute-start.37 = (bf16[128,512]{1,0:T(8,128)(2,1)S(1)}, bf16[128,512]{1,0:T(8,128)(2,1)S(1)}, u32[]{:S(2)}, u32[]{:S(2)}) collective-permute-start(bf16[128,512]{1,0:T(8,128)(2,1)S(1)} %get-tuple-element.115), channel_id=1, source_target_pairs={{0,16},{1,24},{2,2},{3,10},{4,20},{5,28},{6,6},{7,14},{8,17},{9,25... | collective-permute-start | bytes 393224 | tf_op jit(solution)/shard_map/ppermute | solution.py:434
  (18 other events, 105.6 us)

commit v7 on v5

--- a/solution.py
+++ b/solution.py
@@ -12,7 +12,7 @@
 LANES = 128
 CHUNKS = 8
 MARGIN = 8
-VMEM_LIMIT = 12 * 1024 * 1024
+VMEM_LIMIT = 16 * 1024 * 1024
 SMALL_LIMIT = 4 * 1024 * 1024
 FLOPS_PER_US = 1_150_000_000
 
@@ -25,13 +25,13 @@
     return pl.CostEstimate(flops=int(us * FLOPS_PER_US), bytes_accessed=0, transcendentals=0)
 
 
-def call(body, outs, scratch=(), in_specs=None, us=0.5, limit=VMEM_LIMIT):
+def call(body, outs, scratch=(), in_specs=None, us=0.5):
     return pl.pallas_call(
         body,
         out_shape=outs,
         **({} if in_specs is None else {"in_specs": in_specs}),
         scratch_shapes=list(scratch),
-        compiler_params=pltpu.CompilerParams(vmem_limit_bytes=limit),
+        compiler_params=pltpu.CompilerParams(vmem_limit_bytes=VMEM_LIMIT),
         cost_estimate=cost(us),
     )
 
@@ -174,11 +174,12 @@
     return start, parts[0][j, start : start + size, :].astype(F32)
 
 
-def filter_forward(parts, kinds, tables, length, width):
+def filter_forward(parts, kinds, tables, length, width, after=()):
     count = len(parts)
+    inputs = count + len(tables)
 
     def body(*refs):
-        forward_body(refs[:count], kinds, *refs[count:])
+        forward_body(refs[:count], kinds, *refs[count:inputs], *refs[inputs + len(after) :])
 
     wide = jax.ShapeDtypeStruct((length, width), F32)
     return call(
@@ -189,8 +190,9 @@
             pltpu.VMEM((length, width), F32),
             pltpu.VMEM((length, width), F32),
         ],
-        us=3.2,
-    )(*parts, *tables)
+        in_specs=[VMEM] * inputs + [HBM] * len(after),
+        us=2.1,
+    )(*parts, *tables, *after)
 
 
 def filter_backward(parts, kinds, tables, saved, length, width, after=()):
@@ -228,28 +230,6 @@
     )(value, *after)
 
 
-def loaded(values, after):
-    count = len(values)
-
-    def body(*refs):
-        sources, outs, arrived = refs[:count], refs[count + 1 : 2 * count + 1], refs[-1]
-        copies = [pltpu.make_async_copy(a, b, arrived.at[n]) for n, (a, b) in enumerate(zip(sources, outs))]
-        for copy in copies:
-            copy.start()
-        for copy in copies:
-            copy.wait()
-
-    return pl.pallas_call(
-        body,
-        out_shape=tuple(pltpu.VMEM(value.shape, value.dtype) for value in values),
-        in_specs=[HBM] * (count + 1),
-        out_specs=(VMEM,) * count,
-        scratch_shapes=[pltpu.SemaphoreType.DMA((count,))],
-        compiler_params=pltpu.CompilerParams(vmem_limit_bytes=SMALL_LIMIT),
-        cost_estimate=cost(1.3),
-    )(*[pltpu.with_memory_space_constraint(value, pltpu.HBM) for value in values], after)
-
-
 def column_blocks(rows):
     length, width = rows.shape[0], rows.shape[1] // 4
 
@@ -264,9 +244,7 @@
             copy.wait()
 
     block = jax.ShapeDtypeStruct((length, width), rows.dtype)
-    return call(body, (block,) * 3, [pltpu.SemaphoreType.DMA((3,))], in_specs=[HBM], us=0.7, limit=SMALL_LIMIT)(
-        pltpu.with_memory_space_constraint(rows, pltpu.HBM)
-    )
+    return call(body, (block,) * 3, [pltpu.SemaphoreType.DMA((3,))], in_specs=[HBM], us=0.7)(rows)
 
 
 def fetched(block):
@@ -303,16 +281,17 @@
     )(*pieces, weight, *after)
 
 
-def add_far(left, right):
-    def body(left, right, out):
-        out[...] = (left[...].astype(F32) + right[...].astype(F32)).astype(BF16)
-
-    return call(body, jax.ShapeDtypeStruct(left.shape, BF16), limit=SMALL_LIMIT)(left, right)
-
-
-def channel_sums(pieces, other, weight, after=()):
+def add_far(left, right, after):
+    def body(left, right, *refs):
+        refs[-1][...] = (left[...].astype(F32) + right[...].astype(F32)).astype(BF16)
+
+    specs = [VMEM] * 2 + [HBM] * len(after)
+    return call(body, jax.ShapeDtypeStruct(left.shape, BF16), in_specs=specs)(left, right, *after)
+
+
+def channel_sums(pieces, other, weight, after=(), after_add=()):
     own, far, give, give_far = project(pieces, other, weight, after)
-    passed = add_far(far, flipped(give_far, "ctx", 1))
+    passed = add_far(far, flipped(give_far, "ctx", 1), after_add)
     return (own, flipped(give, "ctx", 1), flipped(passed, "ctx", 2)), passed
 
 
@@ -405,7 +384,6 @@
         second_body,
         (square(BF16), square(BF16), square(F32), square(F32)),
         in_specs=[VMEM] * 4 + [HBM] * len(after),
-        limit=SMALL_LIMIT,
     )(keeps[0], givens[0], keeps[1], givens[1], *after)
 
     def third_body(keep_z, given_z, keep_x, given_x, *refs):
@@ -418,7 +396,7 @@
                 out[:, columns] = both(mine, other, at, slice(None)).astype(BF16)
 
     block = jax.ShapeDtypeStruct((part, 2 * piece), BF16)
-    give, keep = call(third_body, (block, block), in_specs=[VMEM] * 4 + [HBM] * len(after_second), limit=SMALL_LIMIT)(
+    give, keep = call(third_body, (block, block), in_specs=[VMEM] * 4 + [HBM] * len(after_second))(
         next_z, flipped(give_z, "fsdp", 2), next_x, flipped(give_x, "fsdp", 1), *after_second
     )
 
@@ -428,13 +406,13 @@
         first[...] = jnp.where(swap, given[...].astype(F32), keep[...].astype(F32)).astype(BF16)
         second[...] = jnp.where(swap, keep[...].astype(F32), given[...].astype(F32)).astype(BF16)
 
-    blocks = call(order_body, (block, block), limit=SMALL_LIMIT)(keep, flipped(give, "ctx", 2))
+    blocks = call(order_body, (block, block))(keep, flipped(give, "ctx", 2))
     arrived = [lax.ppermute(value, ("fsdp", "ctx"), final_pairs(flip)) for flip, value in enumerate(blocks)]
 
     def last_body(first, second, out):
         out[...] = (first[...].astype(F32) + second[...].astype(F32)).astype(BF16)
 
-    return call(last_body, block, limit=SMALL_LIMIT)(*arrived), give
+    return call(last_body, block)(*arrived), give
 
 
 def turned(pieces):
@@ -446,7 +424,7 @@
         for mask, piece in ((0, a), (1, b), (2 ^ side, c), (3 ^ side, d)):
             out[:, block_at(me ^ mask, part)] = piece[...].T
 
-    return call(body, jax.ShapeDtypeStruct((depth, 4 * part), pieces[0].dtype), us=0.4, limit=SMALL_LIMIT)(*pieces)
+    return call(body, jax.ShapeDtypeStruct((depth, 4 * part), pieces[0].dtype), us=0.4)(*pieces)
 
 
 def weight_gradient(rows, values, after=()):
@@ -477,18 +455,18 @@
 def four_by_eight(tokens, weights, tables, out_weight, grad_mixed):
     length, width = 4 * tokens.shape[0], weights.shape[2] // 4
     own, near, far = column_blocks(tokens)
-    weights, out_weight = loaded((weights, out_weight), near)
     here = (own, flipped(near, "ctx", 1))
     feats_here, passed = channel_sums(here, 0, weights)
     far = later(fetched(far), passed)
     there = (far, flipped(far, "fsdp", 1))
     grad_own, grad_near, grad_far = column_blocks(grad_mixed)
     grad_here = (grad_own, flipped(grad_near, "ctx", 1))
-    grad_far = fetched(later(grad_far, feats_here[2]))
+    grad_far = fetched(later(grad_far, far))
     grad_there = (grad_far, flipped(grad_far, "fsdp", 1))
-    feats_there, _ = channel_sums(there, 1, weights)
-    grads_here, _ = channel_sums(grad_here, 0, out_weight[None])
-    *saved, gated = filter_forward(by_token(feats_here, feats_there), sum_of_three, tables, length, width)
+    feats_there, passed = channel_sums(there, 1, weights, feats_here[2:], (grad_far,))
+    grads_here, _ = channel_sums(grad_here, 0, out_weight[None], (passed,))
+    feats = by_token(feats_here, feats_there)
+    *saved, gated = filter_forward(feats, sum_of_three, tables, length, width, grads_here[2:])
     grads_there, _ = channel_sums(grad_there, 1, out_weight[None], (gated,))
     gated = gated[None]
     gated_far = flipped(gated, "ctx", 2)

time: 103 us -> 101 us (0.981)
  local copies, waits for them, and re-layouts: 3.71 us -> 7.7 us
  starting transfers between devices: 50.2 us -> 47.1 us
  Pallas kernels: 26.1 us -> 23.6 us
    unnamed x20 -> x34, local copies, waits for them, and re-layouts: 2.95 us -> 6.95 us
    ppermute x32, starting transfers between devices: 31.5 us -> 28.1 us  [flipped(): lax.ppermute(value, axis, [(source, source ^ mask) for source in range(co...]
    pallas_call x2, Pallas kernels: 2.28 us -> 0.17 us  [column_blocks(): call(body, (block,) * 3, [pltpu.SemaphoreType.DMA((3,))], in_specs=[HBM],...]
    ppermute x32, waiting for transfers between devices: 13.7 us -> 15.2 us  [flipped(): lax.ppermute(value, axis, [(source, source ^ mask) for source in range(co...]
    ppermute x2, waiting for transfers between devices: 2.63 us -> 1.13 us  [fetched(): return lax.ppermute(block, ('fsdp', 'ctx'), pairs)]
    ppermute x4, starting transfers between devices: 14.8 us -> 16 us  [block_sums(): lax.ppermute(value, ('fsdp', 'ctx'), final_pairs(flip))]
    pallas_call x11 -> x10, Pallas kernels: 4.49 us -> 3.31 us  [the longest x2 1.38 us: block_sums(): return (call(last_body, block)(*arrived), give)]
    ppermute x2, starting transfers between devices: 3.99 us -> 2.95 us  [fetched(): return lax.ppermute(block, ('fsdp', 'ctx'), pairs)]
  transfers between devices with their start and end apart: 38 -> 38, of which waited for: 13 -> 15; matrix products, arithmetic and copies ran while one was open for 1% -> 2% of each run, Pallas kernels for 24% -> 22%
where the time goes in v7:
time: 101 us
  starting transfers between devices  47.1 us (47%)
  Pallas kernels  23.6 us (23%)
  waiting for transfers between devices  20.9 us (21%)
  local copies, waits for them, and re-layouts  7.7 us (8%)
    ppermute x32, starting transfers between devices, flipped(): lax.ppermute(value, axis, [(source, source ^ mask) for source in range(co...  28.1 us
    ppermute x4, starting transfers between devices, block_sums(): lax.ppermute(value, ('fsdp', 'ctx'), final_pairs(flip))  16 us
    ppermute x32, waiting for transfers between devices, flipped(): lax.ppermute(value, axis, [(source, source ^ mask) for source in range(co...  15.2 us
    unnamed x34, local copies, waits for them, and re-layouts  6.95 us
    pallas_call x2, Pallas kernels, weight_gradient(): pl.pallas_call(body, out_shape=(jax.ShapeDtypeStruct((groups, depth, chan...  6.58 us
    ppermute x4, waiting for transfers between devices, block_sums(): lax.ppermute(value, ('fsdp', 'ctx'), final_pairs(flip))  4.55 us
    pallas_call x4, Pallas kernels, project(): call(body, (jax.ShapeDtypeStruct((groups, length, width), F32), sums, sum...  4.39 us
    ppermute x2, starting transfers between devices, fetched(): return lax.ppermute(block, ('fsdp', 'ctx'), pairs)  2.95 us
  transfers between devices with their start and end apart: 38, of which 15 were waited for; matrix products, arithmetic and copies ran while one was open for 2% of the time, Pallas kernels for 22%

profile of v7, /device:TPU:1, one launch (start us, length us, event | category | flops | bytes accessed | tf_op | source)
XLA Modules:
  0.0 101.0 jit_solution(10562409107630194465)
XLA Ops:
  0.7 1.2 %copy-done.4 = bf16[128,4096]{1,0:T(8,128)(2,1)S(1)} copy-done((bf16[128,4096]{1,0:T(8,128)(2,1)S(1)}, bf16[128,4096]{1,0:T(8,128)(2,1)}, u32[]{:S(2)}) %copy-start.4) | copy-done | bytes 1048600
  2.1 2.7 %collective-permute-start.2 = (bf16[128,1024]{1,0:T(8,128)(2,1)S(1)}, bf16[128,1024]{1,0:T(8,128)(2,1)S(1)}, u32[]{:S(2)}, u32[]{:S(2)}) collective-permute-start(bf16[128,1024]{1,0:T(8,128)(2,1)S(1)} %get-tuple-element.65), channel_id=1, source_target_pairs={{0,2},{1,3},{2,0},{3,1},{4,7},{5,6},{6,5},{7,4},{8,10},{9,11},{10,... | collective-permute-start | bytes 786440 | tf_op jit(solution)/shard_map/ppermute | solution.py:252
  4.8 1.9 %copy-done.1 = bf16[1024,3,512]{2,0,1:T(8,128)(2,1)S(1)} copy-done((bf16[1024,3,512]{2,0,1:T(8,128)(2,1)S(1)}, bf16[1024,3,512]{2,0,1:T(8,128)(2,1)}, u32[]{:S(2)}) %copy-start.1) | copy-done | bytes 3145752
  6.7 1.3 %shard_map.112 = (f32[3,256,128]{2,1,0:T(8,128)S(1)}, bf16[3,256,128]{2,1,0:T(8,128)(2,1)S(1)}, bf16[3,256,128]{2,1,0:T(8,128)(2,1)S(1)}, bf16[3,256,128]{2,1,0:T(8,128)(2,1)S(1)}) custom-call(bf16[128,1024]{1,0:T(8,128)(2,1)S(1)} %get-tuple-element.61.first.a, bf16[128,1024]{1,0:T(8,128)(2,1)S(1)} %collective-permute-done.second.b, ...), custom_call_target="tpu_custom_call" | custom-call | flops 1552499968 | tf_op jit(solution)/shard_map/pallas_call | solution.py:275
  9.1 1.1 %collective-permute-done.3.right = bf16[3,256,128]{2,1,0:T(8,128)(2,1)S(1)} collective-permute-done((bf16[3,256,128]{2,1,0:T(8,128)(2,1)S(1)}, bf16[3,256,128]{2,1,0:T(8,128)(2,1)S(1)}, u32[]{:S(2)}, u32[]{:S(2)}) %collective-permute-start.3) | collective-permute-done | bytes 196640 | tf_op jit(solution)/shard_map/ppermute | solution.py:41
  10.3 1.1 %collective-permute-done.2.refs_0_ = bf16[128,1024]{1,0:T(8,128)(2,1)S(1)} collective-permute-done((bf16[128,1024]{1,0:T(8,128)(2,1)S(1)}, bf16[128,1024]{1,0:T(8,128)(2,1)S(1)}, u32[]{:S(2)}, u32[]{:S(2)}) %collective-permute-start.2) | collective-permute-done | bytes 262176 | tf_op jit(solution)/shard_map/ppermute | solution.py:252
  11.4 1.4 %collective-permute-start.4 = (bf16[128,1024]{1,0:T(8,128)(2,1)S(1)}, bf16[128,1024]{1,0:T(8,128)(2,1)S(1)}, u32[]{:S(2)}, u32[]{:S(2)}) collective-permute-start(bf16[128,1024]{1,0:T(8,128)(2,1)S(1)} %shard_map.114.first.refs_1_.c), channel_id=1, source_target_pairs={{0,4},{4,0},{8,12},{12,8},{16,20},{20,16},{24,28},{28,24},{1,5},{5... | collective-permute-start | bytes 786440 | tf_op jit(solution)/shard_map/ppermute | solution.py:41
  12.8 1.2 %collective-permute-start.5 = (bf16[3,256,128]{2,1,0:T(8,128)(2,1)S(1)}, bf16[3,256,128]{2,1,0:T(8,128)(2,1)S(1)}, u32[]{:S(2)}, u32[]{:S(2)}) collective-permute-start(bf16[3,256,128]{2,1,0:T(8,128)(2,1)S(1)} %shard_map.113.refs_1_), channel_id=1, source_target_pairs={{0,2},{1,3},{2,0},{3,1},{4,6},{5,7},{6,4},{7,5},{8,10},{9,11},{10,... | collective-permute-start | bytes 589832 | tf_op jit(solution)/shard_map/ppermute | solution.py:41
  15.1 3.8 %collective-permute-done.5.refs_0_.refs_5_ = bf16[3,256,128]{2,1,0:T(8,128)(2,1)S(1)} collective-permute-done((bf16[3,256,128]{2,1,0:T(8,128)(2,1)S(1)}, bf16[3,256,128]{2,1,0:T(8,128)(2,1)S(1)}, u32[]{:S(2)}, u32[]{:S(2)}) %collective-permute-start.5) | collective-permute-done | bytes 196640 | tf_op jit(solution)/shard_map/ppermute | solution.py:41
  18.9 1.9 %shard_map.115 = (f32[3,256,128]{2,1,0:T(8,128)S(1)}, bf16[3,256,128]{2,1,0:T(8,128)(2,1)S(1)}, bf16[3,256,128]{2,1,0:T(8,128)(2,1)S(1)}, bf16[3,256,128]{2,1,0:T(8,128)(2,1)}) custom-call(bf16[128,1024]{1,0:T(8,128)(2,1)S(1)} %shard_map.114.first.refs_1_.c, bf16[128,1024]{1,0:T(8,128)(2,1)S(1)} %collective-permute-done.4.second.d, ...), custom_call_target="tpu_custom_call" | custom-call | flops 1552499968 | tf_op jit(solution)/shard_map/pallas_call | solution.py:275
  23.0 2.0 %collective-permute-start.6 = (bf16[3,256,128]{2,1,0:T(8,128)(2,1)}, bf16[3,256,128]{2,1,0:T(8,128)(2,1)}, u32[]{:S(2)}, u32[]{:S(2)}) collective-permute-start(bf16[3,256,128]{2,1,0:T(8,128)(2,1)} %get-tuple-element.69), channel_id=1, source_target_pairs={{0,1},{1,0},{2,3},{3,2},{4,5},{5,4},{6,7},{7,6},{8,9},{9,8},{10,11... | collective-permute-start | bytes 589832 | tf_op jit(solution)/shard_map/ppermute | solution.py:41
  27.3 1.1 %shard_map.118.refs_0_ = bf16[3,256,128]{2,1,0:T(8,128)(2,1)S(1)} custom-call(bf16[3,256,128]{2,1,0:T(8,128)(2,1)S(1)} %copy-done.12, bf16[3,256,128]{2,1,0:T(8,128)(2,1)} %collective-permute-done.6.right, bf16[128,1024]{1,0:T(8,128)(2,1)S(1)} %collective-permute-done.7.refs_0_.first.c), custom_call_target="tpu_custom_call" | custom-call | flops 575000000 | tf_op jit(solution)/shard_map/pallas_call | solution.py:289
  28.4 1.3 %collective-permute-start.8 = (bf16[3,256,128]{2,1,0:T(8,128)(2,1)S(1)}, bf16[3,256,128]{2,1,0:T(8,128)(2,1)S(1)}, u32[]{:S(2)}, u32[]{:S(2)}) collective-permute-start(bf16[3,256,128]{2,1,0:T(8,128)(2,1)S(1)} %shard_map.118.refs_0_), channel_id=1, source_target_pairs={{0,2},{1,3},{2,0},{3,1},{4,6},{5,7},{6,4},{7,5},{8,10},{9,11},{10,... | collective-permute-start | bytes 589832 | tf_op jit(solution)/shard_map/ppermute | solution.py:41
  32.9 3.3 %collective-permute-done.12.refs_11_.refs_5_ = bf16[1,256,128]{2,1,0:T(8,128)(2,1)S(1)} collective-permute-done((bf16[1,256,128]{2,1,0:T(8,128)(2,1)S(1)}, bf16[1,256,128]{2,1,0:T(8,128)(2,1)S(1)}, u32[]{:S(2)}, u32[]{:S(2)}) %collective-permute-start.12) | collective-permute-done | bytes 65568 | tf_op jit(solution)/shard_map/ppermute | solution.py:41
  36.2 2.2 %shard_map.121 = (f32[512,128]{1,0:T(8,128)S(1)}, f32[512,128]{1,0:T(8,128)S(1)}, f32[512,128]{1,0:T(8,128)S(1)}, f32[512,128]{1,0:T(8,128)S(1)}, bf16[512,128]{1,0:T(8,128)(2,1)S(1)}) custom-call(f32[3,256,128]{2,1,0:T(8,128)S(1)} %copy-done.16, bf16[3,256,128]{2,1,0:T(8,128)(2,1)S(1)} %collective-permute-done.1.refs_1_, ...), custom_call_target="tpu_custom_call" | custom-call | flops 2415000064 | tf_op jit(solution)/shard_map/pallas_call | solution.py:185
  43.0 2.4 %collective-permute-done.13.far.refs_1_ = bf16[1,512,128]{2,1,0:T(8,128)(2,1)S(1)} collective-permute-done((bf16[1,512,128]{2,1,0:T(8,128)(2,1)S(1)}, bf16[1,512,128]{2,1,0:T(8,128)(2,1)S(1)}, u32[]{:S(2)}, u32[]{:S(2)}) %collective-permute-start.13) | collective-permute-done | bytes 131104 | tf_op jit(solution)/shard_map/ppermute | solution.py:41
  45.4 1.3 %collective-permute-start.15 = (bf16[1,512,128]{2,1,0:T(8,128)(2,1)S(1)}, bf16[1,512,128]{2,1,0:T(8,128)(2,1)S(1)}, u32[]{:S(2)}, u32[]{:S(2)}) collective-permute-start(bf16[1,512,128]{2,1,0:T(8,128)(2,1)S(1)} %collective-permute-done.13.far.refs_1_), channel_id=1, source_target_pairs={{0,1},{1,0},{2,3},{3,2},{4,5},{5,4},{6,7},{7,6},{8,9},{9,8},{10,11... | collective-permute-start | bytes 393224 | tf_op jit(solution)/shard_map/ppermute | solution.py:41
  46.8 2.1 %shard_map.127.refs_0_ = bf16[3,512,128]{2,1,0:T(8,128)(2,1)S(1)} custom-call(f32[1,256,128]{2,1,0:T(8,128)S(1)} %get-tuple-element.87.refs_0_, bf16[1,256,128]{2,1,0:T(8,128)(2,1)S(1)} %collective-permute-done.20.refs_1_, bf16[1,256,128]{2,1,0:T(8,128)(2,1)S(1)} %collective-permute-done.23.refs_2_, f32[1,256,128]{2,1,0:T(8,128)S(1)} %get-tuple-element.91.refs_3_, ...), custom_call_target="tpu_custom_call" | custom-call | flops 2415000064 | tf_op jit(solution)/shard_map/pallas_call | solution.py:205
  51.7 1.3 %collective-permute-start.17 = (bf16[256,512]{1,0:T(8,128)(2,1)S(1)}, bf16[256,512]{1,0:T(8,128)(2,1)S(1)}, u32[]{:S(2)}, u32[]{:S(2)}) collective-permute-start(bf16[256,512]{1,0:T(8,128)(2,1)S(1)} %get-tuple-element.82), channel_id=1, source_target_pairs={{0,8},{4,12},{8,0},{12,4},{16,24},{20,28},{24,16},{28,20},{1,9},{5... | collective-permute-start | bytes 786440 | tf_op jit(solution)/shard_map/ppermute | solution.py:41
  53.6 1.8 %collective-permute-start.26 = (bf16[3,512,128]{2,1,0:T(8,128)(2,1)S(1)}, bf16[3,512,128]{2,1,0:T(8,128)(2,1)S(1)}, u32[]{:S(2)}, u32[]{:S(2)}) collective-permute-start(bf16[3,512,128]{2,1,0:T(8,128)(2,1)S(1)} %shard_map.128.own), channel_id=1, source_target_pairs={{0,1},{1,0},{2,3},{3,2},{4,5},{5,4},{6,7},{7,6},{8,9},{9,8},{10,11... | collective-permute-start | bytes 1179656 | tf_op jit(solution)/shard_map/ppermute | solution.py:41
  56.0 1.9 %shard_map.131 = (f32[1,1024,512]{2,1,0:T(8,128)}, f32[8,128]{1,0:T(8,128)S(1)}) custom-call(bf16[1024,512]{1,0:T(8,128)(2,1)S(1)} %shard_map.130.rows, bf16[1,512,512]{2,1,0:T(8,128)(2,1)S(1)} %get-tuple-element.78.whole.values), custom_call_target="tpu_custom_call" | custom-call | flops 1724999936 | tf_op jit(solution)/shard_map/pallas_call | solution.py:440
  58.8 1.7 %collective-permute-start.27 = (bf16[3,512,128]{2,1,0:T(8,128)(2,1)S(1)}, bf16[3,512,128]{2,1,0:T(8,128)(2,1)S(1)}, u32[]{:S(2)}, u32[]{:S(2)}) collective-permute-start(bf16[3,512,128]{2,1,0:T(8,128)(2,1)S(1)} %shard_map.132.far), channel_id=1, source_target_pairs={{0,1},{1,0},{2,3},{3,2},{4,5},{5,4},{6,7},{7,6},{8,9},{9,8},{10,11... | collective-permute-start | bytes 1179656 | tf_op jit(solution)/shard_map/ppermute | solution.py:41
  60.7 1.4 %collective-permute-start.18 = (bf16[256,256]{1,0:T(8,128)(2,1)S(1)}, bf16[256,256]{1,0:T(8,128)(2,1)S(1)}, u32[]{:S(2)}, u32[]{:S(2)}) collective-permute-start(bf16[256,256]{1,0:T(8,128)(2,1)S(1)} %get-tuple-element.84), channel_id=1, source_target_pairs={{0,8},{4,12},{8,0},{12,4},{16,24},{20,28},{24,16},{28,20},{1,9},{5... | collective-permute-start | bytes 393224 | tf_op jit(solution)/shard_map/ppermute | solution.py:41
  63.0 1.7 %shard_map.133 = (bf16[3,512,512]{2,1,0:T(8,128)(2,1)S(1)}, bf16[512,256]{1,0:T(8,128)(2,1)S(1)}, bf16[256,512]{1,0:T(8,128)(2,1)S(1)}) custom-call(bf16[3,512,128]{2,1,0:T(8,128)(2,1)S(1)} %shard_map.128.own, bf16[3,512,128]{2,1,0:T(8,128)(2,1)S(1)} %shard_map.132.far, bf16[3,512,128]{2,1,0:T(8,128)(2,1)S(1)} %collective-permute-done.26.near, ...), custom_call_target="tpu_custom_call" | custom-call | flops 2070000000 | tf_op jit(solution)/shard_map/pallas_call | solution.py:341
  66.9 4.7 %shard_map.138 = (f32[3,1024,512]{2,1,0:T(8,128)}, f32[8,128]{1,0:T(8,128)S(1)}) custom-call(bf16[1024,512]{1,0:T(8,128)(2,1)S(1)} %shard_map.129.refs_4_.rows, bf16[3,512,512]{2,1,0:T(8,128)(2,1)S(1)} %get-tuple-element.103.whole.values, bf16[128,512]{1,0:T(8,128)(2,1)S(1)} %get-tuple-element.100.refs_0_), custom_call_target="tpu_custom_call" | custom-call | flops 5175000064 | tf_op jit(solution)/shard_map/pallas_call | solution.py:440
  71.6 1.5 %shard_map.137 = (bf16[512,256]{1,0:T(8,128)(2,1)S(1)}, bf16[256,512]{1,0:T(8,128)(2,1)S(1)}) custom-call(bf16[3,512,512]{2,1,0:T(8,128)(2,1)S(1)} %get-tuple-element.103.whole.values, bf16[3,1024,512]{2,1,0:T(8,128)(2,1)S(1)} %bitcast.12), custom_call_target="tpu_custom_call" | custom-call | flops 1380000000 | tf_op jit(solution)/shard_map/pallas_call | solution.py:347
  75.5 1.6 %collective-permute-done.33.given_z = bf16[256,256]{1,0:T(8,128)(2,1)S(1)} collective-permute-done((bf16[256,256]{1,0:T(8,128)(2,1)S(1)}, bf16[256,256]{1,0:T(8,128)(2,1)S(1)}, u32[]{:S(2)}, u32[]{:S(2)}) %collective-permute-start.33) | collective-permute-done | bytes 131104 | tf_op jit(solution)/shard_map/ppermute | solution.py:41
  78.9 6.5 %collective-permute-start.29 = (bf16[128,512]{1,0:T(8,128)(2,1)S(1)}, bf16[128,512]{1,0:T(8,128)(2,1)S(1)}, u32[]{:S(2)}, u32[]{:S(2)}) collective-permute-start(bf16[128,512]{1,0:T(8,128)(2,1)S(1)} %get-tuple-element.101), channel_id=1, source_target_pairs={{0,0},{1,8},{2,18},{3,26},{4,4},{5,12},{6,22},{7,30},{8,1},{9,9},{... | collective-permute-start | bytes 393224 | tf_op jit(solution)/shard_map/ppermute | solution.py:410
  85.4 4.0 %collective-permute-start.30 = (bf16[128,512]{1,0:T(8,128)(2,1)S(1)}, bf16[128,512]{1,0:T(8,128)(2,1)S(1)}, u32[]{:S(2)}, u32[]{:S(2)}) collective-permute-start(bf16[128,512]{1,0:T(8,128)(2,1)S(1)} %get-tuple-element.102), channel_id=1, source_target_pairs={{0,16},{1,24},{2,2},{3,10},{4,20},{5,28},{6,6},{7,14},{8,17},{9,25... | collective-permute-start | bytes 393224 | tf_op jit(solution)/shard_map/ppermute | solution.py:410
  89.5 2.7 %collective-permute-start.36 = (bf16[128,512]{1,0:T(8,128)(2,1)S(1)}, bf16[128,512]{1,0:T(8,128)(2,1)S(1)}, u32[]{:S(2)}, u32[]{:S(2)}) collective-permute-start(bf16[128,512]{1,0:T(8,128)(2,1)S(1)} %get-tuple-element.114), channel_id=1, source_target_pairs={{0,0},{1,8},{2,18},{3,26},{4,4},{5,12},{6,22},{7,30},{8,1},{9,9},{... | collective-permute-start | bytes 393224 | tf_op jit(solution)/shard_map/ppermute | solution.py:410
  92.2 2.8 %collective-permute-start.37 = (bf16[128,512]{1,0:T(8,128)(2,1)S(1)}, bf16[128,512]{1,0:T(8,128)(2,1)S(1)}, u32[]{:S(2)}, u32[]{:S(2)}) collective-permute-start(bf16[128,512]{1,0:T(8,128)(2,1)S(1)} %get-tuple-element.115), channel_id=1, source_target_pairs={{0,16},{1,24},{2,2},{3,10},{4,20},{5,28},{6,6},{7,14},{8,17},{9,25... | collective-permute-start | bytes 393224 | tf_op jit(solution)/shard_map/ppermute | solution.py:410
  96.8 3.5 %collective-permute-done.37.second = bf16[128,512]{1,0:T(8,128)(2,1)S(1)} collective-permute-done((bf16[128,512]{1,0:T(8,128)(2,1)S(1)}, bf16[128,512]{1,0:T(8,128)(2,1)S(1)}, u32[]{:S(2)}, u32[]{:S(2)}) %collective-permute-start.37) | collective-permute-done | bytes 131104 | tf_op jit(solution)/shard_map/ppermute | solution.py:410
  (113 shorter events, 29.5 us)
Async XLA Ops:
  2.1 9.3 %collective-permute-start.2 = (bf16[128,1024]{1,0:T(8,128)(2,1)S(1)}, bf16[128,1024]{1,0:T(8,128)(2,1)S(1)}, u32[]{:S(2)}, u32[]{:S(2)}) collective-permute-start(bf16[128,1024]{1,0:T(8,128)(2,1)S(1)} %get-tuple-element.65), channel_id=1, source_target_pairs={{0,2},{1,3},{2,0},{3,1},{4,7},{5,6},{6,5},{7,4},{8,10},{9,11},{10,... | collective-permute-start | bytes 786440 | tf_op jit(solution)/shard_map/ppermute | solution.py:252
  11.4 7.5 %collective-permute-start.4 = (bf16[128,1024]{1,0:T(8,128)(2,1)S(1)}, bf16[128,1024]{1,0:T(8,128)(2,1)S(1)}, u32[]{:S(2)}, u32[]{:S(2)}) collective-permute-start(bf16[128,1024]{1,0:T(8,128)(2,1)S(1)} %shard_map.114.first.refs_1_.c), channel_id=1, source_target_pairs={{0,4},{4,0},{8,12},{12,8},{16,20},{20,16},{24,28},{28,24},{1,5},{5... | collective-permute-start | bytes 786440 | tf_op jit(solution)/shard_map/ppermute | solution.py:41
  12.8 6.1 %collective-permute-start.5 = (bf16[3,256,128]{2,1,0:T(8,128)(2,1)S(1)}, bf16[3,256,128]{2,1,0:T(8,128)(2,1)S(1)}, u32[]{:S(2)}, u32[]{:S(2)}) collective-permute-start(bf16[3,256,128]{2,1,0:T(8,128)(2,1)S(1)} %shard_map.113.refs_1_), channel_id=1, source_target_pairs={{0,2},{1,3},{2,0},{3,1},{4,6},{5,7},{6,4},{7,5},{8,10},{9,11},{10,... | collective-permute-start | bytes 589832 | tf_op jit(solution)/shard_map/ppermute | solution.py:41
  14.1 15.5 %collective-permute-start.10 = (bf16[128,1024]{1,0:T(8,128)(2,1)S(1)}, bf16[128,1024]{1,0:T(8,128)(2,1)S(1)}, u32[]{:S(2)}, u32[]{:S(2)}) collective-permute-start(bf16[128,1024]{1,0:T(8,128)(2,1)S(1)} %get-tuple-element.74), channel_id=1, source_target_pairs={{0,1},{1,0},{2,3},{3,2},{4,5},{5,4},{6,7},{7,6},{8,9},{9,8},{10,11... | collective-permute-start | bytes 786440 | tf_op jit(solution)/shard_map/ppermute | solution.py:41
  14.8 11.5 %collective-permute-start.7 = (bf16[128,1024]{1,0:T(8,128)(2,1)S(1)}, bf16[128,1024]{1,0:T(8,128)(2,1)S(1)}, u32[]{:S(2)}, u32[]{:S(2)}) collective-permute-start(bf16[128,1024]{1,0:T(8,128)(2,1)S(1)} %shard_map.117), channel_id=1, source_target_pairs={{0,2},{1,3},{2,0},{3,1},{4,7},{5,6},{6,5},{7,4},{8,10},{9,11},{10,... | collective-permute-start | bytes 786440 | tf_op jit(solution)/shard_map/ppermute | solution.py:252
  25.7 7.2 %collective-permute-start.1 = (bf16[3,256,128]{2,1,0:T(8,128)(2,1)}, bf16[3,256,128]{2,1,0:T(8,128)(2,1)S(1)}, u32[]{:S(2)}, u32[]{:S(2)}) collective-permute-start(bf16[3,256,128]{2,1,0:T(8,128)(2,1)} %copy-done.7), channel_id=1, source_target_pairs={{0,1},{1,0},{2,3},{3,2},{4,5},{5,4},{6,7},{7,6},{8,9},{9,8},{10,11... | collective-permute-start | bytes 589832 | tf_op jit(solution)/shard_map/ppermute | solution.py:41
  25.8 7.1 %collective-permute-start.9 = (bf16[3,256,128]{2,1,0:T(8,128)(2,1)}, bf16[3,256,128]{2,1,0:T(8,128)(2,1)S(1)}, u32[]{:S(2)}, u32[]{:S(2)}) collective-permute-start(bf16[3,256,128]{2,1,0:T(8,128)(2,1)} %copy-done.10), channel_id=1, source_target_pairs={{0,1},{1,0},{2,3},{3,2},{4,5},{5,4},{6,7},{7,6},{8,9},{9,8},{10,11... | collective-permute-start | bytes 589832 | tf_op jit(solution)/shard_map/ppermute | solution.py:41
  28.4 7.9 %collective-permute-start.8 = (bf16[3,256,128]{2,1,0:T(8,128)(2,1)S(1)}, bf16[3,256,128]{2,1,0:T(8,128)(2,1)S(1)}, u32[]{:S(2)}, u32[]{:S(2)}) collective-permute-start(bf16[3,256,128]{2,1,0:T(8,128)(2,1)S(1)} %shard_map.118.refs_0_), channel_id=1, source_target_pairs={{0,2},{1,3},{2,0},{3,1},{4,6},{5,7},{6,4},{7,5},{8,10},{9,11},{10,... | collective-permute-start | bytes 589832 | tf_op jit(solution)/shard_map/ppermute | solution.py:41
  31.0 7.9 %collective-permute-start.21 = (bf16[128,1024]{1,0:T(8,128)(2,1)S(1)}, bf16[128,1024]{1,0:T(8,128)(2,1)S(1)}, u32[]{:S(2)}, u32[]{:S(2)}) collective-permute-start(bf16[128,1024]{1,0:T(8,128)(2,1)S(1)} %collective-permute-done.7.refs_0_.first.c), channel_id=1, source_target_pairs={{0,4},{4,0},{8,12},{12,8},{16,20},{20,16},{24,28},{28,24},{1,5},{5... | collective-permute-start | bytes 786440 | tf_op jit(solution)/shard_map/ppermute | solution.py:41
  32.0 4.2 %collective-permute-start.12 = (bf16[1,256,128]{2,1,0:T(8,128)(2,1)S(1)}, bf16[1,256,128]{2,1,0:T(8,128)(2,1)S(1)}, u32[]{:S(2)}, u32[]{:S(2)}) collective-permute-start(bf16[1,256,128]{2,1,0:T(8,128)(2,1)S(1)} %shard_map.120), channel_id=1, source_target_pairs={{0,2},{1,3},{2,0},{3,1},{4,6},{5,7},{6,4},{7,5},{8,10},{9,11},{10,... | collective-permute-start | bytes 196616 | tf_op jit(solution)/shard_map/ppermute | solution.py:41
  40.3 5.1 %collective-permute-start.13 = (bf16[1,512,128]{2,1,0:T(8,128)(2,1)S(1)}, bf16[1,512,128]{2,1,0:T(8,128)(2,1)S(1)}, u32[]{:S(2)}, u32[]{:S(2)}) collective-permute-start(bf16[1,512,128]{2,1,0:T(8,128)(2,1)S(1)} %bitcast.17), channel_id=1, source_target_pairs={{0,2},{1,3},{2,0},{3,1},{4,6},{5,7},{6,4},{7,5},{8,10},{9,11},{10,... | collective-permute-start | bytes 393224 | tf_op jit(solution)/shard_map/ppermute | solution.py:41
  41.3 5.4 %collective-permute-start.20 = (bf16[1,256,128]{2,1,0:T(8,128)(2,1)S(1)}, bf16[1,256,128]{2,1,0:T(8,128)(2,1)S(1)}, u32[]{:S(2)}, u32[]{:S(2)}) collective-permute-start(bf16[1,256,128]{2,1,0:T(8,128)(2,1)S(1)} %get-tuple-element.88), channel_id=1, source_target_pairs={{0,1},{1,0},{2,3},{3,2},{4,5},{5,4},{6,7},{7,6},{8,9},{9,8},{10,11... | collective-permute-start | bytes 196616 | tf_op jit(solution)/shard_map/ppermute | solution.py:41
  41.6 5.1 %collective-permute-start.24 = (bf16[1,256,128]{2,1,0:T(8,128)(2,1)S(1)}, bf16[1,256,128]{2,1,0:T(8,128)(2,1)S(1)}, u32[]{:S(2)}, u32[]{:S(2)}) collective-permute-start(bf16[1,256,128]{2,1,0:T(8,128)(2,1)S(1)} %get-tuple-element.92), channel_id=1, source_target_pairs={{0,1},{1,0},{2,3},{3,2},{4,5},{5,4},{6,7},{7,6},{8,9},{9,8},{10,11... | collective-permute-start | bytes 196616 | tf_op jit(solution)/shard_map/ppermute | solution.py:41
  41.8 5.0 %collective-permute-start.23 = (bf16[1,256,128]{2,1,0:T(8,128)(2,1)S(1)}, bf16[1,256,128]{2,1,0:T(8,128)(2,1)S(1)}, u32[]{:S(2)}, u32[]{:S(2)}) collective-permute-start(bf16[1,256,128]{2,1,0:T(8,128)(2,1)S(1)} %shard_map.126), channel_id=1, source_target_pairs={{0,2},{1,3},{2,0},{3,1},{4,6},{5,7},{6,4},{7,5},{8,10},{9,11},{10,... | collective-permute-start | bytes 196616 | tf_op jit(solution)/shard_map/ppermute | solution.py:41
  42.4 7.6 %collective-permute-start.14 = (bf16[1,512,128]{2,1,0:T(8,128)(2,1)S(1)}, bf16[1,512,128]{2,1,0:T(8,128)(2,1)S(1)}, u32[]{:S(2)}, u32[]{:S(2)}) collective-permute-start(bf16[1,512,128]{2,1,0:T(8,128)(2,1)S(1)} %bitcast.18), channel_id=1, source_target_pairs={{0,1},{1,0},{2,3},{3,2},{4,5},{5,4},{6,7},{7,6},{8,9},{9,8},{10,11... | collective-permute-start | bytes 393224 | tf_op jit(solution)/shard_map/ppermute | solution.py:41
  45.4 4.6 %collective-permute-start.15 = (bf16[1,512,128]{2,1,0:T(8,128)(2,1)S(1)}, bf16[1,512,128]{2,1,0:T(8,128)(2,1)S(1)}, u32[]{:S(2)}, u32[]{:S(2)}) collective-permute-start(bf16[1,512,128]{2,1,0:T(8,128)(2,1)S(1)} %collective-permute-done.13.far.refs_1_), channel_id=1, source_target_pairs={{0,1},{1,0},{2,3},{3,2},{4,5},{5,4},{6,7},{7,6},{8,9},{9,8},{10,11... | collective-permute-start | bytes 393224 | tf_op jit(solution)/shard_map/ppermute | solution.py:41
  49.0 9.9 %collective-permute-start.25 = (bf16[3,512,128]{2,1,0:T(8,128)(2,1)S(1)}, bf16[3,512,128]{2,1,0:T(8,128)(2,1)S(1)}, u32[]{:S(2)}, u32[]{:S(2)}) collective-permute-start(bf16[3,512,128]{2,1,0:T(8,128)(2,1)S(1)} %shard_map.128.own), channel_id=1, source_target_pairs={{0,2},{1,3},{2,0},{3,1},{4,6},{5,7},{6,4},{7,5},{8,10},{9,11},{10,... | collective-permute-start | bytes 1179656 | tf_op jit(solution)/shard_map/ppermute | solution.py:41
  50.6 7.2 %collective-permute-start.16 = (bf16[512,256]{1,0:T(8,128)(2,1)S(1)}, bf16[512,256]{1,0:T(8,128)(2,1)S(1)}, u32[]{:S(2)}, u32[]{:S(2)}) collective-permute-start(bf16[512,256]{1,0:T(8,128)(2,1)S(1)} %get-tuple-element.80), channel_id=1, source_target_pairs={{0,4},{4,0},{8,12},{12,8},{16,20},{20,16},{24,28},{28,24},{1,5},{5... | collective-permute-start | bytes 786440 | tf_op jit(solution)/shard_map/ppermute | solution.py:41
  51.7 6.4 %collective-permute-start.17 = (bf16[256,512]{1,0:T(8,128)(2,1)S(1)}, bf16[256,512]{1,0:T(8,128)(2,1)S(1)}, u32[]{:S(2)}, u32[]{:S(2)}) collective-permute-start(bf16[256,512]{1,0:T(8,128)(2,1)S(1)} %get-tuple-element.82), channel_id=1, source_target_pairs={{0,8},{4,12},{8,0},{12,4},{16,24},{20,28},{24,16},{28,20},{1,9},{5... | collective-permute-start | bytes 786440 | tf_op jit(solution)/shard_map/ppermute | solution.py:41
  53.6 9.4 %collective-permute-start.26 = (bf16[3,512,128]{2,1,0:T(8,128)(2,1)S(1)}, bf16[3,512,128]{2,1,0:T(8,128)(2,1)S(1)}, u32[]{:S(2)}, u32[]{:S(2)}) collective-permute-start(bf16[3,512,128]{2,1,0:T(8,128)(2,1)S(1)} %shard_map.128.own), channel_id=1, source_target_pairs={{0,1},{1,0},{2,3},{3,2},{4,5},{5,4},{6,7},{7,6},{8,9},{9,8},{10,11... | collective-permute-start | bytes 1179656 | tf_op jit(solution)/shard_map/ppermute | solution.py:41
  58.8 4.2 %collective-permute-start.27 = (bf16[3,512,128]{2,1,0:T(8,128)(2,1)S(1)}, bf16[3,512,128]{2,1,0:T(8,128)(2,1)S(1)}, u32[]{:S(2)}, u32[]{:S(2)}) collective-permute-start(bf16[3,512,128]{2,1,0:T(8,128)(2,1)S(1)} %shard_map.132.far), channel_id=1, source_target_pairs={{0,1},{1,0},{2,3},{3,2},{4,5},{5,4},{6,7},{7,6},{8,9},{9,8},{10,11... | collective-permute-start | bytes 1179656 | tf_op jit(solution)/shard_map/ppermute | solution.py:41
  60.7 5.3 %collective-permute-start.18 = (bf16[256,256]{1,0:T(8,128)(2,1)S(1)}, bf16[256,256]{1,0:T(8,128)(2,1)S(1)}, u32[]{:S(2)}, u32[]{:S(2)}) collective-permute-start(bf16[256,256]{1,0:T(8,128)(2,1)S(1)} %get-tuple-element.84), channel_id=1, source_target_pairs={{0,8},{4,12},{8,0},{12,4},{16,24},{20,28},{24,16},{28,20},{1,9},{5... | collective-permute-start | bytes 393224 | tf_op jit(solution)/shard_map/ppermute | solution.py:41
  62.1 4.8 %collective-permute-start.19 = (bf16[256,256]{1,0:T(8,128)(2,1)S(1)}, bf16[256,256]{1,0:T(8,128)(2,1)S(1)}, u32[]{:S(2)}, u32[]{:S(2)}) collective-permute-start(bf16[256,256]{1,0:T(8,128)(2,1)S(1)} %get-tuple-element.86), channel_id=1, source_target_pairs={{0,4},{4,0},{8,12},{12,8},{16,20},{20,16},{24,28},{28,24},{1,5},{5... | collective-permute-start | bytes 393224 | tf_op jit(solution)/shard_map/ppermute | solution.py:41
  64.8 8.3 %collective-permute-start.31 = (bf16[512,256]{1,0:T(8,128)(2,1)S(1)}, bf16[512,256]{1,0:T(8,128)(2,1)S(1)}, u32[]{:S(2)}, u32[]{:S(2)}) collective-permute-start(bf16[512,256]{1,0:T(8,128)(2,1)S(1)} %get-tuple-element.98.refs_0_), channel_id=1, source_target_pairs={{0,4},{4,0},{8,12},{12,8},{16,20},{20,16},{24,28},{28,24},{1,5},{5... | collective-permute-start | bytes 786440 | tf_op jit(solution)/shard_map/ppermute | solution.py:41
  65.4 7.7 %collective-permute-start.32 = (bf16[256,512]{1,0:T(8,128)(2,1)S(1)}, bf16[256,512]{1,0:T(8,128)(2,1)S(1)}, u32[]{:S(2)}, u32[]{:S(2)}) collective-permute-start(bf16[256,512]{1,0:T(8,128)(2,1)S(1)} %get-tuple-element.106), channel_id=1, source_target_pairs={{0,8},{4,12},{8,0},{12,4},{16,24},{20,28},{24,16},{28,20},{1,9},{5... | collective-permute-start | bytes 786440 | tf_op jit(solution)/shard_map/ppermute | solution.py:41
  73.6 4.1 %collective-permute-start.34 = (bf16[256,256]{1,0:T(8,128)(2,1)S(1)}, bf16[256,256]{1,0:T(8,128)(2,1)S(1)}, u32[]{:S(2)}, u32[]{:S(2)}) collective-permute-start(bf16[256,256]{1,0:T(8,128)(2,1)S(1)} %get-tuple-element.111), channel_id=1, source_target_pairs={{0,4},{4,0},{8,12},{12,8},{16,20},{20,16},{24,28},{28,24},{1,5},{5... | collective-permute-start | bytes 393224 | tf_op jit(solution)/shard_map/ppermute | solution.py:41
  74.6 4.2 %collective-permute-start.28 = (bf16[128,512]{1,0:T(8,128)(2,1)S(1)}, bf16[128,512]{1,0:T(8,128)(2,1)S(1)}, u32[]{:S(2)}, u32[]{:S(2)}) collective-permute-start(bf16[128,512]{1,0:T(8,128)(2,1)S(1)} %get-tuple-element.100.refs_0_), channel_id=1, source_target_pairs={{0,2},{1,3},{2,0},{3,1},{4,6},{5,7},{6,4},{7,5},{8,10},{9,11},{10,... | collective-permute-start | bytes 393224 | tf_op jit(solution)/shard_map/ppermute | solution.py:41
  77.8 11.6 %collective-permute-start.35 = (bf16[128,512]{1,0:T(8,128)(2,1)S(1)}, bf16[128,512]{1,0:T(8,128)(2,1)S(1)}, u32[]{:S(2)}, u32[]{:S(2)}) collective-permute-start(bf16[128,512]{1,0:T(8,128)(2,1)S(1)} %get-tuple-element.113), channel_id=1, source_target_pairs={{0,2},{1,3},{2,0},{3,1},{4,6},{5,7},{6,4},{7,5},{8,10},{9,11},{10,... | collective-permute-start | bytes 393224 | tf_op jit(solution)/shard_map/ppermute | solution.py:41
  78.9 16.2 %collective-permute-start.29 = (bf16[128,512]{1,0:T(8,128)(2,1)S(1)}, bf16[128,512]{1,0:T(8,128)(2,1)S(1)}, u32[]{:S(2)}, u32[]{:S(2)}) collective-permute-start(bf16[128,512]{1,0:T(8,128)(2,1)S(1)} %get-tuple-element.101), channel_id=1, source_target_pairs={{0,0},{1,8},{2,18},{3,26},{4,4},{5,12},{6,22},{7,30},{8,1},{9,9},{... | collective-permute-start | bytes 393224 | tf_op jit(solution)/shard_map/ppermute | solution.py:410
  85.4 9.7 %collective-permute-start.30 = (bf16[128,512]{1,0:T(8,128)(2,1)S(1)}, bf16[128,512]{1,0:T(8,128)(2,1)S(1)}, u32[]{:S(2)}, u32[]{:S(2)}) collective-permute-start(bf16[128,512]{1,0:T(8,128)(2,1)S(1)} %get-tuple-element.102), channel_id=1, source_target_pairs={{0,16},{1,24},{2,2},{3,10},{4,20},{5,28},{6,6},{7,14},{8,17},{9,25... | collective-permute-start | bytes 393224 | tf_op jit(solution)/shard_map/ppermute | solution.py:410
  89.5 7.3 %collective-permute-start.36 = (bf16[128,512]{1,0:T(8,128)(2,1)S(1)}, bf16[128,512]{1,0:T(8,128)(2,1)S(1)}, u32[]{:S(2)}, u32[]{:S(2)}) collective-permute-start(bf16[128,512]{1,0:T(8,128)(2,1)S(1)} %get-tuple-element.114), channel_id=1, source_target_pairs={{0,0},{1,8},{2,18},{3,26},{4,4},{5,12},{6,22},{7,30},{8,1},{9,9},{... | collective-permute-start | bytes 393224 | tf_op jit(solution)/shard_map/ppermute | solution.py:410
  92.2 8.1 %collective-permute-start.37 = (bf16[128,512]{1,0:T(8,128)(2,1)S(1)}, bf16[128,512]{1,0:T(8,128)(2,1)S(1)}, u32[]{:S(2)}, u32[]{:S(2)}) collective-permute-start(bf16[128,512]{1,0:T(8,128)(2,1)S(1)} %get-tuple-element.115), channel_id=1, source_target_pairs={{0,16},{1,24},{2,2},{3,10},{4,20},{5,28},{6,6},{7,14},{8,17},{9,25... | collective-permute-start | bytes 393224 | tf_op jit(solution)/shard_map/ppermute | solution.py:410
  (23 other events, 126.1 us)

commit v8 on v7

--- a/solution.py
+++ b/solution.py
@@ -457,7 +457,7 @@
     own, near, far = column_blocks(tokens)
     here = (own, flipped(near, "ctx", 1))
     feats_here, passed = channel_sums(here, 0, weights)
-    far = later(fetched(far), passed)
+    far = later(fetched(far), passed, *tables)
     there = (far, flipped(far, "fsdp", 1))
     grad_own, grad_near, grad_far = column_blocks(grad_mixed)
     grad_here = (grad_own, flipped(grad_near, "ctx", 1))

time: 101 us -> 99.5 us (0.985)
  waiting for transfers between devices: 20.9 us -> 25 us
  local copies, waits for them, and re-layouts: 7.7 us -> 3.9 us
  Pallas kernels: 23.6 us -> 21.9 us
    unnamed x34 -> x12, local copies, waits for them, and re-layouts: 6.95 us -> 3.14 us
    ppermute x32, waiting for transfers between devices: 15.2 us -> 17.3 us  [flipped(): lax.ppermute(value, axis, [(source, source ^ mask) for source in range(co...]
    ppermute x2, waiting for transfers between devices: 1.13 us -> 3.2 us  [fetched(): return lax.ppermute(block, ('fsdp', 'ctx'), pairs)]
  transfers between devices with their start and end apart: 38 -> 38, of which waited for: 15 -> 16; matrix products, arithmetic and copies ran while one was open for 2% -> 2% of each run, Pallas kernels for 22% -> 21%
where the time goes in v8:
time: 99.5 us; the launch traced here: 99.1 us
  starting transfers between devices  46.6 us (47%)
  waiting for transfers between devices  25 us (25%)
  Pallas kernels  21.9 us (22%)
  local copies, waits for them, and re-layouts  3.9 us (4%)
    ppermute x32, starting transfers between devices, flipped(): lax.ppermute(value, axis, [(source, source ^ mask) for source in range(co...  27.7 us
    ppermute x32, waiting for transfers between devices, flipped(): lax.ppermute(value, axis, [(source, source ^ mask) for source in range(co...  17.3 us
    ppermute x4, starting transfers between devices, block_sums(): lax.ppermute(value, ('fsdp', 'ctx'), final_pairs(flip))  16 us
    pallas_call x2, Pallas kernels, weight_gradient(): pl.pallas_call(body, out_shape=(jax.ShapeDtypeStruct((groups, depth, chan...  6.58 us
    ppermute x4, waiting for transfers between devices, block_sums(): lax.ppermute(value, ('fsdp', 'ctx'), final_pairs(flip))  4.55 us
    pallas_call x4, Pallas kernels, project(): call(body, (jax.ShapeDtypeStruct((groups, length, width), F32), sums, sum...  3.76 us
    ppermute x2, waiting for transfers between devices, fetched(): return lax.ppermute(block, ('fsdp', 'ctx'), pairs)  3.2 us
    unnamed x12, local copies, waits for them, and re-layouts  3.14 us
  transfers between devices with their start and end apart: 38, of which 16 were waited for; matrix products, arithmetic and copies ran while one was open for 2% of the time, Pallas kernels for 21%

profile of v8, /device:TPU:1, one launch (start us, length us, event | category | flops | bytes accessed | tf_op | source)
XLA Modules:
  0.0 99.1 jit_solution(16388763881898008864)
XLA Ops:
  2.1 2.7 %collective-permute-start.2 = (bf16[128,1024]{1,0:T(8,128)(2,1)S(1)}, bf16[128,1024]{1,0:T(8,128)(2,1)S(1)}, u32[]{:S(2)}, u32[]{:S(2)}) collective-permute-start(bf16[128,1024]{1,0:T(8,128)(2,1)S(1)} %get-tuple-element.65), channel_id=1, source_target_pairs={{0,2},{1,3},{2,0},{3,1},{4,7},{5,6},{6,5},{7,4},{8,10},{9,11},{10,... | collective-permute-start | bytes 786440 | tf_op jit(solution)/shard_map/ppermute | solution.py:252
  4.8 1.9 %copy-done.1 = bf16[1024,3,512]{2,0,1:T(8,128)(2,1)S(1)} copy-done((bf16[1024,3,512]{2,0,1:T(8,128)(2,1)S(1)}, bf16[1024,3,512]{2,0,1:T(8,128)(2,1)}, u32[]{:S(2)}) %copy-start.1) | copy-done | bytes 3145752
  6.7 1.3 %shard_map.112 = (f32[3,256,128]{2,1,0:T(8,128)S(1)}, bf16[3,256,128]{2,1,0:T(8,128)(2,1)S(1)}, bf16[3,256,128]{2,1,0:T(8,128)(2,1)S(1)}, bf16[3,256,128]{2,1,0:T(8,128)(2,1)S(1)}) custom-call(bf16[128,1024]{1,0:T(8,128)(2,1)S(1)} %get-tuple-element.61.first.a, bf16[128,1024]{1,0:T(8,128)(2,1)S(1)} %collective-permute-done.second.b, ...), custom_call_target="tpu_custom_call" | custom-call | flops 1552499968 | tf_op jit(solution)/shard_map/pallas_call | solution.py:275
  10.0 1.4 %collective-permute-done.2.refs_0_ = bf16[128,1024]{1,0:T(8,128)(2,1)S(1)} collective-permute-done((bf16[128,1024]{1,0:T(8,128)(2,1)S(1)}, bf16[128,1024]{1,0:T(8,128)(2,1)S(1)}, u32[]{:S(2)}, u32[]{:S(2)}) %collective-permute-start.2) | collective-permute-done | bytes 262176 | tf_op jit(solution)/shard_map/ppermute | solution.py:252
  11.4 1.4 %collective-permute-start.4 = (bf16[128,1024]{1,0:T(8,128)(2,1)S(1)}, bf16[128,1024]{1,0:T(8,128)(2,1)S(1)}, u32[]{:S(2)}, u32[]{:S(2)}) collective-permute-start(bf16[128,1024]{1,0:T(8,128)(2,1)S(1)} %shard_map.114.first.refs_1_.c), channel_id=1, source_target_pairs={{0,4},{4,0},{8,12},{12,8},{16,20},{20,16},{24,28},{28,24},{1,5},{5... | collective-permute-start | bytes 786440 | tf_op jit(solution)/shard_map/ppermute | solution.py:41
  15.1 3.8 %collective-permute-done.5.refs_0_.refs_5_ = bf16[3,256,128]{2,1,0:T(8,128)(2,1)S(1)} collective-permute-done((bf16[3,256,128]{2,1,0:T(8,128)(2,1)S(1)}, bf16[3,256,128]{2,1,0:T(8,128)(2,1)S(1)}, u32[]{:S(2)}, u32[]{:S(2)}) %collective-permute-start.5) | collective-permute-done | bytes 196640 | tf_op jit(solution)/shard_map/ppermute | solution.py:41
  18.9 1.3 %shard_map.115 = (f32[3,256,128]{2,1,0:T(8,128)S(1)}, bf16[3,256,128]{2,1,0:T(8,128)(2,1)S(1)}, bf16[3,256,128]{2,1,0:T(8,128)(2,1)S(1)}, bf16[3,256,128]{2,1,0:T(8,128)(2,1)S(1)}) custom-call(bf16[128,1024]{1,0:T(8,128)(2,1)S(1)} %shard_map.114.first.refs_1_.c, bf16[128,1024]{1,0:T(8,128)(2,1)S(1)} %collective-permute-done.4.second.d, ...), custom_call_target="tpu_custom_call" | custom-call | flops 1552499968 | tf_op jit(solution)/shard_map/pallas_call | solution.py:275
  20.2 2.0 %collective-permute-start.6 = (bf16[3,256,128]{2,1,0:T(8,128)(2,1)S(1)}, bf16[3,256,128]{2,1,0:T(8,128)(2,1)S(1)}, u32[]{:S(2)}, u32[]{:S(2)}) collective-permute-start(bf16[3,256,128]{2,1,0:T(8,128)(2,1)S(1)} %get-tuple-element.69), channel_id=1, source_target_pairs={{0,1},{1,0},{2,3},{3,2},{4,5},{5,4},{6,7},{7,6},{8,9},{9,8},{10,11... | collective-permute-start | bytes 589832 | tf_op jit(solution)/shard_map/ppermute | solution.py:41
  22.8 1.8 %collective-permute-done.7.refs_0_.first.c = bf16[128,1024]{1,0:T(8,128)(2,1)S(1)} collective-permute-done((bf16[128,1024]{1,0:T(8,128)(2,1)S(1)}, bf16[128,1024]{1,0:T(8,128)(2,1)S(1)}, u32[]{:S(2)}, u32[]{:S(2)}) %collective-permute-start.7) | collective-permute-done | bytes 262176 | tf_op jit(solution)/shard_map/ppermute | solution.py:252
  26.5 1.5 %collective-permute-start.11 = (bf16[1,256,128]{2,1,0:T(8,128)(2,1)S(1)}, bf16[1,256,128]{2,1,0:T(8,128)(2,1)S(1)}, u32[]{:S(2)}, u32[]{:S(2)}) collective-permute-start(bf16[1,256,128]{2,1,0:T(8,128)(2,1)S(1)} %get-tuple-element.76), channel_id=1, source_target_pairs={{0,1},{1,0},{2,3},{3,2},{4,5},{5,4},{6,7},{7,6},{8,9},{9,8},{10,11... | collective-permute-start | bytes 196616 | tf_op jit(solution)/shard_map/ppermute | solution.py:41
  29.2 2.9 %collective-permute-done.12.refs_11_.refs_5_ = bf16[1,256,128]{2,1,0:T(8,128)(2,1)S(1)} collective-permute-done((bf16[1,256,128]{2,1,0:T(8,128)(2,1)S(1)}, bf16[1,256,128]{2,1,0:T(8,128)(2,1)S(1)}, u32[]{:S(2)}, u32[]{:S(2)}) %collective-permute-start.12) | collective-permute-done | bytes 65568 | tf_op jit(solution)/shard_map/ppermute | solution.py:41
  32.1 2.2 %shard_map.121 = (f32[512,128]{1,0:T(8,128)S(1)}, f32[512,128]{1,0:T(8,128)S(1)}, f32[512,128]{1,0:T(8,128)S(1)}, f32[512,128]{1,0:T(8,128)S(1)}, bf16[512,128]{1,0:T(8,128)(2,1)S(1)}) custom-call(f32[3,256,128]{2,1,0:T(8,128)S(1)} %get-tuple-element.63.refs_0_, bf16[3,256,128]{2,1,0:T(8,128)(2,1)S(1)} %collective-permute-done.1.refs_1_, ...), custom_call_target="tpu_custom_call" | custom-call | flops 2415000064 | tf_op jit(solution)/shard_map/pallas_call | solution.py:185
  34.3 2.2 %collective-permute-done.21.second.d = bf16[128,1024]{1,0:T(8,128)(2,1)S(1)} collective-permute-done((bf16[128,1024]{1,0:T(8,128)(2,1)S(1)}, bf16[128,1024]{1,0:T(8,128)(2,1)S(1)}, u32[]{:S(2)}, u32[]{:S(2)}) %collective-permute-start.21) | collective-permute-done | bytes 262176 | tf_op jit(solution)/shard_map/ppermute | solution.py:41
  37.0 1.6 %collective-permute-start.22 = (bf16[1,256,128]{2,1,0:T(8,128)(2,1)S(1)}, bf16[1,256,128]{2,1,0:T(8,128)(2,1)S(1)}, u32[]{:S(2)}, u32[]{:S(2)}) collective-permute-start(bf16[1,256,128]{2,1,0:T(8,128)(2,1)S(1)} %get-tuple-element.90), channel_id=1, source_target_pairs={{0,1},{1,0},{2,3},{3,2},{4,5},{5,4},{6,7},{7,6},{8,9},{9,8},{10,11... | collective-permute-start | bytes 196616 | tf_op jit(solution)/shard_map/ppermute | solution.py:41
  41.4 2.2 %collective-permute-done.13.far.refs_1_ = bf16[1,512,128]{2,1,0:T(8,128)(2,1)S(1)} collective-permute-done((bf16[1,512,128]{2,1,0:T(8,128)(2,1)S(1)}, bf16[1,512,128]{2,1,0:T(8,128)(2,1)S(1)}, u32[]{:S(2)}, u32[]{:S(2)}) %collective-permute-start.13) | collective-permute-done | bytes 131104 | tf_op jit(solution)/shard_map/ppermute | solution.py:41
  45.0 2.1 %shard_map.127.refs_0_ = bf16[3,512,128]{2,1,0:T(8,128)(2,1)S(1)} custom-call(f32[1,256,128]{2,1,0:T(8,128)S(1)} %get-tuple-element.87.refs_0_, bf16[1,256,128]{2,1,0:T(8,128)(2,1)S(1)} %collective-permute-done.20.refs_1_, bf16[1,256,128]{2,1,0:T(8,128)(2,1)S(1)} %collective-permute-done.23.refs_2_, f32[1,256,128]{2,1,0:T(8,128)S(1)} %get-tuple-element.91.refs_3_, ...), custom_call_target="tpu_custom_call" | custom-call | flops 2415000064 | tf_op jit(solution)/shard_map/pallas_call | solution.py:205
  47.2 1.3 %collective-permute-start.25 = (bf16[3,512,128]{2,1,0:T(8,128)(2,1)S(1)}, bf16[3,512,128]{2,1,0:T(8,128)(2,1)S(1)}, u32[]{:S(2)}, u32[]{:S(2)}) collective-permute-start(bf16[3,512,128]{2,1,0:T(8,128)(2,1)S(1)} %shard_map.128.own), channel_id=1, source_target_pairs={{0,2},{1,3},{2,0},{3,1},{4,6},{5,7},{6,4},{7,5},{8,10},{9,11},{10,... | collective-permute-start | bytes 1179656 | tf_op jit(solution)/shard_map/ppermute | solution.py:41
  49.2 1.4 %collective-permute-start.17 = (bf16[256,512]{1,0:T(8,128)(2,1)S(1)}, bf16[256,512]{1,0:T(8,128)(2,1)S(1)}, u32[]{:S(2)}, u32[]{:S(2)}) collective-permute-start(bf16[256,512]{1,0:T(8,128)(2,1)S(1)} %get-tuple-element.82), channel_id=1, source_target_pairs={{0,8},{4,12},{8,0},{12,4},{16,24},{20,28},{24,16},{28,20},{1,9},{5... | collective-permute-start | bytes 786440 | tf_op jit(solution)/shard_map/ppermute | solution.py:41
  51.2 1.7 %collective-permute-start.26 = (bf16[3,512,128]{2,1,0:T(8,128)(2,1)S(1)}, bf16[3,512,128]{2,1,0:T(8,128)(2,1)S(1)}, u32[]{:S(2)}, u32[]{:S(2)}) collective-permute-start(bf16[3,512,128]{2,1,0:T(8,128)(2,1)S(1)} %shard_map.128.own), channel_id=1, source_target_pairs={{0,1},{1,0},{2,3},{3,2},{4,5},{5,4},{6,7},{7,6},{8,9},{9,8},{10,11... | collective-permute-start | bytes 1179656 | tf_op jit(solution)/shard_map/ppermute | solution.py:41
  53.5 1.9 %shard_map.131 = (f32[1,1024,512]{2,1,0:T(8,128)}, f32[8,128]{1,0:T(8,128)S(1)}) custom-call(bf16[1024,512]{1,0:T(8,128)(2,1)S(1)} %shard_map.130.rows, bf16[1,512,512]{2,1,0:T(8,128)(2,1)S(1)} %get-tuple-element.78.whole.values), custom_call_target="tpu_custom_call" | custom-call | flops 1724999936 | tf_op jit(solution)/shard_map/pallas_call | solution.py:440
  57.0 1.7 %collective-permute-start.27 = (bf16[3,512,128]{2,1,0:T(8,128)(2,1)S(1)}, bf16[3,512,128]{2,1,0:T(8,128)(2,1)S(1)}, u32[]{:S(2)}, u32[]{:S(2)}) collective-permute-start(bf16[3,512,128]{2,1,0:T(8,128)(2,1)S(1)} %shard_map.132.far), channel_id=1, source_target_pairs={{0,1},{1,0},{2,3},{3,2},{4,5},{5,4},{6,7},{7,6},{8,9},{9,8},{10,11... | collective-permute-start | bytes 1179656 | tf_op jit(solution)/shard_map/ppermute | solution.py:41
  58.9 1.4 %collective-permute-start.18 = (bf16[256,256]{1,0:T(8,128)(2,1)S(1)}, bf16[256,256]{1,0:T(8,128)(2,1)S(1)}, u32[]{:S(2)}, u32[]{:S(2)}) collective-permute-start(bf16[256,256]{1,0:T(8,128)(2,1)S(1)} %get-tuple-element.84), channel_id=1, source_target_pairs={{0,8},{4,12},{8,0},{12,4},{16,24},{20,28},{24,16},{28,20},{1,9},{5... | collective-permute-start | bytes 393224 | tf_op jit(solution)/shard_map/ppermute | solution.py:41
  60.9 1.7 %shard_map.133 = (bf16[3,512,512]{2,1,0:T(8,128)(2,1)S(1)}, bf16[512,256]{1,0:T(8,128)(2,1)S(1)}, bf16[256,512]{1,0:T(8,128)(2,1)S(1)}) custom-call(bf16[3,512,128]{2,1,0:T(8,128)(2,1)S(1)} %shard_map.128.own, bf16[3,512,128]{2,1,0:T(8,128)(2,1)S(1)} %shard_map.132.far, bf16[3,512,128]{2,1,0:T(8,128)(2,1)S(1)} %collective-permute-done.26.near, ...), custom_call_target="tpu_custom_call" | custom-call | flops 2070000000 | tf_op jit(solution)/shard_map/pallas_call | solution.py:341
  65.1 4.7 %shard_map.138 = (f32[3,1024,512]{2,1,0:T(8,128)}, f32[8,128]{1,0:T(8,128)S(1)}) custom-call(bf16[1024,512]{1,0:T(8,128)(2,1)S(1)} %shard_map.129.refs_4_.rows, bf16[3,512,512]{2,1,0:T(8,128)(2,1)S(1)} %get-tuple-element.103.whole.values, bf16[128,512]{1,0:T(8,128)(2,1)S(1)} %get-tuple-element.100.refs_0_), custom_call_target="tpu_custom_call" | custom-call | flops 5175000064 | tf_op jit(solution)/shard_map/pallas_call | solution.py:440
  69.8 1.4 %shard_map.137 = (bf16[512,256]{1,0:T(8,128)(2,1)S(1)}, bf16[256,512]{1,0:T(8,128)(2,1)S(1)}) custom-call(bf16[3,512,512]{2,1,0:T(8,128)(2,1)S(1)} %get-tuple-element.103.whole.values, bf16[3,1024,512]{2,1,0:T(8,128)(2,1)S(1)} %bitcast.12), custom_call_target="tpu_custom_call" | custom-call | flops 1380000000 | tf_op jit(solution)/shard_map/pallas_call | solution.py:347
  73.3 2.0 %collective-permute-done.33.given_z = bf16[256,256]{1,0:T(8,128)(2,1)S(1)} collective-permute-done((bf16[256,256]{1,0:T(8,128)(2,1)S(1)}, bf16[256,256]{1,0:T(8,128)(2,1)S(1)}, u32[]{:S(2)}, u32[]{:S(2)}) %collective-permute-start.33) | collective-permute-done | bytes 131104 | tf_op jit(solution)/shard_map/ppermute | solution.py:41
  75.7 1.3 %collective-permute-start.35 = (bf16[128,512]{1,0:T(8,128)(2,1)S(1)}, bf16[128,512]{1,0:T(8,128)(2,1)S(1)}, u32[]{:S(2)}, u32[]{:S(2)}) collective-permute-start(bf16[128,512]{1,0:T(8,128)(2,1)S(1)} %get-tuple-element.113), channel_id=1, source_target_pairs={{0,2},{1,3},{2,0},{3,1},{4,6},{5,7},{6,4},{7,5},{8,10},{9,11},{10,... | collective-permute-start | bytes 393224 | tf_op jit(solution)/shard_map/ppermute | solution.py:41
  77.1 6.5 %collective-permute-start.29 = (bf16[128,512]{1,0:T(8,128)(2,1)S(1)}, bf16[128,512]{1,0:T(8,128)(2,1)S(1)}, u32[]{:S(2)}, u32[]{:S(2)}) collective-permute-start(bf16[128,512]{1,0:T(8,128)(2,1)S(1)} %get-tuple-element.101), channel_id=1, source_target_pairs={{0,0},{1,8},{2,18},{3,26},{4,4},{5,12},{6,22},{7,30},{8,1},{9,9},{... | collective-permute-start | bytes 393224 | tf_op jit(solution)/shard_map/ppermute | solution.py:410
  83.6 3.9 %collective-permute-start.30 = (bf16[128,512]{1,0:T(8,128)(2,1)S(1)}, bf16[128,512]{1,0:T(8,128)(2,1)S(1)}, u32[]{:S(2)}, u32[]{:S(2)}) collective-permute-start(bf16[128,512]{1,0:T(8,128)(2,1)S(1)} %get-tuple-element.102), channel_id=1, source_target_pairs={{0,16},{1,24},{2,2},{3,10},{4,20},{5,28},{6,6},{7,14},{8,17},{9,25... | collective-permute-start | bytes 393224 | tf_op jit(solution)/shard_map/ppermute | solution.py:410
  87.6 2.7 %collective-permute-start.36 = (bf16[128,512]{1,0:T(8,128)(2,1)S(1)}, bf16[128,512]{1,0:T(8,128)(2,1)S(1)}, u32[]{:S(2)}, u32[]{:S(2)}) collective-permute-start(bf16[128,512]{1,0:T(8,128)(2,1)S(1)} %get-tuple-element.114), channel_id=1, source_target_pairs={{0,0},{1,8},{2,18},{3,26},{4,4},{5,12},{6,22},{7,30},{8,1},{9,9},{... | collective-permute-start | bytes 393224 | tf_op jit(solution)/shard_map/ppermute | solution.py:410
  90.4 2.8 %collective-permute-start.37 = (bf16[128,512]{1,0:T(8,128)(2,1)S(1)}, bf16[128,512]{1,0:T(8,128)(2,1)S(1)}, u32[]{:S(2)}, u32[]{:S(2)}) collective-permute-start(bf16[128,512]{1,0:T(8,128)(2,1)S(1)} %get-tuple-element.115), channel_id=1, source_target_pairs={{0,16},{1,24},{2,2},{3,10},{4,20},{5,28},{6,6},{7,14},{8,17},{9,25... | collective-permute-start | bytes 393224 | tf_op jit(solution)/shard_map/ppermute | solution.py:410
  95.1 3.3 %collective-permute-done.37.second = bf16[128,512]{1,0:T(8,128)(2,1)S(1)} collective-permute-done((bf16[128,512]{1,0:T(8,128)(2,1)S(1)}, bf16[128,512]{1,0:T(8,128)(2,1)S(1)}, u32[]{:S(2)}, u32[]{:S(2)}) %collective-permute-start.37) | collective-permute-done | bytes 131104 | tf_op jit(solution)/shard_map/ppermute | solution.py:410
  (91 shorter events, 26.1 us)
Async XLA Ops:
  2.1 9.3 %collective-permute-start.2 = (bf16[128,1024]{1,0:T(8,128)(2,1)S(1)}, bf16[128,1024]{1,0:T(8,128)(2,1)S(1)}, u32[]{:S(2)}, u32[]{:S(2)}) collective-permute-start(bf16[128,1024]{1,0:T(8,128)(2,1)S(1)} %get-tuple-element.65), channel_id=1, source_target_pairs={{0,2},{1,3},{2,0},{3,1},{4,7},{5,6},{6,5},{7,4},{8,10},{9,11},{10,... | collective-permute-start | bytes 786440 | tf_op jit(solution)/shard_map/ppermute | solution.py:252
  11.4 7.5 %collective-permute-start.4 = (bf16[128,1024]{1,0:T(8,128)(2,1)S(1)}, bf16[128,1024]{1,0:T(8,128)(2,1)S(1)}, u32[]{:S(2)}, u32[]{:S(2)}) collective-permute-start(bf16[128,1024]{1,0:T(8,128)(2,1)S(1)} %shard_map.114.first.refs_1_.c), channel_id=1, source_target_pairs={{0,4},{4,0},{8,12},{12,8},{16,20},{20,16},{24,28},{28,24},{1,5},{5... | collective-permute-start | bytes 786440 | tf_op jit(solution)/shard_map/ppermute | solution.py:41
  12.8 6.1 %collective-permute-start.5 = (bf16[3,256,128]{2,1,0:T(8,128)(2,1)S(1)}, bf16[3,256,128]{2,1,0:T(8,128)(2,1)S(1)}, u32[]{:S(2)}, u32[]{:S(2)}) collective-permute-start(bf16[3,256,128]{2,1,0:T(8,128)(2,1)S(1)} %shard_map.113.refs_1_), channel_id=1, source_target_pairs={{0,2},{1,3},{2,0},{3,1},{4,6},{5,7},{6,4},{7,5},{8,10},{9,11},{10,... | collective-permute-start | bytes 589832 | tf_op jit(solution)/shard_map/ppermute | solution.py:41
  14.1 11.8 %collective-permute-start.10 = (bf16[128,1024]{1,0:T(8,128)(2,1)S(1)}, bf16[128,1024]{1,0:T(8,128)(2,1)S(1)}, u32[]{:S(2)}, u32[]{:S(2)}) collective-permute-start(bf16[128,1024]{1,0:T(8,128)(2,1)S(1)} %get-tuple-element.74), channel_id=1, source_target_pairs={{0,1},{1,0},{2,3},{3,2},{4,5},{5,4},{6,7},{7,6},{8,9},{9,8},{10,11... | collective-permute-start | bytes 786440 | tf_op jit(solution)/shard_map/ppermute | solution.py:41
  14.8 9.7 %collective-permute-start.7 = (bf16[128,1024]{1,0:T(8,128)(2,1)S(1)}, bf16[128,1024]{1,0:T(8,128)(2,1)S(1)}, u32[]{:S(2)}, u32[]{:S(2)}) collective-permute-start(bf16[128,1024]{1,0:T(8,128)(2,1)S(1)} %shard_map.117), channel_id=1, source_target_pairs={{0,2},{1,3},{2,0},{3,1},{4,7},{5,6},{6,5},{7,4},{8,10},{9,11},{10,... | collective-permute-start | bytes 786440 | tf_op jit(solution)/shard_map/ppermute | solution.py:252
  20.2 4.3 %collective-permute-start.6 = (bf16[3,256,128]{2,1,0:T(8,128)(2,1)S(1)}, bf16[3,256,128]{2,1,0:T(8,128)(2,1)S(1)}, u32[]{:S(2)}, u32[]{:S(2)}) collective-permute-start(bf16[3,256,128]{2,1,0:T(8,128)(2,1)S(1)} %get-tuple-element.69), channel_id=1, source_target_pairs={{0,1},{1,0},{2,3},{3,2},{4,5},{5,4},{6,7},{7,6},{8,9},{9,8},{10,11... | collective-permute-start | bytes 589832 | tf_op jit(solution)/shard_map/ppermute | solution.py:41
  22.2 7.0 %collective-permute-start.1 = (bf16[3,256,128]{2,1,0:T(8,128)(2,1)S(1)}, bf16[3,256,128]{2,1,0:T(8,128)(2,1)S(1)}, u32[]{:S(2)}, u32[]{:S(2)}) collective-permute-start(bf16[3,256,128]{2,1,0:T(8,128)(2,1)S(1)} %get-tuple-element.64), channel_id=1, source_target_pairs={{0,1},{1,0},{2,3},{3,2},{4,5},{5,4},{6,7},{7,6},{8,9},{9,8},{10,11... | collective-permute-start | bytes 589832 | tf_op jit(solution)/shard_map/ppermute | solution.py:41
  22.3 6.9 %collective-permute-start.9 = (bf16[3,256,128]{2,1,0:T(8,128)(2,1)S(1)}, bf16[3,256,128]{2,1,0:T(8,128)(2,1)S(1)}, u32[]{:S(2)}, u32[]{:S(2)}) collective-permute-start(bf16[3,256,128]{2,1,0:T(8,128)(2,1)S(1)} %get-tuple-element.72), channel_id=1, source_target_pairs={{0,1},{1,0},{2,3},{3,2},{4,5},{5,4},{6,7},{7,6},{8,9},{9,8},{10,11... | collective-permute-start | bytes 589832 | tf_op jit(solution)/shard_map/ppermute | solution.py:41
  24.6 7.5 %collective-permute-start.8 = (bf16[3,256,128]{2,1,0:T(8,128)(2,1)S(1)}, bf16[3,256,128]{2,1,0:T(8,128)(2,1)S(1)}, u32[]{:S(2)}, u32[]{:S(2)}) collective-permute-start(bf16[3,256,128]{2,1,0:T(8,128)(2,1)S(1)} %shard_map.118.refs_0_), channel_id=1, source_target_pairs={{0,2},{1,3},{2,0},{3,1},{4,6},{5,7},{6,4},{7,5},{8,10},{9,11},{10,... | collective-permute-start | bytes 589832 | tf_op jit(solution)/shard_map/ppermute | solution.py:41
  29.2 7.2 %collective-permute-start.21 = (bf16[128,1024]{1,0:T(8,128)(2,1)S(1)}, bf16[128,1024]{1,0:T(8,128)(2,1)S(1)}, u32[]{:S(2)}, u32[]{:S(2)}) collective-permute-start(bf16[128,1024]{1,0:T(8,128)(2,1)S(1)} %collective-permute-done.7.refs_0_.first.c), channel_id=1, source_target_pairs={{0,4},{4,0},{8,12},{12,8},{16,20},{20,16},{24,28},{28,24},{1,5},{5... | collective-permute-start | bytes 786440 | tf_op jit(solution)/shard_map/ppermute | solution.py:41
  38.6 5.1 %collective-permute-start.13 = (bf16[1,512,128]{2,1,0:T(8,128)(2,1)S(1)}, bf16[1,512,128]{2,1,0:T(8,128)(2,1)S(1)}, u32[]{:S(2)}, u32[]{:S(2)}) collective-permute-start(bf16[1,512,128]{2,1,0:T(8,128)(2,1)S(1)} %bitcast.17), channel_id=1, source_target_pairs={{0,2},{1,3},{2,0},{3,1},{4,6},{5,7},{6,4},{7,5},{8,10},{9,11},{10,... | collective-permute-start | bytes 393224 | tf_op jit(solution)/shard_map/ppermute | solution.py:41
  39.8 5.1 %collective-permute-start.20 = (bf16[1,256,128]{2,1,0:T(8,128)(2,1)S(1)}, bf16[1,256,128]{2,1,0:T(8,128)(2,1)S(1)}, u32[]{:S(2)}, u32[]{:S(2)}) collective-permute-start(bf16[1,256,128]{2,1,0:T(8,128)(2,1)S(1)} %get-tuple-element.88), channel_id=1, source_target_pairs={{0,1},{1,0},{2,3},{3,2},{4,5},{5,4},{6,7},{7,6},{8,9},{9,8},{10,11... | collective-permute-start | bytes 196616 | tf_op jit(solution)/shard_map/ppermute | solution.py:41
  40.2 4.8 %collective-permute-start.24 = (bf16[1,256,128]{2,1,0:T(8,128)(2,1)S(1)}, bf16[1,256,128]{2,1,0:T(8,128)(2,1)S(1)}, u32[]{:S(2)}, u32[]{:S(2)}) collective-permute-start(bf16[1,256,128]{2,1,0:T(8,128)(2,1)S(1)} %get-tuple-element.92), channel_id=1, source_target_pairs={{0,1},{1,0},{2,3},{3,2},{4,5},{5,4},{6,7},{7,6},{8,9},{9,8},{10,11... | collective-permute-start | bytes 196616 | tf_op jit(solution)/shard_map/ppermute | solution.py:41
  40.4 4.7 %collective-permute-start.23 = (bf16[1,256,128]{2,1,0:T(8,128)(2,1)S(1)}, bf16[1,256,128]{2,1,0:T(8,128)(2,1)S(1)}, u32[]{:S(2)}, u32[]{:S(2)}) collective-permute-start(bf16[1,256,128]{2,1,0:T(8,128)(2,1)S(1)} %shard_map.126), channel_id=1, source_target_pairs={{0,2},{1,3},{2,0},{3,1},{4,6},{5,7},{6,4},{7,5},{8,10},{9,11},{10,... | collective-permute-start | bytes 196616 | tf_op jit(solution)/shard_map/ppermute | solution.py:41
  40.8 7.7 %collective-permute-start.14 = (bf16[1,512,128]{2,1,0:T(8,128)(2,1)S(1)}, bf16[1,512,128]{2,1,0:T(8,128)(2,1)S(1)}, u32[]{:S(2)}, u32[]{:S(2)}) collective-permute-start(bf16[1,512,128]{2,1,0:T(8,128)(2,1)S(1)} %bitcast.18), channel_id=1, source_target_pairs={{0,1},{1,0},{2,3},{3,2},{4,5},{5,4},{6,7},{7,6},{8,9},{9,8},{10,11... | collective-permute-start | bytes 393224 | tf_op jit(solution)/shard_map/ppermute | solution.py:41
  43.6 4.9 %collective-permute-start.15 = (bf16[1,512,128]{2,1,0:T(8,128)(2,1)S(1)}, bf16[1,512,128]{2,1,0:T(8,128)(2,1)S(1)}, u32[]{:S(2)}, u32[]{:S(2)}) collective-permute-start(bf16[1,512,128]{2,1,0:T(8,128)(2,1)S(1)} %collective-permute-done.13.far.refs_1_), channel_id=1, source_target_pairs={{0,1},{1,0},{2,3},{3,2},{4,5},{5,4},{6,7},{7,6},{8,9},{9,8},{10,11... | collective-permute-start | bytes 393224 | tf_op jit(solution)/shard_map/ppermute | solution.py:41
  47.2 9.9 %collective-permute-start.25 = (bf16[3,512,128]{2,1,0:T(8,128)(2,1)S(1)}, bf16[3,512,128]{2,1,0:T(8,128)(2,1)S(1)}, u32[]{:S(2)}, u32[]{:S(2)}) collective-permute-start(bf16[3,512,128]{2,1,0:T(8,128)(2,1)S(1)} %shard_map.128.own), channel_id=1, source_target_pairs={{0,2},{1,3},{2,0},{3,1},{4,6},{5,7},{6,4},{7,5},{8,10},{9,11},{10,... | collective-permute-start | bytes 1179656 | tf_op jit(solution)/shard_map/ppermute | solution.py:41
  49.1 6.7 %collective-permute-start.16 = (bf16[512,256]{1,0:T(8,128)(2,1)S(1)}, bf16[512,256]{1,0:T(8,128)(2,1)S(1)}, u32[]{:S(2)}, u32[]{:S(2)}) collective-permute-start(bf16[512,256]{1,0:T(8,128)(2,1)S(1)} %get-tuple-element.80), channel_id=1, source_target_pairs={{0,4},{4,0},{8,12},{12,8},{16,20},{20,16},{24,28},{28,24},{1,5},{5... | collective-permute-start | bytes 786440 | tf_op jit(solution)/shard_map/ppermute | solution.py:41
  49.2 6.7 %collective-permute-start.17 = (bf16[256,512]{1,0:T(8,128)(2,1)S(1)}, bf16[256,512]{1,0:T(8,128)(2,1)S(1)}, u32[]{:S(2)}, u32[]{:S(2)}) collective-permute-start(bf16[256,512]{1,0:T(8,128)(2,1)S(1)} %get-tuple-element.82), channel_id=1, source_target_pairs={{0,8},{4,12},{8,0},{12,4},{16,24},{20,28},{24,16},{28,20},{1,9},{5... | collective-permute-start | bytes 786440 | tf_op jit(solution)/shard_map/ppermute | solution.py:41
  51.2 9.6 %collective-permute-start.26 = (bf16[3,512,128]{2,1,0:T(8,128)(2,1)S(1)}, bf16[3,512,128]{2,1,0:T(8,128)(2,1)S(1)}, u32[]{:S(2)}, u32[]{:S(2)}) collective-permute-start(bf16[3,512,128]{2,1,0:T(8,128)(2,1)S(1)} %shard_map.128.own), channel_id=1, source_target_pairs={{0,1},{1,0},{2,3},{3,2},{4,5},{5,4},{6,7},{7,6},{8,9},{9,8},{10,11... | collective-permute-start | bytes 1179656 | tf_op jit(solution)/shard_map/ppermute | solution.py:41
  57.0 3.9 %collective-permute-start.27 = (bf16[3,512,128]{2,1,0:T(8,128)(2,1)S(1)}, bf16[3,512,128]{2,1,0:T(8,128)(2,1)S(1)}, u32[]{:S(2)}, u32[]{:S(2)}) collective-permute-start(bf16[3,512,128]{2,1,0:T(8,128)(2,1)S(1)} %shard_map.132.far), channel_id=1, source_target_pairs={{0,1},{1,0},{2,3},{3,2},{4,5},{5,4},{6,7},{7,6},{8,9},{9,8},{10,11... | collective-permute-start | bytes 1179656 | tf_op jit(solution)/shard_map/ppermute | solution.py:41
  58.9 5.2 %collective-permute-start.18 = (bf16[256,256]{1,0:T(8,128)(2,1)S(1)}, bf16[256,256]{1,0:T(8,128)(2,1)S(1)}, u32[]{:S(2)}, u32[]{:S(2)}) collective-permute-start(bf16[256,256]{1,0:T(8,128)(2,1)S(1)} %get-tuple-element.84), channel_id=1, source_target_pairs={{0,8},{4,12},{8,0},{12,4},{16,24},{20,28},{24,16},{28,20},{1,9},{5... | collective-permute-start | bytes 393224 | tf_op jit(solution)/shard_map/ppermute | solution.py:41
  60.3 4.8 %collective-permute-start.19 = (bf16[256,256]{1,0:T(8,128)(2,1)S(1)}, bf16[256,256]{1,0:T(8,128)(2,1)S(1)}, u32[]{:S(2)}, u32[]{:S(2)}) collective-permute-start(bf16[256,256]{1,0:T(8,128)(2,1)S(1)} %get-tuple-element.86), channel_id=1, source_target_pairs={{0,4},{4,0},{8,12},{12,8},{16,20},{20,16},{24,28},{28,24},{1,5},{5... | collective-permute-start | bytes 393224 | tf_op jit(solution)/shard_map/ppermute | solution.py:41
  62.6 8.6 %collective-permute-start.31 = (bf16[512,256]{1,0:T(8,128)(2,1)S(1)}, bf16[512,256]{1,0:T(8,128)(2,1)S(1)}, u32[]{:S(2)}, u32[]{:S(2)}) collective-permute-start(bf16[512,256]{1,0:T(8,128)(2,1)S(1)} %get-tuple-element.98.refs_0_), channel_id=1, source_target_pairs={{0,4},{4,0},{8,12},{12,8},{16,20},{20,16},{24,28},{28,24},{1,5},{5... | collective-permute-start | bytes 786440 | tf_op jit(solution)/shard_map/ppermute | solution.py:41
  63.5 7.7 %collective-permute-start.32 = (bf16[256,512]{1,0:T(8,128)(2,1)S(1)}, bf16[256,512]{1,0:T(8,128)(2,1)S(1)}, u32[]{:S(2)}, u32[]{:S(2)}) collective-permute-start(bf16[256,512]{1,0:T(8,128)(2,1)S(1)} %get-tuple-element.106), channel_id=1, source_target_pairs={{0,8},{4,12},{8,0},{12,4},{16,24},{20,28},{24,16},{28,20},{1,9},{5... | collective-permute-start | bytes 786440 | tf_op jit(solution)/shard_map/ppermute | solution.py:41
  71.4 3.9 %collective-permute-start.33 = (bf16[256,256]{1,0:T(8,128)(2,1)S(1)}, bf16[256,256]{1,0:T(8,128)(2,1)S(1)}, u32[]{:S(2)}, u32[]{:S(2)}) collective-permute-start(bf16[256,256]{1,0:T(8,128)(2,1)S(1)} %get-tuple-element.109), channel_id=1, source_target_pairs={{0,8},{4,12},{8,0},{12,4},{16,24},{20,28},{24,16},{28,20},{1,9},{5... | collective-permute-start | bytes 393224 | tf_op jit(solution)/shard_map/ppermute | solution.py:41
  72.4 4.6 %collective-permute-start.28 = (bf16[128,512]{1,0:T(8,128)(2,1)S(1)}, bf16[128,512]{1,0:T(8,128)(2,1)S(1)}, u32[]{:S(2)}, u32[]{:S(2)}) collective-permute-start(bf16[128,512]{1,0:T(8,128)(2,1)S(1)} %get-tuple-element.100.refs_0_), channel_id=1, source_target_pairs={{0,2},{1,3},{2,0},{3,1},{4,6},{5,7},{6,4},{7,5},{8,10},{9,11},{10,... | collective-permute-start | bytes 393224 | tf_op jit(solution)/shard_map/ppermute | solution.py:41
  75.7 11.8 %collective-permute-start.35 = (bf16[128,512]{1,0:T(8,128)(2,1)S(1)}, bf16[128,512]{1,0:T(8,128)(2,1)S(1)}, u32[]{:S(2)}, u32[]{:S(2)}) collective-permute-start(bf16[128,512]{1,0:T(8,128)(2,1)S(1)} %get-tuple-element.113), channel_id=1, source_target_pairs={{0,2},{1,3},{2,0},{3,1},{4,6},{5,7},{6,4},{7,5},{8,10},{9,11},{10,... | collective-permute-start | bytes 393224 | tf_op jit(solution)/shard_map/ppermute | solution.py:41
  77.1 16.1 %collective-permute-start.29 = (bf16[128,512]{1,0:T(8,128)(2,1)S(1)}, bf16[128,512]{1,0:T(8,128)(2,1)S(1)}, u32[]{:S(2)}, u32[]{:S(2)}) collective-permute-start(bf16[128,512]{1,0:T(8,128)(2,1)S(1)} %get-tuple-element.101), channel_id=1, source_target_pairs={{0,0},{1,8},{2,18},{3,26},{4,4},{5,12},{6,22},{7,30},{8,1},{9,9},{... | collective-permute-start | bytes 393224 | tf_op jit(solution)/shard_map/ppermute | solution.py:410
  83.6 9.6 %collective-permute-start.30 = (bf16[128,512]{1,0:T(8,128)(2,1)S(1)}, bf16[128,512]{1,0:T(8,128)(2,1)S(1)}, u32[]{:S(2)}, u32[]{:S(2)}) collective-permute-start(bf16[128,512]{1,0:T(8,128)(2,1)S(1)} %get-tuple-element.102), channel_id=1, source_target_pairs={{0,16},{1,24},{2,2},{3,10},{4,20},{5,28},{6,6},{7,14},{8,17},{9,25... | collective-permute-start | bytes 393224 | tf_op jit(solution)/shard_map/ppermute | solution.py:410
  87.6 7.5 %collective-permute-start.36 = (bf16[128,512]{1,0:T(8,128)(2,1)S(1)}, bf16[128,512]{1,0:T(8,128)(2,1)S(1)}, u32[]{:S(2)}, u32[]{:S(2)}) collective-permute-start(bf16[128,512]{1,0:T(8,128)(2,1)S(1)} %get-tuple-element.114), channel_id=1, source_target_pairs={{0,0},{1,8},{2,18},{3,26},{4,4},{5,12},{6,22},{7,30},{8,1},{9,9},{... | collective-permute-start | bytes 393224 | tf_op jit(solution)/shard_map/ppermute | solution.py:410
  90.4 8.1 %collective-permute-start.37 = (bf16[128,512]{1,0:T(8,128)(2,1)S(1)}, bf16[128,512]{1,0:T(8,128)(2,1)S(1)}, u32[]{:S(2)}, u32[]{:S(2)}) collective-permute-start(bf16[128,512]{1,0:T(8,128)(2,1)S(1)} %get-tuple-element.115), channel_id=1, source_target_pairs={{0,16},{1,24},{2,2},{3,10},{4,20},{5,28},{6,6},{7,14},{8,17},{9,25... | collective-permute-start | bytes 393224 | tf_op jit(solution)/shard_map/ppermute | solution.py:410
  (12 other events, 52.2 us)

commit v9 on v8

--- a/solution.py
+++ b/solution.py
@@ -430,25 +430,30 @@
 def weight_gradient(rows, values, after=()):
     depth, length = rows.shape
     groups, _, channels = values.shape
-    tile = depth // 2
+    tile = 256
+    steps = [(j, i) for j in range(groups) for i in range(depth // tile)]
 
     def body(rows, values, *refs):
-        out, mark = refs[len(after) :]
-        out[0] = dot(rows[...], values[0], (1, 0))
+        out, mark, ready, written = refs[len(after) :]
+        copies = []
+        for n, (j, i) in enumerate(steps):
+            at = slice(i * tile, (i + 1) * tile)
+            ready[j, at, :] = dot(rows[at, :], values[j], (1, 0))
+            copies.append(pltpu.make_async_copy(ready.at[j, at, :], out.at[j, at, :], written.at[n]))
+            copies[-1].start()
         mark[...] = jnp.zeros_like(mark)
-
+        for copy in copies:
+            copy.wait()
+
+    gradient = jax.ShapeDtypeStruct((groups, depth, channels), F32)
     return pl.pallas_call(
         body,
-        out_shape=(jax.ShapeDtypeStruct((groups, depth, channels), F32), jax.ShapeDtypeStruct((8, LANES), F32)),
-        grid=(groups, depth // tile),
-        in_specs=[
-            pl.BlockSpec((tile, length), lambda j, i: (i, 0)),
-            pl.BlockSpec((1, length, channels), lambda j, i: (j, 0, 0)),
-        ]
-        + [HBM] * len(after),
-        out_specs=(pl.BlockSpec((1, tile, channels), lambda j, i: (j, i, 0)), pl.BlockSpec((8, LANES), lambda j, i: (0, 0))),
+        out_shape=(gradient, jax.ShapeDtypeStruct((8, LANES), F32)),
+        in_specs=[VMEM] * 2 + [HBM] * len(after),
+        out_specs=(HBM, VMEM),
+        scratch_shapes=[pltpu.VMEM(gradient.shape, F32), pltpu.SemaphoreType.DMA((len(steps),))],
         compiler_params=pltpu.CompilerParams(vmem_limit_bytes=VMEM_LIMIT),
-        cost_estimate=cost(1.5 * groups),
+        cost_estimate=cost(1.0 * groups),
     )(rows, values, *after)
 
 
@@ -470,12 +475,11 @@
     grads_there, _ = channel_sums(grad_there, 1, out_weight[None], (gated,))
     gated = gated[None]
     gated_far = flipped(gated, "ctx", 2)
-    all_gated = all_channels(gated, gated_far)
-    whole_gated, keeps, gives = output_pieces(all_gated, out_weight[None])
+    grads = filter_backward(by_token(grads_here, grads_there), sum_of_three, tables, saved, length, width)
+    grads = later(grads, gated_far)
+    whole_gated, keeps, gives = output_pieces(all_channels(gated, later(gated_far, grads)), out_weight[None])
     givens = exchange(gives)
     mixed_halves = keeps, givens
-    grads = filter_backward(by_token(grads_here, grads_there), sum_of_three, tables, saved, length, width)
-    grads = later(grads, gated_far)
     grad_out, mark = weight_gradient(turned(grad_here + grad_there), whole_gated)
     token_rows = turned(here + there)
     grads_far = later(flipped(grads, "ctx", 2), *givens, keeps[0], token_rows, mark)

time: 99.5 us -> 98.6 us (level)
  Pallas kernels: 21.9 us -> 20.2 us
  waiting for transfers between devices: 25 us -> 26.4 us
    pallas_call x2, Pallas kernels: 6.58 us -> 4.7 us  [weight_gradient(): pl.pallas_call(body, out_shape=(gradient, jax.ShapeDtypeStruct((8, LANES)...]
    ppermute x32, waiting for transfers between devices: 17.3 us -> 18.7 us  [flipped(): lax.ppermute(value, axis, [(source, source ^ mask) for source in range(co...]
  transfers between devices with their start and end apart: 38 -> 38, of which waited for: 16 -> 17; matrix products, arithmetic and copies ran while one was open for 2% -> 2% of each run, Pallas kernels for 21% -> 19%
where the time goes in v9:
time: 98.6 us; the launch traced here: 98.3 us
  starting transfers between devices  46.2 us (47%)
  waiting for transfers between devices  26.4 us (27%)
  Pallas kernels  20.2 us (20%)
  local copies, waits for them, and re-layouts  3.9 us (4%)
    ppermute x32, starting transfers between devices, flipped(): lax.ppermute(value, axis, [(source, source ^ mask) for source in range(co...  27.4 us
    ppermute x32, waiting for transfers between devices, flipped(): lax.ppermute(value, axis, [(source, source ^ mask) for source in range(co...  18.7 us
    ppermute x4, starting transfers between devices, block_sums(): lax.ppermute(value, ('fsdp', 'ctx'), final_pairs(flip))  15.8 us
    pallas_call x2, Pallas kernels, weight_gradient(): pl.pallas_call(body, out_shape=(gradient, jax.ShapeDtypeStruct((8, LANES)...  4.7 us
    ppermute x4, waiting for transfers between devices, block_sums(): lax.ppermute(value, ('fsdp', 'ctx'), final_pairs(flip))  4.55 us
    pallas_call x4, Pallas kernels, project(): call(body, (jax.ShapeDtypeStruct((groups, length, width), F32), sums, sum...  3.76 us
    ppermute x2, waiting for transfers between devices, fetched(): return lax.ppermute(block, ('fsdp', 'ctx'), pairs)  3.19 us
    unnamed x12, local copies, waits for them, and re-layouts  3.14 us
  transfers between devices with their start and end apart: 38, of which 17 were waited for; matrix products, arithmetic and copies ran while one was open for 2% of the time, Pallas kernels for 19%

profile of v9, /device:TPU:1, one launch (start us, length us, event | category | flops | bytes accessed | tf_op | source)
XLA Modules:
  0.0 98.3 jit_solution(17813464406588534391)
XLA Ops:
  2.1 2.7 %collective-permute-start.2 = (bf16[128,1024]{1,0:T(8,128)(2,1)S(1)}, bf16[128,1024]{1,0:T(8,128)(2,1)S(1)}, u32[]{:S(2)}, u32[]{:S(2)}) collective-permute-start(bf16[128,1024]{1,0:T(8,128)(2,1)S(1)} %get-tuple-element.65), channel_id=1, source_target_pairs={{0,2},{1,3},{2,0},{3,1},{4,7},{5,6},{6,5},{7,4},{8,10},{9,11},{10,... | collective-permute-start | bytes 786440 | tf_op jit(solution)/shard_map/ppermute | solution.py:252
  4.8 1.9 %copy-done.1 = bf16[1024,3,512]{2,0,1:T(8,128)(2,1)S(1)} copy-done((bf16[1024,3,512]{2,0,1:T(8,128)(2,1)S(1)}, bf16[1024,3,512]{2,0,1:T(8,128)(2,1)}, u32[]{:S(2)}) %copy-start.1) | copy-done | bytes 3145752
  6.7 1.3 %shard_map.112 = (f32[3,256,128]{2,1,0:T(8,128)S(1)}, bf16[3,256,128]{2,1,0:T(8,128)(2,1)S(1)}, bf16[3,256,128]{2,1,0:T(8,128)(2,1)S(1)}, bf16[3,256,128]{2,1,0:T(8,128)(2,1)S(1)}) custom-call(bf16[128,1024]{1,0:T(8,128)(2,1)S(1)} %get-tuple-element.61.first.a, bf16[128,1024]{1,0:T(8,128)(2,1)S(1)} %collective-permute-done.second.b, ...), custom_call_target="tpu_custom_call" | custom-call | flops 1552499968 | tf_op jit(solution)/shard_map/pallas_call | solution.py:275
  10.0 1.4 %collective-permute-done.2.refs_0_ = bf16[128,1024]{1,0:T(8,128)(2,1)S(1)} collective-permute-done((bf16[128,1024]{1,0:T(8,128)(2,1)S(1)}, bf16[128,1024]{1,0:T(8,128)(2,1)S(1)}, u32[]{:S(2)}, u32[]{:S(2)}) %collective-permute-start.2) | collective-permute-done | bytes 262176 | tf_op jit(solution)/shard_map/ppermute | solution.py:252
  11.4 1.4 %collective-permute-start.4 = (bf16[128,1024]{1,0:T(8,128)(2,1)S(1)}, bf16[128,1024]{1,0:T(8,128)(2,1)S(1)}, u32[]{:S(2)}, u32[]{:S(2)}) collective-permute-start(bf16[128,1024]{1,0:T(8,128)(2,1)S(1)} %shard_map.114.first.refs_1_.c), channel_id=1, source_target_pairs={{0,4},{4,0},{8,12},{12,8},{16,20},{20,16},{24,28},{28,24},{1,5},{5... | collective-permute-start | bytes 786440 | tf_op jit(solution)/shard_map/ppermute | solution.py:41
  15.1 3.8 %collective-permute-done.5.refs_0_.refs_5_ = bf16[3,256,128]{2,1,0:T(8,128)(2,1)S(1)} collective-permute-done((bf16[3,256,128]{2,1,0:T(8,128)(2,1)S(1)}, bf16[3,256,128]{2,1,0:T(8,128)(2,1)S(1)}, u32[]{:S(2)}, u32[]{:S(2)}) %collective-permute-start.5) | collective-permute-done | bytes 196640 | tf_op jit(solution)/shard_map/ppermute | solution.py:41
  18.9 1.3 %shard_map.115 = (f32[3,256,128]{2,1,0:T(8,128)S(1)}, bf16[3,256,128]{2,1,0:T(8,128)(2,1)S(1)}, bf16[3,256,128]{2,1,0:T(8,128)(2,1)S(1)}, bf16[3,256,128]{2,1,0:T(8,128)(2,1)S(1)}) custom-call(bf16[128,1024]{1,0:T(8,128)(2,1)S(1)} %shard_map.114.first.refs_1_.c, bf16[128,1024]{1,0:T(8,128)(2,1)S(1)} %collective-permute-done.4.second.d, ...), custom_call_target="tpu_custom_call" | custom-call | flops 1552499968 | tf_op jit(solution)/shard_map/pallas_call | solution.py:275
  20.2 2.0 %collective-permute-start.6 = (bf16[3,256,128]{2,1,0:T(8,128)(2,1)S(1)}, bf16[3,256,128]{2,1,0:T(8,128)(2,1)S(1)}, u32[]{:S(2)}, u32[]{:S(2)}) collective-permute-start(bf16[3,256,128]{2,1,0:T(8,128)(2,1)S(1)} %get-tuple-element.69), channel_id=1, source_target_pairs={{0,1},{1,0},{2,3},{3,2},{4,5},{5,4},{6,7},{7,6},{8,9},{9,8},{10,11... | collective-permute-start | bytes 589832 | tf_op jit(solution)/shard_map/ppermute | solution.py:41
  22.8 1.8 %collective-permute-done.7.refs_0_.first.c = bf16[128,1024]{1,0:T(8,128)(2,1)S(1)} collective-permute-done((bf16[128,1024]{1,0:T(8,128)(2,1)S(1)}, bf16[128,1024]{1,0:T(8,128)(2,1)S(1)}, u32[]{:S(2)}, u32[]{:S(2)}) %collective-permute-start.7) | collective-permute-done | bytes 262176 | tf_op jit(solution)/shard_map/ppermute | solution.py:252
  24.6 1.3 %collective-permute-start.8 = (bf16[3,256,128]{2,1,0:T(8,128)(2,1)S(1)}, bf16[3,256,128]{2,1,0:T(8,128)(2,1)S(1)}, u32[]{:S(2)}, u32[]{:S(2)}) collective-permute-start(bf16[3,256,128]{2,1,0:T(8,128)(2,1)S(1)} %shard_map.118.refs_0_), channel_id=1, source_target_pairs={{0,2},{1,3},{2,0},{3,1},{4,6},{5,7},{6,4},{7,5},{8,10},{9,11},{10,... | collective-permute-start | bytes 589832 | tf_op jit(solution)/shard_map/ppermute | solution.py:41
  26.5 1.5 %collective-permute-start.11 = (bf16[1,256,128]{2,1,0:T(8,128)(2,1)S(1)}, bf16[1,256,128]{2,1,0:T(8,128)(2,1)S(1)}, u32[]{:S(2)}, u32[]{:S(2)}) collective-permute-start(bf16[1,256,128]{2,1,0:T(8,128)(2,1)S(1)} %get-tuple-element.76), channel_id=1, source_target_pairs={{0,1},{1,0},{2,3},{3,2},{4,5},{5,4},{6,7},{7,6},{8,9},{9,8},{10,11... | collective-permute-start | bytes 196616 | tf_op jit(solution)/shard_map/ppermute | solution.py:41
  29.2 2.9 %collective-permute-done.12.refs_11_.refs_5_ = bf16[1,256,128]{2,1,0:T(8,128)(2,1)S(1)} collective-permute-done((bf16[1,256,128]{2,1,0:T(8,128)(2,1)S(1)}, bf16[1,256,128]{2,1,0:T(8,128)(2,1)S(1)}, u32[]{:S(2)}, u32[]{:S(2)}) %collective-permute-start.12) | collective-permute-done | bytes 65568 | tf_op jit(solution)/shard_map/ppermute | solution.py:41
  32.1 2.2 %shard_map.121 = (f32[512,128]{1,0:T(8,128)S(1)}, f32[512,128]{1,0:T(8,128)S(1)}, f32[512,128]{1,0:T(8,128)S(1)}, f32[512,128]{1,0:T(8,128)S(1)}, bf16[512,128]{1,0:T(8,128)(2,1)S(1)}) custom-call(f32[3,256,128]{2,1,0:T(8,128)S(1)} %get-tuple-element.63.refs_0_, bf16[3,256,128]{2,1,0:T(8,128)(2,1)S(1)} %collective-permute-done.1.refs_1_, ...), custom_call_target="tpu_custom_call" | custom-call | flops 2415000064 | tf_op jit(solution)/shard_map/pallas_call | solution.py:185
  34.3 2.2 %collective-permute-done.15.second.d = bf16[128,1024]{1,0:T(8,128)(2,1)S(1)} collective-permute-done((bf16[128,1024]{1,0:T(8,128)(2,1)S(1)}, bf16[128,1024]{1,0:T(8,128)(2,1)S(1)}, u32[]{:S(2)}, u32[]{:S(2)}) %collective-permute-start.15) | collective-permute-done | bytes 262176 | tf_op jit(solution)/shard_map/ppermute | solution.py:41
  37.0 1.6 %collective-permute-start.16 = (bf16[1,256,128]{2,1,0:T(8,128)(2,1)S(1)}, bf16[1,256,128]{2,1,0:T(8,128)(2,1)S(1)}, u32[]{:S(2)}, u32[]{:S(2)}) collective-permute-start(bf16[1,256,128]{2,1,0:T(8,128)(2,1)S(1)} %get-tuple-element.81), channel_id=1, source_target_pairs={{0,1},{1,0},{2,3},{3,2},{4,5},{5,4},{6,7},{7,6},{8,9},{9,8},{10,11... | collective-permute-start | bytes 196616 | tf_op jit(solution)/shard_map/ppermute | solution.py:41
  42.7 2.3 %shard_map.124.refs_0_ = bf16[3,512,128]{2,1,0:T(8,128)(2,1)S(1)} custom-call(f32[1,256,128]{2,1,0:T(8,128)S(1)} %get-tuple-element.78.refs_0_, bf16[1,256,128]{2,1,0:T(8,128)(2,1)S(1)} %collective-permute-done.14.refs_1_, bf16[1,256,128]{2,1,0:T(8,128)(2,1)S(1)} %collective-permute-done.17.refs_2_, f32[1,256,128]{2,1,0:T(8,128)S(1)} %get-tuple-element.82.refs_3_, ...), custom_call_target="tpu_custom_call" | custom-call | flops 2415000064 | tf_op jit(solution)/shard_map/pallas_call | solution.py:205
  47.0 1.5 %collective-permute-start.25 = (bf16[3,512,128]{2,1,0:T(8,128)(2,1)S(1)}, bf16[3,512,128]{2,1,0:T(8,128)(2,1)S(1)}, u32[]{:S(2)}, u32[]{:S(2)}) collective-permute-start(bf16[3,512,128]{2,1,0:T(8,128)(2,1)S(1)} %shard_map.125.refs_1_.own), channel_id=1, source_target_pairs={{0,2},{1,3},{2,0},{3,1},{4,6},{5,7},{6,4},{7,5},{8,10},{9,11},{10,... | collective-permute-start | bytes 1179656 | tf_op jit(solution)/shard_map/ppermute | solution.py:41
  49.3 1.4 %collective-permute-start.22 = (bf16[256,512]{1,0:T(8,128)(2,1)S(1)}, bf16[256,512]{1,0:T(8,128)(2,1)S(1)}, u32[]{:S(2)}, u32[]{:S(2)}) collective-permute-start(bf16[256,512]{1,0:T(8,128)(2,1)S(1)} %get-tuple-element.92), channel_id=1, source_target_pairs={{0,8},{4,12},{8,0},{12,4},{16,24},{20,28},{24,16},{28,20},{1,9},{5... | collective-permute-start | bytes 786440 | tf_op jit(solution)/shard_map/ppermute | solution.py:41
  52.8 1.6 %shard_map.132 = (f32[1,1024,512]{2,1,0:T(8,128)}, f32[8,128]{1,0:T(8,128)S(1)}) custom-call(bf16[1024,512]{1,0:T(8,128)(2,1)S(1)} %shard_map.131.rows, bf16[1,512,512]{2,1,0:T(8,128)(2,1)S(1)} %get-tuple-element.88.whole.values), custom_call_target="tpu_custom_call" | custom-call | flops 1150000000 | tf_op jit(solution)/shard_map/pallas_call | solution.py:449
  54.5 2.4 %collective-permute-done.21.given_x.refs_1_ = bf16[512,256]{1,0:T(8,128)(2,1)S(1)} collective-permute-done((bf16[512,256]{1,0:T(8,128)(2,1)S(1)}, bf16[512,256]{1,0:T(8,128)(2,1)S(1)}, u32[]{:S(2)}, u32[]{:S(2)}) %collective-permute-start.21) | collective-permute-done | bytes 262176 | tf_op jit(solution)/shard_map/ppermute | solution.py:41
  58.7 1.4 %collective-permute-start.23 = (bf16[256,256]{1,0:T(8,128)(2,1)S(1)}, bf16[256,256]{1,0:T(8,128)(2,1)S(1)}, u32[]{:S(2)}, u32[]{:S(2)}) collective-permute-start(bf16[256,256]{1,0:T(8,128)(2,1)S(1)} %get-tuple-element.94), channel_id=1, source_target_pairs={{0,8},{4,12},{8,0},{12,4},{16,24},{20,28},{24,16},{28,20},{1,9},{5... | collective-permute-start | bytes 393224 | tf_op jit(solution)/shard_map/ppermute | solution.py:41
  60.9 1.7 %shard_map.134 = (bf16[3,512,512]{2,1,0:T(8,128)(2,1)S(1)}, bf16[512,256]{1,0:T(8,128)(2,1)S(1)}, bf16[256,512]{1,0:T(8,128)(2,1)S(1)}) custom-call(bf16[3,512,128]{2,1,0:T(8,128)(2,1)S(1)} %shard_map.125.refs_1_.own, bf16[3,512,128]{2,1,0:T(8,128)(2,1)S(1)} %shard_map.133.far, bf16[3,512,128]{2,1,0:T(8,128)(2,1)S(1)} %collective-permute-done.26.near, ...), custom_call_target="tpu_custom_call" | custom-call | flops 2070000000 | tf_op jit(solution)/shard_map/pallas_call | solution.py:341
  63.9 1.4 %shard_map.138 = (bf16[512,256]{1,0:T(8,128)(2,1)S(1)}, bf16[256,512]{1,0:T(8,128)(2,1)S(1)}) custom-call(bf16[3,512,512]{2,1,0:T(8,128)(2,1)S(1)} %get-tuple-element.103.whole.values, bf16[3,1024,512]{2,1,0:T(8,128)(2,1)S(1)} %bitcast.12), custom_call_target="tpu_custom_call" | custom-call | flops 1380000000 | tf_op jit(solution)/shard_map/pallas_call | solution.py:347
  65.5 3.1 %shard_map.139 = (f32[3,1024,512]{2,1,0:T(8,128)}, f32[8,128]{1,0:T(8,128)S(1)}) custom-call(bf16[1024,512]{1,0:T(8,128)(2,1)S(1)} %shard_map.130.refs_4_.rows, bf16[3,512,512]{2,1,0:T(8,128)(2,1)S(1)} %get-tuple-element.103.whole.values, bf16[128,512]{1,0:T(8,128)(2,1)S(1)} %get-tuple-element.100.refs_0_), custom_call_target="tpu_custom_call" | custom-call | flops 3449999872 | tf_op jit(solution)/shard_map/pallas_call | solution.py:449
  68.5 1.8 %collective-permute-done.31.given_x = bf16[512,256]{1,0:T(8,128)(2,1)S(1)} collective-permute-done((bf16[512,256]{1,0:T(8,128)(2,1)S(1)}, bf16[512,256]{1,0:T(8,128)(2,1)S(1)}, u32[]{:S(2)}, u32[]{:S(2)}) %collective-permute-start.31) | collective-permute-done | bytes 262176 | tf_op jit(solution)/shard_map/ppermute | solution.py:41
  71.8 1.6 %collective-permute-start.28 = (bf16[128,512]{1,0:T(8,128)(2,1)S(1)}, bf16[128,512]{1,0:T(8,128)(2,1)S(1)}, u32[]{:S(2)}, u32[]{:S(2)}) collective-permute-start(bf16[128,512]{1,0:T(8,128)(2,1)S(1)} %get-tuple-element.100.refs_0_), channel_id=1, source_target_pairs={{0,2},{1,3},{2,0},{3,1},{4,6},{5,7},{6,4},{7,5},{8,10},{9,11},{10,... | collective-permute-start | bytes 393224 | tf_op jit(solution)/shard_map/ppermute | solution.py:41
  76.4 6.3 %collective-permute-start.29 = (bf16[128,512]{1,0:T(8,128)(2,1)S(1)}, bf16[128,512]{1,0:T(8,128)(2,1)S(1)}, u32[]{:S(2)}, u32[]{:S(2)}) collective-permute-start(bf16[128,512]{1,0:T(8,128)(2,1)S(1)} %get-tuple-element.101), channel_id=1, source_target_pairs={{0,0},{1,8},{2,18},{3,26},{4,4},{5,12},{6,22},{7,30},{8,1},{9,9},{... | collective-permute-start | bytes 393224 | tf_op jit(solution)/shard_map/ppermute | solution.py:410
  82.7 3.9 %collective-permute-start.30 = (bf16[128,512]{1,0:T(8,128)(2,1)S(1)}, bf16[128,512]{1,0:T(8,128)(2,1)S(1)}, u32[]{:S(2)}, u32[]{:S(2)}) collective-permute-start(bf16[128,512]{1,0:T(8,128)(2,1)S(1)} %get-tuple-element.102), channel_id=1, source_target_pairs={{0,16},{1,24},{2,2},{3,10},{4,20},{5,28},{6,6},{7,14},{8,17},{9,25... | collective-permute-start | bytes 393224 | tf_op jit(solution)/shard_map/ppermute | solution.py:410
  86.8 2.7 %collective-permute-start.36 = (bf16[128,512]{1,0:T(8,128)(2,1)S(1)}, bf16[128,512]{1,0:T(8,128)(2,1)S(1)}, u32[]{:S(2)}, u32[]{:S(2)}) collective-permute-start(bf16[128,512]{1,0:T(8,128)(2,1)S(1)} %get-tuple-element.114), channel_id=1, source_target_pairs={{0,0},{1,8},{2,18},{3,26},{4,4},{5,12},{6,22},{7,30},{8,1},{9,9},{... | collective-permute-start | bytes 393224 | tf_op jit(solution)/shard_map/ppermute | solution.py:410
  89.5 2.8 %collective-permute-start.37 = (bf16[128,512]{1,0:T(8,128)(2,1)S(1)}, bf16[128,512]{1,0:T(8,128)(2,1)S(1)}, u32[]{:S(2)}, u32[]{:S(2)}) collective-permute-start(bf16[128,512]{1,0:T(8,128)(2,1)S(1)} %get-tuple-element.115), channel_id=1, source_target_pairs={{0,16},{1,24},{2,2},{3,10},{4,20},{5,28},{6,6},{7,14},{8,17},{9,25... | collective-permute-start | bytes 393224 | tf_op jit(solution)/shard_map/ppermute | solution.py:410
  93.1 1.4 %collective-permute-done.36.first = bf16[128,512]{1,0:T(8,128)(2,1)S(1)} collective-permute-done((bf16[128,512]{1,0:T(8,128)(2,1)S(1)}, bf16[128,512]{1,0:T(8,128)(2,1)S(1)}, u32[]{:S(2)}, u32[]{:S(2)}) %collective-permute-start.36) | collective-permute-done | bytes 131104 | tf_op jit(solution)/shard_map/ppermute | solution.py:410
  94.5 3.2 %collective-permute-done.37.second = bf16[128,512]{1,0:T(8,128)(2,1)S(1)} collective-permute-done((bf16[128,512]{1,0:T(8,128)(2,1)S(1)}, bf16[128,512]{1,0:T(8,128)(2,1)S(1)}, u32[]{:S(2)}, u32[]{:S(2)}) %collective-permute-start.37) | collective-permute-done | bytes 131104 | tf_op jit(solution)/shard_map/ppermute | solution.py:410
  (92 shorter events, 27.6 us)
Async XLA Ops:
  2.1 9.3 %collective-permute-start.2 = (bf16[128,1024]{1,0:T(8,128)(2,1)S(1)}, bf16[128,1024]{1,0:T(8,128)(2,1)S(1)}, u32[]{:S(2)}, u32[]{:S(2)}) collective-permute-start(bf16[128,1024]{1,0:T(8,128)(2,1)S(1)} %get-tuple-element.65), channel_id=1, source_target_pairs={{0,2},{1,3},{2,0},{3,1},{4,7},{5,6},{6,5},{7,4},{8,10},{9,11},{10,... | collective-permute-start | bytes 786440 | tf_op jit(solution)/shard_map/ppermute | solution.py:252
  11.4 7.5 %collective-permute-start.4 = (bf16[128,1024]{1,0:T(8,128)(2,1)S(1)}, bf16[128,1024]{1,0:T(8,128)(2,1)S(1)}, u32[]{:S(2)}, u32[]{:S(2)}) collective-permute-start(bf16[128,1024]{1,0:T(8,128)(2,1)S(1)} %shard_map.114.first.refs_1_.c), channel_id=1, source_target_pairs={{0,4},{4,0},{8,12},{12,8},{16,20},{20,16},{24,28},{28,24},{1,5},{5... | collective-permute-start | bytes 786440 | tf_op jit(solution)/shard_map/ppermute | solution.py:41
  12.8 6.1 %collective-permute-start.5 = (bf16[3,256,128]{2,1,0:T(8,128)(2,1)S(1)}, bf16[3,256,128]{2,1,0:T(8,128)(2,1)S(1)}, u32[]{:S(2)}, u32[]{:S(2)}) collective-permute-start(bf16[3,256,128]{2,1,0:T(8,128)(2,1)S(1)} %shard_map.113.refs_1_), channel_id=1, source_target_pairs={{0,2},{1,3},{2,0},{3,1},{4,6},{5,7},{6,4},{7,5},{8,10},{9,11},{10,... | collective-permute-start | bytes 589832 | tf_op jit(solution)/shard_map/ppermute | solution.py:41
  14.1 11.8 %collective-permute-start.10 = (bf16[128,1024]{1,0:T(8,128)(2,1)S(1)}, bf16[128,1024]{1,0:T(8,128)(2,1)S(1)}, u32[]{:S(2)}, u32[]{:S(2)}) collective-permute-start(bf16[128,1024]{1,0:T(8,128)(2,1)S(1)} %get-tuple-element.74), channel_id=1, source_target_pairs={{0,1},{1,0},{2,3},{3,2},{4,5},{5,4},{6,7},{7,6},{8,9},{9,8},{10,11... | collective-permute-start | bytes 786440 | tf_op jit(solution)/shard_map/ppermute | solution.py:41
  14.8 9.7 %collective-permute-start.7 = (bf16[128,1024]{1,0:T(8,128)(2,1)S(1)}, bf16[128,1024]{1,0:T(8,128)(2,1)S(1)}, u32[]{:S(2)}, u32[]{:S(2)}) collective-permute-start(bf16[128,1024]{1,0:T(8,128)(2,1)S(1)} %shard_map.117), channel_id=1, source_target_pairs={{0,2},{1,3},{2,0},{3,1},{4,7},{5,6},{6,5},{7,4},{8,10},{9,11},{10,... | collective-permute-start | bytes 786440 | tf_op jit(solution)/shard_map/ppermute | solution.py:252
  20.2 4.3 %collective-permute-start.6 = (bf16[3,256,128]{2,1,0:T(8,128)(2,1)S(1)}, bf16[3,256,128]{2,1,0:T(8,128)(2,1)S(1)}, u32[]{:S(2)}, u32[]{:S(2)}) collective-permute-start(bf16[3,256,128]{2,1,0:T(8,128)(2,1)S(1)} %get-tuple-element.69), channel_id=1, source_target_pairs={{0,1},{1,0},{2,3},{3,2},{4,5},{5,4},{6,7},{7,6},{8,9},{9,8},{10,11... | collective-permute-start | bytes 589832 | tf_op jit(solution)/shard_map/ppermute | solution.py:41
  22.3 7.0 %collective-permute-start.1 = (bf16[3,256,128]{2,1,0:T(8,128)(2,1)S(1)}, bf16[3,256,128]{2,1,0:T(8,128)(2,1)S(1)}, u32[]{:S(2)}, u32[]{:S(2)}) collective-permute-start(bf16[3,256,128]{2,1,0:T(8,128)(2,1)S(1)} %get-tuple-element.64), channel_id=1, source_target_pairs={{0,1},{1,0},{2,3},{3,2},{4,5},{5,4},{6,7},{7,6},{8,9},{9,8},{10,11... | collective-permute-start | bytes 589832 | tf_op jit(solution)/shard_map/ppermute | solution.py:41
  22.3 6.9 %collective-permute-start.9 = (bf16[3,256,128]{2,1,0:T(8,128)(2,1)S(1)}, bf16[3,256,128]{2,1,0:T(8,128)(2,1)S(1)}, u32[]{:S(2)}, u32[]{:S(2)}) collective-permute-start(bf16[3,256,128]{2,1,0:T(8,128)(2,1)S(1)} %get-tuple-element.72), channel_id=1, source_target_pairs={{0,1},{1,0},{2,3},{3,2},{4,5},{5,4},{6,7},{7,6},{8,9},{9,8},{10,11... | collective-permute-start | bytes 589832 | tf_op jit(solution)/shard_map/ppermute | solution.py:41
  24.6 7.5 %collective-permute-start.8 = (bf16[3,256,128]{2,1,0:T(8,128)(2,1)S(1)}, bf16[3,256,128]{2,1,0:T(8,128)(2,1)S(1)}, u32[]{:S(2)}, u32[]{:S(2)}) collective-permute-start(bf16[3,256,128]{2,1,0:T(8,128)(2,1)S(1)} %shard_map.118.refs_0_), channel_id=1, source_target_pairs={{0,2},{1,3},{2,0},{3,1},{4,6},{5,7},{6,4},{7,5},{8,10},{9,11},{10,... | collective-permute-start | bytes 589832 | tf_op jit(solution)/shard_map/ppermute | solution.py:41
  28.9 3.2 %collective-permute-start.12 = (bf16[1,256,128]{2,1,0:T(8,128)(2,1)S(1)}, bf16[1,256,128]{2,1,0:T(8,128)(2,1)S(1)}, u32[]{:S(2)}, u32[]{:S(2)}) collective-permute-start(bf16[1,256,128]{2,1,0:T(8,128)(2,1)S(1)} %shard_map.120), channel_id=1, source_target_pairs={{0,2},{1,3},{2,0},{3,1},{4,6},{5,7},{6,4},{7,5},{8,10},{9,11},{10,... | collective-permute-start | bytes 196616 | tf_op jit(solution)/shard_map/ppermute | solution.py:41
  29.2 7.2 %collective-permute-start.15 = (bf16[128,1024]{1,0:T(8,128)(2,1)S(1)}, bf16[128,1024]{1,0:T(8,128)(2,1)S(1)}, u32[]{:S(2)}, u32[]{:S(2)}) collective-permute-start(bf16[128,1024]{1,0:T(8,128)(2,1)S(1)} %collective-permute-done.7.refs_0_.first.c), channel_id=1, source_target_pairs={{0,4},{4,0},{8,12},{12,8},{16,20},{20,16},{24,28},{28,24},{1,5},{5... | collective-permute-start | bytes 786440 | tf_op jit(solution)/shard_map/ppermute | solution.py:41
  38.6 3.4 %collective-permute-start.14 = (bf16[1,256,128]{2,1,0:T(8,128)(2,1)S(1)}, bf16[1,256,128]{2,1,0:T(8,128)(2,1)S(1)}, u32[]{:S(2)}, u32[]{:S(2)}) collective-permute-start(bf16[1,256,128]{2,1,0:T(8,128)(2,1)S(1)} %get-tuple-element.79), channel_id=1, source_target_pairs={{0,1},{1,0},{2,3},{3,2},{4,5},{5,4},{6,7},{7,6},{8,9},{9,8},{10,11... | collective-permute-start | bytes 196616 | tf_op jit(solution)/shard_map/ppermute | solution.py:41
  38.6 3.3 %collective-permute-start.18 = (bf16[1,256,128]{2,1,0:T(8,128)(2,1)S(1)}, bf16[1,256,128]{2,1,0:T(8,128)(2,1)S(1)}, u32[]{:S(2)}, u32[]{:S(2)}) collective-permute-start(bf16[1,256,128]{2,1,0:T(8,128)(2,1)S(1)} %get-tuple-element.83), channel_id=1, source_target_pairs={{0,1},{1,0},{2,3},{3,2},{4,5},{5,4},{6,7},{7,6},{8,9},{9,8},{10,11... | collective-permute-start | bytes 196616 | tf_op jit(solution)/shard_map/ppermute | solution.py:41
  39.5 3.2 %collective-permute-start.17 = (bf16[1,256,128]{2,1,0:T(8,128)(2,1)S(1)}, bf16[1,256,128]{2,1,0:T(8,128)(2,1)S(1)}, u32[]{:S(2)}, u32[]{:S(2)}) collective-permute-start(bf16[1,256,128]{2,1,0:T(8,128)(2,1)S(1)} %shard_map.123), channel_id=1, source_target_pairs={{0,2},{1,3},{2,0},{3,1},{4,6},{5,7},{6,4},{7,5},{8,10},{9,11},{10,... | collective-permute-start | bytes 196616 | tf_op jit(solution)/shard_map/ppermute | solution.py:41
  40.8 4.9 %collective-permute-start.13 = (bf16[1,512,128]{2,1,0:T(8,128)(2,1)S(1)}, bf16[1,512,128]{2,1,0:T(8,128)(2,1)S(1)}, u32[]{:S(2)}, u32[]{:S(2)}) collective-permute-start(bf16[1,512,128]{2,1,0:T(8,128)(2,1)S(1)} %bitcast.17), channel_id=1, source_target_pairs={{0,2},{1,3},{2,0},{3,1},{4,6},{5,7},{6,4},{7,5},{8,10},{9,11},{10,... | collective-permute-start | bytes 393224 | tf_op jit(solution)/shard_map/ppermute | solution.py:41
  41.0 7.5 %collective-permute-start.19 = (bf16[1,512,128]{2,1,0:T(8,128)(2,1)S(1)}, bf16[1,512,128]{2,1,0:T(8,128)(2,1)S(1)}, u32[]{:S(2)}, u32[]{:S(2)}) collective-permute-start(bf16[1,512,128]{2,1,0:T(8,128)(2,1)S(1)} %bitcast.18), channel_id=1, source_target_pairs={{0,1},{1,0},{2,3},{3,2},{4,5},{5,4},{6,7},{7,6},{8,9},{9,8},{10,11... | collective-permute-start | bytes 393224 | tf_op jit(solution)/shard_map/ppermute | solution.py:41
  47.0 10.8 %collective-permute-start.25 = (bf16[3,512,128]{2,1,0:T(8,128)(2,1)S(1)}, bf16[3,512,128]{2,1,0:T(8,128)(2,1)S(1)}, u32[]{:S(2)}, u32[]{:S(2)}) collective-permute-start(bf16[3,512,128]{2,1,0:T(8,128)(2,1)S(1)} %shard_map.125.refs_1_.own), channel_id=1, source_target_pairs={{0,2},{1,3},{2,0},{3,1},{4,6},{5,7},{6,4},{7,5},{8,10},{9,11},{10,... | collective-permute-start | bytes 1179656 | tf_op jit(solution)/shard_map/ppermute | solution.py:41
  49.2 7.6 %collective-permute-start.21 = (bf16[512,256]{1,0:T(8,128)(2,1)S(1)}, bf16[512,256]{1,0:T(8,128)(2,1)S(1)}, u32[]{:S(2)}, u32[]{:S(2)}) collective-permute-start(bf16[512,256]{1,0:T(8,128)(2,1)S(1)} %get-tuple-element.90), channel_id=1, source_target_pairs={{0,4},{4,0},{8,12},{12,8},{16,20},{20,16},{24,28},{28,24},{1,5},{5... | collective-permute-start | bytes 786440 | tf_op jit(solution)/shard_map/ppermute | solution.py:41
  49.3 7.5 %collective-permute-start.22 = (bf16[256,512]{1,0:T(8,128)(2,1)S(1)}, bf16[256,512]{1,0:T(8,128)(2,1)S(1)}, u32[]{:S(2)}, u32[]{:S(2)}) collective-permute-start(bf16[256,512]{1,0:T(8,128)(2,1)S(1)} %get-tuple-element.92), channel_id=1, source_target_pairs={{0,8},{4,12},{8,0},{12,4},{16,24},{20,28},{24,16},{28,20},{1,9},{5... | collective-permute-start | bytes 786440 | tf_op jit(solution)/shard_map/ppermute | solution.py:41
  51.3 9.6 %collective-permute-start.26 = (bf16[3,512,128]{2,1,0:T(8,128)(2,1)S(1)}, bf16[3,512,128]{2,1,0:T(8,128)(2,1)S(1)}, u32[]{:S(2)}, u32[]{:S(2)}) collective-permute-start(bf16[3,512,128]{2,1,0:T(8,128)(2,1)S(1)} %shard_map.125.refs_1_.own), channel_id=1, source_target_pairs={{0,1},{1,0},{2,3},{3,2},{4,5},{5,4},{6,7},{7,6},{8,9},{9,8},{10,11... | collective-permute-start | bytes 1179656 | tf_op jit(solution)/shard_map/ppermute | solution.py:41
  58.7 6.7 %collective-permute-start.23 = (bf16[256,256]{1,0:T(8,128)(2,1)S(1)}, bf16[256,256]{1,0:T(8,128)(2,1)S(1)}, u32[]{:S(2)}, u32[]{:S(2)}) collective-permute-start(bf16[256,256]{1,0:T(8,128)(2,1)S(1)} %get-tuple-element.94), channel_id=1, source_target_pairs={{0,8},{4,12},{8,0},{12,4},{16,24},{20,28},{24,16},{28,20},{1,9},{5... | collective-permute-start | bytes 393224 | tf_op jit(solution)/shard_map/ppermute | solution.py:41
  60.1 5.3 %collective-permute-start.24 = (bf16[256,256]{1,0:T(8,128)(2,1)S(1)}, bf16[256,256]{1,0:T(8,128)(2,1)S(1)}, u32[]{:S(2)}, u32[]{:S(2)}) collective-permute-start(bf16[256,256]{1,0:T(8,128)(2,1)S(1)} %get-tuple-element.96), channel_id=1, source_target_pairs={{0,4},{4,0},{8,12},{12,8},{16,20},{20,16},{24,28},{28,24},{1,5},{5... | collective-permute-start | bytes 393224 | tf_op jit(solution)/shard_map/ppermute | solution.py:41
  62.7 7.6 %collective-permute-start.31 = (bf16[512,256]{1,0:T(8,128)(2,1)S(1)}, bf16[512,256]{1,0:T(8,128)(2,1)S(1)}, u32[]{:S(2)}, u32[]{:S(2)}) collective-permute-start(bf16[512,256]{1,0:T(8,128)(2,1)S(1)} %get-tuple-element.98.refs_0_), channel_id=1, source_target_pairs={{0,4},{4,0},{8,12},{12,8},{16,20},{20,16},{24,28},{28,24},{1,5},{5... | collective-permute-start | bytes 786440 | tf_op jit(solution)/shard_map/ppermute | solution.py:41
  63.3 7.0 %collective-permute-start.32 = (bf16[256,512]{1,0:T(8,128)(2,1)S(1)}, bf16[256,512]{1,0:T(8,128)(2,1)S(1)}, u32[]{:S(2)}, u32[]{:S(2)}) collective-permute-start(bf16[256,512]{1,0:T(8,128)(2,1)S(1)} %get-tuple-element.106), channel_id=1, source_target_pairs={{0,8},{4,12},{8,0},{12,4},{16,24},{20,28},{24,16},{28,20},{1,9},{5... | collective-permute-start | bytes 786440 | tf_op jit(solution)/shard_map/ppermute | solution.py:41
  70.5 3.9 %collective-permute-start.33 = (bf16[256,256]{1,0:T(8,128)(2,1)S(1)}, bf16[256,256]{1,0:T(8,128)(2,1)S(1)}, u32[]{:S(2)}, u32[]{:S(2)}) collective-permute-start(bf16[256,256]{1,0:T(8,128)(2,1)S(1)} %get-tuple-element.109), channel_id=1, source_target_pairs={{0,8},{4,12},{8,0},{12,4},{16,24},{20,28},{24,16},{28,20},{1,9},{5... | collective-permute-start | bytes 393224 | tf_op jit(solution)/shard_map/ppermute | solution.py:41
  71.3 3.8 %collective-permute-start.34 = (bf16[256,256]{1,0:T(8,128)(2,1)S(1)}, bf16[256,256]{1,0:T(8,128)(2,1)S(1)}, u32[]{:S(2)}, u32[]{:S(2)}) collective-permute-start(bf16[256,256]{1,0:T(8,128)(2,1)S(1)} %get-tuple-element.111), channel_id=1, source_target_pairs={{0,4},{4,0},{8,12},{12,8},{16,20},{20,16},{24,28},{28,24},{1,5},{5... | collective-permute-start | bytes 393224 | tf_op jit(solution)/shard_map/ppermute | solution.py:41
  71.8 4.5 %collective-permute-start.28 = (bf16[128,512]{1,0:T(8,128)(2,1)S(1)}, bf16[128,512]{1,0:T(8,128)(2,1)S(1)}, u32[]{:S(2)}, u32[]{:S(2)}) collective-permute-start(bf16[128,512]{1,0:T(8,128)(2,1)S(1)} %get-tuple-element.100.refs_0_), channel_id=1, source_target_pairs={{0,2},{1,3},{2,0},{3,1},{4,6},{5,7},{6,4},{7,5},{8,10},{9,11},{10,... | collective-permute-start | bytes 393224 | tf_op jit(solution)/shard_map/ppermute | solution.py:41
  75.2 11.5 %collective-permute-start.35 = (bf16[128,512]{1,0:T(8,128)(2,1)S(1)}, bf16[128,512]{1,0:T(8,128)(2,1)S(1)}, u32[]{:S(2)}, u32[]{:S(2)}) collective-permute-start(bf16[128,512]{1,0:T(8,128)(2,1)S(1)} %get-tuple-element.113), channel_id=1, source_target_pairs={{0,2},{1,3},{2,0},{3,1},{4,6},{5,7},{6,4},{7,5},{8,10},{9,11},{10,... | collective-permute-start | bytes 393224 | tf_op jit(solution)/shard_map/ppermute | solution.py:41
  76.4 16.0 %collective-permute-start.29 = (bf16[128,512]{1,0:T(8,128)(2,1)S(1)}, bf16[128,512]{1,0:T(8,128)(2,1)S(1)}, u32[]{:S(2)}, u32[]{:S(2)}) collective-permute-start(bf16[128,512]{1,0:T(8,128)(2,1)S(1)} %get-tuple-element.101), channel_id=1, source_target_pairs={{0,0},{1,8},{2,18},{3,26},{4,4},{5,12},{6,22},{7,30},{8,1},{9,9},{... | collective-permute-start | bytes 393224 | tf_op jit(solution)/shard_map/ppermute | solution.py:410
  82.7 9.6 %collective-permute-start.30 = (bf16[128,512]{1,0:T(8,128)(2,1)S(1)}, bf16[128,512]{1,0:T(8,128)(2,1)S(1)}, u32[]{:S(2)}, u32[]{:S(2)}) collective-permute-start(bf16[128,512]{1,0:T(8,128)(2,1)S(1)} %get-tuple-element.102), channel_id=1, source_target_pairs={{0,16},{1,24},{2,2},{3,10},{4,20},{5,28},{6,6},{7,14},{8,17},{9,25... | collective-permute-start | bytes 393224 | tf_op jit(solution)/shard_map/ppermute | solution.py:410
  86.8 7.7 %collective-permute-start.36 = (bf16[128,512]{1,0:T(8,128)(2,1)S(1)}, bf16[128,512]{1,0:T(8,128)(2,1)S(1)}, u32[]{:S(2)}, u32[]{:S(2)}) collective-permute-start(bf16[128,512]{1,0:T(8,128)(2,1)S(1)} %get-tuple-element.114), channel_id=1, source_target_pairs={{0,0},{1,8},{2,18},{3,26},{4,4},{5,12},{6,22},{7,30},{8,1},{9,9},{... | collective-permute-start | bytes 393224 | tf_op jit(solution)/shard_map/ppermute | solution.py:410
  89.5 8.1 %collective-permute-start.37 = (bf16[128,512]{1,0:T(8,128)(2,1)S(1)}, bf16[128,512]{1,0:T(8,128)(2,1)S(1)}, u32[]{:S(2)}, u32[]{:S(2)}) collective-permute-start(bf16[128,512]{1,0:T(8,128)(2,1)S(1)} %get-tuple-element.115), channel_id=1, source_target_pairs={{0,16},{1,24},{2,2},{3,10},{4,20},{5,28},{6,6},{7,14},{8,17},{9,25... | collective-permute-start | bytes 393224 | tf_op jit(solution)/shard_map/ppermute | solution.py:410
  (12 other events, 50.2 us)

commit v10 on v9

--- a/solution.py
+++ b/solution.py
@@ -471,7 +471,7 @@
     feats_there, passed = channel_sums(there, 1, weights, feats_here[2:], (grad_far,))
     grads_here, _ = channel_sums(grad_here, 0, out_weight[None], (passed,))
     feats = by_token(feats_here, feats_there)
-    *saved, gated = filter_forward(feats, sum_of_three, tables, length, width, grads_here[2:])
+    *saved, gated = filter_forward(feats, sum_of_three, tables, length, width, (grads_here[2], grad_there[1]))
     grads_there, _ = channel_sums(grad_there, 1, out_weight[None], (gated,))
     gated = gated[None]
     gated_far = flipped(gated, "ctx", 2)

time: 98.6 us -> 98.2 us (level)
  waiting for transfers between devices: 26.4 us -> 25 us
    ppermute x32, waiting for transfers between devices: 18.7 us -> 17.3 us  [flipped(): lax.ppermute(value, axis, [(source, source ^ mask) for source in range(co...]
  transfers between devices with their start and end apart: 38 -> 38, of which waited for: 17 -> 17; matrix products, arithmetic and copies ran while one was open for 2% -> 2% of each run, Pallas kernels for 19% -> 17%
where the time goes in v10:
time: 98.2 us; the launch traced here: 97.9 us
  starting transfers between devices  47.1 us (48%)
  waiting for transfers between devices  25 us (25%)
  Pallas kernels  20.2 us (21%)
  local copies, waits for them, and re-layouts  3.9 us (4%)
    ppermute x32, starting transfers between devices, flipped(): lax.ppermute(value, axis, [(source, source ^ mask) for source in range(co...  27.3 us
    ppermute x32, waiting for transfers between devices, flipped(): lax.ppermute(value, axis, [(source, source ^ mask) for source in range(co...  17.3 us
    ppermute x4, starting transfers between devices, block_sums(): lax.ppermute(value, ('fsdp', 'ctx'), final_pairs(flip))  16.8 us
    pallas_call x2, Pallas kernels, weight_gradient(): pl.pallas_call(body, out_shape=(gradient, jax.ShapeDtypeStruct((8, LANES)...  4.7 us
    ppermute x4, waiting for transfers between devices, block_sums(): lax.ppermute(value, ('fsdp', 'ctx'), final_pairs(flip))  4.55 us
    pallas_call x4, Pallas kernels, project(): call(body, (jax.ShapeDtypeStruct((groups, length, width), F32), sums, sum...  3.77 us
    ppermute x2, waiting for transfers between devices, fetched(): return lax.ppermute(block, ('fsdp', 'ctx'), pairs)  3.19 us
    unnamed x12, local copies, waits for them, and re-layouts  3.14 us
  transfers between devices with their start and end apart: 38, of which 17 were waited for; matrix products, arithmetic and copies ran while one was open for 2% of the time, Pallas kernels for 17%

profile of v10, /device:TPU:1, one launch (start us, length us, event | category | flops | bytes accessed | tf_op | source)
XLA Modules:
  0.0 97.9 jit_solution(15574976187253821979)
XLA Ops:
  2.1 2.7 %collective-permute-start.2 = (bf16[128,1024]{1,0:T(8,128)(2,1)S(1)}, bf16[128,1024]{1,0:T(8,128)(2,1)S(1)}, u32[]{:S(2)}, u32[]{:S(2)}) collective-permute-start(bf16[128,1024]{1,0:T(8,128)(2,1)S(1)} %get-tuple-element.65), channel_id=1, source_target_pairs={{0,2},{1,3},{2,0},{3,1},{4,7},{5,6},{6,5},{7,4},{8,10},{9,11},{10,... | collective-permute-start | bytes 786440 | tf_op jit(solution)/shard_map/ppermute | solution.py:252
  4.8 1.9 %copy-done.1 = bf16[1024,3,512]{2,0,1:T(8,128)(2,1)S(1)} copy-done((bf16[1024,3,512]{2,0,1:T(8,128)(2,1)S(1)}, bf16[1024,3,512]{2,0,1:T(8,128)(2,1)}, u32[]{:S(2)}) %copy-start.1) | copy-done | bytes 3145752
  6.7 1.3 %shard_map.112 = (f32[3,256,128]{2,1,0:T(8,128)S(1)}, bf16[3,256,128]{2,1,0:T(8,128)(2,1)S(1)}, bf16[3,256,128]{2,1,0:T(8,128)(2,1)S(1)}, bf16[3,256,128]{2,1,0:T(8,128)(2,1)S(1)}) custom-call(bf16[128,1024]{1,0:T(8,128)(2,1)S(1)} %get-tuple-element.61.first.a, bf16[128,1024]{1,0:T(8,128)(2,1)S(1)} %collective-permute-done.second.b, ...), custom_call_target="tpu_custom_call" | custom-call | flops 1552499968 | tf_op jit(solution)/shard_map/pallas_call | solution.py:275
  10.0 1.4 %collective-permute-done.2.refs_0_ = bf16[128,1024]{1,0:T(8,128)(2,1)S(1)} collective-permute-done((bf16[128,1024]{1,0:T(8,128)(2,1)S(1)}, bf16[128,1024]{1,0:T(8,128)(2,1)S(1)}, u32[]{:S(2)}, u32[]{:S(2)}) %collective-permute-start.2) | collective-permute-done | bytes 262176 | tf_op jit(solution)/shard_map/ppermute | solution.py:252
  11.4 1.4 %collective-permute-start.4 = (bf16[128,1024]{1,0:T(8,128)(2,1)S(1)}, bf16[128,1024]{1,0:T(8,128)(2,1)S(1)}, u32[]{:S(2)}, u32[]{:S(2)}) collective-permute-start(bf16[128,1024]{1,0:T(8,128)(2,1)S(1)} %shard_map.114.first.refs_1_.c), channel_id=1, source_target_pairs={{0,4},{4,0},{8,12},{12,8},{16,20},{20,16},{24,28},{28,24},{1,5},{5... | collective-permute-start | bytes 786440 | tf_op jit(solution)/shard_map/ppermute | solution.py:41
  12.8 1.2 %collective-permute-start.5 = (bf16[3,256,128]{2,1,0:T(8,128)(2,1)S(1)}, bf16[3,256,128]{2,1,0:T(8,128)(2,1)S(1)}, u32[]{:S(2)}, u32[]{:S(2)}) collective-permute-start(bf16[3,256,128]{2,1,0:T(8,128)(2,1)S(1)} %shard_map.113.refs_1_), channel_id=1, source_target_pairs={{0,2},{1,3},{2,0},{3,1},{4,6},{5,7},{6,4},{7,5},{8,10},{9,11},{10,... | collective-permute-start | bytes 589832 | tf_op jit(solution)/shard_map/ppermute | solution.py:41
  15.1 3.8 %collective-permute-done.5.refs_0_.refs_5_ = bf16[3,256,128]{2,1,0:T(8,128)(2,1)S(1)} collective-permute-done((bf16[3,256,128]{2,1,0:T(8,128)(2,1)S(1)}, bf16[3,256,128]{2,1,0:T(8,128)(2,1)S(1)}, u32[]{:S(2)}, u32[]{:S(2)}) %collective-permute-start.5) | collective-permute-done | bytes 196640 | tf_op jit(solution)/shard_map/ppermute | solution.py:41
  18.9 1.3 %shard_map.115 = (f32[3,256,128]{2,1,0:T(8,128)S(1)}, bf16[3,256,128]{2,1,0:T(8,128)(2,1)S(1)}, bf16[3,256,128]{2,1,0:T(8,128)(2,1)S(1)}, bf16[3,256,128]{2,1,0:T(8,128)(2,1)S(1)}) custom-call(bf16[128,1024]{1,0:T(8,128)(2,1)S(1)} %shard_map.114.first.refs_1_.c, bf16[128,1024]{1,0:T(8,128)(2,1)S(1)} %collective-permute-done.4.second.d, ...), custom_call_target="tpu_custom_call" | custom-call | flops 1552499968 | tf_op jit(solution)/shard_map/pallas_call | solution.py:275
  20.2 2.0 %collective-permute-start.6 = (bf16[3,256,128]{2,1,0:T(8,128)(2,1)S(1)}, bf16[3,256,128]{2,1,0:T(8,128)(2,1)S(1)}, u32[]{:S(2)}, u32[]{:S(2)}) collective-permute-start(bf16[3,256,128]{2,1,0:T(8,128)(2,1)S(1)} %get-tuple-element.69), channel_id=1, source_target_pairs={{0,1},{1,0},{2,3},{3,2},{4,5},{5,4},{6,7},{7,6},{8,9},{9,8},{10,11... | collective-permute-start | bytes 589832 | tf_op jit(solution)/shard_map/ppermute | solution.py:41
  22.8 1.8 %collective-permute-done.7.refs_0_.first.c = bf16[128,1024]{1,0:T(8,128)(2,1)S(1)} collective-permute-done((bf16[128,1024]{1,0:T(8,128)(2,1)S(1)}, bf16[128,1024]{1,0:T(8,128)(2,1)S(1)}, u32[]{:S(2)}, u32[]{:S(2)}) %collective-permute-start.7) | collective-permute-done | bytes 262176 | tf_op jit(solution)/shard_map/ppermute | solution.py:252
  25.2 1.4 %collective-permute-start.8 = (bf16[3,256,128]{2,1,0:T(8,128)(2,1)S(1)}, bf16[3,256,128]{2,1,0:T(8,128)(2,1)S(1)}, u32[]{:S(2)}, u32[]{:S(2)}) collective-permute-start(bf16[3,256,128]{2,1,0:T(8,128)(2,1)S(1)} %shard_map.118.refs_0_), channel_id=1, source_target_pairs={{0,2},{1,3},{2,0},{3,1},{4,6},{5,7},{6,4},{7,5},{8,10},{9,11},{10,... | collective-permute-start | bytes 589832 | tf_op jit(solution)/shard_map/ppermute | solution.py:41
  29.2 1.9 %collective-permute-done.13.refs_12_.second.d = bf16[128,1024]{1,0:T(8,128)(2,1)S(1)} collective-permute-done((bf16[128,1024]{1,0:T(8,128)(2,1)S(1)}, bf16[128,1024]{1,0:T(8,128)(2,1)S(1)}, u32[]{:S(2)}, u32[]{:S(2)}) %collective-permute-start.13) | collective-permute-done | bytes 262176 | tf_op jit(solution)/shard_map/ppermute | solution.py:41
  31.1 2.0 %collective-permute-done.12.refs_11_.refs_5_ = bf16[1,256,128]{2,1,0:T(8,128)(2,1)S(1)} collective-permute-done((bf16[1,256,128]{2,1,0:T(8,128)(2,1)S(1)}, bf16[1,256,128]{2,1,0:T(8,128)(2,1)S(1)}, u32[]{:S(2)}, u32[]{:S(2)}) %collective-permute-start.12) | collective-permute-done | bytes 65568 | tf_op jit(solution)/shard_map/ppermute | solution.py:41
  33.2 2.2 %shard_map.121 = (f32[512,128]{1,0:T(8,128)S(1)}, f32[512,128]{1,0:T(8,128)S(1)}, f32[512,128]{1,0:T(8,128)S(1)}, f32[512,128]{1,0:T(8,128)S(1)}, bf16[512,128]{1,0:T(8,128)(2,1)S(1)}) custom-call(f32[3,256,128]{2,1,0:T(8,128)S(1)} %get-tuple-element.63.refs_0_, bf16[3,256,128]{2,1,0:T(8,128)(2,1)S(1)} %collective-permute-done.1.refs_1_, ...), custom_call_target="tpu_custom_call" | custom-call | flops 2415000064 | tf_op jit(solution)/shard_map/pallas_call | solution.py:185
  37.7 1.4 %collective-permute-start.17 = (bf16[1,256,128]{2,1,0:T(8,128)(2,1)S(1)}, bf16[1,256,128]{2,1,0:T(8,128)(2,1)S(1)}, u32[]{:S(2)}, u32[]{:S(2)}) collective-permute-start(bf16[1,256,128]{2,1,0:T(8,128)(2,1)S(1)} %shard_map.123), channel_id=1, source_target_pairs={{0,2},{1,3},{2,0},{3,1},{4,6},{5,7},{6,4},{7,5},{8,10},{9,11},{10,... | collective-permute-start | bytes 196616 | tf_op jit(solution)/shard_map/ppermute | solution.py:41
  40.8 2.3 %shard_map.124.refs_0_ = bf16[3,512,128]{2,1,0:T(8,128)(2,1)S(1)} custom-call(f32[1,256,128]{2,1,0:T(8,128)S(1)} %get-tuple-element.78.refs_0_, bf16[1,256,128]{2,1,0:T(8,128)(2,1)S(1)} %collective-permute-done.15.refs_1_, bf16[1,256,128]{2,1,0:T(8,128)(2,1)S(1)} %collective-permute-done.17.refs_2_, f32[1,256,128]{2,1,0:T(8,128)S(1)} %get-tuple-element.82.refs_3_, ...), custom_call_target="tpu_custom_call" | custom-call | flops 2415000064 | tf_op jit(solution)/shard_map/pallas_call | solution.py:205
  43.9 1.3 %collective-permute-start.20 = (bf16[1,512,128]{2,1,0:T(8,128)(2,1)S(1)}, bf16[1,512,128]{2,1,0:T(8,128)(2,1)S(1)}, u32[]{:S(2)}, u32[]{:S(2)}) collective-permute-start(bf16[1,512,128]{2,1,0:T(8,128)(2,1)S(1)} %shard_map.126.far), channel_id=1, source_target_pairs={{0,1},{1,0},{2,3},{3,2},{4,5},{5,4},{6,7},{7,6},{8,9},{9,8},{10,11... | collective-permute-start | bytes 393224 | tf_op jit(solution)/shard_map/ppermute | solution.py:41
  45.1 1.6 %collective-permute-start.25 = (bf16[3,512,128]{2,1,0:T(8,128)(2,1)S(1)}, bf16[3,512,128]{2,1,0:T(8,128)(2,1)S(1)}, u32[]{:S(2)}, u32[]{:S(2)}) collective-permute-start(bf16[3,512,128]{2,1,0:T(8,128)(2,1)S(1)} %shard_map.125.refs_1_.own), channel_id=1, source_target_pairs={{0,2},{1,3},{2,0},{3,1},{4,6},{5,7},{6,4},{7,5},{8,10},{9,11},{10,... | collective-permute-start | bytes 1179656 | tf_op jit(solution)/shard_map/ppermute | solution.py:41
  48.6 1.3 %collective-permute-start.22 = (bf16[256,512]{1,0:T(8,128)(2,1)S(1)}, bf16[256,512]{1,0:T(8,128)(2,1)S(1)}, u32[]{:S(2)}, u32[]{:S(2)}) collective-permute-start(bf16[256,512]{1,0:T(8,128)(2,1)S(1)} %get-tuple-element.92), channel_id=1, source_target_pairs={{0,8},{4,12},{8,0},{12,4},{16,24},{20,28},{24,16},{28,20},{1,9},{5... | collective-permute-start | bytes 786440 | tf_op jit(solution)/shard_map/ppermute | solution.py:41
  52.1 1.6 %shard_map.132 = (f32[1,1024,512]{2,1,0:T(8,128)}, f32[8,128]{1,0:T(8,128)S(1)}) custom-call(bf16[1024,512]{1,0:T(8,128)(2,1)S(1)} %shard_map.131.rows, bf16[1,512,512]{2,1,0:T(8,128)(2,1)S(1)} %get-tuple-element.88.whole.values), custom_call_target="tpu_custom_call" | custom-call | flops 1150000000 | tf_op jit(solution)/shard_map/pallas_call | solution.py:449
  57.4 1.4 %collective-permute-start.23 = (bf16[256,256]{1,0:T(8,128)(2,1)S(1)}, bf16[256,256]{1,0:T(8,128)(2,1)S(1)}, u32[]{:S(2)}, u32[]{:S(2)}) collective-permute-start(bf16[256,256]{1,0:T(8,128)(2,1)S(1)} %get-tuple-element.94), channel_id=1, source_target_pairs={{0,8},{4,12},{8,0},{12,4},{16,24},{20,28},{24,16},{28,20},{1,9},{5... | collective-permute-start | bytes 393224 | tf_op jit(solution)/shard_map/ppermute | solution.py:41
  59.9 1.7 %shard_map.134 = (bf16[3,512,512]{2,1,0:T(8,128)(2,1)S(1)}, bf16[512,256]{1,0:T(8,128)(2,1)S(1)}, bf16[256,512]{1,0:T(8,128)(2,1)S(1)}) custom-call(bf16[3,512,128]{2,1,0:T(8,128)(2,1)S(1)} %shard_map.125.refs_1_.own, bf16[3,512,128]{2,1,0:T(8,128)(2,1)S(1)} %shard_map.133.far, bf16[3,512,128]{2,1,0:T(8,128)(2,1)S(1)} %collective-permute-done.26.near, ...), custom_call_target="tpu_custom_call" | custom-call | flops 2070000000 | tf_op jit(solution)/shard_map/pallas_call | solution.py:341
  62.9 1.4 %shard_map.138 = (bf16[512,256]{1,0:T(8,128)(2,1)S(1)}, bf16[256,512]{1,0:T(8,128)(2,1)S(1)}) custom-call(bf16[3,512,512]{2,1,0:T(8,128)(2,1)S(1)} %get-tuple-element.103.whole.values, bf16[3,1024,512]{2,1,0:T(8,128)(2,1)S(1)} %bitcast.12), custom_call_target="tpu_custom_call" | custom-call | flops 1380000000 | tf_op jit(solution)/shard_map/pallas_call | solution.py:347
  64.4 3.1 %shard_map.139 = (f32[3,1024,512]{2,1,0:T(8,128)}, f32[8,128]{1,0:T(8,128)S(1)}) custom-call(bf16[1024,512]{1,0:T(8,128)(2,1)S(1)} %shard_map.130.refs_4_.rows, bf16[3,512,512]{2,1,0:T(8,128)(2,1)S(1)} %get-tuple-element.103.whole.values, bf16[128,512]{1,0:T(8,128)(2,1)S(1)} %get-tuple-element.100.refs_0_), custom_call_target="tpu_custom_call" | custom-call | flops 3449999872 | tf_op jit(solution)/shard_map/pallas_call | solution.py:449
  67.5 1.5 %collective-permute-done.31.given_x = bf16[512,256]{1,0:T(8,128)(2,1)S(1)} collective-permute-done((bf16[512,256]{1,0:T(8,128)(2,1)S(1)}, bf16[512,256]{1,0:T(8,128)(2,1)S(1)}, u32[]{:S(2)}, u32[]{:S(2)}) %collective-permute-start.31) | collective-permute-done | bytes 262176 | tf_op jit(solution)/shard_map/ppermute | solution.py:41
  71.5 1.5 %collective-permute-done.33.given_z = bf16[256,256]{1,0:T(8,128)(2,1)S(1)} collective-permute-done((bf16[256,256]{1,0:T(8,128)(2,1)S(1)}, bf16[256,256]{1,0:T(8,128)(2,1)S(1)}, u32[]{:S(2)}, u32[]{:S(2)}) %collective-permute-start.33) | collective-permute-done | bytes 131104 | tf_op jit(solution)/shard_map/ppermute | solution.py:41
  73.0 1.3 %collective-permute-done.34.given_x = bf16[256,256]{1,0:T(8,128)(2,1)S(1)} collective-permute-done((bf16[256,256]{1,0:T(8,128)(2,1)S(1)}, bf16[256,256]{1,0:T(8,128)(2,1)S(1)}, u32[]{:S(2)}, u32[]{:S(2)}) %collective-permute-start.34) | collective-permute-done | bytes 131104 | tf_op jit(solution)/shard_map/ppermute | solution.py:41
  75.0 7.3 %collective-permute-start.29 = (bf16[128,512]{1,0:T(8,128)(2,1)S(1)}, bf16[128,512]{1,0:T(8,128)(2,1)S(1)}, u32[]{:S(2)}, u32[]{:S(2)}) collective-permute-start(bf16[128,512]{1,0:T(8,128)(2,1)S(1)} %get-tuple-element.101), channel_id=1, source_target_pairs={{0,0},{1,8},{2,18},{3,26},{4,4},{5,12},{6,22},{7,30},{8,1},{9,9},{... | collective-permute-start | bytes 393224 | tf_op jit(solution)/shard_map/ppermute | solution.py:410
  82.3 3.9 %collective-permute-start.30 = (bf16[128,512]{1,0:T(8,128)(2,1)S(1)}, bf16[128,512]{1,0:T(8,128)(2,1)S(1)}, u32[]{:S(2)}, u32[]{:S(2)}) collective-permute-start(bf16[128,512]{1,0:T(8,128)(2,1)S(1)} %get-tuple-element.102), channel_id=1, source_target_pairs={{0,16},{1,24},{2,2},{3,10},{4,20},{5,28},{6,6},{7,14},{8,17},{9,25... | collective-permute-start | bytes 393224 | tf_op jit(solution)/shard_map/ppermute | solution.py:410
  86.3 2.7 %collective-permute-start.36 = (bf16[128,512]{1,0:T(8,128)(2,1)S(1)}, bf16[128,512]{1,0:T(8,128)(2,1)S(1)}, u32[]{:S(2)}, u32[]{:S(2)}) collective-permute-start(bf16[128,512]{1,0:T(8,128)(2,1)S(1)} %get-tuple-element.114), channel_id=1, source_target_pairs={{0,0},{1,8},{2,18},{3,26},{4,4},{5,12},{6,22},{7,30},{8,1},{9,9},{... | collective-permute-start | bytes 393224 | tf_op jit(solution)/shard_map/ppermute | solution.py:410
  89.1 2.8 %collective-permute-start.37 = (bf16[128,512]{1,0:T(8,128)(2,1)S(1)}, bf16[128,512]{1,0:T(8,128)(2,1)S(1)}, u32[]{:S(2)}, u32[]{:S(2)}) collective-permute-start(bf16[128,512]{1,0:T(8,128)(2,1)S(1)} %get-tuple-element.115), channel_id=1, source_target_pairs={{0,16},{1,24},{2,2},{3,10},{4,20},{5,28},{6,6},{7,14},{8,17},{9,25... | collective-permute-start | bytes 393224 | tf_op jit(solution)/shard_map/ppermute | solution.py:410
  93.7 3.5 %collective-permute-done.37.second = bf16[128,512]{1,0:T(8,128)(2,1)S(1)} collective-permute-done((bf16[128,512]{1,0:T(8,128)(2,1)S(1)}, bf16[128,512]{1,0:T(8,128)(2,1)S(1)}, u32[]{:S(2)}, u32[]{:S(2)}) %collective-permute-start.37) | collective-permute-done | bytes 131104 | tf_op jit(solution)/shard_map/ppermute | solution.py:410
  (92 shorter events, 28.9 us)
Async XLA Ops:
  2.1 9.3 %collective-permute-start.2 = (bf16[128,1024]{1,0:T(8,128)(2,1)S(1)}, bf16[128,1024]{1,0:T(8,128)(2,1)S(1)}, u32[]{:S(2)}, u32[]{:S(2)}) collective-permute-start(bf16[128,1024]{1,0:T(8,128)(2,1)S(1)} %get-tuple-element.65), channel_id=1, source_target_pairs={{0,2},{1,3},{2,0},{3,1},{4,7},{5,6},{6,5},{7,4},{8,10},{9,11},{10,... | collective-permute-start | bytes 786440 | tf_op jit(solution)/shard_map/ppermute | solution.py:252
  11.4 7.5 %collective-permute-start.4 = (bf16[128,1024]{1,0:T(8,128)(2,1)S(1)}, bf16[128,1024]{1,0:T(8,128)(2,1)S(1)}, u32[]{:S(2)}, u32[]{:S(2)}) collective-permute-start(bf16[128,1024]{1,0:T(8,128)(2,1)S(1)} %shard_map.114.first.refs_1_.c), channel_id=1, source_target_pairs={{0,4},{4,0},{8,12},{12,8},{16,20},{20,16},{24,28},{28,24},{1,5},{5... | collective-permute-start | bytes 786440 | tf_op jit(solution)/shard_map/ppermute | solution.py:41
  12.8 6.1 %collective-permute-start.5 = (bf16[3,256,128]{2,1,0:T(8,128)(2,1)S(1)}, bf16[3,256,128]{2,1,0:T(8,128)(2,1)S(1)}, u32[]{:S(2)}, u32[]{:S(2)}) collective-permute-start(bf16[3,256,128]{2,1,0:T(8,128)(2,1)S(1)} %shard_map.113.refs_1_), channel_id=1, source_target_pairs={{0,2},{1,3},{2,0},{3,1},{4,6},{5,7},{6,4},{7,5},{8,10},{9,11},{10,... | collective-permute-start | bytes 589832 | tf_op jit(solution)/shard_map/ppermute | solution.py:41
  14.1 12.4 %collective-permute-start.10 = (bf16[128,1024]{1,0:T(8,128)(2,1)S(1)}, bf16[128,1024]{1,0:T(8,128)(2,1)S(1)}, u32[]{:S(2)}, u32[]{:S(2)}) collective-permute-start(bf16[128,1024]{1,0:T(8,128)(2,1)S(1)} %get-tuple-element.74), channel_id=1, source_target_pairs={{0,1},{1,0},{2,3},{3,2},{4,5},{5,4},{6,7},{7,6},{8,9},{9,8},{10,11... | collective-permute-start | bytes 786440 | tf_op jit(solution)/shard_map/ppermute | solution.py:41
  14.8 9.7 %collective-permute-start.7 = (bf16[128,1024]{1,0:T(8,128)(2,1)S(1)}, bf16[128,1024]{1,0:T(8,128)(2,1)S(1)}, u32[]{:S(2)}, u32[]{:S(2)}) collective-permute-start(bf16[128,1024]{1,0:T(8,128)(2,1)S(1)} %shard_map.117), channel_id=1, source_target_pairs={{0,2},{1,3},{2,0},{3,1},{4,7},{5,6},{6,5},{7,4},{8,10},{9,11},{10,... | collective-permute-start | bytes 786440 | tf_op jit(solution)/shard_map/ppermute | solution.py:252
  20.2 4.9 %collective-permute-start.6 = (bf16[3,256,128]{2,1,0:T(8,128)(2,1)S(1)}, bf16[3,256,128]{2,1,0:T(8,128)(2,1)S(1)}, u32[]{:S(2)}, u32[]{:S(2)}) collective-permute-start(bf16[3,256,128]{2,1,0:T(8,128)(2,1)S(1)} %get-tuple-element.69), channel_id=1, source_target_pairs={{0,1},{1,0},{2,3},{3,2},{4,5},{5,4},{6,7},{7,6},{8,9},{9,8},{10,11... | collective-permute-start | bytes 589832 | tf_op jit(solution)/shard_map/ppermute | solution.py:41
  22.3 7.0 %collective-permute-start.1 = (bf16[3,256,128]{2,1,0:T(8,128)(2,1)S(1)}, bf16[3,256,128]{2,1,0:T(8,128)(2,1)S(1)}, u32[]{:S(2)}, u32[]{:S(2)}) collective-permute-start(bf16[3,256,128]{2,1,0:T(8,128)(2,1)S(1)} %get-tuple-element.64), channel_id=1, source_target_pairs={{0,1},{1,0},{2,3},{3,2},{4,5},{5,4},{6,7},{7,6},{8,9},{9,8},{10,11... | collective-permute-start | bytes 589832 | tf_op jit(solution)/shard_map/ppermute | solution.py:41
  22.3 6.9 %collective-permute-start.9 = (bf16[3,256,128]{2,1,0:T(8,128)(2,1)S(1)}, bf16[3,256,128]{2,1,0:T(8,128)(2,1)S(1)}, u32[]{:S(2)}, u32[]{:S(2)}) collective-permute-start(bf16[3,256,128]{2,1,0:T(8,128)(2,1)S(1)} %get-tuple-element.72), channel_id=1, source_target_pairs={{0,1},{1,0},{2,3},{3,2},{4,5},{5,4},{6,7},{7,6},{8,9},{9,8},{10,11... | collective-permute-start | bytes 589832 | tf_op jit(solution)/shard_map/ppermute | solution.py:41
  24.5 6.6 %collective-permute-start.13 = (bf16[128,1024]{1,0:T(8,128)(2,1)S(1)}, bf16[128,1024]{1,0:T(8,128)(2,1)S(1)}, u32[]{:S(2)}, u32[]{:S(2)}) collective-permute-start(bf16[128,1024]{1,0:T(8,128)(2,1)S(1)} %collective-permute-done.7.refs_0_.first.c), channel_id=1, source_target_pairs={{0,4},{4,0},{8,12},{12,8},{16,20},{20,16},{24,28},{28,24},{1,5},{5... | collective-permute-start | bytes 786440 | tf_op jit(solution)/shard_map/ppermute | solution.py:41
  25.2 8.0 %collective-permute-start.8 = (bf16[3,256,128]{2,1,0:T(8,128)(2,1)S(1)}, bf16[3,256,128]{2,1,0:T(8,128)(2,1)S(1)}, u32[]{:S(2)}, u32[]{:S(2)}) collective-permute-start(bf16[3,256,128]{2,1,0:T(8,128)(2,1)S(1)} %shard_map.118.refs_0_), channel_id=1, source_target_pairs={{0,2},{1,3},{2,0},{3,1},{4,6},{5,7},{6,4},{7,5},{8,10},{9,11},{10,... | collective-permute-start | bytes 589832 | tf_op jit(solution)/shard_map/ppermute | solution.py:41
  28.9 4.2 %collective-permute-start.12 = (bf16[1,256,128]{2,1,0:T(8,128)(2,1)S(1)}, bf16[1,256,128]{2,1,0:T(8,128)(2,1)S(1)}, u32[]{:S(2)}, u32[]{:S(2)}) collective-permute-start(bf16[1,256,128]{2,1,0:T(8,128)(2,1)S(1)} %shard_map.120), channel_id=1, source_target_pairs={{0,2},{1,3},{2,0},{3,1},{4,6},{5,7},{6,4},{7,5},{8,10},{9,11},{10,... | collective-permute-start | bytes 196616 | tf_op jit(solution)/shard_map/ppermute | solution.py:41
  36.7 3.4 %collective-permute-start.15 = (bf16[1,256,128]{2,1,0:T(8,128)(2,1)S(1)}, bf16[1,256,128]{2,1,0:T(8,128)(2,1)S(1)}, u32[]{:S(2)}, u32[]{:S(2)}) collective-permute-start(bf16[1,256,128]{2,1,0:T(8,128)(2,1)S(1)} %get-tuple-element.79), channel_id=1, source_target_pairs={{0,1},{1,0},{2,3},{3,2},{4,5},{5,4},{6,7},{7,6},{8,9},{9,8},{10,11... | collective-permute-start | bytes 196616 | tf_op jit(solution)/shard_map/ppermute | solution.py:41
  36.8 3.3 %collective-permute-start.18 = (bf16[1,256,128]{2,1,0:T(8,128)(2,1)S(1)}, bf16[1,256,128]{2,1,0:T(8,128)(2,1)S(1)}, u32[]{:S(2)}, u32[]{:S(2)}) collective-permute-start(bf16[1,256,128]{2,1,0:T(8,128)(2,1)S(1)} %get-tuple-element.83), channel_id=1, source_target_pairs={{0,1},{1,0},{2,3},{3,2},{4,5},{5,4},{6,7},{7,6},{8,9},{9,8},{10,11... | collective-permute-start | bytes 196616 | tf_op jit(solution)/shard_map/ppermute | solution.py:41
  39.0 4.9 %collective-permute-start.14 = (bf16[1,512,128]{2,1,0:T(8,128)(2,1)S(1)}, bf16[1,512,128]{2,1,0:T(8,128)(2,1)S(1)}, u32[]{:S(2)}, u32[]{:S(2)}) collective-permute-start(bf16[1,512,128]{2,1,0:T(8,128)(2,1)S(1)} %bitcast.17), channel_id=1, source_target_pairs={{0,2},{1,3},{2,0},{3,1},{4,6},{5,7},{6,4},{7,5},{8,10},{9,11},{10,... | collective-permute-start | bytes 393224 | tf_op jit(solution)/shard_map/ppermute | solution.py:41
  39.2 7.5 %collective-permute-start.19 = (bf16[1,512,128]{2,1,0:T(8,128)(2,1)S(1)}, bf16[1,512,128]{2,1,0:T(8,128)(2,1)S(1)}, u32[]{:S(2)}, u32[]{:S(2)}) collective-permute-start(bf16[1,512,128]{2,1,0:T(8,128)(2,1)S(1)} %bitcast.18), channel_id=1, source_target_pairs={{0,1},{1,0},{2,3},{3,2},{4,5},{5,4},{6,7},{7,6},{8,9},{9,8},{10,11... | collective-permute-start | bytes 393224 | tf_op jit(solution)/shard_map/ppermute | solution.py:41
  45.1 10.9 %collective-permute-start.25 = (bf16[3,512,128]{2,1,0:T(8,128)(2,1)S(1)}, bf16[3,512,128]{2,1,0:T(8,128)(2,1)S(1)}, u32[]{:S(2)}, u32[]{:S(2)}) collective-permute-start(bf16[3,512,128]{2,1,0:T(8,128)(2,1)S(1)} %shard_map.125.refs_1_.own), channel_id=1, source_target_pairs={{0,2},{1,3},{2,0},{3,1},{4,6},{5,7},{6,4},{7,5},{8,10},{9,11},{10,... | collective-permute-start | bytes 1179656 | tf_op jit(solution)/shard_map/ppermute | solution.py:41
  47.4 7.6 %collective-permute-start.21 = (bf16[512,256]{1,0:T(8,128)(2,1)S(1)}, bf16[512,256]{1,0:T(8,128)(2,1)S(1)}, u32[]{:S(2)}, u32[]{:S(2)}) collective-permute-start(bf16[512,256]{1,0:T(8,128)(2,1)S(1)} %get-tuple-element.90), channel_id=1, source_target_pairs={{0,4},{4,0},{8,12},{12,8},{16,20},{20,16},{24,28},{28,24},{1,5},{5... | collective-permute-start | bytes 786440 | tf_op jit(solution)/shard_map/ppermute | solution.py:41
  48.6 7.2 %collective-permute-start.22 = (bf16[256,512]{1,0:T(8,128)(2,1)S(1)}, bf16[256,512]{1,0:T(8,128)(2,1)S(1)}, u32[]{:S(2)}, u32[]{:S(2)}) collective-permute-start(bf16[256,512]{1,0:T(8,128)(2,1)S(1)} %get-tuple-element.92), channel_id=1, source_target_pairs={{0,8},{4,12},{8,0},{12,4},{16,24},{20,28},{24,16},{28,20},{1,9},{5... | collective-permute-start | bytes 786440 | tf_op jit(solution)/shard_map/ppermute | solution.py:41
  50.5 9.4 %collective-permute-start.26 = (bf16[3,512,128]{2,1,0:T(8,128)(2,1)S(1)}, bf16[3,512,128]{2,1,0:T(8,128)(2,1)S(1)}, u32[]{:S(2)}, u32[]{:S(2)}) collective-permute-start(bf16[3,512,128]{2,1,0:T(8,128)(2,1)S(1)} %shard_map.125.refs_1_.own), channel_id=1, source_target_pairs={{0,1},{1,0},{2,3},{3,2},{4,5},{5,4},{6,7},{7,6},{8,9},{9,8},{10,11... | collective-permute-start | bytes 1179656 | tf_op jit(solution)/shard_map/ppermute | solution.py:41
  56.1 3.8 %collective-permute-start.27 = (bf16[3,512,128]{2,1,0:T(8,128)(2,1)S(1)}, bf16[3,512,128]{2,1,0:T(8,128)(2,1)S(1)}, u32[]{:S(2)}, u32[]{:S(2)}) collective-permute-start(bf16[3,512,128]{2,1,0:T(8,128)(2,1)S(1)} %shard_map.133.far), channel_id=1, source_target_pairs={{0,1},{1,0},{2,3},{3,2},{4,5},{5,4},{6,7},{7,6},{8,9},{9,8},{10,11... | collective-permute-start | bytes 1179656 | tf_op jit(solution)/shard_map/ppermute | solution.py:41
  57.4 6.9 %collective-permute-start.23 = (bf16[256,256]{1,0:T(8,128)(2,1)S(1)}, bf16[256,256]{1,0:T(8,128)(2,1)S(1)}, u32[]{:S(2)}, u32[]{:S(2)}) collective-permute-start(bf16[256,256]{1,0:T(8,128)(2,1)S(1)} %get-tuple-element.94), channel_id=1, source_target_pairs={{0,8},{4,12},{8,0},{12,4},{16,24},{20,28},{24,16},{28,20},{1,9},{5... | collective-permute-start | bytes 393224 | tf_op jit(solution)/shard_map/ppermute | solution.py:41
  58.8 5.6 %collective-permute-start.24 = (bf16[256,256]{1,0:T(8,128)(2,1)S(1)}, bf16[256,256]{1,0:T(8,128)(2,1)S(1)}, u32[]{:S(2)}, u32[]{:S(2)}) collective-permute-start(bf16[256,256]{1,0:T(8,128)(2,1)S(1)} %get-tuple-element.96), channel_id=1, source_target_pairs={{0,4},{4,0},{8,12},{12,8},{16,20},{20,16},{24,28},{28,24},{1,5},{5... | collective-permute-start | bytes 393224 | tf_op jit(solution)/shard_map/ppermute | solution.py:41
  61.6 7.4 %collective-permute-start.31 = (bf16[512,256]{1,0:T(8,128)(2,1)S(1)}, bf16[512,256]{1,0:T(8,128)(2,1)S(1)}, u32[]{:S(2)}, u32[]{:S(2)}) collective-permute-start(bf16[512,256]{1,0:T(8,128)(2,1)S(1)} %get-tuple-element.98.refs_0_), channel_id=1, source_target_pairs={{0,4},{4,0},{8,12},{12,8},{16,20},{20,16},{24,28},{28,24},{1,5},{5... | collective-permute-start | bytes 786440 | tf_op jit(solution)/shard_map/ppermute | solution.py:41
  62.0 7.0 %collective-permute-start.32 = (bf16[256,512]{1,0:T(8,128)(2,1)S(1)}, bf16[256,512]{1,0:T(8,128)(2,1)S(1)}, u32[]{:S(2)}, u32[]{:S(2)}) collective-permute-start(bf16[256,512]{1,0:T(8,128)(2,1)S(1)} %get-tuple-element.106), channel_id=1, source_target_pairs={{0,8},{4,12},{8,0},{12,4},{16,24},{20,28},{24,16},{28,20},{1,9},{5... | collective-permute-start | bytes 786440 | tf_op jit(solution)/shard_map/ppermute | solution.py:41
  69.1 3.9 %collective-permute-start.33 = (bf16[256,256]{1,0:T(8,128)(2,1)S(1)}, bf16[256,256]{1,0:T(8,128)(2,1)S(1)}, u32[]{:S(2)}, u32[]{:S(2)}) collective-permute-start(bf16[256,256]{1,0:T(8,128)(2,1)S(1)} %get-tuple-element.109), channel_id=1, source_target_pairs={{0,8},{4,12},{8,0},{12,4},{16,24},{20,28},{24,16},{28,20},{1,9},{5... | collective-permute-start | bytes 393224 | tf_op jit(solution)/shard_map/ppermute | solution.py:41
  70.2 4.1 %collective-permute-start.34 = (bf16[256,256]{1,0:T(8,128)(2,1)S(1)}, bf16[256,256]{1,0:T(8,128)(2,1)S(1)}, u32[]{:S(2)}, u32[]{:S(2)}) collective-permute-start(bf16[256,256]{1,0:T(8,128)(2,1)S(1)} %get-tuple-element.111), channel_id=1, source_target_pairs={{0,4},{4,0},{8,12},{12,8},{16,20},{20,16},{24,28},{28,24},{1,5},{5... | collective-permute-start | bytes 393224 | tf_op jit(solution)/shard_map/ppermute | solution.py:41
  70.7 4.2 %collective-permute-start.28 = (bf16[128,512]{1,0:T(8,128)(2,1)S(1)}, bf16[128,512]{1,0:T(8,128)(2,1)S(1)}, u32[]{:S(2)}, u32[]{:S(2)}) collective-permute-start(bf16[128,512]{1,0:T(8,128)(2,1)S(1)} %get-tuple-element.100.refs_0_), channel_id=1, source_target_pairs={{0,2},{1,3},{2,0},{3,1},{4,6},{5,7},{6,4},{7,5},{8,10},{9,11},{10,... | collective-permute-start | bytes 393224 | tf_op jit(solution)/shard_map/ppermute | solution.py:41
  74.4 11.8 %collective-permute-start.35 = (bf16[128,512]{1,0:T(8,128)(2,1)S(1)}, bf16[128,512]{1,0:T(8,128)(2,1)S(1)}, u32[]{:S(2)}, u32[]{:S(2)}) collective-permute-start(bf16[128,512]{1,0:T(8,128)(2,1)S(1)} %get-tuple-element.113), channel_id=1, source_target_pairs={{0,2},{1,3},{2,0},{3,1},{4,6},{5,7},{6,4},{7,5},{8,10},{9,11},{10,... | collective-permute-start | bytes 393224 | tf_op jit(solution)/shard_map/ppermute | solution.py:41
  75.0 16.9 %collective-permute-start.29 = (bf16[128,512]{1,0:T(8,128)(2,1)S(1)}, bf16[128,512]{1,0:T(8,128)(2,1)S(1)}, u32[]{:S(2)}, u32[]{:S(2)}) collective-permute-start(bf16[128,512]{1,0:T(8,128)(2,1)S(1)} %get-tuple-element.101), channel_id=1, source_target_pairs={{0,0},{1,8},{2,18},{3,26},{4,4},{5,12},{6,22},{7,30},{8,1},{9,9},{... | collective-permute-start | bytes 393224 | tf_op jit(solution)/shard_map/ppermute | solution.py:410
  82.3 9.6 %collective-permute-start.30 = (bf16[128,512]{1,0:T(8,128)(2,1)S(1)}, bf16[128,512]{1,0:T(8,128)(2,1)S(1)}, u32[]{:S(2)}, u32[]{:S(2)}) collective-permute-start(bf16[128,512]{1,0:T(8,128)(2,1)S(1)} %get-tuple-element.102), channel_id=1, source_target_pairs={{0,16},{1,24},{2,2},{3,10},{4,20},{5,28},{6,6},{7,14},{8,17},{9,25... | collective-permute-start | bytes 393224 | tf_op jit(solution)/shard_map/ppermute | solution.py:410
  86.3 7.4 %collective-permute-start.36 = (bf16[128,512]{1,0:T(8,128)(2,1)S(1)}, bf16[128,512]{1,0:T(8,128)(2,1)S(1)}, u32[]{:S(2)}, u32[]{:S(2)}) collective-permute-start(bf16[128,512]{1,0:T(8,128)(2,1)S(1)} %get-tuple-element.114), channel_id=1, source_target_pairs={{0,0},{1,8},{2,18},{3,26},{4,4},{5,12},{6,22},{7,30},{8,1},{9,9},{... | collective-permute-start | bytes 393224 | tf_op jit(solution)/shard_map/ppermute | solution.py:410
  89.1 8.1 %collective-permute-start.37 = (bf16[128,512]{1,0:T(8,128)(2,1)S(1)}, bf16[128,512]{1,0:T(8,128)(2,1)S(1)}, u32[]{:S(2)}, u32[]{:S(2)}) collective-permute-start(bf16[128,512]{1,0:T(8,128)(2,1)S(1)} %get-tuple-element.115), channel_id=1, source_target_pairs={{0,16},{1,24},{2,2},{3,10},{4,20},{5,28},{6,6},{7,14},{8,17},{9,25... | collective-permute-start | bytes 393224 | tf_op jit(solution)/shard_map/ppermute | solution.py:410
  (12 other events, 49.6 us)

commit v11 on v10

--- a/solution.py
+++ b/solution.py
@@ -244,7 +244,9 @@
             copy.wait()
 
     block = jax.ShapeDtypeStruct((length, width), rows.dtype)
-    return call(body, (block,) * 3, [pltpu.SemaphoreType.DMA((3,))], in_specs=[HBM], us=0.7)(rows)
+    return call(body, (block,) * 3, [pltpu.SemaphoreType.DMA((3,))], in_specs=[HBM], us=0.7)(
+        pltpu.with_memory_space_constraint(rows, pltpu.HBM)
+    )
 
 
 def fetched(block):

time: 98.2 us -> 98.1 us (level)
  Pallas kernels: 20.2 us -> 22.3 us
  local copies, waits for them, and re-layouts: 3.9 us -> 2.66 us
    pallas_call x2, Pallas kernels: 0.17 us -> 2.28 us  [column_blocks(): call(body, (block,) * 3, [pltpu.SemaphoreType.DMA((3,))], in_specs=[HBM],...]
    unnamed x12 -> x8, local copies, waits for them, and re-layouts: 3.14 us -> 1.9 us
  transfers between devices with their start and end apart: 38 -> 38, of which waited for: 17 -> 17; matrix products, arithmetic and copies ran while one was open for 2% -> 2% of each run, Pallas kernels for 17% -> 18%
where the time goes in v11:
time: 98.1 us; the launch traced here: 97.7 us
  starting transfers between devices  47 us (48%)
  waiting for transfers between devices  24.1 us (25%)
  Pallas kernels  22.3 us (23%)
  local copies, waits for them, and re-layouts  2.66 us (3%)
    ppermute x32, starting transfers between devices, flipped(): lax.ppermute(value, axis, [(source, source ^ mask) for source in range(co...  27.2 us
    ppermute x4, starting transfers between devices, block_sums(): lax.ppermute(value, ('fsdp', 'ctx'), final_pairs(flip))  16.8 us
    ppermute x32, waiting for transfers between devices, flipped(): lax.ppermute(value, axis, [(source, source ^ mask) for source in range(co...  16.4 us
    pallas_call x2, Pallas kernels, weight_gradient(): pl.pallas_call(body, out_shape=(gradient, jax.ShapeDtypeStruct((8, LANES)...  4.7 us
    ppermute x4, waiting for transfers between devices, block_sums(): lax.ppermute(value, ('fsdp', 'ctx'), final_pairs(flip))  4.55 us
    pallas_call x4, Pallas kernels, project(): call(body, (jax.ShapeDtypeStruct((groups, length, width), F32), sums, sum...  3.77 us
    ppermute x2, waiting for transfers between devices, fetched(): return lax.ppermute(block, ('fsdp', 'ctx'), pairs)  3.18 us
    ppermute x2, starting transfers between devices, fetched(): return lax.ppermute(block, ('fsdp', 'ctx'), pairs)  2.94 us
  transfers between devices with their start and end apart: 38, of which 17 were waited for; matrix products, arithmetic and copies ran while one was open for 2% of the time, Pallas kernels for 18%

profile of v11, /device:TPU:1, one launch (start us, length us, event | category | flops | bytes accessed | tf_op | source)
XLA Modules:
  0.0 97.7 jit_solution(368783621290552284)
XLA Ops:
  1.9 2.7 %collective-permute-start.2 = (bf16[128,1024]{1,0:T(8,128)(2,1)S(1)}, bf16[128,1024]{1,0:T(8,128)(2,1)S(1)}, u32[]{:S(2)}, u32[]{:S(2)}) collective-permute-start(bf16[128,1024]{1,0:T(8,128)(2,1)S(1)} %get-tuple-element.65), channel_id=1, source_target_pairs={{0,2},{1,3},{2,0},{3,1},{4,7},{5,6},{6,5},{7,4},{8,10},{9,11},{10,... | collective-permute-start | bytes 786440 | tf_op jit(solution)/shard_map/ppermute | solution.py:254
  4.7 1.9 %copy-done.1 = bf16[1024,3,512]{2,0,1:T(8,128)(2,1)S(1)} copy-done((bf16[1024,3,512]{2,0,1:T(8,128)(2,1)S(1)}, bf16[1024,3,512]{2,0,1:T(8,128)(2,1)}, u32[]{:S(2)}) %copy-start.1) | copy-done | bytes 3145752
  6.5 1.3 %shard_map.112 = (f32[3,256,128]{2,1,0:T(8,128)S(1)}, bf16[3,256,128]{2,1,0:T(8,128)(2,1)S(1)}, bf16[3,256,128]{2,1,0:T(8,128)(2,1)S(1)}, bf16[3,256,128]{2,1,0:T(8,128)(2,1)S(1)}) custom-call(bf16[128,1024]{1,0:T(8,128)(2,1)S(1)} %get-tuple-element.61.first.a, bf16[128,1024]{1,0:T(8,128)(2,1)S(1)} %collective-permute-done.second.b, ...), custom_call_target="tpu_custom_call" | custom-call | flops 1552499968 | tf_op jit(solution)/shard_map/pallas_call | solution.py:277
  9.8 1.4 %collective-permute-done.2.refs_0_ = bf16[128,1024]{1,0:T(8,128)(2,1)S(1)} collective-permute-done((bf16[128,1024]{1,0:T(8,128)(2,1)S(1)}, bf16[128,1024]{1,0:T(8,128)(2,1)S(1)}, u32[]{:S(2)}, u32[]{:S(2)}) %collective-permute-start.2) | collective-permute-done | bytes 262176 | tf_op jit(solution)/shard_map/ppermute | solution.py:254
  11.2 1.4 %collective-permute-start.4 = (bf16[128,1024]{1,0:T(8,128)(2,1)S(1)}, bf16[128,1024]{1,0:T(8,128)(2,1)S(1)}, u32[]{:S(2)}, u32[]{:S(2)}) collective-permute-start(bf16[128,1024]{1,0:T(8,128)(2,1)S(1)} %shard_map.114.first.refs_1_.c), channel_id=1, source_target_pairs={{0,4},{4,0},{8,12},{12,8},{16,20},{20,16},{24,28},{28,24},{1,5},{5... | collective-permute-start | bytes 786440 | tf_op jit(solution)/shard_map/ppermute | solution.py:41
  15.9 2.8 %collective-permute-done.5.refs_0_.refs_5_ = bf16[3,256,128]{2,1,0:T(8,128)(2,1)S(1)} collective-permute-done((bf16[3,256,128]{2,1,0:T(8,128)(2,1)S(1)}, bf16[3,256,128]{2,1,0:T(8,128)(2,1)S(1)}, u32[]{:S(2)}, u32[]{:S(2)}) %collective-permute-start.5) | collective-permute-done | bytes 196640 | tf_op jit(solution)/shard_map/ppermute | solution.py:41
  18.7 1.3 %shard_map.115 = (f32[3,256,128]{2,1,0:T(8,128)S(1)}, bf16[3,256,128]{2,1,0:T(8,128)(2,1)S(1)}, bf16[3,256,128]{2,1,0:T(8,128)(2,1)S(1)}, bf16[3,256,128]{2,1,0:T(8,128)(2,1)S(1)}) custom-call(bf16[128,1024]{1,0:T(8,128)(2,1)S(1)} %shard_map.114.first.refs_1_.c, bf16[128,1024]{1,0:T(8,128)(2,1)S(1)} %collective-permute-done.4.second.d, ...), custom_call_target="tpu_custom_call" | custom-call | flops 1552499968 | tf_op jit(solution)/shard_map/pallas_call | solution.py:277
  20.1 2.0 %collective-permute-start.6 = (bf16[3,256,128]{2,1,0:T(8,128)(2,1)S(1)}, bf16[3,256,128]{2,1,0:T(8,128)(2,1)S(1)}, u32[]{:S(2)}, u32[]{:S(2)}) collective-permute-start(bf16[3,256,128]{2,1,0:T(8,128)(2,1)S(1)} %get-tuple-element.69), channel_id=1, source_target_pairs={{0,1},{1,0},{2,3},{3,2},{4,5},{5,4},{6,7},{7,6},{8,9},{9,8},{10,11... | collective-permute-start | bytes 589832 | tf_op jit(solution)/shard_map/ppermute | solution.py:41
  22.6 1.8 %collective-permute-done.7.refs_0_.first.c = bf16[128,1024]{1,0:T(8,128)(2,1)S(1)} collective-permute-done((bf16[128,1024]{1,0:T(8,128)(2,1)S(1)}, bf16[128,1024]{1,0:T(8,128)(2,1)S(1)}, u32[]{:S(2)}, u32[]{:S(2)}) %collective-permute-start.7) | collective-permute-done | bytes 262176 | tf_op jit(solution)/shard_map/ppermute | solution.py:254
  25.0 1.3 %collective-permute-start.8 = (bf16[3,256,128]{2,1,0:T(8,128)(2,1)S(1)}, bf16[3,256,128]{2,1,0:T(8,128)(2,1)S(1)}, u32[]{:S(2)}, u32[]{:S(2)}) collective-permute-start(bf16[3,256,128]{2,1,0:T(8,128)(2,1)S(1)} %shard_map.118.refs_0_), channel_id=1, source_target_pairs={{0,2},{1,3},{2,0},{3,1},{4,6},{5,7},{6,4},{7,5},{8,10},{9,11},{10,... | collective-permute-start | bytes 589832 | tf_op jit(solution)/shard_map/ppermute | solution.py:41
  29.1 1.9 %collective-permute-done.13.refs_12_.second.d = bf16[128,1024]{1,0:T(8,128)(2,1)S(1)} collective-permute-done((bf16[128,1024]{1,0:T(8,128)(2,1)S(1)}, bf16[128,1024]{1,0:T(8,128)(2,1)S(1)}, u32[]{:S(2)}, u32[]{:S(2)}) %collective-permute-start.13) | collective-permute-done | bytes 262176 | tf_op jit(solution)/shard_map/ppermute | solution.py:41
  31.0 2.0 %collective-permute-done.12.refs_11_.refs_5_ = bf16[1,256,128]{2,1,0:T(8,128)(2,1)S(1)} collective-permute-done((bf16[1,256,128]{2,1,0:T(8,128)(2,1)S(1)}, bf16[1,256,128]{2,1,0:T(8,128)(2,1)S(1)}, u32[]{:S(2)}, u32[]{:S(2)}) %collective-permute-start.12) | collective-permute-done | bytes 65568 | tf_op jit(solution)/shard_map/ppermute | solution.py:41
  33.0 2.3 %shard_map.121 = (f32[512,128]{1,0:T(8,128)S(1)}, f32[512,128]{1,0:T(8,128)S(1)}, f32[512,128]{1,0:T(8,128)S(1)}, f32[512,128]{1,0:T(8,128)S(1)}, bf16[512,128]{1,0:T(8,128)(2,1)S(1)}) custom-call(f32[3,256,128]{2,1,0:T(8,128)S(1)} %get-tuple-element.63.refs_0_, bf16[3,256,128]{2,1,0:T(8,128)(2,1)S(1)} %collective-permute-done.1.refs_1_, ...), custom_call_target="tpu_custom_call" | custom-call | flops 2415000064 | tf_op jit(solution)/shard_map/pallas_call | solution.py:185
  37.7 1.3 %collective-permute-start.17 = (bf16[1,256,128]{2,1,0:T(8,128)(2,1)S(1)}, bf16[1,256,128]{2,1,0:T(8,128)(2,1)S(1)}, u32[]{:S(2)}, u32[]{:S(2)}) collective-permute-start(bf16[1,256,128]{2,1,0:T(8,128)(2,1)S(1)} %shard_map.123), channel_id=1, source_target_pairs={{0,2},{1,3},{2,0},{3,1},{4,6},{5,7},{6,4},{7,5},{8,10},{9,11},{10,... | collective-permute-start | bytes 196616 | tf_op jit(solution)/shard_map/ppermute | solution.py:41
  40.9 2.1 %shard_map.124.refs_0_ = bf16[3,512,128]{2,1,0:T(8,128)(2,1)S(1)} custom-call(f32[1,256,128]{2,1,0:T(8,128)S(1)} %get-tuple-element.78.refs_0_, bf16[1,256,128]{2,1,0:T(8,128)(2,1)S(1)} %collective-permute-done.15.refs_1_, bf16[1,256,128]{2,1,0:T(8,128)(2,1)S(1)} %collective-permute-done.17.refs_2_, f32[1,256,128]{2,1,0:T(8,128)S(1)} %get-tuple-element.82.refs_3_, ...), custom_call_target="tpu_custom_call" | custom-call | flops 2415000064 | tf_op jit(solution)/shard_map/pallas_call | solution.py:205
  43.9 1.3 %collective-permute-start.20 = (bf16[1,512,128]{2,1,0:T(8,128)(2,1)S(1)}, bf16[1,512,128]{2,1,0:T(8,128)(2,1)S(1)}, u32[]{:S(2)}, u32[]{:S(2)}) collective-permute-start(bf16[1,512,128]{2,1,0:T(8,128)(2,1)S(1)} %shard_map.126.far), channel_id=1, source_target_pairs={{0,1},{1,0},{2,3},{3,2},{4,5},{5,4},{6,7},{7,6},{8,9},{9,8},{10,11... | collective-permute-start | bytes 393224 | tf_op jit(solution)/shard_map/ppermute | solution.py:41
  45.2 1.4 %collective-permute-start.25 = (bf16[3,512,128]{2,1,0:T(8,128)(2,1)S(1)}, bf16[3,512,128]{2,1,0:T(8,128)(2,1)S(1)}, u32[]{:S(2)}, u32[]{:S(2)}) collective-permute-start(bf16[3,512,128]{2,1,0:T(8,128)(2,1)S(1)} %shard_map.125.refs_1_.own), channel_id=1, source_target_pairs={{0,2},{1,3},{2,0},{3,1},{4,6},{5,7},{6,4},{7,5},{8,10},{9,11},{10,... | collective-permute-start | bytes 1179656 | tf_op jit(solution)/shard_map/ppermute | solution.py:41
  48.4 1.3 %collective-permute-start.22 = (bf16[256,512]{1,0:T(8,128)(2,1)S(1)}, bf16[256,512]{1,0:T(8,128)(2,1)S(1)}, u32[]{:S(2)}, u32[]{:S(2)}) collective-permute-start(bf16[256,512]{1,0:T(8,128)(2,1)S(1)} %get-tuple-element.92), channel_id=1, source_target_pairs={{0,8},{4,12},{8,0},{12,4},{16,24},{20,28},{24,16},{28,20},{1,9},{5... | collective-permute-start | bytes 786440 | tf_op jit(solution)/shard_map/ppermute | solution.py:41
  51.9 1.6 %shard_map.132 = (f32[1,1024,512]{2,1,0:T(8,128)}, f32[8,128]{1,0:T(8,128)S(1)}) custom-call(bf16[1024,512]{1,0:T(8,128)(2,1)S(1)} %shard_map.131.rows, bf16[1,512,512]{2,1,0:T(8,128)(2,1)S(1)} %get-tuple-element.88.whole.values), custom_call_target="tpu_custom_call" | custom-call | flops 1150000000 | tf_op jit(solution)/shard_map/pallas_call | solution.py:451
  53.6 1.2 %collective-permute-done.21.given_x.refs_1_ = bf16[512,256]{1,0:T(8,128)(2,1)S(1)} collective-permute-done((bf16[512,256]{1,0:T(8,128)(2,1)S(1)}, bf16[512,256]{1,0:T(8,128)(2,1)S(1)}, u32[]{:S(2)}, u32[]{:S(2)}) %collective-permute-start.21) | collective-permute-done | bytes 262176 | tf_op jit(solution)/shard_map/ppermute | solution.py:41
  57.2 1.4 %collective-permute-start.23 = (bf16[256,256]{1,0:T(8,128)(2,1)S(1)}, bf16[256,256]{1,0:T(8,128)(2,1)S(1)}, u32[]{:S(2)}, u32[]{:S(2)}) collective-permute-start(bf16[256,256]{1,0:T(8,128)(2,1)S(1)} %get-tuple-element.94), channel_id=1, source_target_pairs={{0,8},{4,12},{8,0},{12,4},{16,24},{20,28},{24,16},{28,20},{1,9},{5... | collective-permute-start | bytes 393224 | tf_op jit(solution)/shard_map/ppermute | solution.py:41
  59.7 1.7 %shard_map.134 = (bf16[3,512,512]{2,1,0:T(8,128)(2,1)S(1)}, bf16[512,256]{1,0:T(8,128)(2,1)S(1)}, bf16[256,512]{1,0:T(8,128)(2,1)S(1)}) custom-call(bf16[3,512,128]{2,1,0:T(8,128)(2,1)S(1)} %shard_map.125.refs_1_.own, bf16[3,512,128]{2,1,0:T(8,128)(2,1)S(1)} %shard_map.133.far, bf16[3,512,128]{2,1,0:T(8,128)(2,1)S(1)} %collective-permute-done.26.near, ...), custom_call_target="tpu_custom_call" | custom-call | flops 2070000000 | tf_op jit(solution)/shard_map/pallas_call | solution.py:343
  62.7 1.4 %shard_map.138 = (bf16[512,256]{1,0:T(8,128)(2,1)S(1)}, bf16[256,512]{1,0:T(8,128)(2,1)S(1)}) custom-call(bf16[3,512,512]{2,1,0:T(8,128)(2,1)S(1)} %get-tuple-element.103.whole.values, bf16[3,1024,512]{2,1,0:T(8,128)(2,1)S(1)} %bitcast.12), custom_call_target="tpu_custom_call" | custom-call | flops 1380000000 | tf_op jit(solution)/shard_map/pallas_call | solution.py:349
  64.2 3.1 %shard_map.139 = (f32[3,1024,512]{2,1,0:T(8,128)}, f32[8,128]{1,0:T(8,128)S(1)}) custom-call(bf16[1024,512]{1,0:T(8,128)(2,1)S(1)} %shard_map.130.refs_4_.rows, bf16[3,512,512]{2,1,0:T(8,128)(2,1)S(1)} %get-tuple-element.103.whole.values, bf16[128,512]{1,0:T(8,128)(2,1)S(1)} %get-tuple-element.100.refs_0_), custom_call_target="tpu_custom_call" | custom-call | flops 3449999872 | tf_op jit(solution)/shard_map/pallas_call | solution.py:451
  67.3 1.5 %collective-permute-done.31.given_x = bf16[512,256]{1,0:T(8,128)(2,1)S(1)} collective-permute-done((bf16[512,256]{1,0:T(8,128)(2,1)S(1)}, bf16[512,256]{1,0:T(8,128)(2,1)S(1)}, u32[]{:S(2)}, u32[]{:S(2)}) %collective-permute-start.31) | collective-permute-done | bytes 262176 | tf_op jit(solution)/shard_map/ppermute | solution.py:41
  71.4 1.5 %collective-permute-done.33.given_z = bf16[256,256]{1,0:T(8,128)(2,1)S(1)} collective-permute-done((bf16[256,256]{1,0:T(8,128)(2,1)S(1)}, bf16[256,256]{1,0:T(8,128)(2,1)S(1)}, u32[]{:S(2)}, u32[]{:S(2)}) %collective-permute-start.33) | collective-permute-done | bytes 131104 | tf_op jit(solution)/shard_map/ppermute | solution.py:41
  72.9 1.3 %collective-permute-done.34.given_x = bf16[256,256]{1,0:T(8,128)(2,1)S(1)} collective-permute-done((bf16[256,256]{1,0:T(8,128)(2,1)S(1)}, bf16[256,256]{1,0:T(8,128)(2,1)S(1)}, u32[]{:S(2)}, u32[]{:S(2)}) %collective-permute-start.34) | collective-permute-done | bytes 131104 | tf_op jit(solution)/shard_map/ppermute | solution.py:41
  74.8 7.3 %collective-permute-start.29 = (bf16[128,512]{1,0:T(8,128)(2,1)S(1)}, bf16[128,512]{1,0:T(8,128)(2,1)S(1)}, u32[]{:S(2)}, u32[]{:S(2)}) collective-permute-start(bf16[128,512]{1,0:T(8,128)(2,1)S(1)} %get-tuple-element.101), channel_id=1, source_target_pairs={{0,0},{1,8},{2,18},{3,26},{4,4},{5,12},{6,22},{7,30},{8,1},{9,9},{... | collective-permute-start | bytes 393224 | tf_op jit(solution)/shard_map/ppermute | solution.py:412
  82.2 3.9 %collective-permute-start.30 = (bf16[128,512]{1,0:T(8,128)(2,1)S(1)}, bf16[128,512]{1,0:T(8,128)(2,1)S(1)}, u32[]{:S(2)}, u32[]{:S(2)}) collective-permute-start(bf16[128,512]{1,0:T(8,128)(2,1)S(1)} %get-tuple-element.102), channel_id=1, source_target_pairs={{0,16},{1,24},{2,2},{3,10},{4,20},{5,28},{6,6},{7,14},{8,17},{9,25... | collective-permute-start | bytes 393224 | tf_op jit(solution)/shard_map/ppermute | solution.py:412
  86.2 2.7 %collective-permute-start.36 = (bf16[128,512]{1,0:T(8,128)(2,1)S(1)}, bf16[128,512]{1,0:T(8,128)(2,1)S(1)}, u32[]{:S(2)}, u32[]{:S(2)}) collective-permute-start(bf16[128,512]{1,0:T(8,128)(2,1)S(1)} %get-tuple-element.114), channel_id=1, source_target_pairs={{0,0},{1,8},{2,18},{3,26},{4,4},{5,12},{6,22},{7,30},{8,1},{9,9},{... | collective-permute-start | bytes 393224 | tf_op jit(solution)/shard_map/ppermute | solution.py:412
  88.9 2.8 %collective-permute-start.37 = (bf16[128,512]{1,0:T(8,128)(2,1)S(1)}, bf16[128,512]{1,0:T(8,128)(2,1)S(1)}, u32[]{:S(2)}, u32[]{:S(2)}) collective-permute-start(bf16[128,512]{1,0:T(8,128)(2,1)S(1)} %get-tuple-element.115), channel_id=1, source_target_pairs={{0,16},{1,24},{2,2},{3,10},{4,20},{5,28},{6,6},{7,14},{8,17},{9,25... | collective-permute-start | bytes 393224 | tf_op jit(solution)/shard_map/ppermute | solution.py:412
  93.5 3.5 %collective-permute-done.37.second = bf16[128,512]{1,0:T(8,128)(2,1)S(1)} collective-permute-done((bf16[128,512]{1,0:T(8,128)(2,1)S(1)}, bf16[128,512]{1,0:T(8,128)(2,1)S(1)}, u32[]{:S(2)}, u32[]{:S(2)}) %collective-permute-start.37) | collective-permute-done | bytes 131104 | tf_op jit(solution)/shard_map/ppermute | solution.py:412
  (88 shorter events, 30.0 us)
Async XLA Ops:
  1.9 9.3 %collective-permute-start.2 = (bf16[128,1024]{1,0:T(8,128)(2,1)S(1)}, bf16[128,1024]{1,0:T(8,128)(2,1)S(1)}, u32[]{:S(2)}, u32[]{:S(2)}) collective-permute-start(bf16[128,1024]{1,0:T(8,128)(2,1)S(1)} %get-tuple-element.65), channel_id=1, source_target_pairs={{0,2},{1,3},{2,0},{3,1},{4,7},{5,6},{6,5},{7,4},{8,10},{9,11},{10,... | collective-permute-start | bytes 786440 | tf_op jit(solution)/shard_map/ppermute | solution.py:254
  11.2 7.5 %collective-permute-start.4 = (bf16[128,1024]{1,0:T(8,128)(2,1)S(1)}, bf16[128,1024]{1,0:T(8,128)(2,1)S(1)}, u32[]{:S(2)}, u32[]{:S(2)}) collective-permute-start(bf16[128,1024]{1,0:T(8,128)(2,1)S(1)} %shard_map.114.first.refs_1_.c), channel_id=1, source_target_pairs={{0,4},{4,0},{8,12},{12,8},{16,20},{20,16},{24,28},{28,24},{1,5},{5... | collective-permute-start | bytes 786440 | tf_op jit(solution)/shard_map/ppermute | solution.py:41
  12.6 6.1 %collective-permute-start.5 = (bf16[3,256,128]{2,1,0:T(8,128)(2,1)S(1)}, bf16[3,256,128]{2,1,0:T(8,128)(2,1)S(1)}, u32[]{:S(2)}, u32[]{:S(2)}) collective-permute-start(bf16[3,256,128]{2,1,0:T(8,128)(2,1)S(1)} %shard_map.113.refs_1_), channel_id=1, source_target_pairs={{0,2},{1,3},{2,0},{3,1},{4,6},{5,7},{6,4},{7,5},{8,10},{9,11},{10,... | collective-permute-start | bytes 589832 | tf_op jit(solution)/shard_map/ppermute | solution.py:41
  15.0 11.3 %collective-permute-start.10 = (bf16[128,1024]{1,0:T(8,128)(2,1)S(1)}, bf16[128,1024]{1,0:T(8,128)(2,1)S(1)}, u32[]{:S(2)}, u32[]{:S(2)}) collective-permute-start(bf16[128,1024]{1,0:T(8,128)(2,1)S(1)} %get-tuple-element.74), channel_id=1, source_target_pairs={{0,1},{1,0},{2,3},{3,2},{4,5},{5,4},{6,7},{7,6},{8,9},{9,8},{10,11... | collective-permute-start | bytes 786440 | tf_op jit(solution)/shard_map/ppermute | solution.py:41
  15.7 8.7 %collective-permute-start.7 = (bf16[128,1024]{1,0:T(8,128)(2,1)S(1)}, bf16[128,1024]{1,0:T(8,128)(2,1)S(1)}, u32[]{:S(2)}, u32[]{:S(2)}) collective-permute-start(bf16[128,1024]{1,0:T(8,128)(2,1)S(1)} %shard_map.117), channel_id=1, source_target_pairs={{0,2},{1,3},{2,0},{3,1},{4,7},{5,6},{6,5},{7,4},{8,10},{9,11},{10,... | collective-permute-start | bytes 786440 | tf_op jit(solution)/shard_map/ppermute | solution.py:254
  20.1 4.9 %collective-permute-start.6 = (bf16[3,256,128]{2,1,0:T(8,128)(2,1)S(1)}, bf16[3,256,128]{2,1,0:T(8,128)(2,1)S(1)}, u32[]{:S(2)}, u32[]{:S(2)}) collective-permute-start(bf16[3,256,128]{2,1,0:T(8,128)(2,1)S(1)} %get-tuple-element.69), channel_id=1, source_target_pairs={{0,1},{1,0},{2,3},{3,2},{4,5},{5,4},{6,7},{7,6},{8,9},{9,8},{10,11... | collective-permute-start | bytes 589832 | tf_op jit(solution)/shard_map/ppermute | solution.py:41
  22.1 7.0 %collective-permute-start.1 = (bf16[3,256,128]{2,1,0:T(8,128)(2,1)S(1)}, bf16[3,256,128]{2,1,0:T(8,128)(2,1)S(1)}, u32[]{:S(2)}, u32[]{:S(2)}) collective-permute-start(bf16[3,256,128]{2,1,0:T(8,128)(2,1)S(1)} %get-tuple-element.64), channel_id=1, source_target_pairs={{0,1},{1,0},{2,3},{3,2},{4,5},{5,4},{6,7},{7,6},{8,9},{9,8},{10,11... | collective-permute-start | bytes 589832 | tf_op jit(solution)/shard_map/ppermute | solution.py:41
  22.2 7.0 %collective-permute-start.9 = (bf16[3,256,128]{2,1,0:T(8,128)(2,1)S(1)}, bf16[3,256,128]{2,1,0:T(8,128)(2,1)S(1)}, u32[]{:S(2)}, u32[]{:S(2)}) collective-permute-start(bf16[3,256,128]{2,1,0:T(8,128)(2,1)S(1)} %get-tuple-element.72), channel_id=1, source_target_pairs={{0,1},{1,0},{2,3},{3,2},{4,5},{5,4},{6,7},{7,6},{8,9},{9,8},{10,11... | collective-permute-start | bytes 589832 | tf_op jit(solution)/shard_map/ppermute | solution.py:41
  24.4 6.6 %collective-permute-start.13 = (bf16[128,1024]{1,0:T(8,128)(2,1)S(1)}, bf16[128,1024]{1,0:T(8,128)(2,1)S(1)}, u32[]{:S(2)}, u32[]{:S(2)}) collective-permute-start(bf16[128,1024]{1,0:T(8,128)(2,1)S(1)} %collective-permute-done.7.refs_0_.first.c), channel_id=1, source_target_pairs={{0,4},{4,0},{8,12},{12,8},{16,20},{20,16},{24,28},{28,24},{1,5},{5... | collective-permute-start | bytes 786440 | tf_op jit(solution)/shard_map/ppermute | solution.py:41
  25.0 8.0 %collective-permute-start.8 = (bf16[3,256,128]{2,1,0:T(8,128)(2,1)S(1)}, bf16[3,256,128]{2,1,0:T(8,128)(2,1)S(1)}, u32[]{:S(2)}, u32[]{:S(2)}) collective-permute-start(bf16[3,256,128]{2,1,0:T(8,128)(2,1)S(1)} %shard_map.118.refs_0_), channel_id=1, source_target_pairs={{0,2},{1,3},{2,0},{3,1},{4,6},{5,7},{6,4},{7,5},{8,10},{9,11},{10,... | collective-permute-start | bytes 589832 | tf_op jit(solution)/shard_map/ppermute | solution.py:41
  28.8 4.2 %collective-permute-start.12 = (bf16[1,256,128]{2,1,0:T(8,128)(2,1)S(1)}, bf16[1,256,128]{2,1,0:T(8,128)(2,1)S(1)}, u32[]{:S(2)}, u32[]{:S(2)}) collective-permute-start(bf16[1,256,128]{2,1,0:T(8,128)(2,1)S(1)} %shard_map.120), channel_id=1, source_target_pairs={{0,2},{1,3},{2,0},{3,1},{4,6},{5,7},{6,4},{7,5},{8,10},{9,11},{10,... | collective-permute-start | bytes 196616 | tf_op jit(solution)/shard_map/ppermute | solution.py:41
  36.8 3.4 %collective-permute-start.15 = (bf16[1,256,128]{2,1,0:T(8,128)(2,1)S(1)}, bf16[1,256,128]{2,1,0:T(8,128)(2,1)S(1)}, u32[]{:S(2)}, u32[]{:S(2)}) collective-permute-start(bf16[1,256,128]{2,1,0:T(8,128)(2,1)S(1)} %get-tuple-element.79), channel_id=1, source_target_pairs={{0,1},{1,0},{2,3},{3,2},{4,5},{5,4},{6,7},{7,6},{8,9},{9,8},{10,11... | collective-permute-start | bytes 196616 | tf_op jit(solution)/shard_map/ppermute | solution.py:41
  36.8 3.3 %collective-permute-start.18 = (bf16[1,256,128]{2,1,0:T(8,128)(2,1)S(1)}, bf16[1,256,128]{2,1,0:T(8,128)(2,1)S(1)}, u32[]{:S(2)}, u32[]{:S(2)}) collective-permute-start(bf16[1,256,128]{2,1,0:T(8,128)(2,1)S(1)} %get-tuple-element.83), channel_id=1, source_target_pairs={{0,1},{1,0},{2,3},{3,2},{4,5},{5,4},{6,7},{7,6},{8,9},{9,8},{10,11... | collective-permute-start | bytes 196616 | tf_op jit(solution)/shard_map/ppermute | solution.py:41
  39.0 4.9 %collective-permute-start.14 = (bf16[1,512,128]{2,1,0:T(8,128)(2,1)S(1)}, bf16[1,512,128]{2,1,0:T(8,128)(2,1)S(1)}, u32[]{:S(2)}, u32[]{:S(2)}) collective-permute-start(bf16[1,512,128]{2,1,0:T(8,128)(2,1)S(1)} %bitcast.17), channel_id=1, source_target_pairs={{0,2},{1,3},{2,0},{3,1},{4,6},{5,7},{6,4},{7,5},{8,10},{9,11},{10,... | collective-permute-start | bytes 393224 | tf_op jit(solution)/shard_map/ppermute | solution.py:41
  39.2 7.4 %collective-permute-start.19 = (bf16[1,512,128]{2,1,0:T(8,128)(2,1)S(1)}, bf16[1,512,128]{2,1,0:T(8,128)(2,1)S(1)}, u32[]{:S(2)}, u32[]{:S(2)}) collective-permute-start(bf16[1,512,128]{2,1,0:T(8,128)(2,1)S(1)} %bitcast.18), channel_id=1, source_target_pairs={{0,1},{1,0},{2,3},{3,2},{4,5},{5,4},{6,7},{7,6},{8,9},{9,8},{10,11... | collective-permute-start | bytes 393224 | tf_op jit(solution)/shard_map/ppermute | solution.py:41
  45.2 10.7 %collective-permute-start.25 = (bf16[3,512,128]{2,1,0:T(8,128)(2,1)S(1)}, bf16[3,512,128]{2,1,0:T(8,128)(2,1)S(1)}, u32[]{:S(2)}, u32[]{:S(2)}) collective-permute-start(bf16[3,512,128]{2,1,0:T(8,128)(2,1)S(1)} %shard_map.125.refs_1_.own), channel_id=1, source_target_pairs={{0,2},{1,3},{2,0},{3,1},{4,6},{5,7},{6,4},{7,5},{8,10},{9,11},{10,... | collective-permute-start | bytes 1179656 | tf_op jit(solution)/shard_map/ppermute | solution.py:41
  47.2 7.6 %collective-permute-start.21 = (bf16[512,256]{1,0:T(8,128)(2,1)S(1)}, bf16[512,256]{1,0:T(8,128)(2,1)S(1)}, u32[]{:S(2)}, u32[]{:S(2)}) collective-permute-start(bf16[512,256]{1,0:T(8,128)(2,1)S(1)} %get-tuple-element.90), channel_id=1, source_target_pairs={{0,4},{4,0},{8,12},{12,8},{16,20},{20,16},{24,28},{28,24},{1,5},{5... | collective-permute-start | bytes 786440 | tf_op jit(solution)/shard_map/ppermute | solution.py:41
  48.4 7.2 %collective-permute-start.22 = (bf16[256,512]{1,0:T(8,128)(2,1)S(1)}, bf16[256,512]{1,0:T(8,128)(2,1)S(1)}, u32[]{:S(2)}, u32[]{:S(2)}) collective-permute-start(bf16[256,512]{1,0:T(8,128)(2,1)S(1)} %get-tuple-element.92), channel_id=1, source_target_pairs={{0,8},{4,12},{8,0},{12,4},{16,24},{20,28},{24,16},{28,20},{1,9},{5... | collective-permute-start | bytes 786440 | tf_op jit(solution)/shard_map/ppermute | solution.py:41
  50.3 9.4 %collective-permute-start.26 = (bf16[3,512,128]{2,1,0:T(8,128)(2,1)S(1)}, bf16[3,512,128]{2,1,0:T(8,128)(2,1)S(1)}, u32[]{:S(2)}, u32[]{:S(2)}) collective-permute-start(bf16[3,512,128]{2,1,0:T(8,128)(2,1)S(1)} %shard_map.125.refs_1_.own), channel_id=1, source_target_pairs={{0,1},{1,0},{2,3},{3,2},{4,5},{5,4},{6,7},{7,6},{8,9},{9,8},{10,11... | collective-permute-start | bytes 1179656 | tf_op jit(solution)/shard_map/ppermute | solution.py:41
  55.9 3.8 %collective-permute-start.27 = (bf16[3,512,128]{2,1,0:T(8,128)(2,1)S(1)}, bf16[3,512,128]{2,1,0:T(8,128)(2,1)S(1)}, u32[]{:S(2)}, u32[]{:S(2)}) collective-permute-start(bf16[3,512,128]{2,1,0:T(8,128)(2,1)S(1)} %shard_map.133.far), channel_id=1, source_target_pairs={{0,1},{1,0},{2,3},{3,2},{4,5},{5,4},{6,7},{7,6},{8,9},{9,8},{10,11... | collective-permute-start | bytes 1179656 | tf_op jit(solution)/shard_map/ppermute | solution.py:41
  57.2 6.9 %collective-permute-start.23 = (bf16[256,256]{1,0:T(8,128)(2,1)S(1)}, bf16[256,256]{1,0:T(8,128)(2,1)S(1)}, u32[]{:S(2)}, u32[]{:S(2)}) collective-permute-start(bf16[256,256]{1,0:T(8,128)(2,1)S(1)} %get-tuple-element.94), channel_id=1, source_target_pairs={{0,8},{4,12},{8,0},{12,4},{16,24},{20,28},{24,16},{28,20},{1,9},{5... | collective-permute-start | bytes 393224 | tf_op jit(solution)/shard_map/ppermute | solution.py:41
  58.6 5.6 %collective-permute-start.24 = (bf16[256,256]{1,0:T(8,128)(2,1)S(1)}, bf16[256,256]{1,0:T(8,128)(2,1)S(1)}, u32[]{:S(2)}, u32[]{:S(2)}) collective-permute-start(bf16[256,256]{1,0:T(8,128)(2,1)S(1)} %get-tuple-element.96), channel_id=1, source_target_pairs={{0,4},{4,0},{8,12},{12,8},{16,20},{20,16},{24,28},{28,24},{1,5},{5... | collective-permute-start | bytes 393224 | tf_op jit(solution)/shard_map/ppermute | solution.py:41
  61.5 7.4 %collective-permute-start.31 = (bf16[512,256]{1,0:T(8,128)(2,1)S(1)}, bf16[512,256]{1,0:T(8,128)(2,1)S(1)}, u32[]{:S(2)}, u32[]{:S(2)}) collective-permute-start(bf16[512,256]{1,0:T(8,128)(2,1)S(1)} %get-tuple-element.98.refs_0_), channel_id=1, source_target_pairs={{0,4},{4,0},{8,12},{12,8},{16,20},{20,16},{24,28},{28,24},{1,5},{5... | collective-permute-start | bytes 786440 | tf_op jit(solution)/shard_map/ppermute | solution.py:41
  61.9 7.0 %collective-permute-start.32 = (bf16[256,512]{1,0:T(8,128)(2,1)S(1)}, bf16[256,512]{1,0:T(8,128)(2,1)S(1)}, u32[]{:S(2)}, u32[]{:S(2)}) collective-permute-start(bf16[256,512]{1,0:T(8,128)(2,1)S(1)} %get-tuple-element.106), channel_id=1, source_target_pairs={{0,8},{4,12},{8,0},{12,4},{16,24},{20,28},{24,16},{28,20},{1,9},{5... | collective-permute-start | bytes 786440 | tf_op jit(solution)/shard_map/ppermute | solution.py:41
  69.0 3.9 %collective-permute-start.33 = (bf16[256,256]{1,0:T(8,128)(2,1)S(1)}, bf16[256,256]{1,0:T(8,128)(2,1)S(1)}, u32[]{:S(2)}, u32[]{:S(2)}) collective-permute-start(bf16[256,256]{1,0:T(8,128)(2,1)S(1)} %get-tuple-element.109), channel_id=1, source_target_pairs={{0,8},{4,12},{8,0},{12,4},{16,24},{20,28},{24,16},{28,20},{1,9},{5... | collective-permute-start | bytes 393224 | tf_op jit(solution)/shard_map/ppermute | solution.py:41
  70.1 4.1 %collective-permute-start.34 = (bf16[256,256]{1,0:T(8,128)(2,1)S(1)}, bf16[256,256]{1,0:T(8,128)(2,1)S(1)}, u32[]{:S(2)}, u32[]{:S(2)}) collective-permute-start(bf16[256,256]{1,0:T(8,128)(2,1)S(1)} %get-tuple-element.111), channel_id=1, source_target_pairs={{0,4},{4,0},{8,12},{12,8},{16,20},{20,16},{24,28},{28,24},{1,5},{5... | collective-permute-start | bytes 393224 | tf_op jit(solution)/shard_map/ppermute | solution.py:41
  70.5 4.2 %collective-permute-start.28 = (bf16[128,512]{1,0:T(8,128)(2,1)S(1)}, bf16[128,512]{1,0:T(8,128)(2,1)S(1)}, u32[]{:S(2)}, u32[]{:S(2)}) collective-permute-start(bf16[128,512]{1,0:T(8,128)(2,1)S(1)} %get-tuple-element.100.refs_0_), channel_id=1, source_target_pairs={{0,2},{1,3},{2,0},{3,1},{4,6},{5,7},{6,4},{7,5},{8,10},{9,11},{10,... | collective-permute-start | bytes 393224 | tf_op jit(solution)/shard_map/ppermute | solution.py:41
  74.3 11.9 %collective-permute-start.35 = (bf16[128,512]{1,0:T(8,128)(2,1)S(1)}, bf16[128,512]{1,0:T(8,128)(2,1)S(1)}, u32[]{:S(2)}, u32[]{:S(2)}) collective-permute-start(bf16[128,512]{1,0:T(8,128)(2,1)S(1)} %get-tuple-element.113), channel_id=1, source_target_pairs={{0,2},{1,3},{2,0},{3,1},{4,6},{5,7},{6,4},{7,5},{8,10},{9,11},{10,... | collective-permute-start | bytes 393224 | tf_op jit(solution)/shard_map/ppermute | solution.py:41
  74.8 16.9 %collective-permute-start.29 = (bf16[128,512]{1,0:T(8,128)(2,1)S(1)}, bf16[128,512]{1,0:T(8,128)(2,1)S(1)}, u32[]{:S(2)}, u32[]{:S(2)}) collective-permute-start(bf16[128,512]{1,0:T(8,128)(2,1)S(1)} %get-tuple-element.101), channel_id=1, source_target_pairs={{0,0},{1,8},{2,18},{3,26},{4,4},{5,12},{6,22},{7,30},{8,1},{9,9},{... | collective-permute-start | bytes 393224 | tf_op jit(solution)/shard_map/ppermute | solution.py:412
  82.2 9.6 %collective-permute-start.30 = (bf16[128,512]{1,0:T(8,128)(2,1)S(1)}, bf16[128,512]{1,0:T(8,128)(2,1)S(1)}, u32[]{:S(2)}, u32[]{:S(2)}) collective-permute-start(bf16[128,512]{1,0:T(8,128)(2,1)S(1)} %get-tuple-element.102), channel_id=1, source_target_pairs={{0,16},{1,24},{2,2},{3,10},{4,20},{5,28},{6,6},{7,14},{8,17},{9,25... | collective-permute-start | bytes 393224 | tf_op jit(solution)/shard_map/ppermute | solution.py:412
  86.2 7.4 %collective-permute-start.36 = (bf16[128,512]{1,0:T(8,128)(2,1)S(1)}, bf16[128,512]{1,0:T(8,128)(2,1)S(1)}, u32[]{:S(2)}, u32[]{:S(2)}) collective-permute-start(bf16[128,512]{1,0:T(8,128)(2,1)S(1)} %get-tuple-element.114), channel_id=1, source_target_pairs={{0,0},{1,8},{2,18},{3,26},{4,4},{5,12},{6,22},{7,30},{8,1},{9,9},{... | collective-permute-start | bytes 393224 | tf_op jit(solution)/shard_map/ppermute | solution.py:412
  88.9 8.1 %collective-permute-start.37 = (bf16[128,512]{1,0:T(8,128)(2,1)S(1)}, bf16[128,512]{1,0:T(8,128)(2,1)S(1)}, u32[]{:S(2)}, u32[]{:S(2)}) collective-permute-start(bf16[128,512]{1,0:T(8,128)(2,1)S(1)} %get-tuple-element.115), channel_id=1, source_target_pairs={{0,16},{1,24},{2,2},{3,10},{4,20},{5,28},{6,6},{7,14},{8,17},{9,25... | collective-permute-start | bytes 393224 | tf_op jit(solution)/shard_map/ppermute | solution.py:412
  (10 other events, 39.7 us)
